TPU v7x, 32 devices: a whole 2x2x4 slice. The times are simulated.
32 devices in a mesh: dp: 4 (over x, core), latent: 8 (over z, y).
Axes of the slice: x: 2, y: 2, z: 4, core: 2. Of those that a mesh axis runs over, the one named last changes fastest.
Arguments:
- activations: bfloat16 [4096, 8192], P(('dp', 'latent')), may hold values from -6 to 6
- owner_ids: int32 [4096, 2], P(('dp', 'latent')), may hold values from 0 to 7, all different within a row; in each aligned block of 128 rows (0 to 127, 128 to 255, ...) at most 34 rows name the same one
- block_mask: int32 [4096, 2, 8], P(('dp', 'latent')), may hold values 0 or 1
- latent_codes: bfloat16 [4096, 2, 1024], P(('dp', 'latent')), may hold values from 0.099609375 to 4
- w_dec: bfloat16 [8192, 8192], P('latent', 'dp'), may hold values from -0.125 to 0.125
- b_dec: float32 [8192], replicated, may hold values from -3 to 3
Outputs:
- rebuilt: bfloat16 [4096, 8192], P(('dp', 'latent'))
- decoder_grad: bfloat16 [8192, 8192], P('latent', 'dp')
Inputs may be any that keep to these rules, and one draw needn't show every extreme that they name: `owner_ids`: each row names 2 different owners; among the rows of one device no owner is named more than 34 times, and in every draw some device names some owner exactly 34 times.
All inputs are finite; a program needn't handle non-finite values. No bound on the sum of `block_mask` on one device may be relied on, other than what follows from the above.
Results may differ from a plain program's by a relative error of at most 0.0047.
Values may be sent and summed in bfloat16 or wider, within the bound.
No kernel may reach another device: no remote copies, remote signals or barrier semaphores. Data moves between devices by JAX's collectives and lax.ppermute only.
A program may use at most 128 MiB of HBM per device.

v0:
```python
import jax
import jax.numpy as jnp
from jax import lax
from jax.sharding import PartitionSpec as P

loss_scale = 1.0 / 32.0


def on_device(activations, owner_ids, block_mask, latent_codes, w_dec, b_dec):
    row_count, visit_count = owner_ids.shape
    block_count = block_mask.shape[2]
    slab_width = latent_codes.shape[2]
    block_width = slab_width // block_count
    model_width = activations.shape[1]
    owners = lax.axis_size("latent")
    groups = lax.axis_size("dp")
    capacity = row_count * visit_count // owners + 2
    live = block_mask.astype(latent_codes.dtype)[:, :, :, None]
    used = (latent_codes.reshape(row_count, visit_count, block_count, block_width) * live).reshape(
        -1, slab_width
    )
    onehot = (owner_ids[:, :, None] == lax.broadcasted_iota(jnp.int32, (1, 1, owners), 2)).astype(
        jnp.int32
    )
    per_row = jnp.sum(onehot, axis=1)
    before = jnp.cumsum(per_row, axis=0) - per_row
    position = jnp.sum(onehot * before[:, None, :], axis=2)
    target_slot = (owner_ids * capacity + position).reshape(-1)
    outgoing = jnp.zeros((owners * capacity, slab_width), latent_codes.dtype)
    outgoing = outgoing.at[target_slot].set(used).reshape(owners, capacity, slab_width)
    arrived = lax.all_to_all(outgoing, "latent", split_axis=0, concat_axis=0, tiled=True)
    copies = lax.all_gather(arrived, "dp", axis=0, tiled=True)
    arrived_flat = arrived.reshape(owners * capacity, slab_width)
    decoded = jnp.dot(
        arrived_flat,
        lax.all_gather(w_dec, "dp", axis=1, tiled=True),
        preferred_element_type=jnp.float32,
    ).astype(jnp.bfloat16)
    returned = lax.all_to_all(
        decoded.reshape(owners, capacity, model_width),
        "latent",
        split_axis=0,
        concat_axis=0,
        tiled=True,
    )
    returned = returned.reshape(owners * capacity, model_width)
    gathered = returned[target_slot].reshape(row_count, visit_count, model_width)
    rebuilt_wide = b_dec[None, :] + jnp.sum(gathered, axis=1, dtype=jnp.float32)
    errors = (rebuilt_wide - activations.astype(jnp.float32)).astype(jnp.bfloat16)
    error_slots = jnp.zeros((owners * capacity, model_width), jnp.bfloat16)
    error_slots = error_slots.at[target_slot].set(jnp.repeat(errors, visit_count, axis=0))
    error_slots = error_slots.reshape(1, owners, capacity, model_width)
    error_parts = lax.all_to_all(
        lax.all_to_all(error_slots, "dp", split_axis=3, concat_axis=0, tiled=True),
        "latent",
        split_axis=1,
        concat_axis=1,
        tiled=True,
    )
    error_parts = error_parts.reshape(groups * owners, capacity, error_parts.shape[3])
    gradient = (
        jnp.einsum("nsi,nsd->id", copies, error_parts, preferred_element_type=jnp.float32)
        * loss_scale
    )
    return (rebuilt_wide.astype(jnp.bfloat16), gradient.astype(jnp.bfloat16))


def solution(mesh):
    placed = (
        P(("dp", "latent"), None),
        P(("dp", "latent"), None),
        P(("dp", "latent"), None, None),
        P(("dp", "latent"), None, None),
        P("latent", "dp"),
        P(),
    )
    return jax.shard_map(
        on_device,
        mesh=mesh,
        in_specs=placed,
        out_specs=(P(("dp", "latent"), None), P("latent", "dp")),
        check_vma=False,
    )
```

profile of v0, /device:TPU:0, one launch (start us, length us, event | category | flops | bytes accessed | tf_op | source)
XLA Modules:
  0.0 636.7 jit_solution(6496495569384241110)
XLA Ops:
  7.2 0.0 copy-start.3
  7.2 0.0 copy-start.4
  7.2 0.0 copy-start.1
  7.2 0.0 all-gather.3.cloned.1.call-start
  7.2 0.7 all-gather.3.cloned.1.call-update
  7.9 0.7 convert_reduce_fusion
  8.6 0.1 copy.24
  8.7 0.2 reduce_window_sum.11
  9.0 0.0 copy-done.3
  9.0 0.1 copy.27
  9.1 0.1 reshape.77
  9.3 0.0 copy-done.4
  9.3 0.1 copy.28
  9.4 0.0 copy-done.1
  9.4 0.2 reshape.78
  9.6 0.3 mul.35
  10.0 1.9 scatter_custom_fusion
  11.8 0.2 reshape.79
  12.0 24.8 %all_to_all.33 = bf16[8,34,1024]{2,1,0:T(8,128)(2,1)S(1)} all-to-all(bf16[8,34,1024]{2,1,0:T(8,128)(2,1)S(1)} %reshape.79), channel_id=1, replica_groups=mesh['dp'=4,'latent'=8] {'latent'}, dimensions={0} | all-to-all | bytes 1114112 | tf_op jit(solution)/shard_map/all_to_all | solution.py:31
  36.8 0.2 reshape.80
  36.9 81.3 %all-gather.3.cloned.1.call-done = bf16[1024,8192]{1,0:T(8,128)(2,1)} async-done(((bf16[1024,2048]{1,0:T(8,128)(2,1)}), bf16[1024,8192]{1,0:T(8,128)(2,1)}) %all-gather.3.cloned.1.call-update) | async-done | bytes 16777232 | tf_op jit(solution)/shard_map/all_gather | solution.py:36
  118.2 12.1 %convolution_convert_fusion = bf16[272,8192]{1,0:T(8,128)(2,1)} fusion(bf16[272,1024]{1,0:T(8,128)(2,1)S(1)} %reshape.80, bf16[1024,8192]{1,0:T(8,128)(2,1)} %all-gather.3.cloned.1.call-done), kind=kOutput, calls=%fused_computation.3 | convolution fusion | flops 4565630976 | bytes 21790720 | tf_op jit(solution)/shard_map/dot_general | solution.py:34
  130.4 4.7 reshape.81
  135.1 6.0 all-to-all-start.1
  141.1 116.1 %all-to-all-done.1 = bf16[8,34,8192]{2,1,0:T(8,128)(2,1)} async-done(((bf16[8,34,8192]{2,1,0:T(8,128)(2,1)}), bf16[8,34,8192]{2,1,0:T(8,128)(2,1)}, u32[]{:S(2)}, u32[]{:S(2)}) %all-to-all-start.1) | async-done | bytes 4456480 | tf_op jit(solution)/shard_map/all_to_all | solution.py:39
  257.2 4.7 reshape.82
  261.9 11.8 %gather_fusion = bf16[256,8192]{1,0:T(8,128)(2,1)} fusion(bf16[272,8192]{1,0:T(8,128)(2,1)} %reshape.82, s32[1024]{0:T(1024)S(1)} %pad_clamp_fusion), kind=kCustom, calls=%fused_computation | custom fusion | bytes 8389632 | tf_op jit(solution)/shard_map/gather | solution.py:47
  273.8 9.7 %reshape.86 = f32[128,2,8192]{2,1,0:T(2,128)} reshape(bf16[256,8192]{1,0:T(8,128)(2,1)} %gather_fusion) | data formatting | bytes 12582912 | tf_op jit(solution)/shard_map/convert_element_type | solution.py:48
  283.5 13.5 %reduce_sum.29 = f32[128,8192]{1,0:T(8,128)} reduce(f32[128,2,8192]{2,1,0:T(2,128)} %reshape.86, f32[]{:T(128)} %constant.4.clone.1), dimensions={1}, to_apply=%region_4.5 | reduce | flops 1048576 | bytes 12582916 | tf_op jit(solution)/shard_map/reduce_sum | solution.py:48
  297.0 0.0 copy-done
  297.0 0.0 copy-done.2
  297.0 4.1 subtract_convert_fusion
  301.1 4.1 broadcast_in_dim.8
  305.2 7.4 %reshape.107 = bf16[256,8192]{1,0:T(8,128)(2,1)} reshape(bf16[128,2,8192]{2,1,0:T(2,128)(2,1)} %broadcast_in_dim.8) | data formatting | bytes 8388608 | tf_op jit(solution)/shard_map/reshape | solution.py:51
  312.6 10.2 %scatter_custom_fusion.1 = bf16[272,8192]{1,0:T(8,128)(2,1)} fusion(s32[256]{0:T(256)S(1)} %bitcast.30, bf16[256,8192]{1,0:T(8,128)(2,1)} %reshape.107, bf16[]{:T(256)} %constant.6.clone.1), kind=kCustom, calls=%fused_computation.11 | custom fusion | bytes 4456960 | tf_op jit(solution)/shard_map/scatter | solution.py:51
  322.9 4.9 reshape.84
  327.7 17.6 %copy.30 = bf16[1,8,34,8192]{2,1,0,3:T(8,128)(2,1)} copy(bf16[1,8,34,8192]{3,2,1,0:T(8,128)(2,1)} %reshape.84) | data formatting | bytes 8912896 | tf_op jit(solution)/shard_map/reshape | solution.py:52
  345.3 45.9 %reshape.116 = bf16[4,2,278528]{2,1,0:T(2,128)(2,1)} reshape(bf16[8192,1,8,34]{3,2,1,0:T(8,128)(2,1)} %bitcast.24) | data formatting | bytes 8912896
  391.2 57.2 %all_to_all.34 = bf16[4,2,278528]{2,1,0:T(2,128)(2,1)} all-to-all(bf16[4,2,278528]{2,1,0:T(2,128)(2,1)} %reshape.116), channel_id=1, replica_groups=mesh['dp'=4,'latent'=8] {'dp'}, dimensions={0} | all-to-all | bytes 8912896 | tf_op jit(solution)/shard_map/all_to_all | solution.py:54
  448.4 48.8 %reshape.117 = bf16[8192,1,8,34]{3,2,1,0:T(8,128)(2,1)} reshape(bf16[4,2,278528]{2,1,0:T(2,128)(2,1)} %all_to_all.34) | data formatting | bytes 8912896
  497.2 18.8 %copy.35 = bf16[1,8,34,4,2048]{4,3,2,1,0:T(4,128)(2,1)} copy(bf16[1,8,34,4,2048]{2,1,4,3,0:T(8,128)(2,1)} %bitcast.25) | data formatting | bytes 8912896 | tf_op jit(solution)/shard_map/all_to_all | solution.py:54
  516.0 4.6 all-to-all-start.3
  520.6 0.0 all-gather.5.cloned.1.call-start
  520.7 1.1 copy.29
  521.8 0.0 all-gather.5.cloned.1.call-update
  521.8 25.5 %all-gather.5.cloned.1.call-done = bf16[32,34,1024]{2,0,1:T(8,128)(2,1)} async-done(((bf16[8,34,1024]{2,0,1:T(8,128)(2,1)}), bf16[32,34,1024]{2,0,1:T(8,128)(2,1)}) %all-gather.5.cloned.1.call-update) | async-done | bytes 2228240 | tf_op jit(solution)/shard_map/all_gather | solution.py:32
  547.4 72.0 %all-to-all-done.3 = bf16[4,8,34,2048]{3,0,2,1:T(4,128)(2,1)} async-done(((bf16[4,8,34,2048]{3,0,2,1:T(4,128)(2,1)}), bf16[4,8,34,2048]{3,0,2,1:T(4,128)(2,1)}, u32[]{:S(2)}, u32[]{:S(2)}) %all-to-all-start.3) | async-done | bytes 4456480 | tf_op jit(solution)/shard_map/all_to_all | solution.py:53
  619.3 10.1 %fusion = bf16[1024,2048]{1,0:T(8,128)(2,1)} fusion(bf16[32,34,1024]{2,0,1:T(8,128)(2,1)} %all-gather.5.cloned.1.call-done, bf16[4,8,34,2048]{3,0,2,1:T(4,128)(2,1)} %all-to-all-done.3), kind=kOutput, calls=%fused_computation.5 | convolution fusion | flops 4567597056 | bytes 10878976 | tf_op jit(solution)/shard_map/nsi,nsd->id/dot_general | solution.py:62
  (9 shorter events, 0.1 us)
Async XLA Ops:
  7.2 1.8 copy-start.3
  7.2 2.1 copy-start.4
  7.2 2.2 copy-start.1
  7.2 111.0 %all-gather.3.cloned.1.call-start = ((), (), s32[]{:S(2)}) async-start(), calls=%async_computation.4 | async-start | bytes 20971520 | tf_op jit(solution)/shard_map/all_gather | solution.py:36
  135.1 122.1 %all-to-all-start.1 = ((bf16[8,34,8192]{2,1,0:T(8,128)(2,1)}), bf16[8,34,8192]{2,1,0:T(8,128)(2,1)}, u32[]{:S(2)}, u32[]{:S(2)}) async-start(bf16[8,34,8192]{2,1,0:T(8,128)(2,1)} %reshape.81), calls=%async_computation.1 | async-start | bytes 10485760 | tf_op jit(solution)/shard_map/all_to_all | solution.py:39
  283.5 13.5 %copy-start = (bf16[128,8192]{1,0:T(8,128)(2,1)S(1)}, bf16[128,8192]{1,0:T(8,128)(2,1)}, u32[]{:S(2)}) copy-start(bf16[128,8192]{1,0:T(8,128)(2,1)} %param.6) | copy-start | bytes 6291460
  283.5 13.5 %copy-start.2 = (f32[8192]{0:T(1024)S(1)}, f32[8192]{0:T(1024)}, u32[]{:S(2)}) copy-start(f32[8192]{0:T(1024)} %param.11) | copy-start | bytes 98308
  516.0 103.3 %all-to-all-start.3 = ((bf16[4,8,34,2048]{3,0,2,1:T(4,128)(2,1)}), bf16[4,8,34,2048]{3,0,2,1:T(4,128)(2,1)}, u32[]{:S(2)}, u32[]{:S(2)}) async-start(bf16[4,8,34,2048]{3,0,2,1:T(4,128)(2,1)} %bitcast.26), calls=%async_computation.3 | async-start | bytes 8912896 | tf_op jit(solution)/shard_map/all_to_all | solution.py:53
  520.6 26.7 %all-gather.5.cloned.1.call-start = ((), (), s32[]{:S(2)}) async-start(), calls=%async_computation.5 | async-start | bytes 2785280 | tf_op jit(solution)/shard_map/all_gather | solution.py:32
Sparse Core Ops, SparseCore 0:
  9.6 108.6 all-gather.2
  523.6 23.6 all-gather.4
where the time goes:
time: 643 us; the launch traced here: 637 us
  waiting for transfers between devices  296 us (46%)
  local copies, waits for them, and re-layouts  191 us (30%)
  blocking collectives  81.9 us (13%)
  matrix products  22.2 us (3%)
  other arithmetic  20.4 us (3%)
  between operations  14.6 us (2%)
  starting transfers between devices  10.7 us (2%)
    all_to_all x1, waiting for transfers between devices, on_device(): lax.all_to_all(decoded.reshape(owners, capacity, model_width), 'latent',...  116 us
    unnamed x12, local copies, waits for them, and re-layouts  94.8 us
    all_gather x1, waiting for transfers between devices, on_device(): lax.all_gather(w_dec, 'dp', axis=1, tiled=True)  81.3 us
    all_to_all x1, waiting for transfers between devices, on_device(): lax.all_to_all(lax.all_to_all(error_slots, 'dp', split_axis=3, concat_axi...  72 us
    all_to_all x1, blocking collectives, on_device(): lax.all_to_all(error_slots, 'dp', split_axis=3, concat_axis=0, tiled=True)  57.2 us
    all_gather x1, waiting for transfers between devices, on_device(): copies = lax.all_gather(arrived, 'dp', axis=0, tiled=True)  25.5 us
    all_to_all x1, blocking collectives, on_device(): lax.all_to_all(outgoing, 'latent', split_axis=0, concat_axis=0, tiled=True)  24.8 us
    reshape x2, local copies, waits for them, and re-layouts, on_device(): error_slots = error_slots.reshape(1, owners, capacity, model_width)  22.4 us
  transfers between devices with their start and end apart: 4, of which 4 were waited for; matrix products, arithmetic and copies ran while one was open for 1% of the time, Pallas kernels for 0%

commit v1 on v0

v1 whole, which is shorter than its diff:
```python
import functools

import jax
import jax.numpy as jnp
from jax import lax
from jax.experimental import pallas as pl
from jax.experimental.pallas import tpu as pltpu
from jax.sharding import PartitionSpec as P

loss_scale = 1.0 / 32.0
SPARE = 2
STACK = 8
F32 = jnp.float32
BF16 = jnp.bfloat16


def mm(a, b):
    return jnp.dot(a, b, preferred_element_type=F32)


def swap_matrix(outer, inner):
    size = outer * inner * SPARE
    to = lax.broadcasted_iota(jnp.int32, (size, size), 0)
    at = lax.broadcasted_iota(jnp.int32, (size, size), 1)
    to_inner, to_outer = to // (outer * SPARE), to % (outer * SPARE) // SPARE
    at_outer, at_inner = at // (inner * SPARE), at % (inner * SPARE) // SPARE
    same = (to_inner == at_inner) & (to_outer == at_outer) & (to % SPARE == at % SPARE)
    return same.astype(F32).astype(BF16)


def pack_kernel(me_ref, owner_ref, mask_ref, codes_ref, *outs):
    messages, (pick_ref, pick_spare_ref, place_ref, place_spare_ref) = outs[:-4], outs[-4:]
    owners = len(messages)
    rows, visits = owner_ref.shape
    width = codes_ref.shape[1] // visits
    blocks = mask_ref.shape[1] // visits
    block = width // blocks
    main = rows * visits // owners
    slots = owners * (main + SPARE)
    relative = owner_ref[...] ^ me_ref[0]
    eye = lax.broadcasted_iota(jnp.int32, (rows, rows), 0) == lax.broadcasted_iota(jnp.int32, (rows, rows), 1)
    columns = [relative[:, g : g + 1] for g in range(visits)]
    lanes = [jnp.sum(jnp.where(eye, column, 0), axis=0, keepdims=True) for column in columns]
    column, lane = jnp.concatenate(columns, axis=0), jnp.concatenate(lanes, axis=1)
    total = rows * visits
    down = lax.broadcasted_iota(jnp.int32, (total, total), 0)
    across = lax.broadcasted_iota(jnp.int32, (total, total), 1)
    same = column == lane

    def slot_of(owner, place):
        return jnp.where(place < main, owner * main + place, owners * main + owner * SPARE + place - main)

    slot_lane = slot_of(lane, jnp.sum(jnp.where(same & (down < across), 1, 0), axis=0, keepdims=True))
    slot_column = slot_of(column, jnp.sum(jnp.where(same & (across < down), 1, 0), axis=1, keepdims=True))
    place = (lax.broadcasted_iota(jnp.int32, (slots, total), 0) == slot_lane).astype(F32)
    pick = (lax.broadcasted_iota(jnp.int32, (total, slots), 1) == slot_column).astype(F32)
    place_rows = sum(place[:, g * rows : (g + 1) * rows] for g in range(visits)).astype(BF16)
    pick_rows = sum(pick[g * rows : (g + 1) * rows, :] for g in range(visits)).astype(BF16)
    pick_ref[...] = pick_rows[:, : owners * main]
    pick_spare_ref[...] = pick_rows[:, owners * main :]
    place_ref[...] = place_rows[: owners * main, :]
    place_spare_ref[...] = place_rows[owners * main :, :]
    used = jnp.concatenate(
        [
            jnp.concatenate(
                [
                    codes_ref[:, g * width + b * block : g * width + (b + 1) * block]
                    * mask_ref[:, g * blocks + b : g * blocks + b + 1].astype(F32).astype(BF16)
                    for b in range(blocks)
                ],
                axis=1,
            )
            for g in range(visits)
        ],
        axis=0,
    )
    sorted_codes = mm(place.astype(BF16), used).astype(BF16)
    part = width // STACK
    for k in range(owners):
        for q in range(STACK):
            messages[k][q * main : (q + 1) * main, :] = sorted_codes[
                k * main : (k + 1) * main, q * part : (q + 1) * part
            ]
    spare = jnp.concatenate(
        [sorted_codes[owners * main :, q * part : (q + 1) * part] for q in range(STACK)], axis=0
    )
    spare = mm(swap_matrix(STACK, owners), spare).astype(BF16)
    for k in range(owners):
        messages[k][STACK * main :, :] = spare[k * STACK * SPARE : (k + 1) * STACK * SPARE, :]


def unpack_kernel(*refs):
    messages, out_ref = refs[:-1], refs[-1]
    owners = len(messages)
    main = messages[0].shape[0] // STACK - SPARE
    part = messages[0].shape[1]
    for q in range(STACK):
        for k in range(owners):
            out_ref[k * main : (k + 1) * main, q * part : (q + 1) * part] = messages[k][
                q * main : (q + 1) * main, :
            ]
    spare = jnp.concatenate([message[STACK * main :, :] for message in messages], axis=0)
    spare = mm(swap_matrix(owners, STACK), spare).astype(BF16)
    for q in range(STACK):
        out_ref[owners * main :, q * part : (q + 1) * part] = spare[
            q * owners * SPARE : (q + 1) * owners * SPARE, :
        ]


def decode_kernel(codes_ref, w_ref, *rest):
    messages, spare_ref = rest[:-1], rest[-1]
    owners = len(messages)
    main = messages[0].shape[0] // STACK - SPARE
    q = pl.program_id(0)
    term = mm(codes_ref[...], w_ref[...]).astype(BF16)
    at = pl.multiple_of(q * main, main)
    for k in range(owners):
        messages[k][pl.ds(at, main), :] = term[k * main : (k + 1) * main, :]
    spare_ref[pl.ds(pl.multiple_of(q * owners * SPARE, owners * SPARE), owners * SPARE), :] = term[
        owners * main :, :
    ]

    @pl.when(q == STACK - 1)
    def _():
        spare = mm(swap_matrix(STACK, owners), spare_ref[...]).astype(BF16)
        for k in range(owners):
            messages[k][STACK * main :, :] = spare[k * STACK * SPARE : (k + 1) * STACK * SPARE, :]


def combine_kernel(owners, place_in_ref, pick_ref, pick_spare_ref, place_ref, place_spare_ref, b_ref, act_ref, *rest):
    terms, rest = rest[:owners], rest[owners:]
    rebuilt_ref, messages, (spare_in_ref, spare_out_ref) = rest[-3 - owners], rest[-2 - owners : -2], rest[-2:]
    main = terms[0].shape[0] // STACK - SPARE
    q = pl.program_id(0)

    @pl.when(q == 0)
    def _():
        spare = jnp.concatenate([term[STACK * main :, :] for term in terms], axis=0)
        spare_in_ref[...] = mm(swap_matrix(owners, STACK), spare).astype(BF16)

    at = pl.multiple_of(q * main, main)
    spare_at = pl.ds(pl.multiple_of(q * owners * SPARE, owners * SPARE), owners * SPARE)
    arrived = jnp.concatenate([term[pl.ds(at, main), :] for term in terms], axis=0)
    wide = b_ref[...] + (mm(pick_ref[...], arrived) + mm(pick_spare_ref[...], spare_in_ref[spare_at, :]))
    rebuilt_ref[...] = wide.astype(BF16)
    errors = (wide - act_ref[...].astype(F32)).astype(BF16)
    placed = mm(place_ref[...], errors).astype(BF16)
    for k in range(owners):
        messages[k][pl.ds(at, main), :] = placed[k * main : (k + 1) * main, :]
    spare_out_ref[spare_at, :] = mm(place_spare_ref[...], errors).astype(BF16)

    @pl.when(q == STACK - 1)
    def _():
        spare = mm(swap_matrix(STACK, owners), spare_out_ref[...]).astype(BF16)
        for k in range(owners):
            messages[k][STACK * main :, :] = spare[k * STACK * SPARE : (k + 1) * STACK * SPARE, :]


def turn_kernel(groups, *refs):
    codes, outs, spare_ref = refs[:groups], refs[groups : 2 * groups], refs[2 * groups]
    for j in range(groups):
        main = outs[j].shape[1]
        outs[j][...] = codes[j][:main, :].astype(F32).T.astype(BF16)
    spare = jnp.concatenate([code[outs[0].shape[1] :, :] for code in codes], axis=0)
    spare_ref[...] = spare.astype(F32).T.astype(BF16)


def gradient_kernel(groups, owners, *refs):
    codes, spare_codes_ref = refs[:groups], refs[groups]
    messages = refs[groups + 1 : groups + 1 + groups * owners]
    out_ref, spare_ref = refs[-2:]
    main = messages[0].shape[0] // STACK - SPARE
    q = pl.program_id(0)

    @pl.when(q == 0)
    def _():
        swap = swap_matrix(owners, STACK)
        for j in range(groups):
            spare = jnp.concatenate([m[STACK * main :, :] for m in messages[j * owners : (j + 1) * owners]], axis=0)
            spare_ref[j] = mm(swap, spare).astype(BF16)

    at = pl.multiple_of(q * main, main)
    spare_at = pl.ds(pl.multiple_of(q * owners * SPARE, owners * SPARE), owners * SPARE)
    total = mm(spare_codes_ref[...], jnp.concatenate([spare_ref[j, spare_at, :] for j in range(groups)], axis=0))
    for j in range(groups):
        arrived = jnp.concatenate([m[pl.ds(at, main), :] for m in messages[j * owners : (j + 1) * owners]], axis=0)
        total += mm(codes[j][...], arrived)
    out_ref[...] = (total * loss_scale).astype(BF16)


def whole(shape):
    return pl.BlockSpec(shape, lambda *_: (0,) * len(shape))


def params(mib):
    return pltpu.CompilerParams(vmem_limit_bytes=mib * 2**20)


def cost(flops, moved):
    return pl.CostEstimate(flops=int(flops), bytes_accessed=int(moved), transcendentals=0)


def on_device(activations, owner_ids, block_mask, latent_codes, w_dec, b_dec):
    rows, visits = owner_ids.shape
    width = latent_codes.shape[2]
    model = activations.shape[1]
    owners, groups = lax.axis_size("latent"), lax.axis_size("dp")
    main = rows * visits // owners
    slots = owners * (main + SPARE)
    depth = STACK * (main + SPARE)
    local = w_dec.shape[1]
    part = local // STACK
    me, group = lax.axis_index("latent"), lax.axis_index("dp")

    def move(x, j, k):
        if j == 0 and k == 0:
            return x
        pairs = [(i, i ^ (j * owners + k)) for i in range(groups * owners)]
        return lax.ppermute(x, ("dp", "latent"), pairs)

    far_first = list(range(owners - 1, -1, -1))

    packed = pl.pallas_call(
        pack_kernel,
        grid_spec=pltpu.PrefetchScalarGridSpec(
            num_scalar_prefetch=1,
            grid=(1,),
            in_specs=[whole((rows, visits)), whole((rows, visits * block_mask.shape[2])), whole((rows, visits * width))],
            out_specs=[whole((depth, width // STACK))] * owners
            + [whole((rows, owners * main)), whole((rows, owners * SPARE))]
            + [whole((owners * main, rows)), whole((owners * SPARE, rows))],
        ),
        out_shape=[jax.ShapeDtypeStruct((depth, width // STACK), BF16)] * owners
        + [
            jax.ShapeDtypeStruct(s, BF16)
            for s in [(rows, owners * main), (rows, owners * SPARE), (owners * main, rows), (owners * SPARE, rows)]
        ],
        compiler_params=params(16),
        cost_estimate=cost(2 * slots * rows * visits * width, 4 * rows * visits * width),
        name="pack",
    )(
        me.reshape(1),
        owner_ids,
        block_mask.reshape(rows, -1),
        latent_codes.reshape(rows, -1),
    )
    outgoing, picks = packed[:owners], packed[owners:]
    arrived = [None] * owners
    for k in far_first:
        arrived[k] = move(outgoing[k], 0, k)
    codes = [None] * groups
    codes[0] = pl.pallas_call(
        unpack_kernel,
        out_shape=jax.ShapeDtypeStruct((slots, width), BF16),
        compiler_params=params(8),
        cost_estimate=cost(0, 4 * slots * width),
        name="unpack",
    )(*arrived)
    for j in range(1, groups):
        low = j & -j
        codes[j] = move(codes[j ^ low], low, 0) if j != low else move(codes[0], j, 0)

    decode = pl.pallas_call(
        decode_kernel,
        grid=(STACK,),
        in_specs=[whole((slots, width)), pl.BlockSpec((width, part), lambda q: (0, q))],
        out_specs=[whole((depth, part))] * owners,
        out_shape=[jax.ShapeDtypeStruct((depth, part), BF16)] * owners,
        scratch_shapes=[pltpu.VMEM((STACK * owners * SPARE, part), BF16)],
        compiler_params=params(16),
        cost_estimate=cost(2 * slots * width * local, 2 * (width * local + slots * (width + local))),
        name="decode",
    )
    terms = [None] * groups
    for j in range(groups):
        decoded = decode(codes[j], w_dec)
        terms[j] = [None] * owners
        for k in far_first:
            terms[j][k] = move(decoded[k], j, k)

    rebuilt, errors = None, [None] * groups
    for j in range(groups):
        first = rebuilt is None
        outs = pl.pallas_call(
            functools.partial(combine_kernel, owners),
            grid_spec=pltpu.PrefetchScalarGridSpec(
                num_scalar_prefetch=1,
                grid=(STACK,),
                in_specs=[whole(p.shape) for p in picks]
                + [
                    pl.BlockSpec((1, part), lambda q, at: (0, at[0] * STACK + q)),
                    pl.BlockSpec((rows, part), lambda q, at: (0, at[0] * STACK + q)),
                ]
                + [whole((depth, part))] * owners
                + ([] if first else [pl.BlockSpec(memory_space=pl.ANY)]),
                out_specs=[pl.BlockSpec((rows, part), lambda q, at: (0, at[0] * STACK + q))]
                + [whole((depth, part))] * owners,
                scratch_shapes=[pltpu.VMEM((STACK * owners * SPARE, part), BF16)] * 2,
            ),
            out_shape=[jax.ShapeDtypeStruct((rows, model), BF16)]
            + [jax.ShapeDtypeStruct((depth, part), BF16)] * owners,
            input_output_aliases={} if first else {7 + owners: 0},
            compiler_params=params(16),
            cost_estimate=cost(4 * slots * rows * local, 2 * local * (2 * slots + 2 * rows)),
            name="combine",
        )((group ^ j).reshape(1), *picks, b_dec.reshape(1, -1), activations, *terms[j], *([] if first else [rebuilt]))
        rebuilt = outs[0]
        errors[j] = [None] * owners
        for k in far_first:
            errors[j][k] = move(outs[1 + k], j, k)

    turned = pl.pallas_call(
        functools.partial(turn_kernel, groups),
        out_shape=[jax.ShapeDtypeStruct((width, owners * main), BF16)] * groups
        + [jax.ShapeDtypeStruct((width, groups * owners * SPARE), BF16)],
        compiler_params=params(24),
        cost_estimate=cost(0, 4 * groups * slots * width),
        name="turn",
    )(*codes)
    gradient = pl.pallas_call(
        functools.partial(gradient_kernel, groups, owners),
        grid=(STACK,),
        in_specs=[whole(t.shape) for t in turned] + [whole((depth, part))] * (groups * owners),
        out_specs=pl.BlockSpec((width, part), lambda q: (0, q)),
        out_shape=jax.ShapeDtypeStruct((width, local), BF16),
        scratch_shapes=[pltpu.VMEM((groups, STACK * owners * SPARE, part), BF16)],
        compiler_params=params(32),
        cost_estimate=cost(2 * groups * slots * width * local, 2 * (width * local + groups * slots * (width + local))),
        name="gradient",
    )(*turned, *[m for j in range(groups) for m in errors[j]])
    return rebuilt, gradient


def on_device_wide(activations, owner_ids, block_mask, latent_codes, w_dec, b_dec):
    row_count, visit_count = owner_ids.shape
    block_count = block_mask.shape[2]
    slab_width = latent_codes.shape[2]
    block_width = slab_width // block_count
    model_width = activations.shape[1]
    owners = lax.axis_size("latent")
    groups = lax.axis_size("dp")
    capacity = row_count * visit_count // owners + SPARE
    live = block_mask.astype(latent_codes.dtype)[:, :, :, None]
    used = (latent_codes.reshape(row_count, visit_count, block_count, block_width) * live).reshape(-1, slab_width)
    onehot = (owner_ids[:, :, None] == lax.broadcasted_iota(jnp.int32, (1, 1, owners), 2)).astype(jnp.int32)
    per_row = jnp.sum(onehot, axis=1)
    before = jnp.cumsum(per_row, axis=0) - per_row
    position = jnp.sum(onehot * before[:, None, :], axis=2)
    target_slot = (owner_ids * capacity + position).reshape(-1)
    outgoing = jnp.zeros((owners * capacity, slab_width), latent_codes.dtype)
    outgoing = outgoing.at[target_slot].set(used).reshape(owners, capacity, slab_width)
    arrived = lax.all_to_all(outgoing, "latent", split_axis=0, concat_axis=0, tiled=True)
    copies = lax.all_gather(arrived, "dp", axis=0, tiled=True)
    decoded = mm(copies.reshape(-1, slab_width), w_dec).astype(BF16)
    local = w_dec.shape[1]
    returned = lax.all_to_all(
        decoded.reshape(groups * owners, capacity, local), ("dp", "latent"), split_axis=0, concat_axis=0, tiled=True
    )
    returned = returned.reshape(groups, owners * capacity, local)
    gathered = returned[:, target_slot].reshape(groups, row_count, visit_count, local)
    gathered = jnp.sum(gathered, axis=2, dtype=F32).transpose(1, 0, 2).reshape(row_count, model_width)
    rebuilt_wide = b_dec[None, :] + gathered
    errors = (rebuilt_wide - activations.astype(F32)).astype(BF16)
    parts = jnp.repeat(errors.reshape(row_count, groups, local).transpose(1, 0, 2), visit_count, axis=1)
    error_slots = jnp.zeros((groups, owners * capacity, local), BF16).at[:, target_slot].set(parts)
    error_parts = lax.all_to_all(
        error_slots.reshape(groups * owners, capacity, local), ("dp", "latent"), split_axis=0, concat_axis=0, tiled=True
    )
    gradient = jnp.einsum("nsi,nsd->id", copies, error_parts, preferred_element_type=F32) * loss_scale
    return rebuilt_wide.astype(BF16), gradient.astype(BF16)


def solution(mesh):
    placed = (
        P(("dp", "latent"), None),
        P(("dp", "latent"), None),
        P(("dp", "latent"), None, None),
        P(("dp", "latent"), None, None),
        P("latent", "dp"),
        P(),
    )

    def body(activations, owner_ids, block_mask, latent_codes, w_dec, b_dec):
        owners = mesh.shape["latent"]
        share = owner_ids.size // owners
        fits = share % 16 == 0 and owners * SPARE % 16 == 0 and w_dec.shape[1] % (128 * STACK) == 0
        pick = on_device if fits else on_device_wide
        return pick(activations, owner_ids, block_mask, latent_codes, w_dec, b_dec)

    return jax.shard_map(
        body,
        mesh=mesh,
        in_specs=placed,
        out_specs=(P(("dp", "latent"), None), P("latent", "dp")),
        check_vma=False,
    )
```

time: 643 us -> 311 us (0.48)
  waiting for transfers between devices: 296 us -> 61.6 us
  local copies, waits for them, and re-layouts: 191 us -> 51.9 us
  starting transfers between devices: 10.7 us -> 143 us
  blocking collectives: 81.9 us -> 0 us
  Pallas kernels: 0 us -> 49.3 us
  matrix products: 22.2 us -> 0 us
  other arithmetic: 20.4 us -> 0 us
  between operations: 14.6 us -> 1.17 us
    all_to_all x2 -> x0, waiting for transfers between devices: 188 us -> none  [the longest x1 116 us: on_device(): lax.all_to_all(decoded.reshape(owners, capacity, model_width), 'latent',...]
    ppermute x0 -> x72, starting transfers between devices: none -> 143 us  [move(): return lax.ppermute(x, ('dp', 'latent'), pairs)]
    all_gather x2 -> x0, waiting for transfers between devices: 107 us -> none  [the longest x1 81.3 us: on_device(): lax.all_gather(w_dec, 'dp', axis=1, tiled=True)]
    all_to_all x2 -> x0, blocking collectives: 81.9 us -> none  [the longest x1 57.2 us: on_device(): lax.all_to_all(error_slots, 'dp', split_axis=3, concat_axis=0, tiled=True)]
    ppermute x0 -> x72, waiting for transfers between devices: none -> 61.6 us  [move(): return lax.ppermute(x, ('dp', 'latent'), pairs)]
    pallas_call x0 -> x12, Pallas kernels: none -> 49.3 us  [the longest x4 20.9 us: on_device(): pl.pallas_call(functools.partial(combine_kernel, owners), grid_spec=pltpu...]
    unnamed x12 -> x184, local copies, waits for them, and re-layouts: 94.8 us -> 51.1 us
    reshape x9 -> x1, local copies, waits for them, and re-layouts: 39.9 us -> 0.79 us  [on_device(): block_mask.reshape(rows, -1)]
  transfers between devices with their start and end apart: 4 -> 72, of which waited for: 4 -> 17; matrix products, arithmetic and copies ran while one was open for 1% -> 0% of each run, Pallas kernels for 0% -> 13%
where the time goes in v1:
time: 311 us; the launch traced here: 307 us
  starting transfers between devices  143 us (46%)
  waiting for transfers between devices  61.6 us (20%)
  local copies, waits for them, and re-layouts  51.9 us (17%)
  Pallas kernels  49.3 us (16%)
    ppermute x72, starting transfers between devices, move(): return lax.ppermute(x, ('dp', 'latent'), pairs)  143 us
    ppermute x72, waiting for transfers between devices, move(): return lax.ppermute(x, ('dp', 'latent'), pairs)  61.6 us
    unnamed x184, local copies, waits for them, and re-layouts  51.1 us
    pallas_call x4, Pallas kernels, on_device(): pl.pallas_call(functools.partial(combine_kernel, owners), grid_spec=pltpu...  20.9 us
    pallas_call x4, Pallas kernels, on_device(): decoded = decode(codes[j], w_dec)  16.1 us
    pallas_call x1, Pallas kernels, on_device(): pl.pallas_call(functools.partial(gradient_kernel, groups, owners), grid=(...  9.47 us
  transfers between devices with their start and end apart: 72, of which 17 were waited for; matrix products, arithmetic and copies ran while one was open for 0% of the time, Pallas kernels for 13%

profile of v1, /device:TPU:0, one launch (start us, length us, event | category | flops | bytes accessed | tf_op | source)
XLA Modules:
  0.0 306.6 jit_solution(13183967500845242273)
XLA Ops:
  4.2 3.0 collective-permute-start
  8.7 3.0 collective-permute-start.3
  13.0 3.6 %collective-permute-start.5 = (bf16[272,128]{1,0:T(8,128)(2,1)S(1)}, bf16[272,128]{1,0:T(8,128)(2,1)S(1)}, u32[]{:S(2)}, u32[]{:S(2)}) collective-permute-start(bf16[272,128]{1,0:T(8,128)(2,1)S(1)} %get-tuple-element.97), channel_id=1, source_target_pairs={{0,6},{1,7},{2,4},{3,5},{4,2},{5,3},{6,0},{7,1},{8,14},{9,15},{10,... | collective-permute-start | bytes 208904 | tf_op jit(solution)/shard_map/ppermute | solution.py:219
  16.6 5.8 %collective-permute-done.4.refs_5_ = bf16[272,128]{1,0:T(8,128)(2,1)S(1)} collective-permute-done((bf16[272,128]{1,0:T(8,128)(2,1)S(1)}, bf16[272,128]{1,0:T(8,128)(2,1)S(1)}, u32[]{:S(2)}, u32[]{:S(2)}) %collective-permute-start.4) | collective-permute-done | bytes 69664 | tf_op jit(solution)/shard_map/ppermute | solution.py:219
  27.7 4.1 %decode.7 = (bf16[272,256]{1,0:T(8,128)(2,1)S(1)}, bf16[272,256]{1,0:T(8,128)(2,1)S(1)}, bf16[272,256]{1,0:T(8,128)(2,1)S(1)}, bf16[272,256]{1,0:T(8,128)(2,1)S(...) custom-call(bf16[272,1024]{1,0:T(8,128)(2,1)S(1)} %unpack.1.codes_re, ...), custom_call_target="tpu_custom_call" | custom-call | flops 1140850688 | bytes 5865472 | tf_op jit(solution)/shard_map/decode/pallas_call | solution.py:276
  32.3 2.6 collective-permute-start.35
  37.5 3.4 %collective-permute-start.37 = (bf16[272,256]{1,0:T(8,128)(2,1)S(1)}, bf16[272,256]{1,0:T(8,128)(2,1)S(1)}, u32[]{:S(2)}, u32[]{:S(2)}) collective-permute-start(bf16[272,256]{1,0:T(8,128)(2,1)S(1)} %get-tuple-element.127), channel_id=1, source_target_pairs={{0,4},{1,5},{2,6},{3,7},{4,0},{5,1},{6,2},{7,3},{8,12},{9,13},{10,... | collective-permute-start | bytes 417800 | tf_op jit(solution)/shard_map/ppermute | solution.py:219
  41.6 2.2 collective-permute-start.38
  43.8 2.9 collective-permute-done.36.rest_3_
  51.6 8.8 %collective-permute-done.38.rest_5_ = bf16[272,256]{1,0:T(8,128)(2,1)} collective-permute-done((bf16[272,256]{1,0:T(8,128)(2,1)}, bf16[272,256]{1,0:T(8,128)(2,1)}, u32[]{:S(2)}, u32[]{:S(2)}) %collective-permute-start.38) | collective-permute-done | bytes 139296 | tf_op jit(solution)/shard_map/ppermute | solution.py:219
  64.0 6.1 %combine.4 = (bf16[128,8192]{1,0:T(8,128)(2,1)}, bf16[272,256]{1,0:T(8,128)(2,1)S(1)}, bf16[272,256]{1,0:T(8,128)(2,1)S(1)}, bf16[272,256]{1,0:T(8,128)(2,1)}, b...) custom-call(s32[1]{0:T(128)} %bitcast.6.place_in_ref, ...), custom_call_target="tpu_custom_call" | custom-call | flops 285212672 | bytes 3276800 | tf_op jit(solution)/shard_map/combine/pallas_call | solution.py:284
  74.7 3.3 %decode.5 = (bf16[272,256]{1,0:T(8,128)(2,1)S(1)}, bf16[272,256]{1,0:T(8,128)(2,1)S(1)}, bf16[272,256]{1,0:T(8,128)(2,1)S(1)}, bf16[272,256]{1,0:T(8,128)(2,1)S(...) custom-call(bf16[272,1024]{1,0:T(8,128)(2,1)S(1)} %collective-permut, ...), custom_call_target="tpu_custom_call" | custom-call | flops 1140850688 | bytes 5865472 | tf_op jit(solution)/shard_map/decode/pallas_call | solution.py:276
  78.6 2.5 collective-permute-start.18
  81.1 5.6 %collective-permute-start.19 = (bf16[272,256]{1,0:T(8,128)(2,1)S(1)}, bf16[272,256]{1,0:T(8,128)(2,1)S(1)}, u32[]{:S(2)}, u32[]{:S(2)}) collective-permute-start(bf16[272,256]{1,0:T(8,128)(2,1)S(1)} %get-tuple-element.109), channel_id=1, source_target_pairs={{0,18},{1,19},{2,16},{3,17},{4,22},{5,23},{6,20},{7,21},{8,26},{9,... | collective-permute-start | bytes 417800 | tf_op jit(solution)/shard_map/ppermute | solution.py:219
  87.8 3.2 %collective-permute-start.21 = (bf16[272,256]{1,0:T(8,128)(2,1)S(1)}, bf16[272,256]{1,0:T(8,128)(2,1)S(1)}, u32[]{:S(2)}, u32[]{:S(2)}) collective-permute-start(bf16[272,256]{1,0:T(8,128)(2,1)S(1)} %get-tuple-element.111), channel_id=1, source_target_pairs={{0,20},{1,21},{2,22},{3,23},{4,16},{5,17},{6,18},{7,19},{8,28},{9,... | collective-permute-start | bytes 417800 | tf_op jit(solution)/shard_map/ppermute | solution.py:219
  91.0 11.1 %collective-permute-start.22 = (bf16[272,256]{1,0:T(8,128)(2,1)S(1)}, bf16[272,256]{1,0:T(8,128)(2,1)S(1)}, u32[]{:S(2)}, u32[]{:S(2)}) collective-permute-start(bf16[272,256]{1,0:T(8,128)(2,1)S(1)} %get-tuple-element.112), channel_id=1, source_target_pairs={{0,21},{1,20},{2,23},{3,22},{4,17},{5,16},{6,19},{7,18},{8,29},{9,... | collective-permute-start | bytes 417800 | tf_op jit(solution)/shard_map/ppermute | solution.py:219
  105.7 2.7 collective-permute-start.24
  108.4 4.3 %decode.6 = (bf16[272,256]{1,0:T(8,128)(2,1)S(1)}, bf16[272,256]{1,0:T(8,128)(2,1)S(1)}, bf16[272,256]{1,0:T(8,128)(2,1)S(1)}, bf16[272,256]{1,0:T(8,128)(2,1)S(...) custom-call(bf16[272,1024]{1,0:T(8,128)(2,1)} %collective-permute-do, ...), custom_call_target="tpu_custom_call" | custom-call | flops 1140850688 | bytes 5865472 | tf_op jit(solution)/shard_map/decode/pallas_call | solution.py:276
  121.4 2.6 collective-permute-start.31
  129.1 9.3 %collective-permute-done.30.rest_4_ = bf16[272,256]{1,0:T(8,128)(2,1)S(1)} collective-permute-done((bf16[272,256]{1,0:T(8,128)(2,1)S(1)}, bf16[272,256]{1,0:T(8,128)(2,1)S(1)}, u32[]{:S(2)}, u32[]{:S(2)}) %collective-permute-start.30) | collective-permute-done | bytes 139296 | tf_op jit(solution)/shard_map/ppermute | solution.py:219
  139.3 2.8 collective-permute-done.31.rest_5_
  143.5 2.9 collective-permute-start.44
  147.0 5.1 %collective-permute-start.45 = (bf16[272,256]{1,0:T(8,128)(2,1)}, bf16[272,256]{1,0:T(8,128)(2,1)}, u32[]{:S(2)}, u32[]{:S(2)}) collective-permute-start(bf16[272,256]{1,0:T(8,128)(2,1)} %get-tuple-element.145), channel_id=1, source_target_pairs={{0,5},{1,4},{2,7},{3,6},{4,1},{5,0},{6,3},{7,2},{8,13},{9,12},{10,... | collective-permute-start | bytes 417800 | tf_op jit(solution)/shard_map/ppermute | solution.py:219
  159.4 5.1 %combine.5 = (bf16[128,8192]{1,0:T(8,128)(2,1)}, bf16[272,256]{1,0:T(8,128)(2,1)S(1)}, bf16[272,256]{1,0:T(8,128)(2,1)}, bf16[272,256]{1,0:T(8,128)(2,1)}, bf16[...) custom-call(s32[1]{0:T(128)} %bitcast.5.place_in_ref, ...), custom_call_target="tpu_custom_call", output_to_operand_aliasing={{0}: (15, {})} | custom-call | flops 285212672 | bytes 3276800 | tf_op jit(solution)/shard_map/combine/pallas_call | solution.py:284
  165.9 4.9 %combine.6 = (bf16[128,8192]{1,0:T(8,128)(2,1)}, bf16[272,256]{1,0:T(8,128)(2,1)S(1)}, bf16[272,256]{1,0:T(8,128)(2,1)S(1)}, bf16[272,256]{1,0:T(8,128)(2,1)S(1)...) custom-call(s32[1]{0:T(128)} %bitcast.4.place_in_ref, ...), custom_call_target="tpu_custom_call", output_to_operand_aliasing={{0}: (15, {})} | custom-call | flops 285212672 | bytes 3276800 | tf_op jit(solution)/shard_map/combine/pallas_call | solution.py:284
  175.0 2.6 collective-permute-start.57
  179.2 4.1 %collective-permute-start.58 = (bf16[272,256]{1,0:T(8,128)(2,1)S(1)}, bf16[272,256]{1,0:T(8,128)(2,1)S(1)}, u32[]{:S(2)}, u32[]{:S(2)}) collective-permute-start(bf16[272,256]{1,0:T(8,128)(2,1)S(1)} %get-tuple-element.158), channel_id=1, source_target_pairs={{0,18},{1,19},{2,16},{3,17},{4,22},{5,23},{6,20},{7,21},{8,26},{9,... | collective-permute-start | bytes 417800 | tf_op jit(solution)/shard_map/ppermute | solution.py:219
  183.9 3.7 %collective-permute-start.59 = (bf16[272,256]{1,0:T(8,128)(2,1)S(1)}, bf16[272,256]{1,0:T(8,128)(2,1)S(1)}, u32[]{:S(2)}, u32[]{:S(2)}) collective-permute-start(bf16[272,256]{1,0:T(8,128)(2,1)S(1)} %get-tuple-element.159), channel_id=1, source_target_pairs={{0,19},{1,18},{2,17},{3,16},{4,23},{5,22},{6,21},{7,20},{8,27},{9,... | collective-permute-start | bytes 417800 | tf_op jit(solution)/shard_map/ppermute | solution.py:219
  189.1 3.5 %collective-permute-start.61 = (bf16[272,256]{1,0:T(8,128)(2,1)S(1)}, bf16[272,256]{1,0:T(8,128)(2,1)S(1)}, u32[]{:S(2)}, u32[]{:S(2)}) collective-permute-start(bf16[272,256]{1,0:T(8,128)(2,1)S(1)} %get-tuple-element.161), channel_id=1, source_target_pairs={{0,21},{1,20},{2,23},{3,22},{4,17},{5,16},{6,19},{7,18},{8,29},{9,... | collective-permute-start | bytes 417800 | tf_op jit(solution)/shard_map/ppermute | solution.py:219
  192.7 2.5 collective-permute-start.62
  195.2 4.3 %decode.4 = (bf16[272,256]{1,0:T(8,128)(2,1)S(1)}, bf16[272,256]{1,0:T(8,128)(2,1)S(1)}, bf16[272,256]{1,0:T(8,128)(2,1)S(1)}, bf16[272,256]{1,0:T(8,128)(2,1)S(...) custom-call(bf16[272,1024]{1,0:T(8,128)(2,1)} %collective-permute-do, ...), custom_call_target="tpu_custom_call" | custom-call | flops 1140850688 | bytes 5865472 | tf_op jit(solution)/shard_map/decode/pallas_call | solution.py:276
  200.2 3.2 %collective-permute-start.63 = (bf16[272,256]{1,0:T(8,128)(2,1)S(1)}, bf16[272,256]{1,0:T(8,128)(2,1)S(1)}, u32[]{:S(2)}, u32[]{:S(2)}) collective-permute-start(bf16[272,256]{1,0:T(8,128)(2,1)S(1)} %get-tuple-element.163), channel_id=1, source_target_pairs={{0,23},{1,22},{2,21},{3,20},{4,19},{5,18},{6,17},{7,16},{8,31},{9,... | collective-permute-start | bytes 417800 | tf_op jit(solution)/shard_map/ppermute | solution.py:219
  206.7 4.3 %collective-permute-done.61.refs_26_ = bf16[272,256]{1,0:T(8,128)(2,1)S(1)} collective-permute-done((bf16[272,256]{1,0:T(8,128)(2,1)S(1)}, bf16[272,256]{1,0:T(8,128)(2,1)S(1)}, u32[]{:S(2)}, u32[]{:S(2)}) %collective-permute-start.61) | collective-permute-done | bytes 139296 | tf_op jit(solution)/shard_map/ppermute | solution.py:219
  213.8 3.3 %collective-permute-start.12 = (bf16[272,256]{1,0:T(8,128)(2,1)S(1)}, bf16[272,256]{1,0:T(8,128)(2,1)S(1)}, u32[]{:S(2)}, u32[]{:S(2)}) collective-permute-start(bf16[272,256]{1,0:T(8,128)(2,1)S(1)} %get-tuple-element.102), channel_id=1, source_target_pairs={{0,27},{1,26},{2,25},{3,24},{4,31},{5,30},{6,29},{7,28},{8,19},{9,... | collective-permute-start | bytes 417800 | tf_op jit(solution)/shard_map/ppermute | solution.py:219
  218.2 2.5 collective-permute-start.14
  220.7 5.3 %collective-permute-done.10.rest_1_ = bf16[272,256]{1,0:T(8,128)(2,1)S(1)} collective-permute-done((bf16[272,256]{1,0:T(8,128)(2,1)S(1)}, bf16[272,256]{1,0:T(8,128)(2,1)S(1)}, u32[]{:S(2)}, u32[]{:S(2)}) %collective-permute-start.10) | collective-permute-done | bytes 139296 | tf_op jit(solution)/shard_map/ppermute | solution.py:219
  227.3 3.6 %collective-permute-start.16 = (bf16[272,256]{1,0:T(8,128)(2,1)S(1)}, bf16[272,256]{1,0:T(8,128)(2,1)S(1)}, u32[]{:S(2)}, u32[]{:S(2)}) collective-permute-start(bf16[272,256]{1,0:T(8,128)(2,1)S(1)} %get-tuple-element.106), channel_id=1, source_target_pairs={{0,31},{1,30},{2,29},{3,28},{4,27},{5,26},{6,25},{7,24},{8,23},{9,... | collective-permute-start | bytes 417800 | tf_op jit(solution)/shard_map/ppermute | solution.py:219
  232.4 4.6 %collective-permute-start.50 = (bf16[272,256]{1,0:T(8,128)(2,1)}, bf16[272,256]{1,0:T(8,128)(2,1)}, u32[]{:S(2)}, u32[]{:S(2)}) collective-permute-start(bf16[272,256]{1,0:T(8,128)(2,1)} %get-tuple-element.150), channel_id=1, source_target_pairs={{0,10},{1,11},{2,8},{3,9},{4,14},{5,15},{6,12},{7,13},{8,2},{9,3},... | collective-permute-start | bytes 417800 | tf_op jit(solution)/shard_map/ppermute | solution.py:219
  240.1 5.7 %collective-permute-start.52 = (bf16[272,256]{1,0:T(8,128)(2,1)}, bf16[272,256]{1,0:T(8,128)(2,1)}, u32[]{:S(2)}, u32[]{:S(2)}) collective-permute-start(bf16[272,256]{1,0:T(8,128)(2,1)} %get-tuple-element.152), channel_id=1, source_target_pairs={{0,12},{1,13},{2,14},{3,15},{4,8},{5,9},{6,10},{7,11},{8,4},{9,5},... | collective-permute-start | bytes 417800 | tf_op jit(solution)/shard_map/ppermute | solution.py:219
  246.5 2.8 collective-permute-start.53
  255.6 4.8 %combine.7 = (bf16[128,8192]{1,0:T(8,128)(2,1)}, bf16[272,256]{1,0:T(8,128)(2,1)S(1)}, bf16[272,256]{1,0:T(8,128)(2,1)S(1)}, bf16[272,256]{1,0:T(8,128)(2,1)S(1)...) custom-call(s32[1]{0:T(128)} %bitcast.place_in_ref, ...), custom_call_target="tpu_custom_call", output_to_operand_aliasing={{0}: (15, {})} | custom-call | flops 285212672 | bytes 3276800 | tf_op jit(solution)/shard_map/combine/pallas_call | solution.py:284
  261.7 4.3 %collective-permute-start.55 = (bf16[272,256]{1,0:T(8,128)(2,1)S(1)}, bf16[272,256]{1,0:T(8,128)(2,1)S(1)}, u32[]{:S(2)}, u32[]{:S(2)}) collective-permute-start(bf16[272,256]{1,0:T(8,128)(2,1)S(1)} %copy-done.72), channel_id=1, source_target_pairs={{0,15},{1,14},{2,13},{3,12},{4,11},{5,10},{6,9},{7,8},{8,7},{9,6},... | collective-permute-start | bytes 417800 | tf_op jit(solution)/shard_map/ppermute | solution.py:219
  268.1 6.2 %collective-permute-start.67 = (bf16[272,256]{1,0:T(8,128)(2,1)S(1)}, bf16[272,256]{1,0:T(8,128)(2,1)S(1)}, u32[]{:S(2)}, u32[]{:S(2)}) collective-permute-start(bf16[272,256]{1,0:T(8,128)(2,1)S(1)} %get-tuple-element.167), channel_id=1, source_target_pairs={{0,27},{1,26},{2,25},{3,24},{4,31},{5,30},{6,29},{7,28},{8,19},{9,... | collective-permute-start | bytes 417800 | tf_op jit(solution)/shard_map/ppermute | solution.py:219
  277.8 4.0 %collective-permute-done.65.refs_30_ = bf16[272,256]{1,0:T(8,128)(2,1)S(1)} collective-permute-done((bf16[272,256]{1,0:T(8,128)(2,1)S(1)}, bf16[272,256]{1,0:T(8,128)(2,1)S(1)}, u32[]{:S(2)}, u32[]{:S(2)}) %collective-permute-start.65) | collective-permute-done | bytes 139296 | tf_op jit(solution)/shard_map/ppermute | solution.py:219
  283.3 3.1 collective-permute-start.71
  288.3 5.6 %collective-permute-done.68.refs_33_ = bf16[272,256]{1,0:T(8,128)(2,1)S(1)} collective-permute-done((bf16[272,256]{1,0:T(8,128)(2,1)S(1)}, bf16[272,256]{1,0:T(8,128)(2,1)S(1)}, u32[]{:S(2)}, u32[]{:S(2)}) %collective-permute-start.68) | collective-permute-done | bytes 139296 | tf_op jit(solution)/shard_map/ppermute | solution.py:219
  293.9 3.0 collective-permute-done.69.refs_34_
  297.1 9.5 %gradient.1 = bf16[1024,2048]{1,0:T(8,128)(2,1)} custom-call(bf16[1024,256]{1,0:T(8,128)(2,1)S(1)} %get-tuple-element.135.refs_0_, bf16[1024,256]{1,0:T(8,128)(2,1)S(1)} %get-tuple-element.136.refs_1_, bf16[1024,256]{1,0:T(8,128)(2,1)S(1)} %get-tuple-element.137.refs_2_, bf16[1024,256]{1,0:T(8,128)(2,1)S(1)} %get-tuple-element.138.refs_3_, ...), custom_call_target="tpu_custom_call" | custom-call | flops 4563402752 | bytes 10878976 | tf_op jit(solution)/shard_map/gradient/pallas_call | solution.py:320
  (293 shorter events, 97.9 us)
Async XLA Ops:
  23.9 48.6 %collective-permute-start.7 = (bf16[272,1024]{1,0:T(8,128)(2,1)S(1)}, bf16[272,1024]{1,0:T(8,128)(2,1)S(1)}, u32[]{:S(2)}, u32[]{:S(2)}) collective-permute-start(bf16[272,1024]{1,0:T(8,128)(2,1)S(1)} %unpack.1.codes_ref.refs_0_), channel_id=1, source_target_pairs={{0,16},{1,17},{2,18},{3,19},{4,20},{5,21},{6,22},{7,23},{8,24},{9,... | collective-permute-start | bytes 1671176 | tf_op jit(solution)/shard_map/ppermute | solution.py:219
  32.3 55.5 %collective-permute-start.25 = (bf16[272,1024]{1,0:T(8,128)(2,1)S(1)}, bf16[272,1024]{1,0:T(8,128)(2,1)}, u32[]{:S(2)}, u32[]{:S(2)}) collective-permute-start(bf16[272,1024]{1,0:T(8,128)(2,1)S(1)} %unpack.1.codes_ref.refs_0_), channel_id=1, source_target_pairs={{0,8},{1,9},{2,10},{3,11},{4,12},{5,13},{6,14},{7,15},{8,0},{9,1},... | collective-permute-start | bytes 1671176 | tf_op jit(solution)/shard_map/ppermute | solution.py:219
  41.6 18.8 %collective-permute-start.38 = (bf16[272,256]{1,0:T(8,128)(2,1)}, bf16[272,256]{1,0:T(8,128)(2,1)}, u32[]{:S(2)}, u32[]{:S(2)}) collective-permute-start(bf16[272,256]{1,0:T(8,128)(2,1)} %get-tuple-element.128), channel_id=1, source_target_pairs={{0,5},{1,4},{2,7},{3,6},{4,1},{5,0},{6,3},{7,2},{8,13},{9,12},{10,... | collective-permute-start | bytes 417800 | tf_op jit(solution)/shard_map/ppermute | solution.py:219
  47.4 13.0 %collective-permute-start.39 = (bf16[272,256]{1,0:T(8,128)(2,1)}, bf16[272,256]{1,0:T(8,128)(2,1)}, u32[]{:S(2)}, u32[]{:S(2)}) collective-permute-start(bf16[272,256]{1,0:T(8,128)(2,1)} %get-tuple-element.129), channel_id=1, source_target_pairs={{0,6},{1,7},{2,4},{3,5},{4,2},{5,3},{6,0},{7,1},{8,14},{9,15},{10,... | collective-permute-start | bytes 417800 | tf_op jit(solution)/shard_map/ppermute | solution.py:219
  72.0 14.6 %collective-permute-start.41 = (bf16[272,256]{1,0:T(8,128)(2,1)S(1)}, bf16[272,256]{1,0:T(8,128)(2,1)S(1)}, u32[]{:S(2)}, u32[]{:S(2)}) collective-permute-start(bf16[272,256]{1,0:T(8,128)(2,1)S(1)} %get-tuple-element.141), channel_id=1, source_target_pairs={{0,1},{1,0},{2,3},{3,2},{4,5},{5,4},{6,7},{7,6},{8,9},{9,8},{10,11... | collective-permute-start | bytes 417800 | tf_op jit(solution)/shard_map/ppermute | solution.py:219
  78.0 13.0 %collective-permute-start.17 = (bf16[272,256]{1,0:T(8,128)(2,1)S(1)}, bf16[272,256]{1,0:T(8,128)(2,1)S(1)}, u32[]{:S(2)}, u32[]{:S(2)}) collective-permute-start(bf16[272,256]{1,0:T(8,128)(2,1)S(1)} %get-tuple-element.107), channel_id=1, source_target_pairs={{0,16},{1,17},{2,18},{3,19},{4,20},{5,21},{6,22},{7,23},{8,24},{9,... | collective-permute-start | bytes 417800 | tf_op jit(solution)/shard_map/ppermute | solution.py:219
  78.6 23.6 %collective-permute-start.18 = (bf16[272,256]{1,0:T(8,128)(2,1)S(1)}, bf16[272,256]{1,0:T(8,128)(2,1)S(1)}, u32[]{:S(2)}, u32[]{:S(2)}) collective-permute-start(bf16[272,256]{1,0:T(8,128)(2,1)S(1)} %get-tuple-element.108), channel_id=1, source_target_pairs={{0,17},{1,16},{2,19},{3,18},{4,21},{5,20},{6,23},{7,22},{8,25},{9,... | collective-permute-start | bytes 417800 | tf_op jit(solution)/shard_map/ppermute | solution.py:219
  81.1 23.9 %collective-permute-start.19 = (bf16[272,256]{1,0:T(8,128)(2,1)S(1)}, bf16[272,256]{1,0:T(8,128)(2,1)S(1)}, u32[]{:S(2)}, u32[]{:S(2)}) collective-permute-start(bf16[272,256]{1,0:T(8,128)(2,1)S(1)} %get-tuple-element.109), channel_id=1, source_target_pairs={{0,18},{1,19},{2,16},{3,17},{4,22},{5,23},{6,20},{7,21},{8,26},{9,... | collective-permute-start | bytes 417800 | tf_op jit(solution)/shard_map/ppermute | solution.py:219
  87.3 25.4 %collective-permute-start.20 = (bf16[272,256]{1,0:T(8,128)(2,1)S(1)}, bf16[272,256]{1,0:T(8,128)(2,1)S(1)}, u32[]{:S(2)}, u32[]{:S(2)}) collective-permute-start(bf16[272,256]{1,0:T(8,128)(2,1)S(1)} %get-tuple-element.110), channel_id=1, source_target_pairs={{0,19},{1,18},{2,17},{3,16},{4,23},{5,22},{6,21},{7,20},{8,27},{9,... | collective-permute-start | bytes 417800 | tf_op jit(solution)/shard_map/ppermute | solution.py:219
  87.8 25.6 %collective-permute-start.21 = (bf16[272,256]{1,0:T(8,128)(2,1)S(1)}, bf16[272,256]{1,0:T(8,128)(2,1)S(1)}, u32[]{:S(2)}, u32[]{:S(2)}) collective-permute-start(bf16[272,256]{1,0:T(8,128)(2,1)S(1)} %get-tuple-element.111), channel_id=1, source_target_pairs={{0,20},{1,21},{2,22},{3,23},{4,16},{5,17},{6,18},{7,19},{8,28},{9,... | collective-permute-start | bytes 417800 | tf_op jit(solution)/shard_map/ppermute | solution.py:219
  91.0 24.4 %collective-permute-start.22 = (bf16[272,256]{1,0:T(8,128)(2,1)S(1)}, bf16[272,256]{1,0:T(8,128)(2,1)S(1)}, u32[]{:S(2)}, u32[]{:S(2)}) collective-permute-start(bf16[272,256]{1,0:T(8,128)(2,1)S(1)} %get-tuple-element.112), channel_id=1, source_target_pairs={{0,21},{1,20},{2,23},{3,22},{4,17},{5,16},{6,19},{7,18},{8,29},{9,... | collective-permute-start | bytes 417800 | tf_op jit(solution)/shard_map/ppermute | solution.py:219
  102.8 13.3 %collective-permute-start.23 = (bf16[272,256]{1,0:T(8,128)(2,1)S(1)}, bf16[272,256]{1,0:T(8,128)(2,1)S(1)}, u32[]{:S(2)}, u32[]{:S(2)}) collective-permute-start(bf16[272,256]{1,0:T(8,128)(2,1)S(1)} %get-tuple-element.113), channel_id=1, source_target_pairs={{0,22},{1,23},{2,20},{3,21},{4,18},{5,19},{6,16},{7,17},{8,30},{9,... | collective-permute-start | bytes 417800 | tf_op jit(solution)/shard_map/ppermute | solution.py:219
  105.7 13.1 %collective-permute-start.24 = (bf16[272,256]{1,0:T(8,128)(2,1)S(1)}, bf16[272,256]{1,0:T(8,128)(2,1)S(1)}, u32[]{:S(2)}, u32[]{:S(2)}) collective-permute-start(bf16[272,256]{1,0:T(8,128)(2,1)S(1)} %get-tuple-element.114), channel_id=1, source_target_pairs={{0,23},{1,22},{2,21},{3,20},{4,19},{5,18},{6,17},{7,16},{8,31},{9,... | collective-permute-start | bytes 417800 | tf_op jit(solution)/shard_map/ppermute | solution.py:219
  119.4 73.3 %collective-permute-start.8 = (bf16[272,1024]{1,0:T(8,128)(2,1)S(1)}, bf16[272,1024]{1,0:T(8,128)(2,1)}, u32[]{:S(2)}, u32[]{:S(2)}) collective-permute-start(bf16[272,1024]{1,0:T(8,128)(2,1)S(1)} %collective-permute-done.7.codes_ref.refs_2_), channel_id=1, source_target_pairs={{0,8},{1,9},{2,10},{3,11},{4,12},{5,13},{6,14},{7,15},{8,0},{9,1},... | collective-permute-start | bytes 1671176 | tf_op jit(solution)/shard_map/ppermute | solution.py:219
  120.0 18.4 %collective-permute-start.30 = (bf16[272,256]{1,0:T(8,128)(2,1)S(1)}, bf16[272,256]{1,0:T(8,128)(2,1)S(1)}, u32[]{:S(2)}, u32[]{:S(2)}) collective-permute-start(bf16[272,256]{1,0:T(8,128)(2,1)S(1)} %get-tuple-element.119), channel_id=1, source_target_pairs={{0,12},{1,13},{2,14},{3,15},{4,8},{5,9},{6,10},{7,11},{8,4},{9,5},... | collective-permute-start | bytes 417800 | tf_op jit(solution)/shard_map/ppermute | solution.py:219
  121.4 20.7 %collective-permute-start.31 = (bf16[272,256]{1,0:T(8,128)(2,1)S(1)}, bf16[272,256]{1,0:T(8,128)(2,1)S(1)}, u32[]{:S(2)}, u32[]{:S(2)}) collective-permute-start(bf16[272,256]{1,0:T(8,128)(2,1)S(1)} %get-tuple-element.120), channel_id=1, source_target_pairs={{0,13},{1,12},{2,15},{3,14},{4,9},{5,8},{6,11},{7,10},{8,5},{9,4},... | collective-permute-start | bytes 417800 | tf_op jit(solution)/shard_map/ppermute | solution.py:219
  124.7 18.1 %collective-permute-start.32 = (bf16[272,256]{1,0:T(8,128)(2,1)S(1)}, bf16[272,256]{1,0:T(8,128)(2,1)S(1)}, u32[]{:S(2)}, u32[]{:S(2)}) collective-permute-start(bf16[272,256]{1,0:T(8,128)(2,1)S(1)} %get-tuple-element.121), channel_id=1, source_target_pairs={{0,14},{1,15},{2,12},{3,13},{4,10},{5,11},{6,8},{7,9},{8,6},{9,7},... | collective-permute-start | bytes 417800 | tf_op jit(solution)/shard_map/ppermute | solution.py:219
  127.0 19.3 %collective-permute-start.33 = (bf16[272,256]{1,0:T(8,128)(2,1)S(1)}, bf16[272,256]{1,0:T(8,128)(2,1)S(1)}, u32[]{:S(2)}, u32[]{:S(2)}) collective-permute-start(bf16[272,256]{1,0:T(8,128)(2,1)S(1)} %get-tuple-element.122), channel_id=1, source_target_pairs={{0,15},{1,14},{2,13},{3,12},{4,11},{5,10},{6,9},{7,8},{8,7},{9,6},... | collective-permute-start | bytes 417800 | tf_op jit(solution)/shard_map/ppermute | solution.py:219
  139.1 31.7 %collective-permute-start.42 = (bf16[272,256]{1,0:T(8,128)(2,1)}, bf16[272,256]{1,0:T(8,128)(2,1)}, u32[]{:S(2)}, u32[]{:S(2)}) collective-permute-start(bf16[272,256]{1,0:T(8,128)(2,1)} %get-tuple-element.142), channel_id=1, source_target_pairs={{0,2},{1,3},{2,0},{3,1},{4,6},{5,7},{6,4},{7,5},{8,10},{9,11},{10,... | collective-permute-start | bytes 417800 | tf_op jit(solution)/shard_map/ppermute | solution.py:219
  142.8 29.2 %collective-permute-start.43 = (bf16[272,256]{1,0:T(8,128)(2,1)}, bf16[272,256]{1,0:T(8,128)(2,1)}, u32[]{:S(2)}, u32[]{:S(2)}) collective-permute-start(bf16[272,256]{1,0:T(8,128)(2,1)} %get-tuple-element.143), channel_id=1, source_target_pairs={{0,3},{1,2},{2,1},{3,0},{4,7},{5,6},{6,5},{7,4},{8,11},{9,10},{10,... | collective-permute-start | bytes 417800 | tf_op jit(solution)/shard_map/ppermute | solution.py:219
  143.5 30.6 %collective-permute-start.44 = (bf16[272,256]{1,0:T(8,128)(2,1)}, bf16[272,256]{1,0:T(8,128)(2,1)}, u32[]{:S(2)}, u32[]{:S(2)}) collective-permute-start(bf16[272,256]{1,0:T(8,128)(2,1)} %get-tuple-element.144), channel_id=1, source_target_pairs={{0,4},{1,5},{2,6},{3,7},{4,0},{5,1},{6,2},{7,3},{8,12},{9,13},{10,... | collective-permute-start | bytes 417800 | tf_op jit(solution)/shard_map/ppermute | solution.py:219
  147.0 28.0 %collective-permute-start.45 = (bf16[272,256]{1,0:T(8,128)(2,1)}, bf16[272,256]{1,0:T(8,128)(2,1)}, u32[]{:S(2)}, u32[]{:S(2)}) collective-permute-start(bf16[272,256]{1,0:T(8,128)(2,1)} %get-tuple-element.145), channel_id=1, source_target_pairs={{0,5},{1,4},{2,7},{3,6},{4,1},{5,0},{6,3},{7,2},{8,13},{9,12},{10,... | collective-permute-start | bytes 417800 | tf_op jit(solution)/shard_map/ppermute | solution.py:219
  174.1 13.5 %collective-permute-start.56 = (bf16[272,256]{1,0:T(8,128)(2,1)S(1)}, bf16[272,256]{1,0:T(8,128)(2,1)S(1)}, u32[]{:S(2)}, u32[]{:S(2)}) collective-permute-start(bf16[272,256]{1,0:T(8,128)(2,1)S(1)} %get-tuple-element.156), channel_id=1, source_target_pairs={{0,16},{1,17},{2,18},{3,19},{4,20},{5,21},{6,22},{7,23},{8,24},{9,... | collective-permute-start | bytes 417800 | tf_op jit(solution)/shard_map/ppermute | solution.py:219
  175.0 13.5 %collective-permute-start.57 = (bf16[272,256]{1,0:T(8,128)(2,1)S(1)}, bf16[272,256]{1,0:T(8,128)(2,1)S(1)}, u32[]{:S(2)}, u32[]{:S(2)}) collective-permute-start(bf16[272,256]{1,0:T(8,128)(2,1)S(1)} %get-tuple-element.157), channel_id=1, source_target_pairs={{0,17},{1,16},{2,19},{3,18},{4,21},{5,20},{6,23},{7,22},{8,25},{9,... | collective-permute-start | bytes 417800 | tf_op jit(solution)/shard_map/ppermute | solution.py:219
  179.2 20.4 %collective-permute-start.58 = (bf16[272,256]{1,0:T(8,128)(2,1)S(1)}, bf16[272,256]{1,0:T(8,128)(2,1)S(1)}, u32[]{:S(2)}, u32[]{:S(2)}) collective-permute-start(bf16[272,256]{1,0:T(8,128)(2,1)S(1)} %get-tuple-element.158), channel_id=1, source_target_pairs={{0,18},{1,19},{2,16},{3,17},{4,22},{5,23},{6,20},{7,21},{8,26},{9,... | collective-permute-start | bytes 417800 | tf_op jit(solution)/shard_map/ppermute | solution.py:219
  183.9 19.4 %collective-permute-start.59 = (bf16[272,256]{1,0:T(8,128)(2,1)S(1)}, bf16[272,256]{1,0:T(8,128)(2,1)S(1)}, u32[]{:S(2)}, u32[]{:S(2)}) collective-permute-start(bf16[272,256]{1,0:T(8,128)(2,1)S(1)} %get-tuple-element.159), channel_id=1, source_target_pairs={{0,19},{1,18},{2,17},{3,16},{4,23},{5,22},{6,21},{7,20},{8,27},{9,... | collective-permute-start | bytes 417800 | tf_op jit(solution)/shard_map/ppermute | solution.py:219
  188.2 17.8 %collective-permute-start.60 = (bf16[272,256]{1,0:T(8,128)(2,1)S(1)}, bf16[272,256]{1,0:T(8,128)(2,1)S(1)}, u32[]{:S(2)}, u32[]{:S(2)}) collective-permute-start(bf16[272,256]{1,0:T(8,128)(2,1)S(1)} %get-tuple-element.160), channel_id=1, source_target_pairs={{0,20},{1,21},{2,22},{3,23},{4,16},{5,17},{6,18},{7,19},{8,28},{9,... | collective-permute-start | bytes 417800 | tf_op jit(solution)/shard_map/ppermute | solution.py:219
  189.1 21.9 %collective-permute-start.61 = (bf16[272,256]{1,0:T(8,128)(2,1)S(1)}, bf16[272,256]{1,0:T(8,128)(2,1)S(1)}, u32[]{:S(2)}, u32[]{:S(2)}) collective-permute-start(bf16[272,256]{1,0:T(8,128)(2,1)S(1)} %get-tuple-element.161), channel_id=1, source_target_pairs={{0,21},{1,20},{2,23},{3,22},{4,17},{5,16},{6,19},{7,18},{8,29},{9,... | collective-permute-start | bytes 417800 | tf_op jit(solution)/shard_map/ppermute | solution.py:219
  192.7 19.0 %collective-permute-start.62 = (bf16[272,256]{1,0:T(8,128)(2,1)S(1)}, bf16[272,256]{1,0:T(8,128)(2,1)S(1)}, u32[]{:S(2)}, u32[]{:S(2)}) collective-permute-start(bf16[272,256]{1,0:T(8,128)(2,1)S(1)} %get-tuple-element.162), channel_id=1, source_target_pairs={{0,22},{1,23},{2,20},{3,21},{4,18},{5,19},{6,16},{7,17},{8,30},{9,... | collective-permute-start | bytes 417800 | tf_op jit(solution)/shard_map/ppermute | solution.py:219
  204.0 13.0 %collective-permute-start.48 = (bf16[272,256]{1,0:T(8,128)(2,1)S(1)}, bf16[272,256]{1,0:T(8,128)(2,1)S(1)}, u32[]{:S(2)}, u32[]{:S(2)}) collective-permute-start(bf16[272,256]{1,0:T(8,128)(2,1)S(1)} %get-tuple-element.148), channel_id=1, source_target_pairs={{0,8},{1,9},{2,10},{3,11},{4,12},{5,13},{6,14},{7,15},{8,0},{9,1},... | collective-permute-start | bytes 417800 | tf_op jit(solution)/shard_map/ppermute | solution.py:219
  211.6 14.3 %collective-permute-start.10 = (bf16[272,256]{1,0:T(8,128)(2,1)S(1)}, bf16[272,256]{1,0:T(8,128)(2,1)S(1)}, u32[]{:S(2)}, u32[]{:S(2)}) collective-permute-start(bf16[272,256]{1,0:T(8,128)(2,1)S(1)} %get-tuple-element.100), channel_id=1, source_target_pairs={{0,25},{1,24},{2,27},{3,26},{4,29},{5,28},{6,31},{7,30},{8,17},{9,... | collective-permute-start | bytes 417800 | tf_op jit(solution)/shard_map/ppermute | solution.py:219
  212.3 14.3 %collective-permute-start.11 = (bf16[272,256]{1,0:T(8,128)(2,1)S(1)}, bf16[272,256]{1,0:T(8,128)(2,1)S(1)}, u32[]{:S(2)}, u32[]{:S(2)}) collective-permute-start(bf16[272,256]{1,0:T(8,128)(2,1)S(1)} %get-tuple-element.101), channel_id=1, source_target_pairs={{0,26},{1,27},{2,24},{3,25},{4,30},{5,31},{6,28},{7,29},{8,18},{9,... | collective-permute-start | bytes 417800 | tf_op jit(solution)/shard_map/ppermute | solution.py:219
  213.8 17.1 %collective-permute-start.12 = (bf16[272,256]{1,0:T(8,128)(2,1)S(1)}, bf16[272,256]{1,0:T(8,128)(2,1)S(1)}, u32[]{:S(2)}, u32[]{:S(2)}) collective-permute-start(bf16[272,256]{1,0:T(8,128)(2,1)S(1)} %get-tuple-element.102), channel_id=1, source_target_pairs={{0,27},{1,26},{2,25},{3,24},{4,31},{5,30},{6,29},{7,28},{8,19},{9,... | collective-permute-start | bytes 417800 | tf_op jit(solution)/shard_map/ppermute | solution.py:219
  217.7 14.1 %collective-permute-start.13 = (bf16[272,256]{1,0:T(8,128)(2,1)S(1)}, bf16[272,256]{1,0:T(8,128)(2,1)S(1)}, u32[]{:S(2)}, u32[]{:S(2)}) collective-permute-start(bf16[272,256]{1,0:T(8,128)(2,1)S(1)} %get-tuple-element.103), channel_id=1, source_target_pairs={{0,28},{1,29},{2,30},{3,31},{4,24},{5,25},{6,26},{7,27},{8,20},{9,... | collective-permute-start | bytes 417800 | tf_op jit(solution)/shard_map/ppermute | solution.py:219
  218.2 20.6 %collective-permute-start.14 = (bf16[272,256]{1,0:T(8,128)(2,1)S(1)}, bf16[272,256]{1,0:T(8,128)(2,1)S(1)}, u32[]{:S(2)}, u32[]{:S(2)}) collective-permute-start(bf16[272,256]{1,0:T(8,128)(2,1)S(1)} %get-tuple-element.104), channel_id=1, source_target_pairs={{0,29},{1,28},{2,31},{3,30},{4,25},{5,24},{6,27},{7,26},{8,21},{9,... | collective-permute-start | bytes 417800 | tf_op jit(solution)/shard_map/ppermute | solution.py:219
  227.3 18.5 %collective-permute-start.16 = (bf16[272,256]{1,0:T(8,128)(2,1)S(1)}, bf16[272,256]{1,0:T(8,128)(2,1)S(1)}, u32[]{:S(2)}, u32[]{:S(2)}) collective-permute-start(bf16[272,256]{1,0:T(8,128)(2,1)S(1)} %get-tuple-element.106), channel_id=1, source_target_pairs={{0,31},{1,30},{2,29},{3,28},{4,27},{5,26},{6,25},{7,24},{8,23},{9,... | collective-permute-start | bytes 417800 | tf_op jit(solution)/shard_map/ppermute | solution.py:219
  231.5 29.0 %collective-permute-start.49 = (bf16[272,256]{1,0:T(8,128)(2,1)}, bf16[272,256]{1,0:T(8,128)(2,1)}, u32[]{:S(2)}, u32[]{:S(2)}) collective-permute-start(bf16[272,256]{1,0:T(8,128)(2,1)} %get-tuple-element.149), channel_id=1, source_target_pairs={{0,9},{1,8},{2,11},{3,10},{4,13},{5,12},{6,15},{7,14},{8,1},{9,0},... | collective-permute-start | bytes 417800 | tf_op jit(solution)/shard_map/ppermute | solution.py:219
  232.4 29.2 %collective-permute-start.50 = (bf16[272,256]{1,0:T(8,128)(2,1)}, bf16[272,256]{1,0:T(8,128)(2,1)}, u32[]{:S(2)}, u32[]{:S(2)}) collective-permute-start(bf16[272,256]{1,0:T(8,128)(2,1)} %get-tuple-element.150), channel_id=1, source_target_pairs={{0,10},{1,11},{2,8},{3,9},{4,14},{5,15},{6,12},{7,13},{8,2},{9,3},... | collective-permute-start | bytes 417800 | tf_op jit(solution)/shard_map/ppermute | solution.py:219
  239.4 26.5 %collective-permute-start.51 = (bf16[272,256]{1,0:T(8,128)(2,1)}, bf16[272,256]{1,0:T(8,128)(2,1)}, u32[]{:S(2)}, u32[]{:S(2)}) collective-permute-start(bf16[272,256]{1,0:T(8,128)(2,1)} %get-tuple-element.151), channel_id=1, source_target_pairs={{0,11},{1,10},{2,9},{3,8},{4,15},{5,14},{6,13},{7,12},{8,3},{9,2},... | collective-permute-start | bytes 417800 | tf_op jit(solution)/shard_map/ppermute | solution.py:219
  240.1 25.8 %collective-permute-start.52 = (bf16[272,256]{1,0:T(8,128)(2,1)}, bf16[272,256]{1,0:T(8,128)(2,1)}, u32[]{:S(2)}, u32[]{:S(2)}) collective-permute-start(bf16[272,256]{1,0:T(8,128)(2,1)} %get-tuple-element.152), channel_id=1, source_target_pairs={{0,12},{1,13},{2,14},{3,15},{4,8},{5,9},{6,10},{7,11},{8,4},{9,5},... | collective-permute-start | bytes 417800 | tf_op jit(solution)/shard_map/ppermute | solution.py:219
  246.5 20.3 %collective-permute-start.53 = (bf16[272,256]{1,0:T(8,128)(2,1)}, bf16[272,256]{1,0:T(8,128)(2,1)}, u32[]{:S(2)}, u32[]{:S(2)}) collective-permute-start(bf16[272,256]{1,0:T(8,128)(2,1)} %get-tuple-element.153), channel_id=1, source_target_pairs={{0,13},{1,12},{2,15},{3,14},{4,9},{5,8},{6,11},{7,10},{8,5},{9,4},... | collective-permute-start | bytes 417800 | tf_op jit(solution)/shard_map/ppermute | solution.py:219
  266.0 15.9 %collective-permute-start.65 = (bf16[272,256]{1,0:T(8,128)(2,1)S(1)}, bf16[272,256]{1,0:T(8,128)(2,1)S(1)}, u32[]{:S(2)}, u32[]{:S(2)}) collective-permute-start(bf16[272,256]{1,0:T(8,128)(2,1)S(1)} %get-tuple-element.165), channel_id=1, source_target_pairs={{0,25},{1,24},{2,27},{3,26},{4,29},{5,28},{6,31},{7,30},{8,17},{9,... | collective-permute-start | bytes 417800 | tf_op jit(solution)/shard_map/ppermute | solution.py:219
  266.8 16.5 %collective-permute-start.66 = (bf16[272,256]{1,0:T(8,128)(2,1)S(1)}, bf16[272,256]{1,0:T(8,128)(2,1)S(1)}, u32[]{:S(2)}, u32[]{:S(2)}) collective-permute-start(bf16[272,256]{1,0:T(8,128)(2,1)S(1)} %get-tuple-element.166), channel_id=1, source_target_pairs={{0,26},{1,27},{2,24},{3,25},{4,30},{5,31},{6,28},{7,29},{8,18},{9,... | collective-permute-start | bytes 417800 | tf_op jit(solution)/shard_map/ppermute | solution.py:219
  268.1 20.1 %collective-permute-start.67 = (bf16[272,256]{1,0:T(8,128)(2,1)S(1)}, bf16[272,256]{1,0:T(8,128)(2,1)S(1)}, u32[]{:S(2)}, u32[]{:S(2)}) collective-permute-start(bf16[272,256]{1,0:T(8,128)(2,1)S(1)} %get-tuple-element.167), channel_id=1, source_target_pairs={{0,27},{1,26},{2,25},{3,24},{4,31},{5,30},{6,29},{7,28},{8,19},{9,... | collective-permute-start | bytes 417800 | tf_op jit(solution)/shard_map/ppermute | solution.py:219
  274.3 19.6 %collective-permute-start.68 = (bf16[272,256]{1,0:T(8,128)(2,1)S(1)}, bf16[272,256]{1,0:T(8,128)(2,1)S(1)}, u32[]{:S(2)}, u32[]{:S(2)}) collective-permute-start(bf16[272,256]{1,0:T(8,128)(2,1)S(1)} %get-tuple-element.168), channel_id=1, source_target_pairs={{0,28},{1,29},{2,30},{3,31},{4,24},{5,25},{6,26},{7,27},{8,20},{9,... | collective-permute-start | bytes 417800 | tf_op jit(solution)/shard_map/ppermute | solution.py:219
  276.3 20.6 %collective-permute-start.69 = (bf16[272,256]{1,0:T(8,128)(2,1)S(1)}, bf16[272,256]{1,0:T(8,128)(2,1)S(1)}, u32[]{:S(2)}, u32[]{:S(2)}) collective-permute-start(bf16[272,256]{1,0:T(8,128)(2,1)S(1)} %get-tuple-element.169), channel_id=1, source_target_pairs={{0,29},{1,28},{2,31},{3,30},{4,25},{5,24},{6,27},{7,26},{8,21},{9,... | collective-permute-start | bytes 417800 | tf_op jit(solution)/shard_map/ppermute | solution.py:219
  281.9 15.1 %collective-permute-start.70 = (bf16[272,256]{1,0:T(8,128)(2,1)S(1)}, bf16[272,256]{1,0:T(8,128)(2,1)S(1)}, u32[]{:S(2)}, u32[]{:S(2)}) collective-permute-start(bf16[272,256]{1,0:T(8,128)(2,1)S(1)} %get-tuple-element.170), channel_id=1, source_target_pairs={{0,30},{1,31},{2,28},{3,29},{4,26},{5,27},{6,24},{7,25},{8,22},{9,... | collective-permute-start | bytes 417800 | tf_op jit(solution)/shard_map/ppermute | solution.py:219
  283.3 13.7 %collective-permute-start.71 = (bf16[272,256]{1,0:T(8,128)(2,1)S(1)}, bf16[272,256]{1,0:T(8,128)(2,1)S(1)}, u32[]{:S(2)}, u32[]{:S(2)}) collective-permute-start(bf16[272,256]{1,0:T(8,128)(2,1)S(1)} %get-tuple-element.171), channel_id=1, source_target_pairs={{0,31},{1,30},{2,29},{3,28},{4,27},{5,26},{6,25},{7,24},{8,23},{9,... | collective-permute-start | bytes 417800 | tf_op jit(solution)/shard_map/ppermute | solution.py:219
  (115 other events, 934.2 us)

commit v2 on v1

v2 whole, which is shorter than its diff:
```python
import functools

import jax
import jax.numpy as jnp
from jax import lax
from jax.experimental import pallas as pl
from jax.experimental.pallas import tpu as pltpu
from jax.sharding import PartitionSpec as P

loss_scale = 1.0 / 32.0
SPARE = 2
STACK = 8
F32 = jnp.float32
BF16 = jnp.bfloat16


def mm(a, b):
    return jnp.dot(a, b, preferred_element_type=F32)


def swap_matrix(outer, inner):
    size = outer * inner * SPARE
    to = lax.broadcasted_iota(jnp.int32, (size, size), 0)
    at = lax.broadcasted_iota(jnp.int32, (size, size), 1)
    to_inner, to_outer = to // (outer * SPARE), to % (outer * SPARE) // SPARE
    at_outer, at_inner = at // (inner * SPARE), at % (inner * SPARE) // SPARE
    same = (to_inner == at_inner) & (to_outer == at_outer) & (to % SPARE == at % SPARE)
    return same.astype(F32).astype(BF16)


def pack_kernel(order, at_ref, owner_ref, mask_ref, codes_ref, *outs):
    messages, (pick_ref, pick_spare_ref, place_ref, place_spare_ref) = outs[:-4], outs[-4:]
    owners = len(messages)
    rows, visits = owner_ref.shape
    width = codes_ref.shape[1] // visits
    blocks = mask_ref.shape[1] // visits
    block = width // blocks
    main = rows * visits // owners
    slots = owners * (main + SPARE)
    apart = owner_ref[...] ^ at_ref[0]
    relative = sum(jnp.where(apart == k, p, 0) for p, k in enumerate(order))
    eye = lax.broadcasted_iota(jnp.int32, (rows, rows), 0) == lax.broadcasted_iota(jnp.int32, (rows, rows), 1)
    columns = [relative[:, g : g + 1] for g in range(visits)]
    lanes = [jnp.sum(jnp.where(eye, column, 0), axis=0, keepdims=True) for column in columns]
    column, lane = jnp.concatenate(columns, axis=0), jnp.concatenate(lanes, axis=1)
    total = rows * visits
    down = lax.broadcasted_iota(jnp.int32, (total, total), 0)
    across = lax.broadcasted_iota(jnp.int32, (total, total), 1)
    same = column == lane

    def slot_of(owner, place):
        return jnp.where(place < main, owner * main + place, owners * main + owner * SPARE + place - main)

    slot_lane = slot_of(lane, jnp.sum(jnp.where(same & (down < across), 1, 0), axis=0, keepdims=True))
    slot_column = slot_of(column, jnp.sum(jnp.where(same & (across < down), 1, 0), axis=1, keepdims=True))
    place = (lax.broadcasted_iota(jnp.int32, (slots, total), 0) == slot_lane).astype(F32)
    pick = (lax.broadcasted_iota(jnp.int32, (total, slots), 1) == slot_column).astype(F32)
    place_rows = sum(place[:, g * rows : (g + 1) * rows] for g in range(visits)).astype(BF16)
    pick_rows = sum(pick[g * rows : (g + 1) * rows, :] for g in range(visits)).astype(BF16)
    pick_ref[...] = pick_rows[:, : owners * main]
    pick_spare_ref[...] = pick_rows[:, owners * main :]
    place_ref[...] = place_rows[: owners * main, :]
    place_spare_ref[...] = place_rows[owners * main :, :]
    used = jnp.concatenate(
        [
            jnp.concatenate(
                [
                    codes_ref[:, g * width + b * block : g * width + (b + 1) * block]
                    * mask_ref[:, g * blocks + b : g * blocks + b + 1].astype(F32).astype(BF16)
                    for b in range(blocks)
                ],
                axis=1,
            )
            for g in range(visits)
        ],
        axis=0,
    )
    sorted_codes = mm(place.astype(BF16), used).astype(BF16)
    part = width // STACK
    for q in range(STACK):
        stack(messages, q, main, sorted_codes[: owners * main, q * part : (q + 1) * part])
    spare = [sorted_codes[owners * main :, q * part : (q + 1) * part] for q in range(STACK)]
    stack_spare(messages, main, jnp.concatenate(spare, axis=0))


def stack(messages, q, main, block):
    for p, message in enumerate(messages):
        message[q * main : (q + 1) * main, :] = block[p * main : (p + 1) * main, :]


def stack_spare(messages, main, spare):
    spare = mm(swap_matrix(STACK, len(messages)), spare).astype(BF16)
    for p, message in enumerate(messages):
        message[STACK * main :, :] = spare[p * STACK * SPARE : (p + 1) * STACK * SPARE, :]


def unstacked(messages, q, main):
    return jnp.concatenate([message[q * main : (q + 1) * main, :] for message in messages], axis=0)


def unstacked_spare(messages, main):
    spare = jnp.concatenate([message[STACK * main :, :] for message in messages], axis=0)
    return mm(swap_matrix(len(messages), STACK), spare).astype(BF16)


def main_of(message):
    return message.shape[0] // STACK - SPARE


def unpack_kernel(owners, *refs):
    messages, out_ref = refs[:owners], refs[owners]
    main, part = main_of(messages[0]), messages[0].shape[1]
    spares = owners * SPARE
    spare = unstacked_spare(messages, main)
    for q in range(STACK):
        out_ref[: owners * main, q * part : (q + 1) * part] = unstacked(messages, q, main)
        out_ref[owners * main :, q * part : (q + 1) * part] = spare[q * spares : (q + 1) * spares, :]


def decode_kernel(owners, codes_ref, w_ref, *rest):
    messages = rest[-owners:]
    main, part = main_of(messages[0]), messages[0].shape[1]
    spares = []
    for q in range(STACK):
        term = mm(codes_ref[...], w_ref[:, q * part : (q + 1) * part]).astype(BF16)
        stack(messages, q, main, term[: owners * main, :])
        spares.append(term[owners * main :, :])
    stack_spare(messages, main, jnp.concatenate(spares, axis=0))


def combine_kernel(owners, place_in_ref, pick_ref, pick_spare_ref, place_ref, place_spare_ref, b_ref, act_ref, *rest):
    terms, rebuilt_ref, messages = rest[:owners], rest[-owners - 1], rest[-owners:]
    main, part = main_of(messages[0]), messages[0].shape[1]
    spares = owners * SPARE
    spare_in = unstacked_spare(terms, main)
    spare_out = []
    for q in range(STACK):
        columns = slice(q * part, (q + 1) * part)
        total = mm(pick_ref[...], unstacked(terms, q, main))
        total += mm(pick_spare_ref[...], spare_in[q * spares : (q + 1) * spares, :])
        wide = b_ref[:, columns] + total
        rebuilt_ref[:, columns] = wide.astype(BF16)
        errors = (wide - act_ref[:, columns].astype(F32)).astype(BF16)
        stack(messages, q, main, mm(place_ref[...], errors).astype(BF16))
        spare_out.append(mm(place_spare_ref[...], errors).astype(BF16))
    stack_spare(messages, main, jnp.concatenate(spare_out, axis=0))


def turn_kernel(chunks, *refs):
    codes, (out_ref, spare_ref) = refs[:chunks], refs[-2:]
    main = out_ref.shape[1] // chunks
    for j in range(chunks):
        out_ref[:, j * main : (j + 1) * main] = codes[j][:main, :].astype(F32).T.astype(BF16)
    spare = jnp.concatenate([code[main:, :] for code in codes], axis=0)
    spare_ref[...] = spare.astype(F32).T.astype(BF16)


def gradient_kernel(chunks, owners, has_base, scale, codes_ref, spare_codes_ref, *refs):
    messages, base_ref, (out_ref, spare_ref) = refs[: chunks * owners], refs[chunks * owners], refs[-2:]
    main, part = main_of(messages[0]), messages[0].shape[1]
    spares = owners * SPARE
    step = pl.program_id(0)
    own = [messages[j * owners : (j + 1) * owners] for j in range(chunks)]

    @pl.when(step == 0)
    def _():
        for j in range(chunks):
            spare_ref[j] = unstacked_spare(own[j], main)

    per = out_ref.shape[1] // part
    for i in range(per):
        q = step * per + i
        at = pl.ds(pl.multiple_of(q * main, main), main)
        spare_at = pl.ds(pl.multiple_of(q * spares, spares), spares)
        columns = slice(i * part, (i + 1) * part)
        arrived = jnp.concatenate([m[at, :] for j in range(chunks) for m in own[j]], axis=0)
        spare = jnp.concatenate([spare_ref[j, spare_at, :] for j in range(chunks)], axis=0)
        total = mm(codes_ref[...], arrived) + mm(spare_codes_ref[...], spare)
        if has_base:
            total += base_ref[:, columns]
        out_ref[:, columns] = (total * scale).astype(out_ref.dtype)


ANYWHERE = pl.BlockSpec(memory_space=pl.ANY)


def whole(shape):
    return pl.BlockSpec(shape, lambda *_: (0,) * len(shape))


def params(mib):
    return pltpu.CompilerParams(vmem_limit_bytes=mib * 2**20)


def cost(flops, moved):
    return pl.CostEstimate(flops=int(flops), bytes_accessed=int(moved), transcendentals=0)


def on_device(activations, owner_ids, block_mask, latent_codes, w_dec, b_dec):
    rows, visits = owner_ids.shape
    width = latent_codes.shape[2]
    model = activations.shape[1]
    owners, groups = lax.axis_size("latent"), lax.axis_size("dp")
    main = rows * visits // owners
    slots = owners * (main + SPARE)
    depth = STACK * (main + SPARE)
    local = w_dec.shape[1]
    part = local // STACK
    place = jnp.stack([lax.axis_index("latent"), lax.axis_index("dp")])
    order = []
    for near in range(1, owners // 2 + 1):
        order += [owners - near] + ([near] if near != owners - near else [])
    order += [0]
    half = owners // 2

    def move(x, j, k):
        if j == 0 and k == 0:
            return x
        pairs = [(i, i ^ (j * owners + k)) for i in range(groups * owners)]
        return lax.ppermute(x, ("dp", "latent"), pairs)

    def move_all(messages, j):
        return [move(message, j, k) for message, k in zip(messages, order)]

    def some(shape, dtype=BF16):
        return jax.ShapeDtypeStruct(shape, dtype)

    packed = pl.pallas_call(
        functools.partial(pack_kernel, order),
        grid_spec=pltpu.PrefetchScalarGridSpec(
            num_scalar_prefetch=1,
            grid=(1,),
            in_specs=[whole((rows, visits)), whole((rows, visits * block_mask.shape[2])), whole((rows, visits * width))],
            out_specs=[whole((depth, width // STACK))] * owners
            + [whole((rows, owners * main)), whole((rows, owners * SPARE))]
            + [whole((owners * main, rows)), whole((owners * SPARE, rows))],
        ),
        out_shape=[some((depth, width // STACK))] * owners
        + [some((rows, owners * main)), some((rows, owners * SPARE))]
        + [some((owners * main, rows)), some((owners * SPARE, rows))],
        compiler_params=params(12),
        cost_estimate=cost(2 * slots * rows * visits * width, 4 * rows * visits * width),
        name="pack",
    )(place, owner_ids, block_mask.reshape(rows, -1), latent_codes.reshape(rows, -1))
    picks = packed[owners:]
    arrived = move_all(packed[:owners], 0)
    codes = [None] * groups
    codes[0] = pl.pallas_call(
        functools.partial(unpack_kernel, owners),
        out_shape=some((slots, width)),
        compiler_params=params(8),
        cost_estimate=cost(0, 4 * slots * width),
        name="unpack",
    )(*arrived)
    for j in range(1, groups):
        low = j & -j
        codes[j] = move(codes[j ^ low], low, 0)

    def decode(j, after):
        return pl.pallas_call(
            functools.partial(decode_kernel, owners),
            grid=(1,),
            in_specs=[whole((slots, width)), whole((width, local))] + [ANYWHERE] * len(after),
            out_specs=[whole((depth, part))] * owners,
            out_shape=[some((depth, part))] * owners,
            compiler_params=params(20),
            cost_estimate=cost(2 * slots * width * local, 2 * (width * local + slots * (width + local))),
            name="decode",
        )(codes[j], w_dec, *after)

    def combine(j, rebuilt, after):
        after = ([] if rebuilt is None else [rebuilt]) + after
        outs = pl.pallas_call(
            functools.partial(combine_kernel, owners),
            grid_spec=pltpu.PrefetchScalarGridSpec(
                num_scalar_prefetch=1,
                grid=(1,),
                in_specs=[whole(p.shape) for p in picks]
                + [pl.BlockSpec((1, local), lambda _, at: (0, at[1] ^ j))]
                + [pl.BlockSpec((rows, local), lambda _, at: (0, at[1] ^ j))]
                + [whole((depth, part))] * owners
                + [ANYWHERE] * len(after),
                out_specs=[pl.BlockSpec((rows, local), lambda _, at: (0, at[1] ^ j))] + [whole((depth, part))] * owners,
            ),
            out_shape=[some((rows, model))] + [some((depth, part))] * owners,
            input_output_aliases={} if rebuilt is None else {7 + owners: 0},
            compiler_params=params(16),
            cost_estimate=cost(4 * slots * rows * local, 2 * local * (2 * slots + 2 * rows)),
            name="combine",
        )(place, *picks, b_dec.reshape(1, -1), activations, *terms[j], *after)
        return outs[0], outs[1:]

    def gradient(chunks, base, scale, dtype, per, after):
        count = len(chunks)
        turned = pl.pallas_call(
            functools.partial(turn_kernel, count),
            out_shape=[some((width, count * owners * main)), some((width, count * owners * SPARE))],
            compiler_params=params(16),
            cost_estimate=cost(0, 4 * count * slots * width),
            name="turn",
        )(*[codes[j] for j in chunks])
        block = pl.BlockSpec((width, per * part), lambda q: (0, q))
        extra = ([] if base is None else [base]) + after
        return pl.pallas_call(
            functools.partial(gradient_kernel, count, owners, base is not None, scale),
            grid=(STACK // per,),
            in_specs=[whole(t.shape) for t in turned]
            + [whole((depth, part))] * (count * owners)
            + ([] if base is None else [block])
            + [ANYWHERE] * len(after),
            out_specs=block,
            out_shape=some((width, local), dtype),
            scratch_shapes=[pltpu.VMEM((count, STACK * owners * SPARE, part), BF16)],
            compiler_params=params(24),
            cost_estimate=cost(2 * count * slots * width * local, 4 * width * local),
            name="gradient",
        )(*turned, *[m for j in chunks for m in errors[j]], *extra)

    terms, errors = [None] * groups, [None] * groups
    for j in range(groups):
        terms[j] = move_all(decode(j, list(terms[j - 2][:half]) if j >= 2 else []), j)
    rebuilt = None
    for j in range(groups):
        ahead = terms[j + 1][:half] if j + 1 < groups else errors[j - 2][:half] if j >= 2 else []
        rebuilt, outgoing = combine(j, rebuilt, list(ahead))
        errors[j] = move_all(outgoing, j)
    early, last = list(range(groups - 1)), [groups - 1]
    base = gradient(early, None, 1.0, F32, 1, list(errors[groups - 1][:half]))
    return rebuilt, gradient(last, base, loss_scale, BF16, 2, [])


def on_device_wide(activations, owner_ids, block_mask, latent_codes, w_dec, b_dec):
    row_count, visit_count = owner_ids.shape
    block_count = block_mask.shape[2]
    slab_width = latent_codes.shape[2]
    block_width = slab_width // block_count
    model_width = activations.shape[1]
    owners = lax.axis_size("latent")
    groups = lax.axis_size("dp")
    capacity = row_count * visit_count // owners + SPARE
    live = block_mask.astype(latent_codes.dtype)[:, :, :, None]
    used = (latent_codes.reshape(row_count, visit_count, block_count, block_width) * live).reshape(-1, slab_width)
    onehot = (owner_ids[:, :, None] == lax.broadcasted_iota(jnp.int32, (1, 1, owners), 2)).astype(jnp.int32)
    per_row = jnp.sum(onehot, axis=1)
    before = jnp.cumsum(per_row, axis=0) - per_row
    position = jnp.sum(onehot * before[:, None, :], axis=2)
    target_slot = (owner_ids * capacity + position).reshape(-1)
    outgoing = jnp.zeros((owners * capacity, slab_width), latent_codes.dtype)
    outgoing = outgoing.at[target_slot].set(used).reshape(owners, capacity, slab_width)
    arrived = lax.all_to_all(outgoing, "latent", split_axis=0, concat_axis=0, tiled=True)
    copies = lax.all_gather(arrived, "dp", axis=0, tiled=True)
    decoded = mm(copies.reshape(-1, slab_width), w_dec).astype(BF16)
    local = w_dec.shape[1]
    returned = lax.all_to_all(
        decoded.reshape(groups * owners, capacity, local), ("dp", "latent"), split_axis=0, concat_axis=0, tiled=True
    )
    returned = returned.reshape(groups, owners * capacity, local)
    gathered = returned[:, target_slot].reshape(groups, row_count, visit_count, local)
    gathered = jnp.sum(gathered, axis=2, dtype=F32).transpose(1, 0, 2).reshape(row_count, model_width)
    rebuilt_wide = b_dec[None, :] + gathered
    errors = (rebuilt_wide - activations.astype(F32)).astype(BF16)
    parts = jnp.repeat(errors.reshape(row_count, groups, local).transpose(1, 0, 2), visit_count, axis=1)
    error_slots = jnp.zeros((groups, owners * capacity, local), BF16).at[:, target_slot].set(parts)
    error_parts = lax.all_to_all(
        error_slots.reshape(groups * owners, capacity, local), ("dp", "latent"), split_axis=0, concat_axis=0, tiled=True
    )
    gradient = jnp.einsum("nsi,nsd->id", copies, error_parts, preferred_element_type=F32) * loss_scale
    return rebuilt_wide.astype(BF16), gradient.astype(BF16)


def solution(mesh):
    placed = (
        P(("dp", "latent"), None),
        P(("dp", "latent"), None),
        P(("dp", "latent"), None, None),
        P(("dp", "latent"), None, None),
        P("latent", "dp"),
        P(),
    )

    def body(activations, owner_ids, block_mask, latent_codes, w_dec, b_dec):
        owners = mesh.shape["latent"]
        share = owner_ids.size // owners
        fits = share % 16 == 0 and owners * SPARE % 16 == 0 and w_dec.shape[1] % (128 * STACK) == 0
        fits = fits and mesh.size & (mesh.size - 1) == 0
        pick = on_device if fits else on_device_wide
        return pick(activations, owner_ids, block_mask, latent_codes, w_dec, b_dec)

    return jax.shard_map(
        body,
        mesh=mesh,
        in_specs=placed,
        out_specs=(P(("dp", "latent"), None), P("latent", "dp")),
        check_vma=False,
    )
```

time: 311 us -> 251 us (0.81); the launches traced: 307 us -> 251 us
  local copies, waits for them, and re-layouts: 51.9 us -> 4.94 us
  Pallas kernels: 49.3 us -> 31.6 us
  starting transfers between devices: 143 us -> 160 us
  waiting for transfers between devices: 61.6 us -> 53.8 us
    unnamed x184 -> x10, local copies, waits for them, and re-layouts: 51.1 us -> 4.14 us
    pallas_call x12 -> x14, Pallas kernels: 49.3 us -> 31.6 us  [the longest x4 12.3 us: combine(): pl.pallas_call(functools.partial(combine_kernel, owners), grid_spec=pltpu...]
    ppermute x72, starting transfers between devices: 143 us -> 160 us  [move(): return lax.ppermute(x, ('dp', 'latent'), pairs)]
    ppermute x72, waiting for transfers between devices: 61.6 us -> 53.8 us  [move(): return lax.ppermute(x, ('dp', 'latent'), pairs)]
  transfers between devices with their start and end apart: 72 -> 72, of which waited for: 17 -> 18; matrix products, arithmetic and copies ran while one was open for 0% -> 0% of each run, Pallas kernels for 13% -> 10%
where the time goes in v2:
time: 251 us
  starting transfers between devices  160 us (64%)
  waiting for transfers between devices  53.8 us (21%)
  Pallas kernels  31.6 us (13%)
  local copies, waits for them, and re-layouts  4.94 us (2%)
    ppermute x72, starting transfers between devices, move(): return lax.ppermute(x, ('dp', 'latent'), pairs)  160 us
    ppermute x72, waiting for transfers between devices, move(): return lax.ppermute(x, ('dp', 'latent'), pairs)  53.8 us
    pallas_call x4, Pallas kernels, combine(): pl.pallas_call(functools.partial(combine_kernel, owners), grid_spec=pltpu...  12.3 us
    pallas_call x2, Pallas kernels, gradient(): pl.pallas_call(functools.partial(gradient_kernel, count, owners, base is...  11.2 us
    pallas_call x4, Pallas kernels, decode(): pl.pallas_call(functools.partial(decode_kernel, owners), grid=(1,), in_sp...  5.81 us
  transfers between devices with their start and end apart: 72, of which 18 were waited for; matrix products, arithmetic and copies ran while one was open for 0% of the time, Pallas kernels for 10%

profile of v2, /device:TPU:0, one launch (start us, length us, event | category | flops | bytes accessed | tf_op | source)
XLA Modules:
  0.0 250.9 jit_solution(305150008476935321)
XLA Ops:
  4.8 6.0 %collective-permute-start = (bf16[272,128]{1,0:T(8,128)(2,1)S(1)}, bf16[272,128]{1,0:T(8,128)(2,1)S(1)}, u32[]{:S(2)}, u32[]{:S(2)}) collective-permute-start(bf16[272,128]{1,0:T(8,128)(2,1)S(1)} %get-tuple-element.90), channel_id=1, source_target_pairs={{0,7},{1,6},{2,5},{3,4},{4,3},{5,2},{6,1},{7,0},{8,15},{9,14},{10,... | collective-permute-start | bytes 208904 | tf_op jit(solution)/shard_map/ppermute | solution.py:220
  11.4 5.2 %collective-permute-start.4 = (bf16[272,128]{1,0:T(8,128)(2,1)S(1)}, bf16[272,128]{1,0:T(8,128)(2,1)S(1)}, u32[]{:S(2)}, u32[]{:S(2)}) collective-permute-start(bf16[272,128]{1,0:T(8,128)(2,1)S(1)} %get-tuple-element.94), channel_id=1, source_target_pairs={{0,5},{1,4},{2,7},{3,6},{4,1},{5,0},{6,3},{7,2},{8,13},{9,12},{10,... | collective-permute-start | bytes 208904 | tf_op jit(solution)/shard_map/ppermute | solution.py:220
  16.6 2.5 collective-permute-start.6
  19.8 2.1 collective-permute-done.5.refs_5_
  23.9 2.2 copy-done
  27.5 3.5 %collective-permute-start.22 = (bf16[272,256]{1,0:T(8,128)(2,1)S(1)}, bf16[272,256]{1,0:T(8,128)(2,1)S(1)}, u32[]{:S(2)}, u32[]{:S(2)}) collective-permute-start(bf16[272,256]{1,0:T(8,128)(2,1)S(1)} %get-tuple-element.110), channel_id=1, source_target_pairs={{0,7},{1,6},{2,5},{3,4},{4,3},{5,2},{6,1},{7,0},{8,15},{9,14},{10,... | collective-permute-start | bytes 417800 | tf_op jit(solution)/shard_map/ppermute | solution.py:220
  32.9 3.4 %collective-permute-done.22.rest_0_ = bf16[272,256]{1,0:T(8,128)(2,1)S(1)} collective-permute-done((bf16[272,256]{1,0:T(8,128)(2,1)S(1)}, bf16[272,256]{1,0:T(8,128)(2,1)S(1)}, u32[]{:S(2)}, u32[]{:S(2)}) %collective-permute-start.22) | collective-permute-done | bytes 139296 | tf_op jit(solution)/shard_map/ppermute | solution.py:220
  36.2 6.4 %collective-permute-start.25 = (bf16[272,256]{1,0:T(8,128)(2,1)S(1)}, bf16[272,256]{1,0:T(8,128)(2,1)S(1)}, u32[]{:S(2)}, u32[]{:S(2)}) collective-permute-start(bf16[272,256]{1,0:T(8,128)(2,1)S(1)} %get-tuple-element.113), channel_id=1, source_target_pairs={{0,2},{1,3},{2,0},{3,1},{4,6},{5,7},{6,4},{7,5},{8,10},{9,11},{10,... | collective-permute-start | bytes 417800 | tf_op jit(solution)/shard_map/ppermute | solution.py:220
  43.2 3.0 %collective-permute-start.39 = (bf16[272,256]{1,0:T(8,128)(2,1)S(1)}, bf16[272,256]{1,0:T(8,128)(2,1)S(1)}, u32[]{:S(2)}, u32[]{:S(2)}) collective-permute-start(bf16[272,256]{1,0:T(8,128)(2,1)S(1)} %get-tuple-element.127), channel_id=1, source_target_pairs={{0,3},{1,2},{2,1},{3,0},{4,7},{5,6},{6,5},{7,4},{8,11},{9,10},{10,... | collective-permute-start | bytes 417800 | tf_op jit(solution)/shard_map/ppermute | solution.py:220
  48.2 5.9 %collective-permute-done.38.rest_4_ = bf16[272,256]{1,0:T(8,128)(2,1)S(1)} collective-permute-done((bf16[272,256]{1,0:T(8,128)(2,1)S(1)}, bf16[272,256]{1,0:T(8,128)(2,1)S(1)}, u32[]{:S(2)}, u32[]{:S(2)}) %collective-permute-start.38) | collective-permute-done | bytes 139296 | tf_op jit(solution)/shard_map/ppermute | solution.py:220
  56.0 8.5 %collective-permute-done.40.rest_6_ = bf16[272,256]{1,0:T(8,128)(2,1)S(1)} collective-permute-done((bf16[272,256]{1,0:T(8,128)(2,1)S(1)}, bf16[272,256]{1,0:T(8,128)(2,1)S(1)}, u32[]{:S(2)}, u32[]{:S(2)}) %collective-permute-start.40) | collective-permute-done | bytes 139296 | tf_op jit(solution)/shard_map/ppermute | solution.py:220
  66.0 2.3 collective-permute-start.26
  69.7 2.5 %collective-permute-start.28 = (bf16[272,256]{1,0:T(8,128)(2,1)S(1)}, bf16[272,256]{1,0:T(8,128)(2,1)S(1)}, u32[]{:S(2)}, u32[]{:S(2)}) collective-permute-start(bf16[272,256]{1,0:T(8,128)(2,1)S(1)} %get-tuple-element.116), channel_id=1, source_target_pairs={{0,22},{1,23},{2,20},{3,21},{4,18},{5,19},{6,16},{7,17},{8,30},{9,... | collective-permute-start | bytes 417800 | tf_op jit(solution)/shard_map/ppermute | solution.py:220
  73.4 2.5 collective-permute-done.26.rest_9_.rest_0_
  75.9 5.4 %collective-permute-start.34 = (bf16[272,256]{1,0:T(8,128)(2,1)S(1)}, bf16[272,256]{1,0:T(8,128)(2,1)S(1)}, u32[]{:S(2)}, u32[]{:S(2)}) collective-permute-start(bf16[272,256]{1,0:T(8,128)(2,1)S(1)} %get-tuple-element.122), channel_id=1, source_target_pairs={{0,13},{1,12},{2,15},{3,14},{4,9},{5,8},{6,11},{7,10},{8,5},{9,4},... | collective-permute-start | bytes 417800 | tf_op jit(solution)/shard_map/ppermute | solution.py:220
  81.3 3.0 %collective-permute-done.27.rest_10_.rest_1_ = bf16[272,256]{1,0:T(8,128)(2,1)S(1)} collective-permute-done((bf16[272,256]{1,0:T(8,128)(2,1)S(1)}, bf16[272,256]{1,0:T(8,128)(2,1)S(1)}, u32[]{:S(2)}, u32[]{:S(2)}) %collective-permute-start.27) | collective-permute-done | bytes 139296 | tf_op jit(solution)/shard_map/ppermute | solution.py:220
  84.2 2.8 %collective-permute-start.36 = (bf16[272,256]{1,0:T(8,128)(2,1)S(1)}, bf16[272,256]{1,0:T(8,128)(2,1)S(1)}, u32[]{:S(2)}, u32[]{:S(2)}) collective-permute-start(bf16[272,256]{1,0:T(8,128)(2,1)S(1)} %get-tuple-element.124), channel_id=1, source_target_pairs={{0,12},{1,13},{2,14},{3,15},{4,8},{5,9},{6,10},{7,11},{8,4},{9,5},... | collective-permute-start | bytes 417800 | tf_op jit(solution)/shard_map/ppermute | solution.py:220
  88.3 3.7 %collective-permute-start.30 = (bf16[272,256]{1,0:T(8,128)(2,1)S(1)}, bf16[272,256]{1,0:T(8,128)(2,1)S(1)}, u32[]{:S(2)}, u32[]{:S(2)}) collective-permute-start(bf16[272,256]{1,0:T(8,128)(2,1)S(1)} %get-tuple-element.118), channel_id=1, source_target_pairs={{0,21},{1,20},{2,23},{3,22},{4,17},{5,16},{6,19},{7,18},{8,29},{9,... | collective-permute-start | bytes 417800 | tf_op jit(solution)/shard_map/ppermute | solution.py:220
  94.8 3.8 %collective-permute-done.36.rest_6_ = bf16[272,256]{1,0:T(8,128)(2,1)S(1)} collective-permute-done((bf16[272,256]{1,0:T(8,128)(2,1)S(1)}, bf16[272,256]{1,0:T(8,128)(2,1)S(1)}, u32[]{:S(2)}, u32[]{:S(2)}) %collective-permute-start.36) | collective-permute-done | bytes 139296 | tf_op jit(solution)/shard_map/ppermute | solution.py:220
  101.3 3.1 %combine.4 = (bf16[128,8192]{1,0:T(8,128)(2,1)}, bf16[272,256]{1,0:T(8,128)(2,1)S(1)}, bf16[272,256]{1,0:T(8,128)(2,1)S(1)}, bf16[272,256]{1,0:T(8,128)(2,1)S(1)...) custom-call(s32[2]{0:T(128)S(1)} %pad_add_fusion.at_ref.place_in_ref, ...), custom_call_target="tpu_custom_call" | custom-call | flops 285212672 | bytes 3276800 | tf_op jit(solution)/shard_map/combine/pallas_call | solution.py:273
  104.4 3.1 %combine.5 = (bf16[128,8192]{1,0:T(8,128)(2,1)}, bf16[272,256]{1,0:T(8,128)(2,1)S(1)}, bf16[272,256]{1,0:T(8,128)(2,1)S(1)}, bf16[272,256]{1,0:T(8,128)(2,1)S(1)...) custom-call(s32[2]{0:T(128)S(1)} %pad_add_fusion.at_ref.place_in_ref, ...), custom_call_target="tpu_custom_call", output_to_operand_aliasing={{0}: (15, {})} | custom-call | flops 285212672 | bytes 3276800 | tf_op jit(solution)/shard_map/combine/pallas_call | solution.py:273
  109.8 2.3 collective-permute-start.43
  112.0 2.7 %collective-permute-start.60 = (bf16[272,256]{1,0:T(8,128)(2,1)S(1)}, bf16[272,256]{1,0:T(8,128)(2,1)S(1)}, u32[]{:S(2)}, u32[]{:S(2)}) collective-permute-start(bf16[272,256]{1,0:T(8,128)(2,1)S(1)} %get-tuple-element.158), channel_id=1, source_target_pairs={{0,13},{1,12},{2,15},{3,14},{4,9},{5,8},{6,11},{7,10},{8,5},{9,4},... | collective-permute-start | bytes 417800 | tf_op jit(solution)/shard_map/ppermute | solution.py:220
  116.3 6.1 %collective-permute-start.61 = (bf16[272,256]{1,0:T(8,128)(2,1)S(1)}, bf16[272,256]{1,0:T(8,128)(2,1)S(1)}, u32[]{:S(2)}, u32[]{:S(2)}) collective-permute-start(bf16[272,256]{1,0:T(8,128)(2,1)S(1)} %get-tuple-element.159), channel_id=1, source_target_pairs={{0,11},{1,10},{2,9},{3,8},{4,15},{5,14},{6,13},{7,12},{8,3},{9,2},... | collective-permute-start | bytes 417800 | tf_op jit(solution)/shard_map/ppermute | solution.py:220
  122.7 2.4 collective-permute-start.14
  126.0 2.8 %collective-permute-done.60.refs_12_ = bf16[272,256]{1,0:T(8,128)(2,1)S(1)} collective-permute-done((bf16[272,256]{1,0:T(8,128)(2,1)S(1)}, bf16[272,256]{1,0:T(8,128)(2,1)S(1)}, u32[]{:S(2)}, u32[]{:S(2)}) %collective-permute-start.60) | collective-permute-done | bytes 139296 | tf_op jit(solution)/shard_map/ppermute | solution.py:220
  128.8 9.9 %collective-permute-start.16 = (bf16[272,256]{1,0:T(8,128)(2,1)S(1)}, bf16[272,256]{1,0:T(8,128)(2,1)S(1)}, u32[]{:S(2)}, u32[]{:S(2)}) collective-permute-start(bf16[272,256]{1,0:T(8,128)(2,1)S(1)} %get-tuple-element.104), channel_id=1, source_target_pairs={{0,30},{1,31},{2,28},{3,29},{4,26},{5,27},{6,24},{7,25},{8,22},{9,... | collective-permute-start | bytes 417800 | tf_op jit(solution)/shard_map/ppermute | solution.py:220
  138.7 3.4 %collective-permute-start.18 = (bf16[272,256]{1,0:T(8,128)(2,1)S(1)}, bf16[272,256]{1,0:T(8,128)(2,1)S(1)}, u32[]{:S(2)}, u32[]{:S(2)}) collective-permute-start(bf16[272,256]{1,0:T(8,128)(2,1)S(1)} %get-tuple-element.106), channel_id=1, source_target_pairs={{0,29},{1,28},{2,31},{3,30},{4,25},{5,24},{6,27},{7,26},{8,21},{9,... | collective-permute-start | bytes 417800 | tf_op jit(solution)/shard_map/ppermute | solution.py:220
  142.0 10.8 %collective-permute-start.19 = (bf16[272,256]{1,0:T(8,128)(2,1)S(1)}, bf16[272,256]{1,0:T(8,128)(2,1)S(1)}, u32[]{:S(2)}, u32[]{:S(2)}) collective-permute-start(bf16[272,256]{1,0:T(8,128)(2,1)S(1)} %get-tuple-element.107), channel_id=1, source_target_pairs={{0,27},{1,26},{2,25},{3,24},{4,31},{5,30},{6,29},{7,28},{8,19},{9,... | collective-permute-start | bytes 417800 | tf_op jit(solution)/shard_map/ppermute | solution.py:220
  154.2 2.4 collective-permute-start.53
  156.6 3.6 %collective-permute-done.19.rest_5_ = bf16[272,256]{1,0:T(8,128)(2,1)S(1)} collective-permute-done((bf16[272,256]{1,0:T(8,128)(2,1)S(1)}, bf16[272,256]{1,0:T(8,128)(2,1)S(1)}, u32[]{:S(2)}, u32[]{:S(2)}) %collective-permute-start.19) | collective-permute-done | bytes 139296 | tf_op jit(solution)/shard_map/ppermute | solution.py:220
  160.1 5.4 %collective-permute-start.54 = (bf16[272,256]{1,0:T(8,128)(2,1)S(1)}, bf16[272,256]{1,0:T(8,128)(2,1)S(1)}, u32[]{:S(2)}, u32[]{:S(2)}) collective-permute-start(bf16[272,256]{1,0:T(8,128)(2,1)S(1)} %get-tuple-element.151), channel_id=1, source_target_pairs={{0,1},{1,0},{2,3},{3,2},{4,5},{5,4},{6,7},{7,6},{8,9},{9,8},{10,11... | collective-permute-start | bytes 417800 | tf_op jit(solution)/shard_map/ppermute | solution.py:220
  167.0 3.1 %combine.6 = (bf16[128,8192]{1,0:T(8,128)(2,1)}, bf16[272,256]{1,0:T(8,128)(2,1)S(1)}, bf16[272,256]{1,0:T(8,128)(2,1)S(1)}, bf16[272,256]{1,0:T(8,128)(2,1)S(1)...) custom-call(s32[2]{0:T(128)S(1)} %pad_add_fusion.at_ref.place_in_ref, ...), custom_call_target="tpu_custom_call", output_to_operand_aliasing={{0}: (15, {})} | custom-call | flops 285212672 | bytes 3276800 | tf_op jit(solution)/shard_map/combine/pallas_call | solution.py:273
  170.1 3.1 %combine.7 = (bf16[128,8192]{1,0:T(8,128)(2,1)}, bf16[272,256]{1,0:T(8,128)(2,1)S(1)}, bf16[272,256]{1,0:T(8,128)(2,1)S(1)}, bf16[272,256]{1,0:T(8,128)(2,1)S(1)...) custom-call(s32[2]{0:T(128)S(1)} %pad_add_fusion.at_ref.place_in_ref, ...), custom_call_target="tpu_custom_call", output_to_operand_aliasing={{0}: (15, {})} | custom-call | flops 285212672 | bytes 3276800 | tf_op jit(solution)/shard_map/combine/pallas_call | solution.py:273
  173.1 2.5 collective-permute-start.57
  180.6 2.9 %collective-permute-start.46 = (bf16[272,256]{1,0:T(8,128)(2,1)S(1)}, bf16[272,256]{1,0:T(8,128)(2,1)S(1)}, u32[]{:S(2)}, u32[]{:S(2)}) collective-permute-start(bf16[272,256]{1,0:T(8,128)(2,1)S(1)} %get-tuple-element.141), channel_id=1, source_target_pairs={{0,25},{1,24},{2,27},{3,26},{4,29},{5,28},{6,31},{7,30},{8,17},{9,... | collective-permute-start | bytes 417800 | tf_op jit(solution)/shard_map/ppermute | solution.py:220
  183.5 7.0 %collective-permute-done.57.refs_4_ = bf16[272,256]{1,0:T(8,128)(2,1)S(1)} collective-permute-done((bf16[272,256]{1,0:T(8,128)(2,1)S(1)}, bf16[272,256]{1,0:T(8,128)(2,1)S(1)}, u32[]{:S(2)}, u32[]{:S(2)}) %collective-permute-start.57) | collective-permute-done | bytes 139296 | tf_op jit(solution)/shard_map/ppermute | solution.py:220
  190.5 3.1 %collective-permute-done.59.refs_6_ = bf16[272,256]{1,0:T(8,128)(2,1)S(1)} collective-permute-done((bf16[272,256]{1,0:T(8,128)(2,1)S(1)}, bf16[272,256]{1,0:T(8,128)(2,1)S(1)}, u32[]{:S(2)}, u32[]{:S(2)}) %collective-permute-start.59) | collective-permute-done | bytes 139296 | tf_op jit(solution)/shard_map/ppermute | solution.py:220
  193.6 6.6 %collective-permute-start.64 = (bf16[272,256]{1,0:T(8,128)(2,1)S(1)}, bf16[272,256]{1,0:T(8,128)(2,1)S(1)}, u32[]{:S(2)}, u32[]{:S(2)}) collective-permute-start(bf16[272,256]{1,0:T(8,128)(2,1)S(1)} %get-tuple-element.162), channel_id=1, source_target_pairs={{0,23},{1,22},{2,21},{3,20},{4,19},{5,18},{6,17},{7,16},{8,31},{9,... | collective-permute-start | bytes 417800 | tf_op jit(solution)/shard_map/ppermute | solution.py:220
  200.6 7.6 %collective-permute-start.67 = (bf16[272,256]{1,0:T(8,128)(2,1)S(1)}, bf16[272,256]{1,0:T(8,128)(2,1)S(1)}, u32[]{:S(2)}, u32[]{:S(2)}) collective-permute-start(bf16[272,256]{1,0:T(8,128)(2,1)S(1)} %get-tuple-element.165), channel_id=1, source_target_pairs={{0,18},{1,19},{2,16},{3,17},{4,22},{5,23},{6,20},{7,21},{8,26},{9,... | collective-permute-start | bytes 417800 | tf_op jit(solution)/shard_map/ppermute | solution.py:220
  208.7 5.6 %collective-permute-start.69 = (bf16[272,256]{1,0:T(8,128)(2,1)S(1)}, bf16[272,256]{1,0:T(8,128)(2,1)S(1)}, u32[]{:S(2)}, u32[]{:S(2)}) collective-permute-start(bf16[272,256]{1,0:T(8,128)(2,1)S(1)} %get-tuple-element.167), channel_id=1, source_target_pairs={{0,19},{1,18},{2,17},{3,16},{4,23},{5,22},{6,21},{7,20},{8,27},{9,... | collective-permute-start | bytes 417800 | tf_op jit(solution)/shard_map/ppermute | solution.py:220
  214.3 3.4 %collective-permute-start.71 = (bf16[272,256]{1,0:T(8,128)(2,1)S(1)}, bf16[272,256]{1,0:T(8,128)(2,1)S(1)}, u32[]{:S(2)}, u32[]{:S(2)}) collective-permute-start(bf16[272,256]{1,0:T(8,128)(2,1)S(1)} %get-tuple-element.169), channel_id=1, source_target_pairs={{0,16},{1,17},{2,18},{3,19},{4,20},{5,21},{6,22},{7,23},{8,24},{9,... | collective-permute-start | bytes 417800 | tf_op jit(solution)/shard_map/ppermute | solution.py:220
  218.5 11.7 %collective-permute-start.49 = (bf16[272,256]{1,0:T(8,128)(2,1)S(1)}, bf16[272,256]{1,0:T(8,128)(2,1)S(1)}, u32[]{:S(2)}, u32[]{:S(2)}) collective-permute-start(bf16[272,256]{1,0:T(8,128)(2,1)S(1)} %get-tuple-element.144), channel_id=1, source_target_pairs={{0,29},{1,28},{2,31},{3,30},{4,25},{5,24},{6,27},{7,26},{8,21},{9,... | collective-permute-start | bytes 417800 | tf_op jit(solution)/shard_map/ppermute | solution.py:220
  230.3 3.5 %collective-permute-start.50 = (bf16[272,256]{1,0:T(8,128)(2,1)S(1)}, bf16[272,256]{1,0:T(8,128)(2,1)S(1)}, u32[]{:S(2)}, u32[]{:S(2)}) collective-permute-start(bf16[272,256]{1,0:T(8,128)(2,1)S(1)} %get-tuple-element.145), channel_id=1, source_target_pairs={{0,27},{1,26},{2,25},{3,24},{4,31},{5,30},{6,29},{7,28},{8,19},{9,... | collective-permute-start | bytes 417800 | tf_op jit(solution)/shard_map/ppermute | solution.py:220
  235.3 6.5 %gradient.2.refs_8_ = f32[1024,2048]{1,0:T(8,128)S(1)} custom-call(bf16[1024,768]{1,0:T(8,128)(2,1)S(1)} %get-tuple-element.148.codes_ref, bf16[1024,48]{1,0:T(8,128)(2,1)S(1)} %get-tuple-element.149.spare_codes_ref, bf16[272,256]{1,0:T(8,128)(2,1)S(1)} %collective-permute-done.53.refs_0_, bf16[272,256]{1,0:T(8,128)(2,1)S(1)} %collective-permute-done.54.refs_1_, ...), custom_call_target="tpu_custom_call" | custom-call | flops 3422552064 | bytes 8388608 | tf_op jit(solution)/shard_map/gradient/pallas_call | solution.py:304
  241.9 2.0 collective-permute-done.51.refs_6_
  243.9 2.4 collective-permute-done.52.refs_7_
  246.3 4.6 %gradient.3 = bf16[1024,2048]{1,0:T(8,128)(2,1)} custom-call(bf16[1024,256]{1,0:T(8,128)(2,1)S(1)} %get-tuple-element.138.codes_ref, bf16[1024,16]{1,0:T(8,128)(2,1)S(1)} %get-tuple-element.139.spare_codes_ref, bf16[272,256]{1,0:T(8,128)(2,1)S(1)} %collective-permute-done.45.refs_24_.refs_0_, bf16[272,256]{1,0:T(8,128)(2,1)S(1)} %collective-permute-done.46.refs_25_.refs_1_, ...), custom_call_target="tpu_custom_call" | custom-call | flops 1140850688 | bytes 8388608 | tf_op jit(solution)/shard_map/gradient/pallas_call | solution.py:304
  (122 shorter events, 42.2 us)
Async XLA Ops:
  22.2 24.0 %collective-permute-start.9 = (bf16[272,1024]{1,0:T(8,128)(2,1)S(1)}, bf16[272,1024]{1,0:T(8,128)(2,1)S(1)}, u32[]{:S(2)}, u32[]{:S(2)}) collective-permute-start(bf16[272,1024]{1,0:T(8,128)(2,1)S(1)} %unpack.1.codes_ref.refs_0_), channel_id=1, source_target_pairs={{0,8},{1,9},{2,10},{3,11},{4,12},{5,13},{6,14},{7,15},{8,0},{9,1},... | collective-permute-start | bytes 1671176 | tf_op jit(solution)/shard_map/ppermute | solution.py:220
  22.3 42.2 %collective-permute-start.7 = (bf16[272,1024]{1,0:T(8,128)(2,1)S(1)}, bf16[272,1024]{1,0:T(8,128)(2,1)S(1)}, u32[]{:S(2)}, u32[]{:S(2)}) collective-permute-start(bf16[272,1024]{1,0:T(8,128)(2,1)S(1)} %unpack.1.codes_ref.refs_0_), channel_id=1, source_target_pairs={{0,16},{1,17},{2,18},{3,19},{4,20},{5,21},{6,22},{7,23},{8,24},{9,... | collective-permute-start | bytes 1671176 | tf_op jit(solution)/shard_map/ppermute | solution.py:220
  46.2 18.2 %collective-permute-start.40 = (bf16[272,256]{1,0:T(8,128)(2,1)S(1)}, bf16[272,256]{1,0:T(8,128)(2,1)S(1)}, u32[]{:S(2)}, u32[]{:S(2)}) collective-permute-start(bf16[272,256]{1,0:T(8,128)(2,1)S(1)} %get-tuple-element.128), channel_id=1, source_target_pairs={{0,4},{1,5},{2,6},{3,7},{4,0},{5,1},{6,2},{7,3},{8,12},{9,13},{10,... | collective-permute-start | bytes 417800 | tf_op jit(solution)/shard_map/ppermute | solution.py:220
  48.0 18.1 %collective-permute-start.10 = (bf16[272,256]{1,0:T(8,128)(2,1)S(1)}, bf16[272,256]{1,0:T(8,128)(2,1)S(1)}, u32[]{:S(2)}, u32[]{:S(2)}) collective-permute-start(bf16[272,256]{1,0:T(8,128)(2,1)S(1)} %get-tuple-element.98), channel_id=1, source_target_pairs={{0,15},{1,14},{2,13},{3,12},{4,11},{5,10},{6,9},{7,8},{8,7},{9,6},... | collective-permute-start | bytes 417800 | tf_op jit(solution)/shard_map/ppermute | solution.py:220
  54.1 14.3 %collective-permute-start.11 = (bf16[272,256]{1,0:T(8,128)(2,1)S(1)}, bf16[272,256]{1,0:T(8,128)(2,1)S(1)}, u32[]{:S(2)}, u32[]{:S(2)}) collective-permute-start(bf16[272,256]{1,0:T(8,128)(2,1)S(1)} %get-tuple-element.99), channel_id=1, source_target_pairs={{0,9},{1,8},{2,11},{3,10},{4,13},{5,12},{6,15},{7,14},{8,1},{9,0},... | collective-permute-start | bytes 417800 | tf_op jit(solution)/shard_map/ppermute | solution.py:220
  54.2 15.5 %collective-permute-start.12 = (bf16[272,256]{1,0:T(8,128)(2,1)S(1)}, bf16[272,256]{1,0:T(8,128)(2,1)S(1)}, u32[]{:S(2)}, u32[]{:S(2)}) collective-permute-start(bf16[272,256]{1,0:T(8,128)(2,1)S(1)} %get-tuple-element.100), channel_id=1, source_target_pairs={{0,14},{1,15},{2,12},{3,13},{4,10},{5,11},{6,8},{7,9},{8,6},{9,7},... | collective-permute-start | bytes 417800 | tf_op jit(solution)/shard_map/ppermute | solution.py:220
  64.5 47.6 %collective-permute-start.8 = (bf16[272,1024]{1,0:T(8,128)(2,1)S(1)}, bf16[272,1024]{1,0:T(8,128)(2,1)S(1)}, u32[]{:S(2)}, u32[]{:S(2)}) collective-permute-start(bf16[272,1024]{1,0:T(8,128)(2,1)S(1)} %collective-permute-done.7.codes_ref.refs_2_), channel_id=1, source_target_pairs={{0,8},{1,9},{2,10},{3,11},{4,12},{5,13},{6,14},{7,15},{8,0},{9,1},... | collective-permute-start | bytes 1671176 | tf_op jit(solution)/shard_map/ppermute | solution.py:220
  68.4 15.9 %collective-permute-start.27 = (bf16[272,256]{1,0:T(8,128)(2,1)S(1)}, bf16[272,256]{1,0:T(8,128)(2,1)S(1)}, u32[]{:S(2)}, u32[]{:S(2)}) collective-permute-start(bf16[272,256]{1,0:T(8,128)(2,1)S(1)} %get-tuple-element.115), channel_id=1, source_target_pairs={{0,17},{1,16},{2,19},{3,18},{4,21},{5,20},{6,23},{7,22},{8,25},{9,... | collective-permute-start | bytes 417800 | tf_op jit(solution)/shard_map/ppermute | solution.py:220
  69.7 14.5 %collective-permute-start.28 = (bf16[272,256]{1,0:T(8,128)(2,1)S(1)}, bf16[272,256]{1,0:T(8,128)(2,1)S(1)}, u32[]{:S(2)}, u32[]{:S(2)}) collective-permute-start(bf16[272,256]{1,0:T(8,128)(2,1)S(1)} %get-tuple-element.116), channel_id=1, source_target_pairs={{0,22},{1,23},{2,20},{3,21},{4,18},{5,19},{6,16},{7,17},{8,30},{9,... | collective-permute-start | bytes 417800 | tf_op jit(solution)/shard_map/ppermute | solution.py:220
  72.3 14.8 %collective-permute-start.29 = (bf16[272,256]{1,0:T(8,128)(2,1)S(1)}, bf16[272,256]{1,0:T(8,128)(2,1)S(1)}, u32[]{:S(2)}, u32[]{:S(2)}) collective-permute-start(bf16[272,256]{1,0:T(8,128)(2,1)S(1)} %get-tuple-element.117), channel_id=1, source_target_pairs={{0,18},{1,19},{2,16},{3,17},{4,22},{5,23},{6,20},{7,21},{8,26},{9,... | collective-permute-start | bytes 417800 | tf_op jit(solution)/shard_map/ppermute | solution.py:220
  84.2 14.4 %collective-permute-start.36 = (bf16[272,256]{1,0:T(8,128)(2,1)S(1)}, bf16[272,256]{1,0:T(8,128)(2,1)S(1)}, u32[]{:S(2)}, u32[]{:S(2)}) collective-permute-start(bf16[272,256]{1,0:T(8,128)(2,1)S(1)} %get-tuple-element.124), channel_id=1, source_target_pairs={{0,12},{1,13},{2,14},{3,15},{4,8},{5,9},{6,10},{7,11},{8,4},{9,5},... | collective-permute-start | bytes 417800 | tf_op jit(solution)/shard_map/ppermute | solution.py:220
  87.1 13.3 %collective-permute-start.37 = (bf16[272,256]{1,0:T(8,128)(2,1)S(1)}, bf16[272,256]{1,0:T(8,128)(2,1)S(1)}, u32[]{:S(2)}, u32[]{:S(2)}) collective-permute-start(bf16[272,256]{1,0:T(8,128)(2,1)S(1)} %get-tuple-element.125), channel_id=1, source_target_pairs={{0,8},{1,9},{2,10},{3,11},{4,12},{5,13},{6,14},{7,15},{8,0},{9,1},... | collective-permute-start | bytes 417800 | tf_op jit(solution)/shard_map/ppermute | solution.py:220
  88.3 19.2 %collective-permute-start.30 = (bf16[272,256]{1,0:T(8,128)(2,1)S(1)}, bf16[272,256]{1,0:T(8,128)(2,1)S(1)}, u32[]{:S(2)}, u32[]{:S(2)}) collective-permute-start(bf16[272,256]{1,0:T(8,128)(2,1)S(1)} %get-tuple-element.118), channel_id=1, source_target_pairs={{0,21},{1,20},{2,23},{3,22},{4,17},{5,16},{6,19},{7,18},{8,29},{9,... | collective-permute-start | bytes 417800 | tf_op jit(solution)/shard_map/ppermute | solution.py:220
  93.6 15.7 %collective-permute-start.31 = (bf16[272,256]{1,0:T(8,128)(2,1)S(1)}, bf16[272,256]{1,0:T(8,128)(2,1)S(1)}, u32[]{:S(2)}, u32[]{:S(2)}) collective-permute-start(bf16[272,256]{1,0:T(8,128)(2,1)S(1)} %get-tuple-element.119), channel_id=1, source_target_pairs={{0,19},{1,18},{2,17},{3,16},{4,23},{5,22},{6,21},{7,20},{8,27},{9,... | collective-permute-start | bytes 417800 | tf_op jit(solution)/shard_map/ppermute | solution.py:220
  109.4 13.0 %collective-permute-start.42 = (bf16[272,256]{1,0:T(8,128)(2,1)S(1)}, bf16[272,256]{1,0:T(8,128)(2,1)S(1)}, u32[]{:S(2)}, u32[]{:S(2)}) collective-permute-start(bf16[272,256]{1,0:T(8,128)(2,1)S(1)} %get-tuple-element.134), channel_id=1, source_target_pairs={{0,9},{1,8},{2,11},{3,10},{4,13},{5,12},{6,15},{7,14},{8,1},{9,0},... | collective-permute-start | bytes 417800 | tf_op jit(solution)/shard_map/ppermute | solution.py:220
  109.8 12.9 %collective-permute-start.43 = (bf16[272,256]{1,0:T(8,128)(2,1)S(1)}, bf16[272,256]{1,0:T(8,128)(2,1)S(1)}, u32[]{:S(2)}, u32[]{:S(2)}) collective-permute-start(bf16[272,256]{1,0:T(8,128)(2,1)S(1)} %get-tuple-element.135), channel_id=1, source_target_pairs={{0,14},{1,15},{2,12},{3,13},{4,10},{5,11},{6,8},{7,9},{8,6},{9,7},... | collective-permute-start | bytes 417800 | tf_op jit(solution)/shard_map/ppermute | solution.py:220
  112.0 13.0 %collective-permute-start.44 = (bf16[272,256]{1,0:T(8,128)(2,1)S(1)}, bf16[272,256]{1,0:T(8,128)(2,1)S(1)}, u32[]{:S(2)}, u32[]{:S(2)}) collective-permute-start(bf16[272,256]{1,0:T(8,128)(2,1)S(1)} %get-tuple-element.136), channel_id=1, source_target_pairs={{0,10},{1,11},{2,8},{3,9},{4,14},{5,15},{6,12},{7,13},{8,2},{9,3},... | collective-permute-start | bytes 417800 | tf_op jit(solution)/shard_map/ppermute | solution.py:220
  112.0 16.8 %collective-permute-start.60 = (bf16[272,256]{1,0:T(8,128)(2,1)S(1)}, bf16[272,256]{1,0:T(8,128)(2,1)S(1)}, u32[]{:S(2)}, u32[]{:S(2)}) collective-permute-start(bf16[272,256]{1,0:T(8,128)(2,1)S(1)} %get-tuple-element.158), channel_id=1, source_target_pairs={{0,13},{1,12},{2,15},{3,14},{4,9},{5,8},{6,11},{7,10},{8,5},{9,4},... | collective-permute-start | bytes 417800 | tf_op jit(solution)/shard_map/ppermute | solution.py:220
  116.3 22.3 %collective-permute-start.61 = (bf16[272,256]{1,0:T(8,128)(2,1)S(1)}, bf16[272,256]{1,0:T(8,128)(2,1)S(1)}, u32[]{:S(2)}, u32[]{:S(2)}) collective-permute-start(bf16[272,256]{1,0:T(8,128)(2,1)S(1)} %get-tuple-element.159), channel_id=1, source_target_pairs={{0,11},{1,10},{2,9},{3,8},{4,15},{5,14},{6,13},{7,12},{8,3},{9,2},... | collective-permute-start | bytes 417800 | tf_op jit(solution)/shard_map/ppermute | solution.py:220
  122.4 16.2 %collective-permute-start.62 = (bf16[272,256]{1,0:T(8,128)(2,1)S(1)}, bf16[272,256]{1,0:T(8,128)(2,1)S(1)}, u32[]{:S(2)}, u32[]{:S(2)}) collective-permute-start(bf16[272,256]{1,0:T(8,128)(2,1)S(1)} %get-tuple-element.160), channel_id=1, source_target_pairs={{0,12},{1,13},{2,14},{3,15},{4,8},{5,9},{6,10},{7,11},{8,4},{9,5},... | collective-permute-start | bytes 417800 | tf_op jit(solution)/shard_map/ppermute | solution.py:220
  122.7 19.4 %collective-permute-start.14 = (bf16[272,256]{1,0:T(8,128)(2,1)S(1)}, bf16[272,256]{1,0:T(8,128)(2,1)S(1)}, u32[]{:S(2)}, u32[]{:S(2)}) collective-permute-start(bf16[272,256]{1,0:T(8,128)(2,1)S(1)} %get-tuple-element.102), channel_id=1, source_target_pairs={{0,31},{1,30},{2,29},{3,28},{4,27},{5,26},{6,25},{7,24},{8,23},{9,... | collective-permute-start | bytes 417800 | tf_op jit(solution)/shard_map/ppermute | solution.py:220
  125.0 27.8 %collective-permute-start.15 = (bf16[272,256]{1,0:T(8,128)(2,1)S(1)}, bf16[272,256]{1,0:T(8,128)(2,1)S(1)}, u32[]{:S(2)}, u32[]{:S(2)}) collective-permute-start(bf16[272,256]{1,0:T(8,128)(2,1)S(1)} %get-tuple-element.103), channel_id=1, source_target_pairs={{0,25},{1,24},{2,27},{3,26},{4,29},{5,28},{6,31},{7,30},{8,17},{9,... | collective-permute-start | bytes 417800 | tf_op jit(solution)/shard_map/ppermute | solution.py:220
  128.8 24.1 %collective-permute-start.16 = (bf16[272,256]{1,0:T(8,128)(2,1)S(1)}, bf16[272,256]{1,0:T(8,128)(2,1)S(1)}, u32[]{:S(2)}, u32[]{:S(2)}) collective-permute-start(bf16[272,256]{1,0:T(8,128)(2,1)S(1)} %get-tuple-element.104), channel_id=1, source_target_pairs={{0,30},{1,31},{2,28},{3,29},{4,26},{5,27},{6,24},{7,25},{8,22},{9,... | collective-permute-start | bytes 417800 | tf_op jit(solution)/shard_map/ppermute | solution.py:220
  138.7 14.3 %collective-permute-start.17 = (bf16[272,256]{1,0:T(8,128)(2,1)S(1)}, bf16[272,256]{1,0:T(8,128)(2,1)S(1)}, u32[]{:S(2)}, u32[]{:S(2)}) collective-permute-start(bf16[272,256]{1,0:T(8,128)(2,1)S(1)} %get-tuple-element.105), channel_id=1, source_target_pairs={{0,26},{1,27},{2,24},{3,25},{4,30},{5,31},{6,28},{7,29},{8,18},{9,... | collective-permute-start | bytes 417800 | tf_op jit(solution)/shard_map/ppermute | solution.py:220
  138.7 15.5 %collective-permute-start.18 = (bf16[272,256]{1,0:T(8,128)(2,1)S(1)}, bf16[272,256]{1,0:T(8,128)(2,1)S(1)}, u32[]{:S(2)}, u32[]{:S(2)}) collective-permute-start(bf16[272,256]{1,0:T(8,128)(2,1)S(1)} %get-tuple-element.106), channel_id=1, source_target_pairs={{0,29},{1,28},{2,31},{3,30},{4,25},{5,24},{6,27},{7,26},{8,21},{9,... | collective-permute-start | bytes 417800 | tf_op jit(solution)/shard_map/ppermute | solution.py:220
  142.0 18.1 %collective-permute-start.19 = (bf16[272,256]{1,0:T(8,128)(2,1)S(1)}, bf16[272,256]{1,0:T(8,128)(2,1)S(1)}, u32[]{:S(2)}, u32[]{:S(2)}) collective-permute-start(bf16[272,256]{1,0:T(8,128)(2,1)S(1)} %get-tuple-element.107), channel_id=1, source_target_pairs={{0,27},{1,26},{2,25},{3,24},{4,31},{5,30},{6,29},{7,28},{8,19},{9,... | collective-permute-start | bytes 417800 | tf_op jit(solution)/shard_map/ppermute | solution.py:220
  152.9 12.7 %collective-permute-start.20 = (bf16[272,256]{1,0:T(8,128)(2,1)S(1)}, bf16[272,256]{1,0:T(8,128)(2,1)S(1)}, u32[]{:S(2)}, u32[]{:S(2)}) collective-permute-start(bf16[272,256]{1,0:T(8,128)(2,1)S(1)} %get-tuple-element.108), channel_id=1, source_target_pairs={{0,28},{1,29},{2,30},{3,31},{4,24},{5,25},{6,26},{7,27},{8,20},{9,... | collective-permute-start | bytes 417800 | tf_op jit(solution)/shard_map/ppermute | solution.py:220
  152.9 14.1 %collective-permute-start.21 = (bf16[272,256]{1,0:T(8,128)(2,1)S(1)}, bf16[272,256]{1,0:T(8,128)(2,1)S(1)}, u32[]{:S(2)}, u32[]{:S(2)}) collective-permute-start(bf16[272,256]{1,0:T(8,128)(2,1)S(1)} %get-tuple-element.109), channel_id=1, source_target_pairs={{0,24},{1,25},{2,26},{3,27},{4,28},{5,29},{6,30},{7,31},{8,16},{9,... | collective-permute-start | bytes 417800 | tf_op jit(solution)/shard_map/ppermute | solution.py:220
  153.0 20.1 %collective-permute-start.63 = (bf16[272,256]{1,0:T(8,128)(2,1)S(1)}, bf16[272,256]{1,0:T(8,128)(2,1)S(1)}, u32[]{:S(2)}, u32[]{:S(2)}) collective-permute-start(bf16[272,256]{1,0:T(8,128)(2,1)S(1)} %get-tuple-element.161), channel_id=1, source_target_pairs={{0,8},{1,9},{2,10},{3,11},{4,12},{5,13},{6,14},{7,15},{8,0},{9,1},... | collective-permute-start | bytes 417800 | tf_op jit(solution)/shard_map/ppermute | solution.py:220
  154.2 21.4 %collective-permute-start.53 = (bf16[272,256]{1,0:T(8,128)(2,1)S(1)}, bf16[272,256]{1,0:T(8,128)(2,1)S(1)}, u32[]{:S(2)}, u32[]{:S(2)}) collective-permute-start(bf16[272,256]{1,0:T(8,128)(2,1)S(1)} %get-tuple-element.150), channel_id=1, source_target_pairs={{0,7},{1,6},{2,5},{3,4},{4,3},{5,2},{6,1},{7,0},{8,15},{9,14},{10,... | collective-permute-start | bytes 417800 | tf_op jit(solution)/shard_map/ppermute | solution.py:220
  160.1 16.9 %collective-permute-start.54 = (bf16[272,256]{1,0:T(8,128)(2,1)S(1)}, bf16[272,256]{1,0:T(8,128)(2,1)S(1)}, u32[]{:S(2)}, u32[]{:S(2)}) collective-permute-start(bf16[272,256]{1,0:T(8,128)(2,1)S(1)} %get-tuple-element.151), channel_id=1, source_target_pairs={{0,1},{1,0},{2,3},{3,2},{4,5},{5,4},{6,7},{7,6},{8,9},{9,8},{10,11... | collective-permute-start | bytes 417800 | tf_op jit(solution)/shard_map/ppermute | solution.py:220
  165.6 13.4 %collective-permute-start.55 = (bf16[272,256]{1,0:T(8,128)(2,1)S(1)}, bf16[272,256]{1,0:T(8,128)(2,1)S(1)}, u32[]{:S(2)}, u32[]{:S(2)}) collective-permute-start(bf16[272,256]{1,0:T(8,128)(2,1)S(1)} %get-tuple-element.152), channel_id=1, source_target_pairs={{0,6},{1,7},{2,4},{3,5},{4,2},{5,3},{6,0},{7,1},{8,14},{9,15},{10,... | collective-permute-start | bytes 417800 | tf_op jit(solution)/shard_map/ppermute | solution.py:220
  167.0 13.6 %collective-permute-start.56 = (bf16[272,256]{1,0:T(8,128)(2,1)S(1)}, bf16[272,256]{1,0:T(8,128)(2,1)S(1)}, u32[]{:S(2)}, u32[]{:S(2)}) collective-permute-start(bf16[272,256]{1,0:T(8,128)(2,1)S(1)} %get-tuple-element.153), channel_id=1, source_target_pairs={{0,2},{1,3},{2,0},{3,1},{4,6},{5,7},{6,4},{7,5},{8,10},{9,11},{10,... | collective-permute-start | bytes 417800 | tf_op jit(solution)/shard_map/ppermute | solution.py:220
  173.1 17.4 %collective-permute-start.57 = (bf16[272,256]{1,0:T(8,128)(2,1)S(1)}, bf16[272,256]{1,0:T(8,128)(2,1)S(1)}, u32[]{:S(2)}, u32[]{:S(2)}) collective-permute-start(bf16[272,256]{1,0:T(8,128)(2,1)S(1)} %get-tuple-element.154), channel_id=1, source_target_pairs={{0,5},{1,4},{2,7},{3,6},{4,1},{5,0},{6,3},{7,2},{8,13},{9,12},{10,... | collective-permute-start | bytes 417800 | tf_op jit(solution)/shard_map/ppermute | solution.py:220
  175.6 14.9 %collective-permute-start.58 = (bf16[272,256]{1,0:T(8,128)(2,1)S(1)}, bf16[272,256]{1,0:T(8,128)(2,1)S(1)}, u32[]{:S(2)}, u32[]{:S(2)}) collective-permute-start(bf16[272,256]{1,0:T(8,128)(2,1)S(1)} %get-tuple-element.155), channel_id=1, source_target_pairs={{0,3},{1,2},{2,1},{3,0},{4,7},{5,6},{6,5},{7,4},{8,11},{9,10},{10,... | collective-permute-start | bytes 417800 | tf_op jit(solution)/shard_map/ppermute | solution.py:220
  177.0 16.5 %collective-permute-start.59 = (bf16[272,256]{1,0:T(8,128)(2,1)S(1)}, bf16[272,256]{1,0:T(8,128)(2,1)S(1)}, u32[]{:S(2)}, u32[]{:S(2)}) collective-permute-start(bf16[272,256]{1,0:T(8,128)(2,1)S(1)} %get-tuple-element.156), channel_id=1, source_target_pairs={{0,4},{1,5},{2,6},{3,7},{4,0},{5,1},{6,2},{7,3},{8,12},{9,13},{10,... | collective-permute-start | bytes 417800 | tf_op jit(solution)/shard_map/ppermute | solution.py:220
  179.0 21.1 %collective-permute-start.45 = (bf16[272,256]{1,0:T(8,128)(2,1)S(1)}, bf16[272,256]{1,0:T(8,128)(2,1)S(1)}, u32[]{:S(2)}, u32[]{:S(2)}) collective-permute-start(bf16[272,256]{1,0:T(8,128)(2,1)S(1)} %get-tuple-element.140), channel_id=1, source_target_pairs={{0,31},{1,30},{2,29},{3,28},{4,27},{5,26},{6,25},{7,24},{8,23},{9,... | collective-permute-start | bytes 417800 | tf_op jit(solution)/shard_map/ppermute | solution.py:220
  180.6 19.5 %collective-permute-start.46 = (bf16[272,256]{1,0:T(8,128)(2,1)S(1)}, bf16[272,256]{1,0:T(8,128)(2,1)S(1)}, u32[]{:S(2)}, u32[]{:S(2)}) collective-permute-start(bf16[272,256]{1,0:T(8,128)(2,1)S(1)} %get-tuple-element.141), channel_id=1, source_target_pairs={{0,25},{1,24},{2,27},{3,26},{4,29},{5,28},{6,31},{7,30},{8,17},{9,... | collective-permute-start | bytes 417800 | tf_op jit(solution)/shard_map/ppermute | solution.py:220
  190.5 17.7 %collective-permute-start.48 = (bf16[272,256]{1,0:T(8,128)(2,1)S(1)}, bf16[272,256]{1,0:T(8,128)(2,1)S(1)}, u32[]{:S(2)}, u32[]{:S(2)}) collective-permute-start(bf16[272,256]{1,0:T(8,128)(2,1)S(1)} %get-tuple-element.143), channel_id=1, source_target_pairs={{0,26},{1,27},{2,24},{3,25},{4,30},{5,31},{6,28},{7,29},{8,18},{9,... | collective-permute-start | bytes 417800 | tf_op jit(solution)/shard_map/ppermute | solution.py:220
  193.6 15.1 %collective-permute-start.64 = (bf16[272,256]{1,0:T(8,128)(2,1)S(1)}, bf16[272,256]{1,0:T(8,128)(2,1)S(1)}, u32[]{:S(2)}, u32[]{:S(2)}) collective-permute-start(bf16[272,256]{1,0:T(8,128)(2,1)S(1)} %get-tuple-element.162), channel_id=1, source_target_pairs={{0,23},{1,22},{2,21},{3,20},{4,19},{5,18},{6,17},{7,16},{8,31},{9,... | collective-permute-start | bytes 417800 | tf_op jit(solution)/shard_map/ppermute | solution.py:220
  200.1 14.1 %collective-permute-start.65 = (bf16[272,256]{1,0:T(8,128)(2,1)S(1)}, bf16[272,256]{1,0:T(8,128)(2,1)S(1)}, u32[]{:S(2)}, u32[]{:S(2)}) collective-permute-start(bf16[272,256]{1,0:T(8,128)(2,1)S(1)} %get-tuple-element.163), channel_id=1, source_target_pairs={{0,17},{1,16},{2,19},{3,18},{4,21},{5,20},{6,23},{7,22},{8,25},{9,... | collective-permute-start | bytes 417800 | tf_op jit(solution)/shard_map/ppermute | solution.py:220
  200.1 14.1 %collective-permute-start.66 = (bf16[272,256]{1,0:T(8,128)(2,1)S(1)}, bf16[272,256]{1,0:T(8,128)(2,1)S(1)}, u32[]{:S(2)}, u32[]{:S(2)}) collective-permute-start(bf16[272,256]{1,0:T(8,128)(2,1)S(1)} %get-tuple-element.164), channel_id=1, source_target_pairs={{0,22},{1,23},{2,20},{3,21},{4,18},{5,19},{6,16},{7,17},{8,30},{9,... | collective-permute-start | bytes 417800 | tf_op jit(solution)/shard_map/ppermute | solution.py:220
  200.6 17.9 %collective-permute-start.67 = (bf16[272,256]{1,0:T(8,128)(2,1)S(1)}, bf16[272,256]{1,0:T(8,128)(2,1)S(1)}, u32[]{:S(2)}, u32[]{:S(2)}) collective-permute-start(bf16[272,256]{1,0:T(8,128)(2,1)S(1)} %get-tuple-element.165), channel_id=1, source_target_pairs={{0,18},{1,19},{2,16},{3,17},{4,22},{5,23},{6,20},{7,21},{8,26},{9,... | collective-permute-start | bytes 417800 | tf_op jit(solution)/shard_map/ppermute | solution.py:220
  208.2 22.1 %collective-permute-start.68 = (bf16[272,256]{1,0:T(8,128)(2,1)S(1)}, bf16[272,256]{1,0:T(8,128)(2,1)S(1)}, u32[]{:S(2)}, u32[]{:S(2)}) collective-permute-start(bf16[272,256]{1,0:T(8,128)(2,1)S(1)} %get-tuple-element.166), channel_id=1, source_target_pairs={{0,21},{1,20},{2,23},{3,22},{4,17},{5,16},{6,19},{7,18},{8,29},{9,... | collective-permute-start | bytes 417800 | tf_op jit(solution)/shard_map/ppermute | solution.py:220
  208.7 25.1 %collective-permute-start.69 = (bf16[272,256]{1,0:T(8,128)(2,1)S(1)}, bf16[272,256]{1,0:T(8,128)(2,1)S(1)}, u32[]{:S(2)}, u32[]{:S(2)}) collective-permute-start(bf16[272,256]{1,0:T(8,128)(2,1)S(1)} %get-tuple-element.167), channel_id=1, source_target_pairs={{0,19},{1,18},{2,17},{3,16},{4,23},{5,22},{6,21},{7,20},{8,27},{9,... | collective-permute-start | bytes 417800 | tf_op jit(solution)/shard_map/ppermute | solution.py:220
  214.2 20.1 %collective-permute-start.70 = (bf16[272,256]{1,0:T(8,128)(2,1)S(1)}, bf16[272,256]{1,0:T(8,128)(2,1)S(1)}, u32[]{:S(2)}, u32[]{:S(2)}) collective-permute-start(bf16[272,256]{1,0:T(8,128)(2,1)S(1)} %get-tuple-element.168), channel_id=1, source_target_pairs={{0,20},{1,21},{2,22},{3,23},{4,16},{5,17},{6,18},{7,19},{8,28},{9,... | collective-permute-start | bytes 417800 | tf_op jit(solution)/shard_map/ppermute | solution.py:220
  214.3 21.1 %collective-permute-start.71 = (bf16[272,256]{1,0:T(8,128)(2,1)S(1)}, bf16[272,256]{1,0:T(8,128)(2,1)S(1)}, u32[]{:S(2)}, u32[]{:S(2)}) collective-permute-start(bf16[272,256]{1,0:T(8,128)(2,1)S(1)} %get-tuple-element.169), channel_id=1, source_target_pairs={{0,16},{1,17},{2,18},{3,19},{4,20},{5,21},{6,22},{7,23},{8,24},{9,... | collective-permute-start | bytes 417800 | tf_op jit(solution)/shard_map/ppermute | solution.py:220
  218.5 23.4 %collective-permute-start.49 = (bf16[272,256]{1,0:T(8,128)(2,1)S(1)}, bf16[272,256]{1,0:T(8,128)(2,1)S(1)}, u32[]{:S(2)}, u32[]{:S(2)}) collective-permute-start(bf16[272,256]{1,0:T(8,128)(2,1)S(1)} %get-tuple-element.144), channel_id=1, source_target_pairs={{0,29},{1,28},{2,31},{3,30},{4,25},{5,24},{6,27},{7,26},{8,21},{9,... | collective-permute-start | bytes 417800 | tf_op jit(solution)/shard_map/ppermute | solution.py:220
  (28 other events, 327.8 us)

commit v3 on v2

--- a/solution.py
+++ b/solution.py
@@ -10,6 +10,14 @@
 loss_scale = 1.0 / 32.0
 SPARE = 2
 STACK = 8
+SENDS = (
+    ["T00", "T01", "C20", "T02", "C21", "T03", "C22", "T10", "C23", "T11", "T12", "T20"]
+    + ["C30", "T13", "C31", "T21", "C32", "T22", "C33", "E00", "T23", "T30", "E01", "T31"]
+    + ["T32", "E02", "T33", "E20", "E03", "E21", "E10", "E22"]
+    + ["E11", "E23", "E30", "E12", "E31", "E13", "E32", "E33"]
+)
+WINDOW = 5
+PIECES = 4
 F32 = jnp.float32
 BF16 = jnp.bfloat16
 
@@ -31,17 +39,17 @@
 def pack_kernel(order, at_ref, owner_ref, mask_ref, codes_ref, *outs):
     messages, (pick_ref, pick_spare_ref, place_ref, place_spare_ref) = outs[:-4], outs[-4:]
     owners = len(messages)
-    rows, visits = owner_ref.shape
+    visits, rows = owner_ref.shape
     width = codes_ref.shape[1] // visits
-    blocks = mask_ref.shape[1] // visits
+    blocks = mask_ref.shape[0] // visits
     block = width // blocks
     main = rows * visits // owners
     slots = owners * (main + SPARE)
     apart = owner_ref[...] ^ at_ref[0]
     relative = sum(jnp.where(apart == k, p, 0) for p, k in enumerate(order))
     eye = lax.broadcasted_iota(jnp.int32, (rows, rows), 0) == lax.broadcasted_iota(jnp.int32, (rows, rows), 1)
-    columns = [relative[:, g : g + 1] for g in range(visits)]
-    lanes = [jnp.sum(jnp.where(eye, column, 0), axis=0, keepdims=True) for column in columns]
+    lanes = [relative[g : g + 1, :] for g in range(visits)]
+    columns = [jnp.sum(jnp.where(eye, lane, 0), axis=1, keepdims=True) for lane in lanes]
     column, lane = jnp.concatenate(columns, axis=0), jnp.concatenate(lanes, axis=1)
     total = rows * visits
     down = lax.broadcasted_iota(jnp.int32, (total, total), 0)
@@ -61,12 +69,12 @@
     pick_spare_ref[...] = pick_rows[:, owners * main :]
     place_ref[...] = place_rows[: owners * main, :]
     place_spare_ref[...] = place_rows[owners * main :, :]
+    live = mask_ref[...].astype(F32).T.astype(BF16)
     used = jnp.concatenate(
         [
             jnp.concatenate(
                 [
-                    codes_ref[:, g * width + b * block : g * width + (b + 1) * block]
-                    * mask_ref[:, g * blocks + b : g * blocks + b + 1].astype(F32).astype(BF16)
+                    codes_ref[:, g * width + b * block : g * width + (b + 1) * block] * live[:, g * blocks + b : g * blocks + b + 1]
                     for b in range(blocks)
                 ],
                 axis=1,
@@ -107,25 +115,43 @@
     return message.shape[0] // STACK - SPARE
 
 
+def cut(codes, pieces):
+    wide = codes.shape[1] // len(pieces)
+    for i, piece in enumerate(pieces):
+        piece[...] = codes[:, i * wide : (i + 1) * wide]
+
+
+def joined(pieces):
+    return jnp.concatenate([piece[...] for piece in pieces], axis=1)
+
+
 def unpack_kernel(owners, *refs):
-    messages, out_ref = refs[:owners], refs[owners]
+    messages, out_ref, pieces = refs[:owners], refs[-1 - PIECES], refs[-PIECES:]
     main, part = main_of(messages[0]), messages[0].shape[1]
     spares = owners * SPARE
     spare = unstacked_spare(messages, main)
     for q in range(STACK):
         out_ref[: owners * main, q * part : (q + 1) * part] = unstacked(messages, q, main)
         out_ref[owners * main :, q * part : (q + 1) * part] = spare[q * spares : (q + 1) * spares, :]
-
-
-def decode_kernel(owners, codes_ref, w_ref, *rest):
-    messages = rest[-owners:]
+    cut(out_ref[...], pieces)
+
+
+def decode_kernel(owners, given, w_ref, *refs):
+    codes = joined(refs[:given])
+    messages, copies = refs[given : given + owners], refs[given + owners :]
+    if copies:
+        cut(codes, copies)
     main, part = main_of(messages[0]), messages[0].shape[1]
     spares = []
     for q in range(STACK):
-        term = mm(codes_ref[...], w_ref[:, q * part : (q + 1) * part]).astype(BF16)
+        term = mm(codes, w_ref[:, q * part : (q + 1) * part]).astype(BF16)
         stack(messages, q, main, term[: owners * main, :])
         spares.append(term[owners * main :, :])
     stack_spare(messages, main, jnp.concatenate(spares, axis=0))
+
+
+def touch_kernel(*refs):
+    refs[-1][...] = jnp.zeros_like(refs[-1])
 
 
 def combine_kernel(owners, place_in_ref, pick_ref, pick_spare_ref, place_ref, place_spare_ref, b_ref, act_ref, *rest):
@@ -146,16 +172,17 @@
     stack_spare(messages, main, jnp.concatenate(spare_out, axis=0))
 
 
-def turn_kernel(chunks, *refs):
-    codes, (out_ref, spare_ref) = refs[:chunks], refs[-2:]
+def turn_kernel(counts, scale, *refs):
+    chunks, (out_ref, spare_ref) = len(counts), refs[-2:]
+    codes = [joined(refs[sum(counts[:j]) : sum(counts[: j + 1])]) for j in range(chunks)]
     main = out_ref.shape[1] // chunks
     for j in range(chunks):
-        out_ref[:, j * main : (j + 1) * main] = codes[j][:main, :].astype(F32).T.astype(BF16)
+        out_ref[:, j * main : (j + 1) * main] = (codes[j][:main, :].astype(F32) * scale).T.astype(BF16)
     spare = jnp.concatenate([code[main:, :] for code in codes], axis=0)
-    spare_ref[...] = spare.astype(F32).T.astype(BF16)
-
-
-def gradient_kernel(chunks, owners, has_base, scale, codes_ref, spare_codes_ref, *refs):
+    spare_ref[...] = (spare.astype(F32) * scale).T.astype(BF16)
+
+
+def gradient_kernel(chunks, owners, has_base, codes_ref, spare_codes_ref, *refs):
     messages, base_ref, (out_ref, spare_ref) = refs[: chunks * owners], refs[chunks * owners], refs[-2:]
     main, part = main_of(messages[0]), messages[0].shape[1]
     spares = owners * SPARE
@@ -178,7 +205,11 @@
         total = mm(codes_ref[...], arrived) + mm(spare_codes_ref[...], spare)
         if has_base:
             total += base_ref[:, columns]
-        out_ref[:, columns] = (total * scale).astype(out_ref.dtype)
+        out_ref[:, columns] = total.astype(out_ref.dtype)
+
+
+def gate_kernel(*_):
+    pass
 
 
 ANYWHERE = pl.BlockSpec(memory_space=pl.ANY)
@@ -206,12 +237,8 @@
     depth = STACK * (main + SPARE)
     local = w_dec.shape[1]
     part = local // STACK
-    place = jnp.stack([lax.axis_index("latent"), lax.axis_index("dp")])
-    order = []
-    for near in range(1, owners // 2 + 1):
-        order += [owners - near] + ([near] if near != owners - near else [])
-    order += [0]
-    half = owners // 2
+    position = jnp.stack([lax.axis_index("latent"), lax.axis_index("dp")])
+    order = [7, 1, 6, 2, 5, 3, 4, 0]
 
     def move(x, j, k):
         if j == 0 and k == 0:
@@ -230,7 +257,7 @@
         grid_spec=pltpu.PrefetchScalarGridSpec(
             num_scalar_prefetch=1,
             grid=(1,),
-            in_specs=[whole((rows, visits)), whole((rows, visits * block_mask.shape[2])), whole((rows, visits * width))],
+            in_specs=[whole((visits, rows)), whole((visits * block_mask.shape[2], rows)), whole((rows, visits * width))],
             out_specs=[whole((depth, width // STACK))] * owners
             + [whole((rows, owners * main)), whole((rows, owners * SPARE))]
             + [whole((owners * main, rows)), whole((owners * SPARE, rows))],
@@ -239,37 +266,44 @@
         + [some((rows, owners * main)), some((rows, owners * SPARE))]
         + [some((owners * main, rows)), some((owners * SPARE, rows))],
         compiler_params=params(12),
-        cost_estimate=cost(2 * slots * rows * visits * width, 4 * rows * visits * width),
+        cost_estimate=cost(2 * slots * rows * visits * width, 0),
         name="pack",
-    )(place, owner_ids, block_mask.reshape(rows, -1), latent_codes.reshape(rows, -1))
+    )(position, owner_ids.T, block_mask.transpose(1, 2, 0).reshape(-1, rows), latent_codes.reshape(rows, -1))
     picks = packed[owners:]
     arrived = move_all(packed[:owners], 0)
-    codes = [None] * groups
-    codes[0] = pl.pallas_call(
+    touched = pl.pallas_call(
+        touch_kernel,
+        in_specs=[whole(w_dec.shape), ANYWHERE],
+        out_shape=some((8, 128), F32),
+        compiler_params=params(12),
+        cost_estimate=cost(0, 2 * width * local),
+        name="touch",
+    )(w_dec, arrived[0])
+    piece = (slots, width // PIECES)
+    own_codes, *sent_codes = pl.pallas_call(
         functools.partial(unpack_kernel, owners),
-        out_shape=some((slots, width)),
+        in_specs=[whole((depth, width // STACK))] * owners + [ANYWHERE],
+        out_shape=[some((slots, width))] + [some(piece)] * PIECES,
         compiler_params=params(8),
         cost_estimate=cost(0, 4 * slots * width),
         name="unpack",
-    )(*arrived)
-    for j in range(1, groups):
-        low = j & -j
-        codes[j] = move(codes[j ^ low], low, 0)
-
-    def decode(j, after):
+    )(*arrived, touched)
+    codes = [[own_codes], [move(own_codes, 1, 0)], [None] * PIECES, [None] * PIECES]
+
+    def decode(j):
+        copied = [piece] * PIECES if j == 2 else []
         return pl.pallas_call(
-            functools.partial(decode_kernel, owners),
-            grid=(1,),
-            in_specs=[whole((slots, width)), whole((width, local))] + [ANYWHERE] * len(after),
-            out_specs=[whole((depth, part))] * owners,
-            out_shape=[some((depth, part))] * owners,
-            compiler_params=params(20),
+            functools.partial(decode_kernel, owners, len(codes[j])),
+            in_specs=[whole((width, local))] + [whole(c.shape) for c in codes[j]],
+            out_specs=[whole((depth, part))] * owners + [whole(c) for c in copied],
+            out_shape=[some((depth, part))] * owners + [some(c) for c in copied],
+            compiler_params=params(16),
             cost_estimate=cost(2 * slots * width * local, 2 * (width * local + slots * (width + local))),
             name="decode",
-        )(codes[j], w_dec, *after)
-
-    def combine(j, rebuilt, after):
-        after = ([] if rebuilt is None else [rebuilt]) + after
+        )(w_dec, *codes[j])
+
+    def combine(j, rebuilt):
+        after = [] if rebuilt is None else [rebuilt]
         outs = pl.pallas_call(
             functools.partial(combine_kernel, owners),
             grid_spec=pltpu.PrefetchScalarGridSpec(
@@ -283,26 +317,28 @@
                 out_specs=[pl.BlockSpec((rows, local), lambda _, at: (0, at[1] ^ j))] + [whole((depth, part))] * owners,
             ),
             out_shape=[some((rows, model))] + [some((depth, part))] * owners,
-            input_output_aliases={} if rebuilt is None else {7 + owners: 0},
+            input_output_aliases={7 + owners: 0} if after else {},
             compiler_params=params(16),
             cost_estimate=cost(4 * slots * rows * local, 2 * local * (2 * slots + 2 * rows)),
             name="combine",
-        )(place, *picks, b_dec.reshape(1, -1), activations, *terms[j], *after)
+        )(position, *picks, b_dec.reshape(1, -1), activations, *terms[j], *after)
         return outs[0], outs[1:]
 
-    def gradient(chunks, base, scale, dtype, per, after):
+    def gradient(chunks, base, dtype, per, after):
         count = len(chunks)
+        pieces = [c for j in chunks for c in codes[j]]
         turned = pl.pallas_call(
-            functools.partial(turn_kernel, count),
+            functools.partial(turn_kernel, [len(codes[j]) for j in chunks], loss_scale),
+            in_specs=[whole(c.shape) for c in pieces],
             out_shape=[some((width, count * owners * main)), some((width, count * owners * SPARE))],
             compiler_params=params(16),
             cost_estimate=cost(0, 4 * count * slots * width),
             name="turn",
-        )(*[codes[j] for j in chunks])
+        )(*pieces)
         block = pl.BlockSpec((width, per * part), lambda q: (0, q))
         extra = ([] if base is None else [base]) + after
         return pl.pallas_call(
-            functools.partial(gradient_kernel, count, owners, base is not None, scale),
+            functools.partial(gradient_kernel, count, owners, base is not None),
             grid=(STACK // per,),
             in_specs=[whole(t.shape) for t in turned]
             + [whole((depth, part))] * (count * owners)
@@ -316,17 +352,41 @@
             name="gradient",
         )(*turned, *[m for j in chunks for m in errors[j]], *extra)
 
-    terms, errors = [None] * groups, [None] * groups
-    for j in range(groups):
-        terms[j] = move_all(decode(j, list(terms[j - 2][:half]) if j >= 2 else []), j)
-    rebuilt = None
-    for j in range(groups):
-        ahead = terms[j + 1][:half] if j + 1 < groups else errors[j - 2][:half] if j >= 2 else []
-        rebuilt, outgoing = combine(j, rebuilt, list(ahead))
-        errors[j] = move_all(outgoing, j)
-    early, last = list(range(groups - 1)), [groups - 1]
-    base = gradient(early, None, 1.0, F32, 1, list(errors[groups - 1][:half]))
-    return rebuilt, gradient(last, base, loss_scale, BF16, 2, [])
+    def gate(messages, after):
+        held = pl.pallas_call(
+            gate_kernel,
+            in_specs=[ANYWHERE] * (len(messages) + len(after)),
+            out_specs=[ANYWHERE] * len(messages),
+            out_shape=[some(m.shape) for m in messages],
+            input_output_aliases={i: i for i in range(len(messages))},
+            compiler_params=params(1),
+            cost_estimate=cost(0, 0),
+            name="gate",
+        )(*messages, *after)
+        return list(held)
+
+    terms, errors, leaving = [[None] * owners for _ in range(groups)], [[None] * owners for _ in range(groups)], {}
+    rebuilt, arrivals, held = None, list(codes[1]), []
+    for kind, j, at in SENDS:
+        j, at = int(j), int(at)
+        if kind == "C":
+            chunk, messages = codes[j], [(sent_codes[at], 2, 0, at) if j == 2 else (leaving["T", 2][owners + at], 1, 0, at)]
+        else:
+            chunk = (terms if kind == "T" else errors)[j]
+            if (kind, j) not in leaving:
+                if kind == "T":
+                    leaving[kind, j] = decode(j)
+                else:
+                    rebuilt, leaving[kind, j] = combine(j, rebuilt)
+            messages = [(leaving[kind, j][p], j, order[p], p) for p in (2 * at, 2 * at + 1)]
+        for message, across, along, place in messages:
+            if across or along:
+                (message,) = held = gate([message], arrivals[-WINDOW:][:1] * (len(arrivals) >= WINDOW) + held)
+                message = move(message, across, along)
+                arrivals.append(message)
+            chunk[place] = message
+    base = gradient([0, 2, 1], None, F32, 1, held[:1])
+    return rebuilt, gradient([3], base, BF16, 2, [])
 
 
 def on_device_wide(activations, owner_ids, block_mask, latent_codes, w_dec, b_dec):
@@ -382,7 +442,7 @@
         owners = mesh.shape["latent"]
         share = owner_ids.size // owners
         fits = share % 16 == 0 and owners * SPARE % 16 == 0 and w_dec.shape[1] % (128 * STACK) == 0
-        fits = fits and mesh.size & (mesh.size - 1) == 0
+        fits = fits and owners == 8 and mesh.shape["dp"] == 4
         pick = on_device if fits else on_device_wide
         return pick(activations, owner_ids, block_mask, latent_codes, w_dec, b_dec)
 

time: 251 us -> 239 us (0.952)
  starting transfers between devices: 160 us -> 135 us
  waiting for transfers between devices: 53.8 us -> 65 us
    ppermute x72 -> x78, starting transfers between devices: 160 us -> 135 us  [move(): return lax.ppermute(x, ('dp', 'latent'), pairs)]
    ppermute x72 -> x78, waiting for transfers between devices: 53.8 us -> 65 us  [move(): return lax.ppermute(x, ('dp', 'latent'), pairs)]
    unnamed x10 -> x13, local copies, waits for them, and re-layouts: 4.14 us -> 5.92 us
    pallas_call x7 -> x78, Pallas kernels: 6.87 us -> 6.99 us  [the longest x4 5.82 us: decode(): pl.pallas_call(functools.partial(decode_kernel, owners, len(codes[j])), i...]
  transfers between devices with their start and end apart: 72 -> 78, of which waited for: 18 -> 23; matrix products, arithmetic and copies ran while one was open for 0% -> 0% of each run, Pallas kernels for 10% -> 11%
where the time goes in v3:
time: 239 us
  starting transfers between devices  135 us (56%)
  waiting for transfers between devices  65 us (27%)
  Pallas kernels  32.1 us (13%)
  local copies, waits for them, and re-layouts  5.92 us (2%)
    ppermute x78, starting transfers between devices, move(): return lax.ppermute(x, ('dp', 'latent'), pairs)  135 us
    ppermute x78, waiting for transfers between devices, move(): return lax.ppermute(x, ('dp', 'latent'), pairs)  65 us
    pallas_call x4, Pallas kernels, combine(): pl.pallas_call(functools.partial(combine_kernel, owners), grid_spec=pltpu...  12.5 us
    pallas_call x2, Pallas kernels, gradient(): pl.pallas_call(functools.partial(gradient_kernel, count, owners, base is...  11.3 us
    unnamed x13, local copies, waits for them, and re-layouts  5.92 us
    pallas_call x4, Pallas kernels, decode(): pl.pallas_call(functools.partial(decode_kernel, owners, len(codes[j])), i...  5.82 us
  transfers between devices with their start and end apart: 78, of which 23 were waited for; matrix products, arithmetic and copies ran while one was open for 0% of the time, Pallas kernels for 11%

profile of v3, /device:TPU:0, one launch (start us, length us, event | category | flops | bytes accessed | tf_op | source)
XLA Modules:
  0.0 239.0 jit_solution(16540944719257617760)
XLA Ops:
  4.7 6.0 %collective-permute-start = (bf16[272,128]{1,0:T(8,128)(2,1)S(1)}, bf16[272,128]{1,0:T(8,128)(2,1)S(1)}, u32[]{:S(2)}, u32[]{:S(2)}) collective-permute-start(bf16[272,128]{1,0:T(8,128)(2,1)S(1)} %get-tuple-element.99), channel_id=1, source_target_pairs={{0,7},{1,6},{2,5},{3,4},{4,3},{5,2},{6,1},{7,0},{8,15},{9,14},{10,... | collective-permute-start | bytes 208904 | tf_op jit(solution)/shard_map/ppermute | solution.py:247
  11.3 5.2 %collective-permute-start.4 = (bf16[272,128]{1,0:T(8,128)(2,1)S(1)}, bf16[272,128]{1,0:T(8,128)(2,1)S(1)}, u32[]{:S(2)}, u32[]{:S(2)}) collective-permute-start(bf16[272,128]{1,0:T(8,128)(2,1)S(1)} %get-tuple-element.103), channel_id=1, source_target_pairs={{0,5},{1,4},{2,7},{3,6},{4,1},{5,0},{6,3},{7,2},{8,13},{9,12},{10,... | collective-permute-start | bytes 208904 | tf_op jit(solution)/shard_map/ppermute | solution.py:247
  16.6 2.5 %collective-permute-start.6 = (bf16[272,128]{1,0:T(8,128)(2,1)S(1)}, bf16[272,128]{1,0:T(8,128)(2,1)S(1)}, u32[]{:S(2)}, u32[]{:S(2)}) collective-permute-start(bf16[272,128]{1,0:T(8,128)(2,1)S(1)} %get-tuple-element.105), channel_id=1, source_target_pairs={{0,4},{1,5},{2,6},{3,7},{4,0},{5,1},{6,2},{7,3},{8,12},{9,13},{10,... | collective-permute-start | bytes 208904 | tf_op jit(solution)/shard_map/ppermute | solution.py:247
  19.0 2.2 copy-done
  24.9 2.9 %collective-permute-start.11 = (bf16[272,256]{1,0:T(8,128)(2,1)S(1)}, bf16[272,256]{1,0:T(8,128)(2,1)S(1)}, u32[]{:S(2)}, u32[]{:S(2)}) collective-permute-start(bf16[272,256]{1,0:T(8,128)(2,1)S(1)} %gate.70.__1_), channel_id=1, source_target_pairs={{0,7},{1,6},{2,5},{3,4},{4,3},{5,2},{6,1},{7,0},{8,15},{9,14},{10,... | collective-permute-start | bytes 417800 | tf_op jit(solution)/shard_map/ppermute | solution.py:247
  32.8 6.9 %collective-permute-start.16 = (bf16[272,256]{1,0:T(8,128)(2,1)S(1)}, bf16[272,256]{1,0:T(8,128)(2,1)S(1)}, u32[]{:S(2)}, u32[]{:S(2)}) collective-permute-start(bf16[272,256]{1,0:T(8,128)(2,1)S(1)} %gate.75.__2_), channel_id=1, source_target_pairs={{0,5},{1,4},{2,7},{3,6},{4,1},{5,0},{6,3},{7,2},{8,13},{9,12},{10,... | collective-permute-start | bytes 417800 | tf_op jit(solution)/shard_map/ppermute | solution.py:247
  41.5 3.0 %collective-permute-start.18 = (bf16[272,256]{1,0:T(8,128)(2,1)S(1)}, bf16[272,256]{1,0:T(8,128)(2,1)S(1)}, u32[]{:S(2)}, u32[]{:S(2)}) collective-permute-start(bf16[272,256]{1,0:T(8,128)(2,1)S(1)} %gate.78.__2_), channel_id=1, source_target_pairs={{0,4},{1,5},{2,6},{3,7},{4,0},{5,1},{6,2},{7,3},{8,12},{9,13},{10,... | collective-permute-start | bytes 417800 | tf_op jit(solution)/shard_map/ppermute | solution.py:247
  48.5 4.0 %collective-permute-start.21 = (bf16[272,256]{1,0:T(8,128)(2,1)S(1)}, bf16[272,256]{1,0:T(8,128)(2,1)S(1)}, u32[]{:S(2)}, u32[]{:S(2)}) collective-permute-start(bf16[272,256]{1,0:T(8,128)(2,1)S(1)} %gate.81.__2_), channel_id=1, source_target_pairs={{0,9},{1,8},{2,11},{3,10},{4,13},{5,12},{6,15},{7,14},{8,1},{9,0},... | collective-permute-start | bytes 417800 | tf_op jit(solution)/shard_map/ppermute | solution.py:247
  54.0 2.4 collective-permute-done.18.__1_.rest_6_
  57.0 2.7 %collective-permute-start.26 = (bf16[272,256]{1,0:T(8,128)(2,1)S(1)}, bf16[272,256]{1,0:T(8,128)(2,1)S(1)}, u32[]{:S(2)}, u32[]{:S(2)}) collective-permute-start(bf16[272,256]{1,0:T(8,128)(2,1)S(1)} %gate.85.__2_), channel_id=1, source_target_pairs={{0,13},{1,12},{2,15},{3,14},{4,9},{5,8},{6,11},{7,10},{8,5},{9,4},... | collective-permute-start | bytes 417800 | tf_op jit(solution)/shard_map/ppermute | solution.py:247
  59.6 2.1 collective-permute-start.25
  63.2 3.6 %collective-permute-start.24 = (bf16[272,256]{1,0:T(8,128)(2,1)S(1)}, bf16[272,256]{1,0:T(8,128)(2,1)S(1)}, u32[]{:S(2)}, u32[]{:S(2)}) collective-permute-start(bf16[272,256]{1,0:T(8,128)(2,1)S(1)} %gate.87.__2_), channel_id=1, source_target_pairs={{0,23},{1,22},{2,21},{3,20},{4,19},{5,18},{6,17},{7,16},{8,31},{9,... | collective-permute-start | bytes 417800 | tf_op jit(solution)/shard_map/ppermute | solution.py:247
  68.0 3.1 %collective-permute-done.26.__1_.rest_4_ = bf16[272,256]{1,0:T(8,128)(2,1)S(1)} collective-permute-done((bf16[272,256]{1,0:T(8,128)(2,1)S(1)}, bf16[272,256]{1,0:T(8,128)(2,1)S(1)}, u32[]{:S(2)}, u32[]{:S(2)}) %collective-permute-start.26) | collective-permute-done | bytes 139296 | tf_op jit(solution)/shard_map/ppermute | solution.py:247
  72.1 2.7 %collective-permute-done.24.__1_.rest_0_ = bf16[272,256]{1,0:T(8,128)(2,1)S(1)} collective-permute-done((bf16[272,256]{1,0:T(8,128)(2,1)S(1)}, bf16[272,256]{1,0:T(8,128)(2,1)S(1)}, u32[]{:S(2)}, u32[]{:S(2)}) %collective-permute-start.24) | collective-permute-done | bytes 139296 | tf_op jit(solution)/shard_map/ppermute | solution.py:247
  76.8 3.6 %collective-permute-start.31 = (bf16[272,256]{1,0:T(8,128)(2,1)S(1)}, bf16[272,256]{1,0:T(8,128)(2,1)S(1)}, u32[]{:S(2)}, u32[]{:S(2)}) collective-permute-start(bf16[272,256]{1,0:T(8,128)(2,1)S(1)} %gate.93.__2_), channel_id=1, source_target_pairs={{0,22},{1,23},{2,20},{3,21},{4,18},{5,19},{6,16},{7,17},{8,30},{9,... | collective-permute-start | bytes 417800 | tf_op jit(solution)/shard_map/ppermute | solution.py:247
  81.8 4.0 %collective-permute-done.28.__1_.rest_6_ = bf16[272,256]{1,0:T(8,128)(2,1)S(1)} collective-permute-done((bf16[272,256]{1,0:T(8,128)(2,1)S(1)}, bf16[272,256]{1,0:T(8,128)(2,1)S(1)}, u32[]{:S(2)}, u32[]{:S(2)}) %collective-permute-start.28) | collective-permute-done | bytes 139296 | tf_op jit(solution)/shard_map/ppermute | solution.py:247
  86.7 2.7 %collective-permute-start.35 = (bf16[272,256]{1,0:T(8,128)(2,1)S(1)}, bf16[272,256]{1,0:T(8,128)(2,1)S(1)}, u32[]{:S(2)}, u32[]{:S(2)}) collective-permute-start(bf16[272,256]{1,0:T(8,128)(2,1)S(1)} %gate.96.__2_), channel_id=1, source_target_pairs={{0,21},{1,20},{2,23},{3,22},{4,17},{5,16},{6,19},{7,18},{8,29},{9,... | collective-permute-start | bytes 417800 | tf_op jit(solution)/shard_map/ppermute | solution.py:247
  89.6 3.1 %combine.4 = (bf16[128,8192]{1,0:T(8,128)(2,1)}, bf16[272,256]{1,0:T(8,128)(2,1)S(1)}, bf16[272,256]{1,0:T(8,128)(2,1)S(1)}, bf16[272,256]{1,0:T(8,128)(2,1)S(1)...) custom-call(s32[2]{0:T(128)S(1)} %pad_add_fusion.at_ref.place_in_ref, ...), custom_call_target="tpu_custom_call" | custom-call | flops 285212672 | bytes 3276800 | tf_op jit(solution)/shard_map/combine/pallas_call | solution.py:307
  92.7 5.4 %collective-permute-start.38 = (bf16[272,256]{1,0:T(8,128)(2,1)S(1)}, bf16[272,256]{1,0:T(8,128)(2,1)S(1)}, u32[]{:S(2)}, u32[]{:S(2)}) collective-permute-start(bf16[272,256]{1,0:T(8,128)(2,1)S(1)} %gate.99.__2_), channel_id=1, source_target_pairs={{0,7},{1,6},{2,5},{3,4},{4,3},{5,2},{6,1},{7,0},{8,15},{9,14},{10,... | collective-permute-start | bytes 417800 | tf_op jit(solution)/shard_map/ppermute | solution.py:247
  98.1 8.6 %collective-permute-done.35.__1_.rest_4_ = bf16[272,256]{1,0:T(8,128)(2,1)S(1)} collective-permute-done((bf16[272,256]{1,0:T(8,128)(2,1)S(1)}, bf16[272,256]{1,0:T(8,128)(2,1)S(1)}, u32[]{:S(2)}, u32[]{:S(2)}) %collective-permute-start.35) | collective-permute-done | bytes 139296 | tf_op jit(solution)/shard_map/ppermute | solution.py:247
  108.9 3.3 %collective-permute-start.39 = (bf16[272,256]{1,0:T(8,128)(2,1)S(1)}, bf16[272,256]{1,0:T(8,128)(2,1)S(1)}, u32[]{:S(2)}, u32[]{:S(2)}) collective-permute-start(bf16[272,256]{1,0:T(8,128)(2,1)S(1)} %gate.104.__2_), channel_id=1, source_target_pairs={{0,25},{1,24},{2,27},{3,26},{4,29},{5,28},{6,31},{7,30},{8,17},{9,... | collective-permute-start | bytes 417800 | tf_op jit(solution)/shard_map/ppermute | solution.py:247
  112.2 2.4 collective-permute-start.46
  118.4 6.0 %collective-permute-start.44 = (bf16[272,256]{1,0:T(8,128)(2,1)S(1)}, bf16[272,256]{1,0:T(8,128)(2,1)S(1)}, u32[]{:S(2)}, u32[]{:S(2)}) collective-permute-start(bf16[272,256]{1,0:T(8,128)(2,1)S(1)} %gate.108.__2_), channel_id=1, source_target_pairs={{0,26},{1,27},{2,24},{3,25},{4,30},{5,31},{6,28},{7,29},{8,18},{9,... | collective-permute-start | bytes 417800 | tf_op jit(solution)/shard_map/ppermute | solution.py:247
  124.4 7.5 %collective-permute-start.47 = (bf16[272,256]{1,0:T(8,128)(2,1)S(1)}, bf16[272,256]{1,0:T(8,128)(2,1)S(1)}, u32[]{:S(2)}, u32[]{:S(2)}) collective-permute-start(bf16[272,256]{1,0:T(8,128)(2,1)S(1)} %gate.110.__2_), channel_id=1, source_target_pairs={{0,27},{1,26},{2,25},{3,24},{4,31},{5,30},{6,29},{7,28},{8,19},{9,... | collective-permute-start | bytes 417800 | tf_op jit(solution)/shard_map/ppermute | solution.py:247
  131.9 3.1 %combine.5 = (bf16[128,8192]{1,0:T(8,128)(2,1)}, bf16[272,256]{1,0:T(8,128)(2,1)S(1)}, bf16[272,256]{1,0:T(8,128)(2,1)S(1)}, bf16[272,256]{1,0:T(8,128)(2,1)S(1)...) custom-call(s32[2]{0:T(128)S(1)} %pad_add_fusion.at_ref.place_in_ref, ...), custom_call_target="tpu_custom_call", output_to_operand_aliasing={{0}: (15, {})} | custom-call | flops 285212672 | bytes 3276800 | tf_op jit(solution)/shard_map/combine/pallas_call | solution.py:307
  135.0 3.5 %collective-permute-start.51 = (bf16[272,256]{1,0:T(8,128)(2,1)S(1)}, bf16[272,256]{1,0:T(8,128)(2,1)S(1)}, u32[]{:S(2)}, u32[]{:S(2)}) collective-permute-start(bf16[272,256]{1,0:T(8,128)(2,1)S(1)} %gate.112.__2_), channel_id=1, source_target_pairs={{0,3},{1,2},{2,1},{3,0},{4,7},{5,6},{6,5},{7,4},{8,11},{9,10},{10,... | collective-permute-start | bytes 417800 | tf_op jit(solution)/shard_map/ppermute | solution.py:247
  138.5 3.2 %collective-permute-done.45.__1_.rest_4_ = bf16[272,256]{1,0:T(8,128)(2,1)S(1)} collective-permute-done((bf16[272,256]{1,0:T(8,128)(2,1)S(1)}, bf16[272,256]{1,0:T(8,128)(2,1)S(1)}, u32[]{:S(2)}, u32[]{:S(2)}) %collective-permute-start.45) | collective-permute-done | bytes 139296 | tf_op jit(solution)/shard_map/ppermute | solution.py:247
  141.7 4.4 %collective-permute-start.50 = (bf16[272,256]{1,0:T(8,128)(2,1)S(1)}, bf16[272,256]{1,0:T(8,128)(2,1)S(1)}, u32[]{:S(2)}, u32[]{:S(2)}) collective-permute-start(bf16[272,256]{1,0:T(8,128)(2,1)S(1)} %gate.114.__2_), channel_id=1, source_target_pairs={{0,24},{1,25},{2,26},{3,27},{4,28},{5,29},{6,30},{7,31},{8,16},{9,... | collective-permute-start | bytes 417800 | tf_op jit(solution)/shard_map/ppermute | solution.py:247
  146.1 3.3 %combine.6 = (bf16[128,8192]{1,0:T(8,128)(2,1)}, bf16[272,256]{1,0:T(8,128)(2,1)S(1)}, bf16[272,256]{1,0:T(8,128)(2,1)S(1)}, bf16[272,256]{1,0:T(8,128)(2,1)S(1)...) custom-call(s32[2]{0:T(128)S(1)} %pad_add_fusion.at_ref.place_in_ref, ...), custom_call_target="tpu_custom_call", output_to_operand_aliasing={{0}: (15, {})} | custom-call | flops 285212672 | bytes 3276800 | tf_op jit(solution)/shard_map/combine/pallas_call | solution.py:307
  149.9 3.3 %collective-permute-start.55 = (bf16[272,256]{1,0:T(8,128)(2,1)S(1)}, bf16[272,256]{1,0:T(8,128)(2,1)S(1)}, u32[]{:S(2)}, u32[]{:S(2)}) collective-permute-start(bf16[272,256]{1,0:T(8,128)(2,1)S(1)} %gate.116.__2_), channel_id=1, source_target_pairs={{0,17},{1,16},{2,19},{3,18},{4,21},{5,20},{6,23},{7,22},{8,25},{9,... | collective-permute-start | bytes 417800 | tf_op jit(solution)/shard_map/ppermute | solution.py:247
  153.3 5.8 %collective-permute-done.49.rest_6_.__1_ = bf16[272,256]{1,0:T(8,128)(2,1)S(1)} collective-permute-done((bf16[272,256]{1,0:T(8,128)(2,1)S(1)}, bf16[272,256]{1,0:T(8,128)(2,1)S(1)}, u32[]{:S(2)}, u32[]{:S(2)}) %collective-permute-start.49) | collective-permute-done | bytes 139296 | tf_op jit(solution)/shard_map/ppermute | solution.py:247
  159.2 3.6 %collective-permute-start.60 = (bf16[272,256]{1,0:T(8,128)(2,1)S(1)}, bf16[272,256]{1,0:T(8,128)(2,1)S(1)}, u32[]{:S(2)}, u32[]{:S(2)}) collective-permute-start(bf16[272,256]{1,0:T(8,128)(2,1)S(1)} %gate.120.__2_), channel_id=1, source_target_pairs={{0,15},{1,14},{2,13},{3,12},{4,11},{5,10},{6,9},{7,8},{8,7},{9,6},... | collective-permute-start | bytes 417800 | tf_op jit(solution)/shard_map/ppermute | solution.py:247
  162.9 6.2 %collective-permute-done.54.__1_.refs_6_ = bf16[272,256]{1,0:T(8,128)(2,1)S(1)} collective-permute-done((bf16[272,256]{1,0:T(8,128)(2,1)S(1)}, bf16[272,256]{1,0:T(8,128)(2,1)S(1)}, u32[]{:S(2)}, u32[]{:S(2)}) %collective-permute-start.54) | collective-permute-done | bytes 139296 | tf_op jit(solution)/shard_map/ppermute | solution.py:247
  169.1 8.3 %collective-permute-start.57 = (bf16[272,256]{1,0:T(8,128)(2,1)S(1)}, bf16[272,256]{1,0:T(8,128)(2,1)S(1)}, u32[]{:S(2)}, u32[]{:S(2)}) collective-permute-start(bf16[272,256]{1,0:T(8,128)(2,1)S(1)} %gate.123.__2_), channel_id=1, source_target_pairs={{0,19},{1,18},{2,17},{3,16},{4,23},{5,22},{6,21},{7,20},{8,27},{9,... | collective-permute-start | bytes 417800 | tf_op jit(solution)/shard_map/ppermute | solution.py:247
  177.4 2.4 %collective-permute-start.67 = (bf16[272,256]{1,0:T(8,128)(2,1)S(1)}, bf16[272,256]{1,0:T(8,128)(2,1)S(1)}, u32[]{:S(2)}, u32[]{:S(2)}) collective-permute-start(bf16[272,256]{1,0:T(8,128)(2,1)S(1)} %gate.125.__2_), channel_id=1, source_target_pairs={{0,10},{1,11},{2,8},{3,9},{4,14},{5,15},{6,12},{7,13},{8,2},{9,3},... | collective-permute-start | bytes 417800 | tf_op jit(solution)/shard_map/ppermute | solution.py:247
  179.8 3.1 %combine.7 = (bf16[128,8192]{1,0:T(8,128)(2,1)}, bf16[272,256]{1,0:T(8,128)(2,1)S(1)}, bf16[272,256]{1,0:T(8,128)(2,1)S(1)}, bf16[272,256]{1,0:T(8,128)(2,1)S(1)...) custom-call(s32[2]{0:T(128)S(1)} %pad_add_fusion.at_ref.place_in_ref, ...), custom_call_target="tpu_custom_call", output_to_operand_aliasing={{0}: (15, {})} | custom-call | flops 285212672 | bytes 3276800 | tf_op jit(solution)/shard_map/combine/pallas_call | solution.py:307
  182.9 3.7 %collective-permute-start.66 = (bf16[272,256]{1,0:T(8,128)(2,1)S(1)}, bf16[272,256]{1,0:T(8,128)(2,1)S(1)}, u32[]{:S(2)}, u32[]{:S(2)}) collective-permute-start(bf16[272,256]{1,0:T(8,128)(2,1)S(1)} %gate.126.__2_), channel_id=1, source_target_pairs={{0,20},{1,21},{2,22},{3,23},{4,16},{5,17},{6,18},{7,19},{8,28},{9,... | collective-permute-start | bytes 417800 | tf_op jit(solution)/shard_map/ppermute | solution.py:247
  186.6 2.0 collective-permute-start.62
  188.7 2.6 %collective-permute-start.64 = (bf16[272,256]{1,0:T(8,128)(2,1)S(1)}, bf16[272,256]{1,0:T(8,128)(2,1)S(1)}, u32[]{:S(2)}, u32[]{:S(2)}) collective-permute-start(bf16[272,256]{1,0:T(8,128)(2,1)S(1)} %gate.129.__2_), channel_id=1, source_target_pairs={{0,25},{1,24},{2,27},{3,26},{4,29},{5,28},{6,31},{7,30},{8,17},{9,... | collective-permute-start | bytes 417800 | tf_op jit(solution)/shard_map/ppermute | solution.py:247
  192.0 8.7 %collective-permute-done.66.__1_.refs_14_ = bf16[272,256]{1,0:T(8,128)(2,1)S(1)} collective-permute-done((bf16[272,256]{1,0:T(8,128)(2,1)S(1)}, bf16[272,256]{1,0:T(8,128)(2,1)S(1)}, u32[]{:S(2)}, u32[]{:S(2)}) %collective-permute-start.66) | collective-permute-done | bytes 139296 | tf_op jit(solution)/shard_map/ppermute | solution.py:247
  200.7 2.8 %collective-permute-start.68 = (bf16[272,256]{1,0:T(8,128)(2,1)S(1)}, bf16[272,256]{1,0:T(8,128)(2,1)S(1)}, u32[]{:S(2)}, u32[]{:S(2)}) collective-permute-start(bf16[272,256]{1,0:T(8,128)(2,1)S(1)} %gate.132.__2_), channel_id=1, source_target_pairs={{0,30},{1,31},{2,28},{3,29},{4,26},{5,27},{6,24},{7,25},{8,22},{9,... | collective-permute-start | bytes 417800 | tf_op jit(solution)/shard_map/ppermute | solution.py:247
  203.5 3.2 %collective-permute-start.69 = (bf16[272,256]{1,0:T(8,128)(2,1)S(1)}, bf16[272,256]{1,0:T(8,128)(2,1)S(1)}, u32[]{:S(2)}, u32[]{:S(2)}) collective-permute-start(bf16[272,256]{1,0:T(8,128)(2,1)S(1)} %gate.133.__2_), channel_id=1, source_target_pairs={{0,26},{1,27},{2,24},{3,25},{4,30},{5,31},{6,28},{7,29},{8,18},{9,... | collective-permute-start | bytes 417800 | tf_op jit(solution)/shard_map/ppermute | solution.py:247
  208.6 5.3 %collective-permute-done.70.__1_.refs_21_ = bf16[272,256]{1,0:T(8,128)(2,1)S(1)} collective-permute-done((bf16[272,256]{1,0:T(8,128)(2,1)S(1)}, bf16[272,256]{1,0:T(8,128)(2,1)S(1)}, u32[]{:S(2)}, u32[]{:S(2)}) %collective-permute-start.70) | collective-permute-done | bytes 139296 | tf_op jit(solution)/shard_map/ppermute | solution.py:247
  215.3 2.5 %collective-permute-start.74 = (bf16[272,256]{1,0:T(8,128)(2,1)S(1)}, bf16[272,256]{1,0:T(8,128)(2,1)S(1)}, u32[]{:S(2)}, u32[]{:S(2)}) collective-permute-start(bf16[272,256]{1,0:T(8,128)(2,1)S(1)} %gate.138.__2_), channel_id=1, source_target_pairs={{0,28},{1,29},{2,30},{3,31},{4,24},{5,25},{6,26},{7,27},{8,20},{9,... | collective-permute-start | bytes 417800 | tf_op jit(solution)/shard_map/ppermute | solution.py:247
  217.8 3.3 %collective-permute-done.75.__1_.refs_22_ = bf16[272,256]{1,0:T(8,128)(2,1)S(1)} collective-permute-done((bf16[272,256]{1,0:T(8,128)(2,1)S(1)}, bf16[272,256]{1,0:T(8,128)(2,1)S(1)}, u32[]{:S(2)}, u32[]{:S(2)}) %collective-permute-start.75) | collective-permute-done | bytes 139296 | tf_op jit(solution)/shard_map/ppermute | solution.py:247
  221.1 3.6 %collective-permute-start.76 = (bf16[272,256]{1,0:T(8,128)(2,1)S(1)}, bf16[272,256]{1,0:T(8,128)(2,1)S(1)}, u32[]{:S(2)}, u32[]{:S(2)}) collective-permute-start(bf16[272,256]{1,0:T(8,128)(2,1)S(1)} %gate.139.refs_24_), channel_id=1, source_target_pairs={{0,24},{1,25},{2,26},{3,27},{4,28},{5,29},{6,30},{7,31},{8,16},{9,... | collective-permute-start | bytes 417800 | tf_op jit(solution)/shard_map/ppermute | solution.py:247
  224.7 6.5 %gradient.2.refs_8_ = f32[1024,2048]{1,0:T(8,128)S(1)} custom-call(bf16[1024,768]{1,0:T(8,128)(2,1)S(1)} %get-tuple-element.185.codes_ref, bf16[1024,48]{1,0:T(8,128)(2,1)S(1)} %get-tuple-element.186.spare_codes_ref, bf16[272,256]{1,0:T(8,128)(2,1)S(1)} %collective-permute-done.38.__1_.refs_0_, bf16[272,256]{1,0:T(8,128)(2,1)S(1)} %collective-permute-done.42.__1_.refs_1_, ...), custom_call_target="tpu_custom_call" | custom-call | flops 3422552064 | bytes 8388608 | tf_op jit(solution)/shard_map/gradient/pallas_call | solution.py:340
  234.3 4.7 %gradient.3 = bf16[1024,2048]{1,0:T(8,128)(2,1)} custom-call(bf16[1024,256]{1,0:T(8,128)(2,1)S(1)} %get-tuple-element.158.codes_ref, bf16[1024,16]{1,0:T(8,128)(2,1)S(1)} %get-tuple-element.159.spare_codes_ref, bf16[272,256]{1,0:T(8,128)(2,1)S(1)} %collective-permute-done.62.__1_.refs_0_, bf16[272,256]{1,0:T(8,128)(2,1)S(1)} %collective-permute-done.64.__1_.refs_1_, ...), custom_call_target="tpu_custom_call" | custom-call | flops 1140850688 | bytes 8388608 | tf_op jit(solution)/shard_map/gradient/pallas_call | solution.py:340
  (207 shorter events, 43.1 us)
Async XLA Ops:
  30.2 15.7 %collective-permute-start.8 = (bf16[272,256]{1,0:T(8,128)(2,1)S(1)}, bf16[272,256]{1,0:T(8,128)(2,1)S(1)}, u32[]{:S(2)}, u32[]{:S(2)}) collective-permute-start(bf16[272,256]{1,0:T(8,128)(2,1)S(1)} %gate.74.__2_), channel_id=1, source_target_pairs={{0,16},{1,17},{2,18},{3,19},{4,20},{5,21},{6,22},{7,23},{8,24},{9,... | collective-permute-start | bytes 417800 | tf_op jit(solution)/shard_map/ppermute | solution.py:247
  32.8 15.5 %collective-permute-start.16 = (bf16[272,256]{1,0:T(8,128)(2,1)S(1)}, bf16[272,256]{1,0:T(8,128)(2,1)S(1)}, u32[]{:S(2)}, u32[]{:S(2)}) collective-permute-start(bf16[272,256]{1,0:T(8,128)(2,1)S(1)} %gate.75.__2_), channel_id=1, source_target_pairs={{0,5},{1,4},{2,7},{3,6},{4,1},{5,0},{6,3},{7,2},{8,13},{9,12},{10,... | collective-permute-start | bytes 417800 | tf_op jit(solution)/shard_map/ppermute | solution.py:247
  40.0 12.5 %collective-permute-start.12 = (bf16[272,256]{1,0:T(8,128)(2,1)S(1)}, bf16[272,256]{1,0:T(8,128)(2,1)S(1)}, u32[]{:S(2)}, u32[]{:S(2)}) collective-permute-start(bf16[272,256]{1,0:T(8,128)(2,1)S(1)} %gate.77.__2_), channel_id=1, source_target_pairs={{0,16},{1,17},{2,18},{3,19},{4,20},{5,21},{6,22},{7,23},{8,24},{9,... | collective-permute-start | bytes 417800 | tf_op jit(solution)/shard_map/ppermute | solution.py:247
  41.5 14.9 %collective-permute-start.18 = (bf16[272,256]{1,0:T(8,128)(2,1)S(1)}, bf16[272,256]{1,0:T(8,128)(2,1)S(1)}, u32[]{:S(2)}, u32[]{:S(2)}) collective-permute-start(bf16[272,256]{1,0:T(8,128)(2,1)S(1)} %gate.78.__2_), channel_id=1, source_target_pairs={{0,4},{1,5},{2,6},{3,7},{4,0},{5,1},{6,2},{7,3},{8,12},{9,13},{10,... | collective-permute-start | bytes 417800 | tf_op jit(solution)/shard_map/ppermute | solution.py:247
  57.0 14.1 %collective-permute-start.26 = (bf16[272,256]{1,0:T(8,128)(2,1)S(1)}, bf16[272,256]{1,0:T(8,128)(2,1)S(1)}, u32[]{:S(2)}, u32[]{:S(2)}) collective-permute-start(bf16[272,256]{1,0:T(8,128)(2,1)S(1)} %gate.85.__2_), channel_id=1, source_target_pairs={{0,13},{1,12},{2,15},{3,14},{4,9},{5,8},{6,11},{7,10},{8,5},{9,4},... | collective-permute-start | bytes 417800 | tf_op jit(solution)/shard_map/ppermute | solution.py:247
  68.0 12.4 %collective-permute-start.23 = (bf16[272,256]{1,0:T(8,128)(2,1)S(1)}, bf16[272,256]{1,0:T(8,128)(2,1)S(1)}, u32[]{:S(2)}, u32[]{:S(2)}) collective-permute-start(bf16[272,256]{1,0:T(8,128)(2,1)S(1)} %gate.89.__2_), channel_id=1, source_target_pairs={{0,8},{1,9},{2,10},{3,11},{4,12},{5,13},{6,14},{7,15},{8,0},{9,1},... | collective-permute-start | bytes 417800 | tf_op jit(solution)/shard_map/ppermute | solution.py:247
  71.1 14.7 %collective-permute-start.28 = (bf16[272,256]{1,0:T(8,128)(2,1)S(1)}, bf16[272,256]{1,0:T(8,128)(2,1)S(1)}, u32[]{:S(2)}, u32[]{:S(2)}) collective-permute-start(bf16[272,256]{1,0:T(8,128)(2,1)S(1)} %gate.90.__2_), channel_id=1, source_target_pairs={{0,12},{1,13},{2,14},{3,15},{4,8},{5,9},{6,10},{7,11},{8,4},{9,5},... | collective-permute-start | bytes 417800 | tf_op jit(solution)/shard_map/ppermute | solution.py:247
  71.1 15.6 %collective-permute-start.32 = (bf16[272,256]{1,0:T(8,128)(2,1)S(1)}, bf16[272,256]{1,0:T(8,128)(2,1)S(1)}, u32[]{:S(2)}, u32[]{:S(2)}) collective-permute-start(bf16[272,256]{1,0:T(8,128)(2,1)S(1)} %gate.91.__2_), channel_id=1, source_target_pairs={{0,8},{1,9},{2,10},{3,11},{4,12},{5,13},{6,14},{7,15},{8,0},{9,1},... | collective-permute-start | bytes 417800 | tf_op jit(solution)/shard_map/ppermute | solution.py:247
  74.8 14.7 %collective-permute-start.27 = (bf16[272,256]{1,0:T(8,128)(2,1)S(1)}, bf16[272,256]{1,0:T(8,128)(2,1)S(1)}, u32[]{:S(2)}, u32[]{:S(2)}) collective-permute-start(bf16[272,256]{1,0:T(8,128)(2,1)S(1)} %gate.92.__2_), channel_id=1, source_target_pairs={{0,8},{1,9},{2,10},{3,11},{4,12},{5,13},{6,14},{7,15},{8,0},{9,1},... | collective-permute-start | bytes 417800 | tf_op jit(solution)/shard_map/ppermute | solution.py:247
  76.8 12.7 %collective-permute-start.31 = (bf16[272,256]{1,0:T(8,128)(2,1)S(1)}, bf16[272,256]{1,0:T(8,128)(2,1)S(1)}, u32[]{:S(2)}, u32[]{:S(2)}) collective-permute-start(bf16[272,256]{1,0:T(8,128)(2,1)S(1)} %gate.93.__2_), channel_id=1, source_target_pairs={{0,22},{1,23},{2,20},{3,21},{4,18},{5,19},{6,16},{7,17},{8,30},{9,... | collective-permute-start | bytes 417800 | tf_op jit(solution)/shard_map/ppermute | solution.py:247
  85.8 12.3 %collective-permute-start.30 = (bf16[272,256]{1,0:T(8,128)(2,1)S(1)}, bf16[272,256]{1,0:T(8,128)(2,1)S(1)}, u32[]{:S(2)}, u32[]{:S(2)}) collective-permute-start(bf16[272,256]{1,0:T(8,128)(2,1)S(1)} %gate.95.__2_), channel_id=1, source_target_pairs={{0,8},{1,9},{2,10},{3,11},{4,12},{5,13},{6,14},{7,15},{8,0},{9,1},... | collective-permute-start | bytes 417800 | tf_op jit(solution)/shard_map/ppermute | solution.py:247
  86.7 20.0 %collective-permute-start.35 = (bf16[272,256]{1,0:T(8,128)(2,1)S(1)}, bf16[272,256]{1,0:T(8,128)(2,1)S(1)}, u32[]{:S(2)}, u32[]{:S(2)}) collective-permute-start(bf16[272,256]{1,0:T(8,128)(2,1)S(1)} %gate.96.__2_), channel_id=1, source_target_pairs={{0,21},{1,20},{2,23},{3,22},{4,17},{5,16},{6,19},{7,18},{8,29},{9,... | collective-permute-start | bytes 417800 | tf_op jit(solution)/shard_map/ppermute | solution.py:247
  89.4 17.3 %collective-permute-start.34 = (bf16[272,256]{1,0:T(8,128)(2,1)S(1)}, bf16[272,256]{1,0:T(8,128)(2,1)S(1)}, u32[]{:S(2)}, u32[]{:S(2)}) collective-permute-start(bf16[272,256]{1,0:T(8,128)(2,1)S(1)} %gate.97.__2_), channel_id=1, source_target_pairs={{0,19},{1,18},{2,17},{3,16},{4,23},{5,22},{6,21},{7,20},{8,27},{9,... | collective-permute-start | bytes 417800 | tf_op jit(solution)/shard_map/ppermute | solution.py:247
  89.5 17.6 %collective-permute-start.33 = (bf16[272,256]{1,0:T(8,128)(2,1)S(1)}, bf16[272,256]{1,0:T(8,128)(2,1)S(1)}, u32[]{:S(2)}, u32[]{:S(2)}) collective-permute-start(bf16[272,256]{1,0:T(8,128)(2,1)S(1)} %gate.98.__2_), channel_id=1, source_target_pairs={{0,8},{1,9},{2,10},{3,11},{4,12},{5,13},{6,14},{7,15},{8,0},{9,1},... | collective-permute-start | bytes 417800 | tf_op jit(solution)/shard_map/ppermute | solution.py:247
  92.7 16.2 %collective-permute-start.38 = (bf16[272,256]{1,0:T(8,128)(2,1)S(1)}, bf16[272,256]{1,0:T(8,128)(2,1)S(1)}, u32[]{:S(2)}, u32[]{:S(2)}) collective-permute-start(bf16[272,256]{1,0:T(8,128)(2,1)S(1)} %gate.99.__2_), channel_id=1, source_target_pairs={{0,7},{1,6},{2,5},{3,4},{4,3},{5,2},{6,1},{7,0},{8,15},{9,14},{10,... | collective-permute-start | bytes 417800 | tf_op jit(solution)/shard_map/ppermute | solution.py:247
  98.1 14.1 %collective-permute-start.42 = (bf16[272,256]{1,0:T(8,128)(2,1)S(1)}, bf16[272,256]{1,0:T(8,128)(2,1)S(1)}, u32[]{:S(2)}, u32[]{:S(2)}) collective-permute-start(bf16[272,256]{1,0:T(8,128)(2,1)S(1)} %gate.100.__2_), channel_id=1, source_target_pairs={{0,1},{1,0},{2,3},{3,2},{4,5},{5,4},{6,7},{7,6},{8,9},{9,8},{10,11... | collective-permute-start | bytes 417800 | tf_op jit(solution)/shard_map/ppermute | solution.py:247
  108.9 15.5 %collective-permute-start.39 = (bf16[272,256]{1,0:T(8,128)(2,1)S(1)}, bf16[272,256]{1,0:T(8,128)(2,1)S(1)}, u32[]{:S(2)}, u32[]{:S(2)}) collective-permute-start(bf16[272,256]{1,0:T(8,128)(2,1)S(1)} %gate.104.__2_), channel_id=1, source_target_pairs={{0,25},{1,24},{2,27},{3,26},{4,29},{5,28},{6,31},{7,30},{8,17},{9,... | collective-permute-start | bytes 417800 | tf_op jit(solution)/shard_map/ppermute | solution.py:247
  115.0 20.0 %collective-permute-start.48 = (bf16[272,256]{1,0:T(8,128)(2,1)S(1)}, bf16[272,256]{1,0:T(8,128)(2,1)S(1)}, u32[]{:S(2)}, u32[]{:S(2)}) collective-permute-start(bf16[272,256]{1,0:T(8,128)(2,1)S(1)} %gate.106.__2_), channel_id=1, source_target_pairs={{0,2},{1,3},{2,0},{3,1},{4,6},{5,7},{6,4},{7,5},{8,10},{9,11},{10,... | collective-permute-start | bytes 417800 | tf_op jit(solution)/shard_map/ppermute | solution.py:247
  115.4 19.6 %collective-permute-start.43 = (bf16[272,256]{1,0:T(8,128)(2,1)S(1)}, bf16[272,256]{1,0:T(8,128)(2,1)S(1)}, u32[]{:S(2)}, u32[]{:S(2)}) collective-permute-start(bf16[272,256]{1,0:T(8,128)(2,1)S(1)} %gate.107.__2_), channel_id=1, source_target_pairs={{0,30},{1,31},{2,28},{3,29},{4,26},{5,27},{6,24},{7,25},{8,22},{9,... | collective-permute-start | bytes 417800 | tf_op jit(solution)/shard_map/ppermute | solution.py:247
  118.4 20.1 %collective-permute-start.44 = (bf16[272,256]{1,0:T(8,128)(2,1)S(1)}, bf16[272,256]{1,0:T(8,128)(2,1)S(1)}, u32[]{:S(2)}, u32[]{:S(2)}) collective-permute-start(bf16[272,256]{1,0:T(8,128)(2,1)S(1)} %gate.108.__2_), channel_id=1, source_target_pairs={{0,26},{1,27},{2,24},{3,25},{4,30},{5,31},{6,28},{7,29},{8,18},{9,... | collective-permute-start | bytes 417800 | tf_op jit(solution)/shard_map/ppermute | solution.py:247
  124.4 17.3 %collective-permute-start.45 = (bf16[272,256]{1,0:T(8,128)(2,1)S(1)}, bf16[272,256]{1,0:T(8,128)(2,1)S(1)}, u32[]{:S(2)}, u32[]{:S(2)}) collective-permute-start(bf16[272,256]{1,0:T(8,128)(2,1)S(1)} %gate.109.__2_), channel_id=1, source_target_pairs={{0,29},{1,28},{2,31},{3,30},{4,25},{5,24},{6,27},{7,26},{8,21},{9,... | collective-permute-start | bytes 417800 | tf_op jit(solution)/shard_map/ppermute | solution.py:247
  124.4 21.7 %collective-permute-start.47 = (bf16[272,256]{1,0:T(8,128)(2,1)S(1)}, bf16[272,256]{1,0:T(8,128)(2,1)S(1)}, u32[]{:S(2)}, u32[]{:S(2)}) collective-permute-start(bf16[272,256]{1,0:T(8,128)(2,1)S(1)} %gate.110.__2_), channel_id=1, source_target_pairs={{0,27},{1,26},{2,25},{3,24},{4,31},{5,30},{6,29},{7,28},{8,19},{9,... | collective-permute-start | bytes 417800 | tf_op jit(solution)/shard_map/ppermute | solution.py:247
  135.0 15.0 %collective-permute-start.52 = (bf16[272,256]{1,0:T(8,128)(2,1)S(1)}, bf16[272,256]{1,0:T(8,128)(2,1)S(1)}, u32[]{:S(2)}, u32[]{:S(2)}) collective-permute-start(bf16[272,256]{1,0:T(8,128)(2,1)S(1)} %gate.111.__2_), channel_id=1, source_target_pairs={{0,5},{1,4},{2,7},{3,6},{4,1},{5,0},{6,3},{7,2},{8,13},{9,12},{10,... | collective-permute-start | bytes 417800 | tf_op jit(solution)/shard_map/ppermute | solution.py:247
  135.0 18.3 %collective-permute-start.51 = (bf16[272,256]{1,0:T(8,128)(2,1)S(1)}, bf16[272,256]{1,0:T(8,128)(2,1)S(1)}, u32[]{:S(2)}, u32[]{:S(2)}) collective-permute-start(bf16[272,256]{1,0:T(8,128)(2,1)S(1)} %gate.112.__2_), channel_id=1, source_target_pairs={{0,3},{1,2},{2,1},{3,0},{4,7},{5,6},{6,5},{7,4},{8,11},{9,10},{10,... | collective-permute-start | bytes 417800 | tf_op jit(solution)/shard_map/ppermute | solution.py:247
  138.5 20.6 %collective-permute-start.49 = (bf16[272,256]{1,0:T(8,128)(2,1)S(1)}, bf16[272,256]{1,0:T(8,128)(2,1)S(1)}, u32[]{:S(2)}, u32[]{:S(2)}) collective-permute-start(bf16[272,256]{1,0:T(8,128)(2,1)S(1)} %gate.113.__2_), channel_id=1, source_target_pairs={{0,28},{1,29},{2,30},{3,31},{4,24},{5,25},{6,26},{7,27},{8,20},{9,... | collective-permute-start | bytes 417800 | tf_op jit(solution)/shard_map/ppermute | solution.py:247
  141.7 17.4 %collective-permute-start.50 = (bf16[272,256]{1,0:T(8,128)(2,1)S(1)}, bf16[272,256]{1,0:T(8,128)(2,1)S(1)}, u32[]{:S(2)}, u32[]{:S(2)}) collective-permute-start(bf16[272,256]{1,0:T(8,128)(2,1)S(1)} %gate.114.__2_), channel_id=1, source_target_pairs={{0,24},{1,25},{2,26},{3,27},{4,28},{5,29},{6,30},{7,31},{8,16},{9,... | collective-permute-start | bytes 417800 | tf_op jit(solution)/shard_map/ppermute | solution.py:247
  146.1 13.1 %collective-permute-start.56 = (bf16[272,256]{1,0:T(8,128)(2,1)S(1)}, bf16[272,256]{1,0:T(8,128)(2,1)S(1)}, u32[]{:S(2)}, u32[]{:S(2)}) collective-permute-start(bf16[272,256]{1,0:T(8,128)(2,1)S(1)} %gate.115.__2_), channel_id=1, source_target_pairs={{0,23},{1,22},{2,21},{3,20},{4,19},{5,18},{6,17},{7,16},{8,31},{9,... | collective-permute-start | bytes 417800 | tf_op jit(solution)/shard_map/ppermute | solution.py:247
  149.9 12.9 %collective-permute-start.55 = (bf16[272,256]{1,0:T(8,128)(2,1)S(1)}, bf16[272,256]{1,0:T(8,128)(2,1)S(1)}, u32[]{:S(2)}, u32[]{:S(2)}) collective-permute-start(bf16[272,256]{1,0:T(8,128)(2,1)S(1)} %gate.116.__2_), channel_id=1, source_target_pairs={{0,17},{1,16},{2,19},{3,18},{4,21},{5,20},{6,23},{7,22},{8,25},{9,... | collective-permute-start | bytes 417800 | tf_op jit(solution)/shard_map/ppermute | solution.py:247
  153.3 15.8 %collective-permute-start.54 = (bf16[272,256]{1,0:T(8,128)(2,1)S(1)}, bf16[272,256]{1,0:T(8,128)(2,1)S(1)}, u32[]{:S(2)}, u32[]{:S(2)}) collective-permute-start(bf16[272,256]{1,0:T(8,128)(2,1)S(1)} %gate.117.__2_), channel_id=1, source_target_pairs={{0,4},{1,5},{2,6},{3,7},{4,0},{5,1},{6,2},{7,3},{8,12},{9,13},{10,... | collective-permute-start | bytes 417800 | tf_op jit(solution)/shard_map/ppermute | solution.py:247
  159.1 18.2 %collective-permute-start.61 = (bf16[272,256]{1,0:T(8,128)(2,1)S(1)}, bf16[272,256]{1,0:T(8,128)(2,1)S(1)}, u32[]{:S(2)}, u32[]{:S(2)}) collective-permute-start(bf16[272,256]{1,0:T(8,128)(2,1)S(1)} %gate.119.__2_), channel_id=1, source_target_pairs={{0,18},{1,19},{2,16},{3,17},{4,22},{5,23},{6,20},{7,21},{8,26},{9,... | collective-permute-start | bytes 417800 | tf_op jit(solution)/shard_map/ppermute | solution.py:247
  159.2 18.2 %collective-permute-start.60 = (bf16[272,256]{1,0:T(8,128)(2,1)S(1)}, bf16[272,256]{1,0:T(8,128)(2,1)S(1)}, u32[]{:S(2)}, u32[]{:S(2)}) collective-permute-start(bf16[272,256]{1,0:T(8,128)(2,1)S(1)} %gate.120.__2_), channel_id=1, source_target_pairs={{0,15},{1,14},{2,13},{3,12},{4,11},{5,10},{6,9},{7,8},{8,7},{9,6},... | collective-permute-start | bytes 417800 | tf_op jit(solution)/shard_map/ppermute | solution.py:247
  162.9 20.0 %collective-permute-start.59 = (bf16[272,256]{1,0:T(8,128)(2,1)S(1)}, bf16[272,256]{1,0:T(8,128)(2,1)S(1)}, u32[]{:S(2)}, u32[]{:S(2)}) collective-permute-start(bf16[272,256]{1,0:T(8,128)(2,1)S(1)} %gate.121.__2_), channel_id=1, source_target_pairs={{0,9},{1,8},{2,11},{3,10},{4,13},{5,12},{6,15},{7,14},{8,1},{9,0},... | collective-permute-start | bytes 417800 | tf_op jit(solution)/shard_map/ppermute | solution.py:247
  169.1 17.5 %collective-permute-start.58 = (bf16[272,256]{1,0:T(8,128)(2,1)S(1)}, bf16[272,256]{1,0:T(8,128)(2,1)S(1)}, u32[]{:S(2)}, u32[]{:S(2)}) collective-permute-start(bf16[272,256]{1,0:T(8,128)(2,1)S(1)} %gate.122.__2_), channel_id=1, source_target_pairs={{0,21},{1,20},{2,23},{3,22},{4,17},{5,16},{6,19},{7,18},{8,29},{9,... | collective-permute-start | bytes 417800 | tf_op jit(solution)/shard_map/ppermute | solution.py:247
  169.1 17.5 %collective-permute-start.57 = (bf16[272,256]{1,0:T(8,128)(2,1)S(1)}, bf16[272,256]{1,0:T(8,128)(2,1)S(1)}, u32[]{:S(2)}, u32[]{:S(2)}) collective-permute-start(bf16[272,256]{1,0:T(8,128)(2,1)S(1)} %gate.123.__2_), channel_id=1, source_target_pairs={{0,19},{1,18},{2,17},{3,16},{4,23},{5,22},{6,21},{7,20},{8,27},{9,... | collective-permute-start | bytes 417800 | tf_op jit(solution)/shard_map/ppermute | solution.py:247
  177.4 13.9 %collective-permute-start.67 = (bf16[272,256]{1,0:T(8,128)(2,1)S(1)}, bf16[272,256]{1,0:T(8,128)(2,1)S(1)}, u32[]{:S(2)}, u32[]{:S(2)}) collective-permute-start(bf16[272,256]{1,0:T(8,128)(2,1)S(1)} %gate.125.__2_), channel_id=1, source_target_pairs={{0,10},{1,11},{2,8},{3,9},{4,14},{5,15},{6,12},{7,13},{8,2},{9,3},... | collective-permute-start | bytes 417800 | tf_op jit(solution)/shard_map/ppermute | solution.py:247
  182.9 17.8 %collective-permute-start.66 = (bf16[272,256]{1,0:T(8,128)(2,1)S(1)}, bf16[272,256]{1,0:T(8,128)(2,1)S(1)}, u32[]{:S(2)}, u32[]{:S(2)}) collective-permute-start(bf16[272,256]{1,0:T(8,128)(2,1)S(1)} %gate.126.__2_), channel_id=1, source_target_pairs={{0,20},{1,21},{2,22},{3,23},{4,16},{5,17},{6,18},{7,19},{8,28},{9,... | collective-permute-start | bytes 417800 | tf_op jit(solution)/shard_map/ppermute | solution.py:247
  186.6 14.0 %collective-permute-start.65 = (bf16[272,256]{1,0:T(8,128)(2,1)S(1)}, bf16[272,256]{1,0:T(8,128)(2,1)S(1)}, u32[]{:S(2)}, u32[]{:S(2)}) collective-permute-start(bf16[272,256]{1,0:T(8,128)(2,1)S(1)} %gate.127.__2_), channel_id=1, source_target_pairs={{0,16},{1,17},{2,18},{3,19},{4,20},{5,21},{6,22},{7,23},{8,24},{9,... | collective-permute-start | bytes 417800 | tf_op jit(solution)/shard_map/ppermute | solution.py:247
  186.6 16.8 %collective-permute-start.62 = (bf16[272,256]{1,0:T(8,128)(2,1)S(1)}, bf16[272,256]{1,0:T(8,128)(2,1)S(1)}, u32[]{:S(2)}, u32[]{:S(2)}) collective-permute-start(bf16[272,256]{1,0:T(8,128)(2,1)S(1)} %gate.128.__2_), channel_id=1, source_target_pairs={{0,31},{1,30},{2,29},{3,28},{4,27},{5,26},{6,25},{7,24},{8,23},{9,... | collective-permute-start | bytes 417800 | tf_op jit(solution)/shard_map/ppermute | solution.py:247
  188.7 18.0 %collective-permute-start.64 = (bf16[272,256]{1,0:T(8,128)(2,1)S(1)}, bf16[272,256]{1,0:T(8,128)(2,1)S(1)}, u32[]{:S(2)}, u32[]{:S(2)}) collective-permute-start(bf16[272,256]{1,0:T(8,128)(2,1)S(1)} %gate.129.__2_), channel_id=1, source_target_pairs={{0,25},{1,24},{2,27},{3,26},{4,29},{5,28},{6,31},{7,30},{8,17},{9,... | collective-permute-start | bytes 417800 | tf_op jit(solution)/shard_map/ppermute | solution.py:247
  191.3 15.5 %collective-permute-start.71 = (bf16[272,256]{1,0:T(8,128)(2,1)S(1)}, bf16[272,256]{1,0:T(8,128)(2,1)S(1)}, u32[]{:S(2)}, u32[]{:S(2)}) collective-permute-start(bf16[272,256]{1,0:T(8,128)(2,1)S(1)} %gate.130.__2_), channel_id=1, source_target_pairs={{0,13},{1,12},{2,15},{3,14},{4,9},{5,8},{6,11},{7,10},{8,5},{9,4},... | collective-permute-start | bytes 417800 | tf_op jit(solution)/shard_map/ppermute | solution.py:247
  200.7 13.3 %collective-permute-start.70 = (bf16[272,256]{1,0:T(8,128)(2,1)S(1)}, bf16[272,256]{1,0:T(8,128)(2,1)S(1)}, u32[]{:S(2)}, u32[]{:S(2)}) collective-permute-start(bf16[272,256]{1,0:T(8,128)(2,1)S(1)} %gate.131.__2_), channel_id=1, source_target_pairs={{0,11},{1,10},{2,9},{3,8},{4,15},{5,14},{6,13},{7,12},{8,3},{9,2},... | collective-permute-start | bytes 417800 | tf_op jit(solution)/shard_map/ppermute | solution.py:247
  200.7 13.3 %collective-permute-start.68 = (bf16[272,256]{1,0:T(8,128)(2,1)S(1)}, bf16[272,256]{1,0:T(8,128)(2,1)S(1)}, u32[]{:S(2)}, u32[]{:S(2)}) collective-permute-start(bf16[272,256]{1,0:T(8,128)(2,1)S(1)} %gate.132.__2_), channel_id=1, source_target_pairs={{0,30},{1,31},{2,28},{3,29},{4,26},{5,27},{6,24},{7,25},{8,22},{9,... | collective-permute-start | bytes 417800 | tf_op jit(solution)/shard_map/ppermute | solution.py:247
  206.7 14.4 %collective-permute-start.75 = (bf16[272,256]{1,0:T(8,128)(2,1)S(1)}, bf16[272,256]{1,0:T(8,128)(2,1)S(1)}, u32[]{:S(2)}, u32[]{:S(2)}) collective-permute-start(bf16[272,256]{1,0:T(8,128)(2,1)S(1)} %gate.134.__2_), channel_id=1, source_target_pairs={{0,12},{1,13},{2,14},{3,15},{4,8},{5,9},{6,10},{7,11},{8,4},{9,5},... | collective-permute-start | bytes 417800 | tf_op jit(solution)/shard_map/ppermute | solution.py:247
  206.8 17.9 %collective-permute-start.77 = (bf16[272,256]{1,0:T(8,128)(2,1)S(1)}, bf16[272,256]{1,0:T(8,128)(2,1)S(1)}, u32[]{:S(2)}, u32[]{:S(2)}) collective-permute-start(bf16[272,256]{1,0:T(8,128)(2,1)S(1)} %gate.135.__2_), channel_id=1, source_target_pairs={{0,8},{1,9},{2,10},{3,11},{4,12},{5,13},{6,14},{7,15},{8,0},{9,1},... | collective-permute-start | bytes 417800 | tf_op jit(solution)/shard_map/ppermute | solution.py:247
  213.9 18.6 %collective-permute-start.72 = (bf16[272,256]{1,0:T(8,128)(2,1)S(1)}, bf16[272,256]{1,0:T(8,128)(2,1)S(1)}, u32[]{:S(2)}, u32[]{:S(2)}) collective-permute-start(bf16[272,256]{1,0:T(8,128)(2,1)S(1)} %gate.136.__2_), channel_id=1, source_target_pairs={{0,29},{1,28},{2,31},{3,30},{4,25},{5,24},{6,27},{7,26},{8,21},{9,... | collective-permute-start | bytes 417800 | tf_op jit(solution)/shard_map/ppermute | solution.py:247
  214.0 18.6 %collective-permute-start.73 = (bf16[272,256]{1,0:T(8,128)(2,1)S(1)}, bf16[272,256]{1,0:T(8,128)(2,1)S(1)}, u32[]{:S(2)}, u32[]{:S(2)}) collective-permute-start(bf16[272,256]{1,0:T(8,128)(2,1)S(1)} %gate.137.__2_), channel_id=1, source_target_pairs={{0,27},{1,26},{2,25},{3,24},{4,31},{5,30},{6,29},{7,28},{8,19},{9,... | collective-permute-start | bytes 417800 | tf_op jit(solution)/shard_map/ppermute | solution.py:247
  215.3 17.3 %collective-permute-start.74 = (bf16[272,256]{1,0:T(8,128)(2,1)S(1)}, bf16[272,256]{1,0:T(8,128)(2,1)S(1)}, u32[]{:S(2)}, u32[]{:S(2)}) collective-permute-start(bf16[272,256]{1,0:T(8,128)(2,1)S(1)} %gate.138.__2_), channel_id=1, source_target_pairs={{0,28},{1,29},{2,30},{3,31},{4,24},{5,25},{6,26},{7,27},{8,20},{9,... | collective-permute-start | bytes 417800 | tf_op jit(solution)/shard_map/ppermute | solution.py:247
  221.1 13.2 %collective-permute-start.76 = (bf16[272,256]{1,0:T(8,128)(2,1)S(1)}, bf16[272,256]{1,0:T(8,128)(2,1)S(1)}, u32[]{:S(2)}, u32[]{:S(2)}) collective-permute-start(bf16[272,256]{1,0:T(8,128)(2,1)S(1)} %gate.139.refs_24_), channel_id=1, source_target_pairs={{0,24},{1,25},{2,26},{3,27},{4,28},{5,29},{6,30},{7,31},{8,16},{9,... | collective-permute-start | bytes 417800 | tf_op jit(solution)/shard_map/ppermute | solution.py:247
  (36 other events, 339.6 us)

commit v4 on v3

--- a/solution.py
+++ b/solution.py
@@ -11,10 +11,9 @@
 SPARE = 2
 STACK = 8
 SENDS = (
-    ["T00", "T01", "C20", "T02", "C21", "T03", "C22", "T10", "C23", "T11", "T12", "T20"]
-    + ["C30", "T13", "C31", "T21", "C32", "T22", "C33", "E00", "T23", "T30", "E01", "T31"]
-    + ["T32", "E02", "T33", "E20", "E03", "E21", "E10", "E22"]
-    + ["E11", "E23", "E30", "E12", "E31", "E13", "E32", "E33"]
+    ["T00", "T01", "C20", "T02", "C21", "T03", "C22", "T10", "C23", "T11", "T12", "T20", "T13", "C30", "T21", "C31"]
+    + ["T22", "C32", "E00", "C33", "T23", "E01", "T30", "T31", "E02", "T32", "E03", "T33", "E20", "E10", "E21", "E22"]
+    + ["E11", "E23", "E12", "E30", "E31", "E13", "E32", "E33"]
 )
 WINDOW = 5
 PIECES = 4
@@ -172,40 +171,54 @@
     stack_spare(messages, main, jnp.concatenate(spare_out, axis=0))
 
 
-def turn_kernel(counts, scale, *refs):
-    chunks, (out_ref, spare_ref) = len(counts), refs[-2:]
-    codes = [joined(refs[sum(counts[:j]) : sum(counts[: j + 1])]) for j in range(chunks)]
-    main = out_ref.shape[1] // chunks
-    for j in range(chunks):
-        out_ref[:, j * main : (j + 1) * main] = (codes[j][:main, :].astype(F32) * scale).T.astype(BF16)
-    spare = jnp.concatenate([code[main:, :] for code in codes], axis=0)
-    spare_ref[...] = (spare.astype(F32) * scale).T.astype(BF16)
-
-
-def gradient_kernel(chunks, owners, has_base, codes_ref, spare_codes_ref, *refs):
-    messages, base_ref, (out_ref, spare_ref) = refs[: chunks * owners], refs[chunks * owners], refs[-2:]
-    main, part = main_of(messages[0]), messages[0].shape[1]
-    spares = owners * SPARE
-    step = pl.program_id(0)
-    own = [messages[j * owners : (j + 1) * owners] for j in range(chunks)]
-
-    @pl.when(step == 0)
-    def _():
-        for j in range(chunks):
-            spare_ref[j] = unstacked_spare(own[j], main)
-
-    per = out_ref.shape[1] // part
-    for i in range(per):
-        q = step * per + i
+def turn_kernel(counts, owners, main, scale, picked, *refs):
+    codes, out_ref = [], refs[-1]
+    for j in range(len(counts)):
+        codes.append(joined(refs[sum(counts[:j]) : sum(counts[: j + 1])]).astype(F32) * scale)
+    at = 0
+    for code, (_, first, count) in zip(codes, picked):
+        out_ref[:, at : at + count * main] = code[first * main : (first + count) * main, :].T.astype(BF16)
+        at += count * main
+    base = owners * main
+    spare = [code[base + f * SPARE : base + (f + n) * SPARE, :] for code, (_, f, n) in zip(codes, picked)]
+    out_ref[:, at:] = jnp.concatenate(spare, axis=0).T.astype(BF16)
+
+
+def gradient_kernel(counts, last, codes_ref, *refs):
+    own = [refs[sum(counts[:i]) : sum(counts[: i + 1])] for i in range(len(counts))]
+    refs = refs[sum(counts) :]
+    main, part = main_of(own[0][0]), own[0][0].shape[1]
+    if last:
+        base_ref, out_ref, *spare_refs, block_ref, sems = refs
+    else:
+        out_ref, *spare_refs = refs[-1 - len(counts) :]
+    for messages, spare_ref in zip(own, spare_refs):
+        spare_ref[...] = unstacked_spare(messages, main).astype(F32)
+
+    def columns_of(q):
+        return pl.ds(pl.multiple_of(q * part, part), part)
+
+    def copy_of(q):
+        return pltpu.make_async_copy(block_ref.at[:, columns_of(q)], out_ref.at[:, columns_of(q)], sems.at[q])
+
+    def block(q, _):
         at = pl.ds(pl.multiple_of(q * main, main), main)
-        spare_at = pl.ds(pl.multiple_of(q * spares, spares), spares)
-        columns = slice(i * part, (i + 1) * part)
-        arrived = jnp.concatenate([m[at, :] for j in range(chunks) for m in own[j]], axis=0)
-        spare = jnp.concatenate([spare_ref[j, spare_at, :] for j in range(chunks)], axis=0)
-        total = mm(codes_ref[...], arrived) + mm(spare_codes_ref[...], spare)
-        if has_base:
-            total += base_ref[:, columns]
-        out_ref[:, columns] = total.astype(out_ref.dtype)
+        arrived = [m[at, :] for messages in own for m in messages]
+        spare = [
+            ref[pl.ds(pl.multiple_of(q * n * SPARE, n * SPARE), n * SPARE), :] for n, ref in zip(counts, spare_refs)
+        ]
+        total = mm(codes_ref[...], jnp.concatenate(arrived + [jnp.concatenate(spare, axis=0).astype(BF16)], axis=0))
+        if last:
+            block_ref[:, columns_of(q)] = (total + base_ref[:, columns_of(q)]).astype(BF16)
+            copy_of(q).start()
+        else:
+            out_ref[:, columns_of(q)] = total
+        return _
+
+    lax.fori_loop(0, STACK, block, 0)
+    if last:
+        for q in range(STACK):
+            copy_of(q).wait()
 
 
 def gate_kernel(*_):
@@ -238,7 +251,7 @@
     local = w_dec.shape[1]
     part = local // STACK
     position = jnp.stack([lax.axis_index("latent"), lax.axis_index("dp")])
-    order = [7, 1, 6, 2, 5, 3, 4, 0]
+    order = [4, 3, 5, 2, 6, 1, 7, 0]
 
     def move(x, j, k):
         if j == 0 and k == 0:
@@ -324,33 +337,34 @@
         )(position, *picks, b_dec.reshape(1, -1), activations, *terms[j], *after)
         return outs[0], outs[1:]
 
-    def gradient(chunks, base, dtype, per, after):
-        count = len(chunks)
-        pieces = [c for j in chunks for c in codes[j]]
+    def gradient(picked, base, after):
+        counts = [n for _, _, n in picked]
+        depths = sum(counts) * (main + SPARE)
+        pieces = [c for j, _, _ in picked for c in codes[j]]
         turned = pl.pallas_call(
-            functools.partial(turn_kernel, [len(codes[j]) for j in chunks], loss_scale),
+            functools.partial(turn_kernel, [len(codes[j]) for j, _, _ in picked], owners, main, loss_scale, picked),
             in_specs=[whole(c.shape) for c in pieces],
-            out_shape=[some((width, count * owners * main)), some((width, count * owners * SPARE))],
+            out_shape=some((width, depths)),
             compiler_params=params(16),
-            cost_estimate=cost(0, 4 * count * slots * width),
+            cost_estimate=cost(0, 4 * width * depths),
             name="turn",
         )(*pieces)
-        block = pl.BlockSpec((width, per * part), lambda q: (0, q))
-        extra = ([] if base is None else [base]) + after
+        last = base is not None
+        spare = [pltpu.VMEM((STACK * n * SPARE, part), F32) for n in counts]
+        buffers = [pltpu.VMEM((width, local), BF16), pltpu.SemaphoreType.DMA((STACK,))] if last else []
         return pl.pallas_call(
-            functools.partial(gradient_kernel, count, owners, base is not None),
-            grid=(STACK // per,),
-            in_specs=[whole(t.shape) for t in turned]
-            + [whole((depth, part))] * (count * owners)
-            + ([] if base is None else [block])
+            functools.partial(gradient_kernel, counts, last),
+            in_specs=[whole(turned.shape)]
+            + [whole((depth, part))] * sum(counts)
+            + [whole((width, local))] * last
             + [ANYWHERE] * len(after),
-            out_specs=block,
-            out_shape=some((width, local), dtype),
-            scratch_shapes=[pltpu.VMEM((count, STACK * owners * SPARE, part), BF16)],
+            out_specs=ANYWHERE if last else whole((width, local)),
+            out_shape=some((width, local), BF16 if last else F32),
+            scratch_shapes=spare + buffers,
             compiler_params=params(24),
-            cost_estimate=cost(2 * count * slots * width * local, 4 * width * local),
+            cost_estimate=cost(2 * depths * width * local, 4 * width * local),
             name="gradient",
-        )(*turned, *[m for j in chunks for m in errors[j]], *extra)
+        )(turned, *[m for j, f, n in picked for m in errors[j][f : f + n]], *([base] if last else []), *after)
 
     def gate(messages, after):
         held = pl.pallas_call(
@@ -385,8 +399,9 @@
                 message = move(message, across, along)
                 arrivals.append(message)
             chunk[place] = message
-    base = gradient([0, 2, 1], None, F32, 1, held[:1])
-    return rebuilt, gradient([3], base, BF16, 2, [])
+    half = owners // 2
+    base = gradient([(0, 0, owners), (2, 0, owners), (1, 0, owners), (3, 0, half)], None, held)
+    return rebuilt, gradient([(3, half, owners - half)], base, [])
 
 
 def on_device_wide(activations, owner_ids, block_mask, latent_codes, w_dec, b_dec):

time: 239 us -> 233 us (0.975)
  waiting for transfers between devices: 65 us -> 51.5 us
  starting transfers between devices: 135 us -> 143 us
    ppermute x78, waiting for transfers between devices: 65 us -> 51.5 us  [move(): return lax.ppermute(x, ('dp', 'latent'), pairs)]
    ppermute x78, starting transfers between devices: 135 us -> 143 us  [move(): return lax.ppermute(x, ('dp', 'latent'), pairs)]
  transfers between devices with their start and end apart: 78 -> 78, of which waited for: 23 -> 19; matrix products, arithmetic and copies ran while one was open for 0% -> 0% of each run, Pallas kernels for 11% -> 11%
where the time goes in v4:
time: 233 us; the launch traced here: 231 us
  starting transfers between devices  143 us (61%)
  waiting for transfers between devices  51.5 us (22%)
  Pallas kernels  30.2 us (13%)
  local copies, waits for them, and re-layouts  4.73 us (2%)
    ppermute x78, starting transfers between devices, move(): return lax.ppermute(x, ('dp', 'latent'), pairs)  143 us
    ppermute x78, waiting for transfers between devices, move(): return lax.ppermute(x, ('dp', 'latent'), pairs)  51.5 us
    pallas_call x4, Pallas kernels, combine(): pl.pallas_call(functools.partial(combine_kernel, owners), grid_spec=pltpu...  12.5 us
    pallas_call x2, Pallas kernels, gradient(): pl.pallas_call(functools.partial(gradient_kernel, counts, last), in_specs...  9.3 us
    pallas_call x4, Pallas kernels, decode(): pl.pallas_call(functools.partial(decode_kernel, owners, len(codes[j])), i...  5.82 us
    unnamed x13, local copies, waits for them, and re-layouts  4.73 us
  transfers between devices with their start and end apart: 78, of which 19 were waited for; matrix products, arithmetic and copies ran while one was open for 0% of the time, Pallas kernels for 11%

profile of v4, /device:TPU:0, one launch (start us, length us, event | category | flops | bytes accessed | tf_op | source)
XLA Modules:
  0.0 230.9 jit_solution(12911533256586550305)
XLA Ops:
  4.7 4.1 %collective-permute-start = (bf16[272,128]{1,0:T(8,128)(2,1)S(1)}, bf16[272,128]{1,0:T(8,128)(2,1)S(1)}, u32[]{:S(2)}, u32[]{:S(2)}) collective-permute-start(bf16[272,128]{1,0:T(8,128)(2,1)S(1)} %get-tuple-element.95), channel_id=1, source_target_pairs={{0,4},{1,5},{2,6},{3,7},{4,0},{5,1},{6,2},{7,3},{8,12},{9,13},{10,... | collective-permute-start | bytes 208904 | tf_op jit(solution)/shard_map/ppermute | solution.py:260
  8.7 2.5 %collective-permute-start.1 = (bf16[272,128]{1,0:T(8,128)(2,1)S(1)}, bf16[272,128]{1,0:T(8,128)(2,1)S(1)}, u32[]{:S(2)}, u32[]{:S(2)}) collective-permute-start(bf16[272,128]{1,0:T(8,128)(2,1)S(1)} %get-tuple-element.96), channel_id=1, source_target_pairs={{0,3},{1,2},{2,1},{3,0},{4,7},{5,6},{6,5},{7,4},{8,11},{9,10},{10,... | collective-permute-start | bytes 208904 | tf_op jit(solution)/shard_map/ppermute | solution.py:260
  11.7 3.9 %collective-permute-start.4 = (bf16[272,128]{1,0:T(8,128)(2,1)S(1)}, bf16[272,128]{1,0:T(8,128)(2,1)S(1)}, u32[]{:S(2)}, u32[]{:S(2)}) collective-permute-start(bf16[272,128]{1,0:T(8,128)(2,1)S(1)} %get-tuple-element.99), channel_id=1, source_target_pairs={{0,6},{1,7},{2,4},{3,5},{4,2},{5,3},{6,0},{7,1},{8,14},{9,15},{10,... | collective-permute-start | bytes 208904 | tf_op jit(solution)/shard_map/ppermute | solution.py:260
  17.1 1.8 collective-permute-start.6
  18.9 2.2 copy-done
  21.1 3.0 %collective-permute-done.6.refs_6_ = bf16[272,128]{1,0:T(8,128)(2,1)S(1)} collective-permute-done((bf16[272,128]{1,0:T(8,128)(2,1)S(1)}, bf16[272,128]{1,0:T(8,128)(2,1)S(1)}, u32[]{:S(2)}, u32[]{:S(2)}) %collective-permute-start.6) | collective-permute-done | bytes 69664 | tf_op jit(solution)/shard_map/ppermute | solution.py:260
  29.3 2.6 %collective-permute-start.13 = (bf16[272,256]{1,0:T(8,128)(2,1)S(1)}, bf16[272,256]{1,0:T(8,128)(2,1)S(1)}, u32[]{:S(2)}, u32[]{:S(2)}) collective-permute-start(bf16[272,256]{1,0:T(8,128)(2,1)S(1)} %gate.73.__2_), channel_id=1, source_target_pairs={{0,2},{1,3},{2,0},{3,1},{4,6},{5,7},{6,4},{7,5},{8,10},{9,11},{10,... | collective-permute-start | bytes 417800 | tf_op jit(solution)/shard_map/ppermute | solution.py:260
  33.3 2.0 collective-permute-done.11.__1_.rest_0_
  35.3 2.9 %collective-permute-start.16 = (bf16[272,256]{1,0:T(8,128)(2,1)S(1)}, bf16[272,256]{1,0:T(8,128)(2,1)S(1)}, u32[]{:S(2)}, u32[]{:S(2)}) collective-permute-start(bf16[272,256]{1,0:T(8,128)(2,1)S(1)} %gate.75.__2_), channel_id=1, source_target_pairs={{0,6},{1,7},{2,4},{3,5},{4,2},{5,3},{6,0},{7,1},{8,14},{9,15},{10,... | collective-permute-start | bytes 417800 | tf_op jit(solution)/shard_map/ppermute | solution.py:260
  38.2 3.6 %collective-permute-done.9.__1_.rest_2_ = bf16[272,256]{1,0:T(8,128)(2,1)S(1)} collective-permute-done((bf16[272,256]{1,0:T(8,128)(2,1)S(1)}, bf16[272,256]{1,0:T(8,128)(2,1)S(1)}, u32[]{:S(2)}, u32[]{:S(2)}) %collective-permute-start.9) | collective-permute-done | bytes 139296 | tf_op jit(solution)/shard_map/ppermute | solution.py:260
  43.4 3.2 %collective-permute-start.20 = (bf16[272,256]{1,0:T(8,128)(2,1)S(1)}, bf16[272,256]{1,0:T(8,128)(2,1)S(1)}, u32[]{:S(2)}, u32[]{:S(2)}) collective-permute-start(bf16[272,256]{1,0:T(8,128)(2,1)S(1)} %gate.78.__2_), channel_id=1, source_target_pairs={{0,7},{1,6},{2,5},{3,4},{4,3},{5,2},{6,1},{7,0},{8,15},{9,14},{10,... | collective-permute-start | bytes 417800 | tf_op jit(solution)/shard_map/ppermute | solution.py:260
  51.9 6.0 %collective-permute-start.24 = (bf16[272,256]{1,0:T(8,128)(2,1)S(1)}, bf16[272,256]{1,0:T(8,128)(2,1)S(1)}, u32[]{:S(2)}, u32[]{:S(2)}) collective-permute-start(bf16[272,256]{1,0:T(8,128)(2,1)S(1)} %gate.83.__2_), channel_id=1, source_target_pairs={{0,13},{1,12},{2,15},{3,14},{4,9},{5,8},{6,11},{7,10},{8,5},{9,4},... | collective-permute-start | bytes 417800 | tf_op jit(solution)/shard_map/ppermute | solution.py:260
  58.3 2.8 %collective-permute-start.22 = (bf16[272,256]{1,0:T(8,128)(2,1)S(1)}, bf16[272,256]{1,0:T(8,128)(2,1)S(1)}, u32[]{:S(2)}, u32[]{:S(2)}) collective-permute-start(bf16[272,256]{1,0:T(8,128)(2,1)S(1)} %gate.85.__2_), channel_id=1, source_target_pairs={{0,14},{1,15},{2,12},{3,13},{4,10},{5,11},{6,8},{7,9},{8,6},{9,7},... | collective-permute-start | bytes 417800 | tf_op jit(solution)/shard_map/ppermute | solution.py:260
  63.7 2.3 collective-permute-start.28
  67.3 2.1 collective-permute-start.26
  70.5 11.1 %collective-permute-done.28.__1_.rest_0_ = bf16[272,256]{1,0:T(8,128)(2,1)S(1)} collective-permute-done((bf16[272,256]{1,0:T(8,128)(2,1)S(1)}, bf16[272,256]{1,0:T(8,128)(2,1)S(1)}, u32[]{:S(2)}, u32[]{:S(2)}) %collective-permute-start.28) | collective-permute-done | bytes 139296 | tf_op jit(solution)/shard_map/ppermute | solution.py:260
  82.3 1.9 collective-permute-start.33
  84.2 3.1 %combine.4 = (bf16[128,8192]{1,0:T(8,128)(2,1)}, bf16[272,256]{1,0:T(8,128)(2,1)S(1)}, bf16[272,256]{1,0:T(8,128)(2,1)S(1)}, bf16[272,256]{1,0:T(8,128)(2,1)S(1)...) custom-call(s32[2]{0:T(128)S(1)} %pad_add_fusion.at_ref.place_in_ref, ...), custom_call_target="tpu_custom_call" | custom-call | flops 285212672 | bytes 3276800 | tf_op jit(solution)/shard_map/combine/pallas_call | solution.py:320
  87.3 5.2 %collective-permute-start.38 = (bf16[272,256]{1,0:T(8,128)(2,1)S(1)}, bf16[272,256]{1,0:T(8,128)(2,1)S(1)}, u32[]{:S(2)}, u32[]{:S(2)}) collective-permute-start(bf16[272,256]{1,0:T(8,128)(2,1)S(1)} %gate.96.__2_), channel_id=1, source_target_pairs={{0,17},{1,16},{2,19},{3,18},{4,21},{5,20},{6,23},{7,22},{8,25},{9,... | collective-permute-start | bytes 417800 | tf_op jit(solution)/shard_map/ppermute | solution.py:260
  94.3 3.6 %collective-permute-start.36 = (bf16[272,256]{1,0:T(8,128)(2,1)S(1)}, bf16[272,256]{1,0:T(8,128)(2,1)S(1)}, u32[]{:S(2)}, u32[]{:S(2)}) collective-permute-start(bf16[272,256]{1,0:T(8,128)(2,1)S(1)} %gate.99.__2_), channel_id=1, source_target_pairs={{0,3},{1,2},{2,1},{3,0},{4,7},{5,6},{6,5},{7,4},{8,11},{9,10},{10,... | collective-permute-start | bytes 417800 | tf_op jit(solution)/shard_map/ppermute | solution.py:260
  102.5 2.8 %collective-permute-start.44 = (bf16[272,256]{1,0:T(8,128)(2,1)S(1)}, bf16[272,256]{1,0:T(8,128)(2,1)S(1)}, u32[]{:S(2)}, u32[]{:S(2)}) collective-permute-start(bf16[272,256]{1,0:T(8,128)(2,1)S(1)} %gate.103.__2_), channel_id=1, source_target_pairs={{0,5},{1,4},{2,7},{3,6},{4,1},{5,0},{6,3},{7,2},{8,13},{9,12},{10,... | collective-permute-start | bytes 417800 | tf_op jit(solution)/shard_map/ppermute | solution.py:260
  105.3 3.3 %collective-permute-done.36.__1_.refs_1_ = bf16[272,256]{1,0:T(8,128)(2,1)S(1)} collective-permute-done((bf16[272,256]{1,0:T(8,128)(2,1)S(1)}, bf16[272,256]{1,0:T(8,128)(2,1)S(1)}, u32[]{:S(2)}, u32[]{:S(2)}) %collective-permute-start.36) | collective-permute-done | bytes 139296 | tf_op jit(solution)/shard_map/ppermute | solution.py:260
  111.4 2.6 %collective-permute-start.41 = (bf16[272,256]{1,0:T(8,128)(2,1)S(1)}, bf16[272,256]{1,0:T(8,128)(2,1)S(1)}, u32[]{:S(2)}, u32[]{:S(2)}) collective-permute-start(bf16[272,256]{1,0:T(8,128)(2,1)S(1)} %gate.106.__2_), channel_id=1, source_target_pairs={{0,27},{1,26},{2,25},{3,24},{4,31},{5,30},{6,29},{7,28},{8,19},{9,... | collective-permute-start | bytes 417800 | tf_op jit(solution)/shard_map/ppermute | solution.py:260
  114.7 5.3 %collective-permute-done.44.__1_.refs_2_ = bf16[272,256]{1,0:T(8,128)(2,1)S(1)} collective-permute-done((bf16[272,256]{1,0:T(8,128)(2,1)S(1)}, bf16[272,256]{1,0:T(8,128)(2,1)S(1)}, u32[]{:S(2)}, u32[]{:S(2)}) %collective-permute-start.44) | collective-permute-done | bytes 139296 | tf_op jit(solution)/shard_map/ppermute | solution.py:260
  120.0 2.8 %collective-permute-start.49 = (bf16[272,256]{1,0:T(8,128)(2,1)S(1)}, bf16[272,256]{1,0:T(8,128)(2,1)S(1)}, u32[]{:S(2)}, u32[]{:S(2)}) collective-permute-start(bf16[272,256]{1,0:T(8,128)(2,1)S(1)} %gate.109.__2_), channel_id=1, source_target_pairs={{0,6},{1,7},{2,4},{3,5},{4,2},{5,3},{6,0},{7,1},{8,14},{9,15},{10,... | collective-permute-start | bytes 417800 | tf_op jit(solution)/shard_map/ppermute | solution.py:260
  122.8 3.2 %collective-permute-start.51 = (bf16[272,256]{1,0:T(8,128)(2,1)S(1)}, bf16[272,256]{1,0:T(8,128)(2,1)S(1)}, u32[]{:S(2)}, u32[]{:S(2)}) collective-permute-start(bf16[272,256]{1,0:T(8,128)(2,1)S(1)} %gate.110.__2_), channel_id=1, source_target_pairs={{0,1},{1,0},{2,3},{3,2},{4,5},{5,4},{6,7},{7,6},{8,9},{9,8},{10,11... | collective-permute-start | bytes 417800 | tf_op jit(solution)/shard_map/ppermute | solution.py:260
  126.1 2.8 %collective-permute-start.47 = (bf16[272,256]{1,0:T(8,128)(2,1)S(1)}, bf16[272,256]{1,0:T(8,128)(2,1)S(1)}, u32[]{:S(2)}, u32[]{:S(2)}) collective-permute-start(bf16[272,256]{1,0:T(8,128)(2,1)S(1)} %gate.111.__2_), channel_id=1, source_target_pairs={{0,30},{1,31},{2,28},{3,29},{4,26},{5,27},{6,24},{7,25},{8,22},{9,... | collective-permute-start | bytes 417800 | tf_op jit(solution)/shard_map/ppermute | solution.py:260
  128.9 3.2 %collective-permute-start.48 = (bf16[272,256]{1,0:T(8,128)(2,1)S(1)}, bf16[272,256]{1,0:T(8,128)(2,1)S(1)}, u32[]{:S(2)}, u32[]{:S(2)}) collective-permute-start(bf16[272,256]{1,0:T(8,128)(2,1)S(1)} %gate.112.__2_), channel_id=1, source_target_pairs={{0,25},{1,24},{2,27},{3,26},{4,29},{5,28},{6,31},{7,30},{8,17},{9,... | collective-permute-start | bytes 417800 | tf_op jit(solution)/shard_map/ppermute | solution.py:260
  132.1 4.4 %collective-permute-done.45.__1_.rest_3_ = bf16[272,256]{1,0:T(8,128)(2,1)S(1)} collective-permute-done((bf16[272,256]{1,0:T(8,128)(2,1)S(1)}, bf16[272,256]{1,0:T(8,128)(2,1)S(1)}, u32[]{:S(2)}, u32[]{:S(2)}) %collective-permute-start.45) | collective-permute-done | bytes 139296 | tf_op jit(solution)/shard_map/ppermute | solution.py:260
  136.5 3.4 %collective-permute-start.50 = (bf16[272,256]{1,0:T(8,128)(2,1)S(1)}, bf16[272,256]{1,0:T(8,128)(2,1)S(1)}, u32[]{:S(2)}, u32[]{:S(2)}) collective-permute-start(bf16[272,256]{1,0:T(8,128)(2,1)S(1)} %gate.114.__2_), channel_id=1, source_target_pairs={{0,31},{1,30},{2,29},{3,28},{4,27},{5,26},{6,25},{7,24},{8,23},{9,... | collective-permute-start | bytes 417800 | tf_op jit(solution)/shard_map/ppermute | solution.py:260
  140.0 2.5 %collective-permute-start.52 = (bf16[272,256]{1,0:T(8,128)(2,1)S(1)}, bf16[272,256]{1,0:T(8,128)(2,1)S(1)}, u32[]{:S(2)}, u32[]{:S(2)}) collective-permute-start(bf16[272,256]{1,0:T(8,128)(2,1)S(1)} %gate.115.__2_), channel_id=1, source_target_pairs={{0,24},{1,25},{2,26},{3,27},{4,28},{5,29},{6,30},{7,31},{8,16},{9,... | collective-permute-start | bytes 417800 | tf_op jit(solution)/shard_map/ppermute | solution.py:260
  142.4 3.1 %combine.5 = (bf16[128,8192]{1,0:T(8,128)(2,1)}, bf16[272,256]{1,0:T(8,128)(2,1)S(1)}, bf16[272,256]{1,0:T(8,128)(2,1)S(1)}, bf16[272,256]{1,0:T(8,128)(2,1)S(1)...) custom-call(s32[2]{0:T(128)S(1)} %pad_add_fusion.at_ref.place_in_ref, ...), custom_call_target="tpu_custom_call", output_to_operand_aliasing={{0}: (15, {})} | custom-call | flops 285212672 | bytes 3276800 | tf_op jit(solution)/shard_map/combine/pallas_call | solution.py:320
  145.5 3.3 %combine.6 = (bf16[128,8192]{1,0:T(8,128)(2,1)}, bf16[272,256]{1,0:T(8,128)(2,1)S(1)}, bf16[272,256]{1,0:T(8,128)(2,1)S(1)}, bf16[272,256]{1,0:T(8,128)(2,1)S(1)...) custom-call(s32[2]{0:T(128)S(1)} %pad_add_fusion.at_ref.place_in_ref, ...), custom_call_target="tpu_custom_call", output_to_operand_aliasing={{0}: (15, {})} | custom-call | flops 285212672 | bytes 3276800 | tf_op jit(solution)/shard_map/combine/pallas_call | solution.py:320
  150.3 2.4 %collective-permute-start.58 = (bf16[272,256]{1,0:T(8,128)(2,1)S(1)}, bf16[272,256]{1,0:T(8,128)(2,1)S(1)}, u32[]{:S(2)}, u32[]{:S(2)}) collective-permute-start(bf16[272,256]{1,0:T(8,128)(2,1)S(1)} %gate.118.__2_), channel_id=1, source_target_pairs={{0,12},{1,13},{2,14},{3,15},{4,8},{5,9},{6,10},{7,11},{8,4},{9,5},... | collective-permute-start | bytes 417800 | tf_op jit(solution)/shard_map/ppermute | solution.py:260
  152.7 4.5 %collective-permute-start.57 = (bf16[272,256]{1,0:T(8,128)(2,1)S(1)}, bf16[272,256]{1,0:T(8,128)(2,1)S(1)}, u32[]{:S(2)}, u32[]{:S(2)}) collective-permute-start(bf16[272,256]{1,0:T(8,128)(2,1)S(1)} %gate.119.__2_), channel_id=1, source_target_pairs={{0,11},{1,10},{2,9},{3,8},{4,15},{5,14},{6,13},{7,12},{8,3},{9,2},... | collective-permute-start | bytes 417800 | tf_op jit(solution)/shard_map/ppermute | solution.py:260
  157.2 3.0 %collective-permute-done.53.__1_.refs_8_ = bf16[272,256]{1,0:T(8,128)(2,1)S(1)} collective-permute-done((bf16[272,256]{1,0:T(8,128)(2,1)S(1)}, bf16[272,256]{1,0:T(8,128)(2,1)S(1)}, u32[]{:S(2)}, u32[]{:S(2)}) %collective-permute-start.53) | collective-permute-done | bytes 139296 | tf_op jit(solution)/shard_map/ppermute | solution.py:260
  161.1 2.8 %collective-permute-start.64 = (bf16[272,256]{1,0:T(8,128)(2,1)S(1)}, bf16[272,256]{1,0:T(8,128)(2,1)S(1)}, u32[]{:S(2)}, u32[]{:S(2)}) collective-permute-start(bf16[272,256]{1,0:T(8,128)(2,1)S(1)} %gate.122.__2_), channel_id=1, source_target_pairs={{0,22},{1,23},{2,20},{3,21},{4,18},{5,19},{6,16},{7,17},{8,30},{9,... | collective-permute-start | bytes 417800 | tf_op jit(solution)/shard_map/ppermute | solution.py:260
  165.0 2.5 %collective-permute-start.62 = (bf16[272,256]{1,0:T(8,128)(2,1)S(1)}, bf16[272,256]{1,0:T(8,128)(2,1)S(1)}, u32[]{:S(2)}, u32[]{:S(2)}) collective-permute-start(bf16[272,256]{1,0:T(8,128)(2,1)S(1)} %gate.124.__2_), channel_id=1, source_target_pairs={{0,13},{1,12},{2,15},{3,14},{4,9},{5,8},{6,11},{7,10},{8,5},{9,4},... | collective-permute-start | bytes 417800 | tf_op jit(solution)/shard_map/ppermute | solution.py:260
  167.4 5.7 %collective-permute-done.56.__1_.refs_10_ = bf16[272,256]{1,0:T(8,128)(2,1)S(1)} collective-permute-done((bf16[272,256]{1,0:T(8,128)(2,1)S(1)}, bf16[272,256]{1,0:T(8,128)(2,1)S(1)}, u32[]{:S(2)}, u32[]{:S(2)}) %collective-permute-start.56) | collective-permute-done | bytes 139296 | tf_op jit(solution)/shard_map/ppermute | solution.py:260
  173.3 3.1 %combine.7 = (bf16[128,8192]{1,0:T(8,128)(2,1)}, bf16[272,256]{1,0:T(8,128)(2,1)S(1)}, bf16[272,256]{1,0:T(8,128)(2,1)S(1)}, bf16[272,256]{1,0:T(8,128)(2,1)S(1)...) custom-call(s32[2]{0:T(128)S(1)} %pad_add_fusion.at_ref.place_in_ref, ...), custom_call_target="tpu_custom_call", output_to_operand_aliasing={{0}: (15, {})} | custom-call | flops 285212672 | bytes 3276800 | tf_op jit(solution)/shard_map/combine/pallas_call | solution.py:320
  176.3 3.6 %collective-permute-start.60 = (bf16[272,256]{1,0:T(8,128)(2,1)S(1)}, bf16[272,256]{1,0:T(8,128)(2,1)S(1)}, u32[]{:S(2)}, u32[]{:S(2)}) collective-permute-start(bf16[272,256]{1,0:T(8,128)(2,1)S(1)} %gate.126.__2_), channel_id=1, source_target_pairs={{0,23},{1,22},{2,21},{3,20},{4,19},{5,18},{6,17},{7,16},{8,31},{9,... | collective-permute-start | bytes 417800 | tf_op jit(solution)/shard_map/ppermute | solution.py:260
  181.3 4.6 %collective-permute-start.68 = (bf16[272,256]{1,0:T(8,128)(2,1)S(1)}, bf16[272,256]{1,0:T(8,128)(2,1)S(1)}, u32[]{:S(2)}, u32[]{:S(2)}) collective-permute-start(bf16[272,256]{1,0:T(8,128)(2,1)S(1)} %gate.128.__2_), channel_id=1, source_target_pairs={{0,14},{1,15},{2,12},{3,13},{4,10},{5,11},{6,8},{7,9},{8,6},{9,7},... | collective-permute-start | bytes 417800 | tf_op jit(solution)/shard_map/ppermute | solution.py:260
  186.1 3.5 %collective-permute-start.66 = (bf16[272,256]{1,0:T(8,128)(2,1)S(1)}, bf16[272,256]{1,0:T(8,128)(2,1)S(1)}, u32[]{:S(2)}, u32[]{:S(2)}) collective-permute-start(bf16[272,256]{1,0:T(8,128)(2,1)S(1)} %gate.130.__2_), channel_id=1, source_target_pairs={{0,28},{1,29},{2,30},{3,31},{4,24},{5,25},{6,26},{7,27},{8,20},{9,... | collective-permute-start | bytes 417800 | tf_op jit(solution)/shard_map/ppermute | solution.py:260
  189.6 5.5 %collective-permute-start.65 = (bf16[272,256]{1,0:T(8,128)(2,1)S(1)}, bf16[272,256]{1,0:T(8,128)(2,1)S(1)}, u32[]{:S(2)}, u32[]{:S(2)}) collective-permute-start(bf16[272,256]{1,0:T(8,128)(2,1)S(1)} %gate.131.__2_), channel_id=1, source_target_pairs={{0,27},{1,26},{2,25},{3,24},{4,31},{5,30},{6,29},{7,28},{8,19},{9,... | collective-permute-start | bytes 417800 | tf_op jit(solution)/shard_map/ppermute | solution.py:260
  195.1 10.1 %collective-permute-start.73 = (bf16[272,256]{1,0:T(8,128)(2,1)S(1)}, bf16[272,256]{1,0:T(8,128)(2,1)S(1)}, u32[]{:S(2)}, u32[]{:S(2)}) collective-permute-start(bf16[272,256]{1,0:T(8,128)(2,1)S(1)} %gate.133.__2_), channel_id=1, source_target_pairs={{0,26},{1,27},{2,24},{3,25},{4,30},{5,31},{6,28},{7,29},{8,18},{9,... | collective-permute-start | bytes 417800 | tf_op jit(solution)/shard_map/ppermute | solution.py:260
  209.1 9.3 %collective-permute-start.72 = (bf16[272,256]{1,0:T(8,128)(2,1)S(1)}, bf16[272,256]{1,0:T(8,128)(2,1)S(1)}, u32[]{:S(2)}, u32[]{:S(2)}) collective-permute-start(bf16[272,256]{1,0:T(8,128)(2,1)S(1)} %gate.137.__2_), channel_id=1, source_target_pairs={{0,25},{1,24},{2,27},{3,26},{4,29},{5,28},{6,31},{7,30},{8,17},{9,... | collective-permute-start | bytes 417800 | tf_op jit(solution)/shard_map/ppermute | solution.py:260
  219.5 6.0 %gradient.2.refs_4_ = f32[1024,2048]{1,0:T(8,128)S(1)} custom-call(bf16[1024,952]{1,0:T(8,128)(2,1)S(1)} %turn.3.codes_ref, bf16[272,256]{1,0:T(8,128)(2,1)S(1)} %collective-permute-done.37.__1_.refs_0_, bf16[272,256]{1,0:T(8,128)(2,1)S(1)} %collective-permute-done.36.__1_.refs_1_, bf16[272,256]{1,0:T(8,128)(2,1)S(1)} %collective-permute-done.44.__1_.refs_2_, ...), custom_call_target="tpu_custom_call" | custom-call | flops 3992977408 | bytes 8388608 | tf_op jit(solution)/shard_map/gradient/pallas_call | solution.py:355
  227.4 3.3 %gradient.3 = bf16[1024,2048]{1,0:T(8,128)(2,1)} custom-call(bf16[1024,136]{1,0:T(8,128)(2,1)S(1)} %turn.2.codes_ref, bf16[272,256]{1,0:T(8,128)(2,1)S(1)} %collective-permute-done.70.refs_0_, bf16[272,256]{1,0:T(8,128)(2,1)S(1)} %collective-permute-done.72.refs_1_, bf16[272,256]{1,0:T(8,128)(2,1)S(1)} %collective-permute-done.74.refs_2_, ...), custom_call_target="tpu_custom_call" | custom-call | flops 570425344 | bytes 8388608 | tf_op jit(solution)/shard_map/gradient/pallas_call | solution.py:355
  (207 shorter events, 47.4 us)
Async XLA Ops:
  28.3 13.5 %collective-permute-start.9 = (bf16[272,256]{1,0:T(8,128)(2,1)S(1)}, bf16[272,256]{1,0:T(8,128)(2,1)S(1)}, u32[]{:S(2)}, u32[]{:S(2)}) collective-permute-start(bf16[272,256]{1,0:T(8,128)(2,1)S(1)} %gate.72.__1_), channel_id=1, source_target_pairs={{0,5},{1,4},{2,7},{3,6},{4,1},{5,0},{6,3},{7,2},{8,13},{9,12},{10,... | collective-permute-start | bytes 417800 | tf_op jit(solution)/shard_map/ppermute | solution.py:260
  29.3 14.1 %collective-permute-start.13 = (bf16[272,256]{1,0:T(8,128)(2,1)S(1)}, bf16[272,256]{1,0:T(8,128)(2,1)S(1)}, u32[]{:S(2)}, u32[]{:S(2)}) collective-permute-start(bf16[272,256]{1,0:T(8,128)(2,1)S(1)} %gate.73.__2_), channel_id=1, source_target_pairs={{0,2},{1,3},{2,0},{3,1},{4,6},{5,7},{6,4},{7,5},{8,10},{9,11},{10,... | collective-permute-start | bytes 417800 | tf_op jit(solution)/shard_map/ppermute | solution.py:260
  31.8 16.2 %collective-permute-start.8 = (bf16[272,256]{1,0:T(8,128)(2,1)S(1)}, bf16[272,256]{1,0:T(8,128)(2,1)S(1)}, u32[]{:S(2)}, u32[]{:S(2)}) collective-permute-start(bf16[272,256]{1,0:T(8,128)(2,1)S(1)} %gate.74.__2_), channel_id=1, source_target_pairs={{0,16},{1,17},{2,18},{3,19},{4,20},{5,21},{6,22},{7,23},{8,24},{9,... | collective-permute-start | bytes 417800 | tf_op jit(solution)/shard_map/ppermute | solution.py:260
  35.3 14.3 %collective-permute-start.16 = (bf16[272,256]{1,0:T(8,128)(2,1)S(1)}, bf16[272,256]{1,0:T(8,128)(2,1)S(1)}, u32[]{:S(2)}, u32[]{:S(2)}) collective-permute-start(bf16[272,256]{1,0:T(8,128)(2,1)S(1)} %gate.75.__2_), channel_id=1, source_target_pairs={{0,6},{1,7},{2,4},{3,5},{4,2},{5,3},{6,0},{7,1},{8,14},{9,15},{10,... | collective-permute-start | bytes 417800 | tf_op jit(solution)/shard_map/ppermute | solution.py:260
  51.9 14.0 %collective-permute-start.24 = (bf16[272,256]{1,0:T(8,128)(2,1)S(1)}, bf16[272,256]{1,0:T(8,128)(2,1)S(1)}, u32[]{:S(2)}, u32[]{:S(2)}) collective-permute-start(bf16[272,256]{1,0:T(8,128)(2,1)S(1)} %gate.83.__2_), channel_id=1, source_target_pairs={{0,13},{1,12},{2,15},{3,14},{4,9},{5,8},{6,11},{7,10},{8,5},{9,4},... | collective-permute-start | bytes 417800 | tf_op jit(solution)/shard_map/ppermute | solution.py:260
  63.7 17.9 %collective-permute-start.28 = (bf16[272,256]{1,0:T(8,128)(2,1)S(1)}, bf16[272,256]{1,0:T(8,128)(2,1)S(1)}, u32[]{:S(2)}, u32[]{:S(2)}) collective-permute-start(bf16[272,256]{1,0:T(8,128)(2,1)S(1)} %gate.87.__2_), channel_id=1, source_target_pairs={{0,20},{1,21},{2,22},{3,23},{4,16},{5,17},{6,18},{7,19},{8,28},{9,... | collective-permute-start | bytes 417800 | tf_op jit(solution)/shard_map/ppermute | solution.py:260
  66.0 15.6 %collective-permute-start.27 = (bf16[272,256]{1,0:T(8,128)(2,1)S(1)}, bf16[272,256]{1,0:T(8,128)(2,1)S(1)}, u32[]{:S(2)}, u32[]{:S(2)}) collective-permute-start(bf16[272,256]{1,0:T(8,128)(2,1)S(1)} %gate.88.__2_), channel_id=1, source_target_pairs={{0,19},{1,18},{2,17},{3,16},{4,23},{5,22},{6,21},{7,20},{8,27},{9,... | collective-permute-start | bytes 417800 | tf_op jit(solution)/shard_map/ppermute | solution.py:260
  67.3 15.0 %collective-permute-start.26 = (bf16[272,256]{1,0:T(8,128)(2,1)S(1)}, bf16[272,256]{1,0:T(8,128)(2,1)S(1)}, u32[]{:S(2)}, u32[]{:S(2)}) collective-permute-start(bf16[272,256]{1,0:T(8,128)(2,1)S(1)} %gate.89.__2_), channel_id=1, source_target_pairs={{0,15},{1,14},{2,13},{3,12},{4,11},{5,10},{6,9},{7,8},{8,7},{9,6},... | collective-permute-start | bytes 417800 | tf_op jit(solution)/shard_map/ppermute | solution.py:260
  69.5 12.8 %collective-permute-start.31 = (bf16[272,256]{1,0:T(8,128)(2,1)S(1)}, bf16[272,256]{1,0:T(8,128)(2,1)S(1)}, u32[]{:S(2)}, u32[]{:S(2)}) collective-permute-start(bf16[272,256]{1,0:T(8,128)(2,1)S(1)} %gate.90.__2_), channel_id=1, source_target_pairs={{0,8},{1,9},{2,10},{3,11},{4,12},{5,13},{6,14},{7,15},{8,0},{9,1},... | collective-permute-start | bytes 417800 | tf_op jit(solution)/shard_map/ppermute | solution.py:260
  70.4 16.9 %collective-permute-start.25 = (bf16[272,256]{1,0:T(8,128)(2,1)S(1)}, bf16[272,256]{1,0:T(8,128)(2,1)S(1)}, u32[]{:S(2)}, u32[]{:S(2)}) collective-permute-start(bf16[272,256]{1,0:T(8,128)(2,1)S(1)} %gate.91.__2_), channel_id=1, source_target_pairs={{0,8},{1,9},{2,10},{3,11},{4,12},{5,13},{6,14},{7,15},{8,0},{9,1},... | collective-permute-start | bytes 417800 | tf_op jit(solution)/shard_map/ppermute | solution.py:260
  81.6 12.4 %collective-permute-start.34 = (bf16[272,256]{1,0:T(8,128)(2,1)S(1)}, bf16[272,256]{1,0:T(8,128)(2,1)S(1)}, u32[]{:S(2)}, u32[]{:S(2)}) collective-permute-start(bf16[272,256]{1,0:T(8,128)(2,1)S(1)} %gate.93.__2_), channel_id=1, source_target_pairs={{0,18},{1,19},{2,16},{3,17},{4,22},{5,23},{6,20},{7,21},{8,26},{9,... | collective-permute-start | bytes 417800 | tf_op jit(solution)/shard_map/ppermute | solution.py:260
  82.3 12.0 %collective-permute-start.29 = (bf16[272,256]{1,0:T(8,128)(2,1)S(1)}, bf16[272,256]{1,0:T(8,128)(2,1)S(1)}, u32[]{:S(2)}, u32[]{:S(2)}) collective-permute-start(bf16[272,256]{1,0:T(8,128)(2,1)S(1)} %gate.94.__2_), channel_id=1, source_target_pairs={{0,8},{1,9},{2,10},{3,11},{4,12},{5,13},{6,14},{7,15},{8,0},{9,1},... | collective-permute-start | bytes 417800 | tf_op jit(solution)/shard_map/ppermute | solution.py:260
  82.3 15.5 %collective-permute-start.33 = (bf16[272,256]{1,0:T(8,128)(2,1)S(1)}, bf16[272,256]{1,0:T(8,128)(2,1)S(1)}, u32[]{:S(2)}, u32[]{:S(2)}) collective-permute-start(bf16[272,256]{1,0:T(8,128)(2,1)S(1)} %gate.95.__2_), channel_id=1, source_target_pairs={{0,22},{1,23},{2,20},{3,21},{4,18},{5,19},{6,16},{7,17},{8,30},{9,... | collective-permute-start | bytes 417800 | tf_op jit(solution)/shard_map/ppermute | solution.py:260
  87.3 12.3 %collective-permute-start.38 = (bf16[272,256]{1,0:T(8,128)(2,1)S(1)}, bf16[272,256]{1,0:T(8,128)(2,1)S(1)}, u32[]{:S(2)}, u32[]{:S(2)}) collective-permute-start(bf16[272,256]{1,0:T(8,128)(2,1)S(1)} %gate.96.__2_), channel_id=1, source_target_pairs={{0,17},{1,16},{2,19},{3,18},{4,21},{5,20},{6,23},{7,22},{8,25},{9,... | collective-permute-start | bytes 417800 | tf_op jit(solution)/shard_map/ppermute | solution.py:260
  94.3 14.4 %collective-permute-start.36 = (bf16[272,256]{1,0:T(8,128)(2,1)S(1)}, bf16[272,256]{1,0:T(8,128)(2,1)S(1)}, u32[]{:S(2)}, u32[]{:S(2)}) collective-permute-start(bf16[272,256]{1,0:T(8,128)(2,1)S(1)} %gate.99.__2_), channel_id=1, source_target_pairs={{0,3},{1,2},{2,1},{3,0},{4,7},{5,6},{6,5},{7,4},{8,11},{9,10},{10,... | collective-permute-start | bytes 417800 | tf_op jit(solution)/shard_map/ppermute | solution.py:260
  101.2 12.8 %collective-permute-start.42 = (bf16[272,256]{1,0:T(8,128)(2,1)S(1)}, bf16[272,256]{1,0:T(8,128)(2,1)S(1)}, u32[]{:S(2)}, u32[]{:S(2)}) collective-permute-start(bf16[272,256]{1,0:T(8,128)(2,1)S(1)} %gate.102.__2_), channel_id=1, source_target_pairs={{0,16},{1,17},{2,18},{3,19},{4,20},{5,21},{6,22},{7,23},{8,24},{9,... | collective-permute-start | bytes 417800 | tf_op jit(solution)/shard_map/ppermute | solution.py:260
  102.5 17.5 %collective-permute-start.44 = (bf16[272,256]{1,0:T(8,128)(2,1)S(1)}, bf16[272,256]{1,0:T(8,128)(2,1)S(1)}, u32[]{:S(2)}, u32[]{:S(2)}) collective-permute-start(bf16[272,256]{1,0:T(8,128)(2,1)S(1)} %gate.103.__2_), channel_id=1, source_target_pairs={{0,5},{1,4},{2,7},{3,6},{4,1},{5,0},{6,3},{7,2},{8,13},{9,12},{10,... | collective-permute-start | bytes 417800 | tf_op jit(solution)/shard_map/ppermute | solution.py:260
  111.4 14.7 %collective-permute-start.41 = (bf16[272,256]{1,0:T(8,128)(2,1)S(1)}, bf16[272,256]{1,0:T(8,128)(2,1)S(1)}, u32[]{:S(2)}, u32[]{:S(2)}) collective-permute-start(bf16[272,256]{1,0:T(8,128)(2,1)S(1)} %gate.106.__2_), channel_id=1, source_target_pairs={{0,27},{1,26},{2,25},{3,24},{4,31},{5,30},{6,29},{7,28},{8,19},{9,... | collective-permute-start | bytes 417800 | tf_op jit(solution)/shard_map/ppermute | solution.py:260
  114.0 14.9 %collective-permute-start.43 = (bf16[272,256]{1,0:T(8,128)(2,1)S(1)}, bf16[272,256]{1,0:T(8,128)(2,1)S(1)}, u32[]{:S(2)}, u32[]{:S(2)}) collective-permute-start(bf16[272,256]{1,0:T(8,128)(2,1)S(1)} %gate.107.__2_), channel_id=1, source_target_pairs={{0,29},{1,28},{2,31},{3,30},{4,25},{5,24},{6,27},{7,26},{8,21},{9,... | collective-permute-start | bytes 417800 | tf_op jit(solution)/shard_map/ppermute | solution.py:260
  120.0 16.5 %collective-permute-start.45 = (bf16[272,256]{1,0:T(8,128)(2,1)S(1)}, bf16[272,256]{1,0:T(8,128)(2,1)S(1)}, u32[]{:S(2)}, u32[]{:S(2)}) collective-permute-start(bf16[272,256]{1,0:T(8,128)(2,1)S(1)} %gate.108.__2_), channel_id=1, source_target_pairs={{0,26},{1,27},{2,24},{3,25},{4,30},{5,31},{6,28},{7,29},{8,18},{9,... | collective-permute-start | bytes 417800 | tf_op jit(solution)/shard_map/ppermute | solution.py:260
  120.0 16.5 %collective-permute-start.49 = (bf16[272,256]{1,0:T(8,128)(2,1)S(1)}, bf16[272,256]{1,0:T(8,128)(2,1)S(1)}, u32[]{:S(2)}, u32[]{:S(2)}) collective-permute-start(bf16[272,256]{1,0:T(8,128)(2,1)S(1)} %gate.109.__2_), channel_id=1, source_target_pairs={{0,6},{1,7},{2,4},{3,5},{4,2},{5,3},{6,0},{7,1},{8,14},{9,15},{10,... | collective-permute-start | bytes 417800 | tf_op jit(solution)/shard_map/ppermute | solution.py:260
  122.8 17.1 %collective-permute-start.51 = (bf16[272,256]{1,0:T(8,128)(2,1)S(1)}, bf16[272,256]{1,0:T(8,128)(2,1)S(1)}, u32[]{:S(2)}, u32[]{:S(2)}) collective-permute-start(bf16[272,256]{1,0:T(8,128)(2,1)S(1)} %gate.110.__2_), channel_id=1, source_target_pairs={{0,1},{1,0},{2,3},{3,2},{4,5},{5,4},{6,7},{7,6},{8,9},{9,8},{10,11... | collective-permute-start | bytes 417800 | tf_op jit(solution)/shard_map/ppermute | solution.py:260
  126.1 22.7 %collective-permute-start.47 = (bf16[272,256]{1,0:T(8,128)(2,1)S(1)}, bf16[272,256]{1,0:T(8,128)(2,1)S(1)}, u32[]{:S(2)}, u32[]{:S(2)}) collective-permute-start(bf16[272,256]{1,0:T(8,128)(2,1)S(1)} %gate.111.__2_), channel_id=1, source_target_pairs={{0,30},{1,31},{2,28},{3,29},{4,26},{5,27},{6,24},{7,25},{8,22},{9,... | collective-permute-start | bytes 417800 | tf_op jit(solution)/shard_map/ppermute | solution.py:260
  128.9 19.9 %collective-permute-start.48 = (bf16[272,256]{1,0:T(8,128)(2,1)S(1)}, bf16[272,256]{1,0:T(8,128)(2,1)S(1)}, u32[]{:S(2)}, u32[]{:S(2)}) collective-permute-start(bf16[272,256]{1,0:T(8,128)(2,1)S(1)} %gate.112.__2_), channel_id=1, source_target_pairs={{0,25},{1,24},{2,27},{3,26},{4,29},{5,28},{6,31},{7,30},{8,17},{9,... | collective-permute-start | bytes 417800 | tf_op jit(solution)/shard_map/ppermute | solution.py:260
  136.5 13.8 %collective-permute-start.54 = (bf16[272,256]{1,0:T(8,128)(2,1)S(1)}, bf16[272,256]{1,0:T(8,128)(2,1)S(1)}, u32[]{:S(2)}, u32[]{:S(2)}) collective-permute-start(bf16[272,256]{1,0:T(8,128)(2,1)S(1)} %gate.113.__2_), channel_id=1, source_target_pairs={{0,7},{1,6},{2,5},{3,4},{4,3},{5,2},{6,1},{7,0},{8,15},{9,14},{10,... | collective-permute-start | bytes 417800 | tf_op jit(solution)/shard_map/ppermute | solution.py:260
  136.5 16.2 %collective-permute-start.50 = (bf16[272,256]{1,0:T(8,128)(2,1)S(1)}, bf16[272,256]{1,0:T(8,128)(2,1)S(1)}, u32[]{:S(2)}, u32[]{:S(2)}) collective-permute-start(bf16[272,256]{1,0:T(8,128)(2,1)S(1)} %gate.114.__2_), channel_id=1, source_target_pairs={{0,31},{1,30},{2,29},{3,28},{4,27},{5,26},{6,25},{7,24},{8,23},{9,... | collective-permute-start | bytes 417800 | tf_op jit(solution)/shard_map/ppermute | solution.py:260
  140.0 17.2 %collective-permute-start.52 = (bf16[272,256]{1,0:T(8,128)(2,1)S(1)}, bf16[272,256]{1,0:T(8,128)(2,1)S(1)}, u32[]{:S(2)}, u32[]{:S(2)}) collective-permute-start(bf16[272,256]{1,0:T(8,128)(2,1)S(1)} %gate.115.__2_), channel_id=1, source_target_pairs={{0,24},{1,25},{2,26},{3,27},{4,28},{5,29},{6,30},{7,31},{8,16},{9,... | collective-permute-start | bytes 417800 | tf_op jit(solution)/shard_map/ppermute | solution.py:260
  148.8 12.3 %collective-permute-start.59 = (bf16[272,256]{1,0:T(8,128)(2,1)S(1)}, bf16[272,256]{1,0:T(8,128)(2,1)S(1)}, u32[]{:S(2)}, u32[]{:S(2)}) collective-permute-start(bf16[272,256]{1,0:T(8,128)(2,1)S(1)} %gate.117.__2_), channel_id=1, source_target_pairs={{0,19},{1,18},{2,17},{3,16},{4,23},{5,22},{6,21},{7,20},{8,27},{9,... | collective-permute-start | bytes 417800 | tf_op jit(solution)/shard_map/ppermute | solution.py:260
  150.3 14.3 %collective-permute-start.58 = (bf16[272,256]{1,0:T(8,128)(2,1)S(1)}, bf16[272,256]{1,0:T(8,128)(2,1)S(1)}, u32[]{:S(2)}, u32[]{:S(2)}) collective-permute-start(bf16[272,256]{1,0:T(8,128)(2,1)S(1)} %gate.118.__2_), channel_id=1, source_target_pairs={{0,12},{1,13},{2,14},{3,15},{4,8},{5,9},{6,10},{7,11},{8,4},{9,5},... | collective-permute-start | bytes 417800 | tf_op jit(solution)/shard_map/ppermute | solution.py:260
  152.7 12.2 %collective-permute-start.57 = (bf16[272,256]{1,0:T(8,128)(2,1)S(1)}, bf16[272,256]{1,0:T(8,128)(2,1)S(1)}, u32[]{:S(2)}, u32[]{:S(2)}) collective-permute-start(bf16[272,256]{1,0:T(8,128)(2,1)S(1)} %gate.119.__2_), channel_id=1, source_target_pairs={{0,11},{1,10},{2,9},{3,8},{4,15},{5,14},{6,13},{7,12},{8,3},{9,2},... | collective-permute-start | bytes 417800 | tf_op jit(solution)/shard_map/ppermute | solution.py:260
  157.2 15.9 %collective-permute-start.56 = (bf16[272,256]{1,0:T(8,128)(2,1)S(1)}, bf16[272,256]{1,0:T(8,128)(2,1)S(1)}, u32[]{:S(2)}, u32[]{:S(2)}) collective-permute-start(bf16[272,256]{1,0:T(8,128)(2,1)S(1)} %gate.120.__2_), channel_id=1, source_target_pairs={{0,21},{1,20},{2,23},{3,22},{4,17},{5,16},{6,19},{7,18},{8,29},{9,... | collective-permute-start | bytes 417800 | tf_op jit(solution)/shard_map/ppermute | solution.py:260
  160.2 16.1 %collective-permute-start.55 = (bf16[272,256]{1,0:T(8,128)(2,1)S(1)}, bf16[272,256]{1,0:T(8,128)(2,1)S(1)}, u32[]{:S(2)}, u32[]{:S(2)}) collective-permute-start(bf16[272,256]{1,0:T(8,128)(2,1)S(1)} %gate.121.__2_), channel_id=1, source_target_pairs={{0,18},{1,19},{2,16},{3,17},{4,22},{5,23},{6,20},{7,21},{8,26},{9,... | collective-permute-start | bytes 417800 | tf_op jit(solution)/shard_map/ppermute | solution.py:260
  161.1 18.9 %collective-permute-start.64 = (bf16[272,256]{1,0:T(8,128)(2,1)S(1)}, bf16[272,256]{1,0:T(8,128)(2,1)S(1)}, u32[]{:S(2)}, u32[]{:S(2)}) collective-permute-start(bf16[272,256]{1,0:T(8,128)(2,1)S(1)} %gate.122.__2_), channel_id=1, source_target_pairs={{0,22},{1,23},{2,20},{3,21},{4,18},{5,19},{6,16},{7,17},{8,30},{9,... | collective-permute-start | bytes 417800 | tf_op jit(solution)/shard_map/ppermute | solution.py:260
  164.7 16.7 %collective-permute-start.63 = (bf16[272,256]{1,0:T(8,128)(2,1)S(1)}, bf16[272,256]{1,0:T(8,128)(2,1)S(1)}, u32[]{:S(2)}, u32[]{:S(2)}) collective-permute-start(bf16[272,256]{1,0:T(8,128)(2,1)S(1)} %gate.123.__2_), channel_id=1, source_target_pairs={{0,17},{1,16},{2,19},{3,18},{4,21},{5,20},{6,23},{7,22},{8,25},{9,... | collective-permute-start | bytes 417800 | tf_op jit(solution)/shard_map/ppermute | solution.py:260
  165.0 21.0 %collective-permute-start.62 = (bf16[272,256]{1,0:T(8,128)(2,1)S(1)}, bf16[272,256]{1,0:T(8,128)(2,1)S(1)}, u32[]{:S(2)}, u32[]{:S(2)}) collective-permute-start(bf16[272,256]{1,0:T(8,128)(2,1)S(1)} %gate.124.__2_), channel_id=1, source_target_pairs={{0,13},{1,12},{2,15},{3,14},{4,9},{5,8},{6,11},{7,10},{8,5},{9,4},... | collective-permute-start | bytes 417800 | tf_op jit(solution)/shard_map/ppermute | solution.py:260
  173.1 13.0 %collective-permute-start.61 = (bf16[272,256]{1,0:T(8,128)(2,1)S(1)}, bf16[272,256]{1,0:T(8,128)(2,1)S(1)}, u32[]{:S(2)}, u32[]{:S(2)}) collective-permute-start(bf16[272,256]{1,0:T(8,128)(2,1)S(1)} %gate.125.__2_), channel_id=1, source_target_pairs={{0,10},{1,11},{2,8},{3,9},{4,14},{5,15},{6,12},{7,13},{8,2},{9,3},... | collective-permute-start | bytes 417800 | tf_op jit(solution)/shard_map/ppermute | solution.py:260
  176.3 13.3 %collective-permute-start.60 = (bf16[272,256]{1,0:T(8,128)(2,1)S(1)}, bf16[272,256]{1,0:T(8,128)(2,1)S(1)}, u32[]{:S(2)}, u32[]{:S(2)}) collective-permute-start(bf16[272,256]{1,0:T(8,128)(2,1)S(1)} %gate.126.__2_), channel_id=1, source_target_pairs={{0,23},{1,22},{2,21},{3,20},{4,19},{5,18},{6,17},{7,16},{8,31},{9,... | collective-permute-start | bytes 417800 | tf_op jit(solution)/shard_map/ppermute | solution.py:260
  180.0 15.1 %collective-permute-start.69 = (bf16[272,256]{1,0:T(8,128)(2,1)S(1)}, bf16[272,256]{1,0:T(8,128)(2,1)S(1)}, u32[]{:S(2)}, u32[]{:S(2)}) collective-permute-start(bf16[272,256]{1,0:T(8,128)(2,1)S(1)} %gate.127.__2_), channel_id=1, source_target_pairs={{0,16},{1,17},{2,18},{3,19},{4,20},{5,21},{6,22},{7,23},{8,24},{9,... | collective-permute-start | bytes 417800 | tf_op jit(solution)/shard_map/ppermute | solution.py:260
  181.3 13.7 %collective-permute-start.68 = (bf16[272,256]{1,0:T(8,128)(2,1)S(1)}, bf16[272,256]{1,0:T(8,128)(2,1)S(1)}, u32[]{:S(2)}, u32[]{:S(2)}) collective-permute-start(bf16[272,256]{1,0:T(8,128)(2,1)S(1)} %gate.128.__2_), channel_id=1, source_target_pairs={{0,14},{1,15},{2,12},{3,13},{4,10},{5,11},{6,8},{7,9},{8,6},{9,7},... | collective-permute-start | bytes 417800 | tf_op jit(solution)/shard_map/ppermute | solution.py:260
  185.9 19.3 %collective-permute-start.67 = (bf16[272,256]{1,0:T(8,128)(2,1)S(1)}, bf16[272,256]{1,0:T(8,128)(2,1)S(1)}, u32[]{:S(2)}, u32[]{:S(2)}) collective-permute-start(bf16[272,256]{1,0:T(8,128)(2,1)S(1)} %gate.129.__2_), channel_id=1, source_target_pairs={{0,9},{1,8},{2,11},{3,10},{4,13},{5,12},{6,15},{7,14},{8,1},{9,0},... | collective-permute-start | bytes 417800 | tf_op jit(solution)/shard_map/ppermute | solution.py:260
  186.1 19.1 %collective-permute-start.66 = (bf16[272,256]{1,0:T(8,128)(2,1)S(1)}, bf16[272,256]{1,0:T(8,128)(2,1)S(1)}, u32[]{:S(2)}, u32[]{:S(2)}) collective-permute-start(bf16[272,256]{1,0:T(8,128)(2,1)S(1)} %gate.130.__2_), channel_id=1, source_target_pairs={{0,28},{1,29},{2,30},{3,31},{4,24},{5,25},{6,26},{7,27},{8,20},{9,... | collective-permute-start | bytes 417800 | tf_op jit(solution)/shard_map/ppermute | solution.py:260
  189.6 17.5 %collective-permute-start.65 = (bf16[272,256]{1,0:T(8,128)(2,1)S(1)}, bf16[272,256]{1,0:T(8,128)(2,1)S(1)}, u32[]{:S(2)}, u32[]{:S(2)}) collective-permute-start(bf16[272,256]{1,0:T(8,128)(2,1)S(1)} %gate.131.__2_), channel_id=1, source_target_pairs={{0,27},{1,26},{2,25},{3,24},{4,31},{5,30},{6,29},{7,28},{8,19},{9,... | collective-permute-start | bytes 417800 | tf_op jit(solution)/shard_map/ppermute | solution.py:260
  195.1 14.1 %collective-permute-start.71 = (bf16[272,256]{1,0:T(8,128)(2,1)S(1)}, bf16[272,256]{1,0:T(8,128)(2,1)S(1)}, u32[]{:S(2)}, u32[]{:S(2)}) collective-permute-start(bf16[272,256]{1,0:T(8,128)(2,1)S(1)} %gate.132.__2_), channel_id=1, source_target_pairs={{0,29},{1,28},{2,31},{3,30},{4,25},{5,24},{6,27},{7,26},{8,21},{9,... | collective-permute-start | bytes 417800 | tf_op jit(solution)/shard_map/ppermute | solution.py:260
  195.1 23.3 %collective-permute-start.73 = (bf16[272,256]{1,0:T(8,128)(2,1)S(1)}, bf16[272,256]{1,0:T(8,128)(2,1)S(1)}, u32[]{:S(2)}, u32[]{:S(2)}) collective-permute-start(bf16[272,256]{1,0:T(8,128)(2,1)S(1)} %gate.133.__2_), channel_id=1, source_target_pairs={{0,26},{1,27},{2,24},{3,25},{4,30},{5,31},{6,28},{7,29},{8,18},{9,... | collective-permute-start | bytes 417800 | tf_op jit(solution)/shard_map/ppermute | solution.py:260
  205.2 14.3 %collective-permute-start.75 = (bf16[272,256]{1,0:T(8,128)(2,1)S(1)}, bf16[272,256]{1,0:T(8,128)(2,1)S(1)}, u32[]{:S(2)}, u32[]{:S(2)}) collective-permute-start(bf16[272,256]{1,0:T(8,128)(2,1)S(1)} %gate.134.__2_), channel_id=1, source_target_pairs={{0,15},{1,14},{2,13},{3,12},{4,11},{5,10},{6,9},{7,8},{8,7},{9,6},... | collective-permute-start | bytes 417800 | tf_op jit(solution)/shard_map/ppermute | solution.py:260
  205.2 14.3 %collective-permute-start.77 = (bf16[272,256]{1,0:T(8,128)(2,1)S(1)}, bf16[272,256]{1,0:T(8,128)(2,1)S(1)}, u32[]{:S(2)}, u32[]{:S(2)}) collective-permute-start(bf16[272,256]{1,0:T(8,128)(2,1)S(1)} %gate.135.__2_), channel_id=1, source_target_pairs={{0,8},{1,9},{2,10},{3,11},{4,12},{5,13},{6,14},{7,15},{8,0},{9,1},... | collective-permute-start | bytes 417800 | tf_op jit(solution)/shard_map/ppermute | solution.py:260
  207.1 19.5 %collective-permute-start.70 = (bf16[272,256]{1,0:T(8,128)(2,1)S(1)}, bf16[272,256]{1,0:T(8,128)(2,1)S(1)}, u32[]{:S(2)}, u32[]{:S(2)}) collective-permute-start(bf16[272,256]{1,0:T(8,128)(2,1)S(1)} %gate.136.__2_), channel_id=1, source_target_pairs={{0,30},{1,31},{2,28},{3,29},{4,26},{5,27},{6,24},{7,25},{8,22},{9,... | collective-permute-start | bytes 417800 | tf_op jit(solution)/shard_map/ppermute | solution.py:260
  209.1 17.5 %collective-permute-start.72 = (bf16[272,256]{1,0:T(8,128)(2,1)S(1)}, bf16[272,256]{1,0:T(8,128)(2,1)S(1)}, u32[]{:S(2)}, u32[]{:S(2)}) collective-permute-start(bf16[272,256]{1,0:T(8,128)(2,1)S(1)} %gate.137.__2_), channel_id=1, source_target_pairs={{0,25},{1,24},{2,27},{3,26},{4,29},{5,28},{6,31},{7,30},{8,17},{9,... | collective-permute-start | bytes 417800 | tf_op jit(solution)/shard_map/ppermute | solution.py:260
  (36 other events, 334.9 us)

commit v5 on v4

--- a/solution.py
+++ b/solution.py
@@ -35,16 +35,15 @@
     return same.astype(F32).astype(BF16)
 
 
-def pack_kernel(order, at_ref, owner_ref, mask_ref, codes_ref, *outs):
+def pack_kernel(order, visits, at_ref, small_ref, codes_ref, *outs):
     messages, (pick_ref, pick_spare_ref, place_ref, place_spare_ref) = outs[:-4], outs[-4:]
     owners = len(messages)
-    visits, rows = owner_ref.shape
-    width = codes_ref.shape[1] // visits
-    blocks = mask_ref.shape[0] // visits
+    rows, width = codes_ref.shape[0], codes_ref.shape[1] // visits
+    blocks = small_ref.shape[0] // visits - 1
     block = width // blocks
     main = rows * visits // owners
     slots = owners * (main + SPARE)
-    apart = owner_ref[...] ^ at_ref[0]
+    apart = small_ref[:visits, :] ^ at_ref[0]
     relative = sum(jnp.where(apart == k, p, 0) for p, k in enumerate(order))
     eye = lax.broadcasted_iota(jnp.int32, (rows, rows), 0) == lax.broadcasted_iota(jnp.int32, (rows, rows), 1)
     lanes = [relative[g : g + 1, :] for g in range(visits)]
@@ -68,7 +67,7 @@
     pick_spare_ref[...] = pick_rows[:, owners * main :]
     place_ref[...] = place_rows[: owners * main, :]
     place_spare_ref[...] = place_rows[owners * main :, :]
-    live = mask_ref[...].astype(F32).T.astype(BF16)
+    live = small_ref[...].astype(F32).T.astype(BF16)[:, visits:]
     used = jnp.concatenate(
         [
             jnp.concatenate(
@@ -215,7 +214,7 @@
             out_ref[:, columns_of(q)] = total
         return _
 
-    lax.fori_loop(0, STACK, block, 0)
+    lax.fori_loop(0, STACK, block, 0, unroll=True)
     if last:
         for q in range(STACK):
             copy_of(q).wait()
@@ -251,7 +250,7 @@
     local = w_dec.shape[1]
     part = local // STACK
     position = jnp.stack([lax.axis_index("latent"), lax.axis_index("dp")])
-    order = [4, 3, 5, 2, 6, 1, 7, 0]
+    order = [4, 1, 5, 2, 6, 3, 7, 0]
 
     def move(x, j, k):
         if j == 0 and k == 0:
@@ -265,12 +264,13 @@
     def some(shape, dtype=BF16):
         return jax.ShapeDtypeStruct(shape, dtype)
 
+    small = jnp.concatenate([owner_ids.T, block_mask.transpose(1, 2, 0).reshape(-1, rows)], axis=0)
     packed = pl.pallas_call(
-        functools.partial(pack_kernel, order),
+        functools.partial(pack_kernel, order, visits),
         grid_spec=pltpu.PrefetchScalarGridSpec(
             num_scalar_prefetch=1,
             grid=(1,),
-            in_specs=[whole((visits, rows)), whole((visits * block_mask.shape[2], rows)), whole((rows, visits * width))],
+            in_specs=[whole(small.shape), whole((rows, visits * width))],
             out_specs=[whole((depth, width // STACK))] * owners
             + [whole((rows, owners * main)), whole((rows, owners * SPARE))]
             + [whole((owners * main, rows)), whole((owners * SPARE, rows))],
@@ -281,7 +281,7 @@
         compiler_params=params(12),
         cost_estimate=cost(2 * slots * rows * visits * width, 0),
         name="pack",
-    )(position, owner_ids.T, block_mask.transpose(1, 2, 0).reshape(-1, rows), latent_codes.reshape(rows, -1))
+    )(position, small, latent_codes.reshape(rows, -1))
     picks = packed[owners:]
     arrived = move_all(packed[:owners], 0)
     touched = pl.pallas_call(

time: 233 us -> 229 us (0.983)
  starting transfers between devices: 143 us -> 125 us
  waiting for transfers between devices: 51.5 us -> 66.9 us
    ppermute x78, starting transfers between devices: 143 us -> 125 us  [move(): return lax.ppermute(x, ('dp', 'latent'), pairs)]
    ppermute x78, waiting for transfers between devices: 51.5 us -> 66.9 us  [move(): return lax.ppermute(x, ('dp', 'latent'), pairs)]
    unnamed x13 -> x9, local copies, waits for them, and re-layouts: 4.73 us -> 3.35 us
  transfers between devices with their start and end apart: 78 -> 78, of which waited for: 19 -> 21; matrix products, arithmetic and copies ran while one was open for 0% -> 0% of each run, Pallas kernels for 11% -> 11%
where the time goes in v5:
time: 229 us; the launch traced here: 225 us
  starting transfers between devices  125 us (55%)
  waiting for transfers between devices  66.9 us (29%)
  Pallas kernels  28.3 us (12%)
  local copies, waits for them, and re-layouts  3.35 us (1%)
    ppermute x78, starting transfers between devices, move(): return lax.ppermute(x, ('dp', 'latent'), pairs)  125 us
    ppermute x78, waiting for transfers between devices, move(): return lax.ppermute(x, ('dp', 'latent'), pairs)  66.9 us
    pallas_call x4, Pallas kernels, combine(): pl.pallas_call(functools.partial(combine_kernel, owners), grid_spec=pltpu...  12.5 us
    pallas_call x2, Pallas kernels, gradient(): pl.pallas_call(functools.partial(gradient_kernel, counts, last), in_specs...  7.39 us
    pallas_call x4, Pallas kernels, decode(): pl.pallas_call(functools.partial(decode_kernel, owners, len(codes[j])), i...  5.82 us
  transfers between devices with their start and end apart: 78, of which 21 were waited for; matrix products, arithmetic and copies ran while one was open for 0% of the time, Pallas kernels for 11%

profile of v5, /device:TPU:0, one launch (start us, length us, event | category | flops | bytes accessed | tf_op | source)
XLA Modules:
  0.0 225.5 jit_solution(15417789589153294120)
XLA Ops:
  4.0 4.0 %collective-permute-start = (bf16[272,128]{1,0:T(8,128)(2,1)S(1)}, bf16[272,128]{1,0:T(8,128)(2,1)S(1)}, u32[]{:S(2)}, u32[]{:S(2)}) collective-permute-start(bf16[272,128]{1,0:T(8,128)(2,1)S(1)} %get-tuple-element.95), channel_id=1, source_target_pairs={{0,4},{1,5},{2,6},{3,7},{4,0},{5,1},{6,2},{7,3},{8,12},{9,13},{10,... | collective-permute-start | bytes 208904 | tf_op jit(solution)/shard_map/ppermute | solution.py:259
  11.4 2.5 %collective-permute-start.4 = (bf16[272,128]{1,0:T(8,128)(2,1)S(1)}, bf16[272,128]{1,0:T(8,128)(2,1)S(1)}, u32[]{:S(2)}, u32[]{:S(2)}) collective-permute-start(bf16[272,128]{1,0:T(8,128)(2,1)S(1)} %get-tuple-element.99), channel_id=1, source_target_pairs={{0,6},{1,7},{2,4},{3,5},{4,2},{5,3},{6,0},{7,1},{8,14},{9,15},{10,... | collective-permute-start | bytes 208904 | tf_op jit(solution)/shard_map/ppermute | solution.py:259
  15.5 2.7 %collective-permute-start.6 = (bf16[272,128]{1,0:T(8,128)(2,1)S(1)}, bf16[272,128]{1,0:T(8,128)(2,1)S(1)}, u32[]{:S(2)}, u32[]{:S(2)}) collective-permute-start(bf16[272,128]{1,0:T(8,128)(2,1)S(1)} %get-tuple-element.101), channel_id=1, source_target_pairs={{0,7},{1,6},{2,5},{3,4},{4,3},{5,2},{6,1},{7,0},{8,15},{9,14},{10,... | collective-permute-start | bytes 208904 | tf_op jit(solution)/shard_map/ppermute | solution.py:259
  18.3 2.2 copy-done
  20.5 2.0 collective-permute-done.6.refs_6_
  31.1 5.5 %collective-permute-done.11.__1_.rest_0_ = bf16[272,256]{1,0:T(8,128)(2,1)S(1)} collective-permute-done((bf16[272,256]{1,0:T(8,128)(2,1)S(1)}, bf16[272,256]{1,0:T(8,128)(2,1)S(1)}, u32[]{:S(2)}, u32[]{:S(2)}) %collective-permute-start.11) | collective-permute-done | bytes 139296 | tf_op jit(solution)/shard_map/ppermute | solution.py:259
  36.6 3.0 %collective-permute-start.16 = (bf16[272,256]{1,0:T(8,128)(2,1)S(1)}, bf16[272,256]{1,0:T(8,128)(2,1)S(1)}, u32[]{:S(2)}, u32[]{:S(2)}) collective-permute-start(bf16[272,256]{1,0:T(8,128)(2,1)S(1)} %gate.75.__2_), channel_id=1, source_target_pairs={{0,6},{1,7},{2,4},{3,5},{4,2},{5,3},{6,0},{7,1},{8,14},{9,15},{10,... | collective-permute-start | bytes 417800 | tf_op jit(solution)/shard_map/ppermute | solution.py:259
  42.1 2.9 %collective-permute-start.20 = (bf16[272,256]{1,0:T(8,128)(2,1)S(1)}, bf16[272,256]{1,0:T(8,128)(2,1)S(1)}, u32[]{:S(2)}, u32[]{:S(2)}) collective-permute-start(bf16[272,256]{1,0:T(8,128)(2,1)S(1)} %gate.78.__2_), channel_id=1, source_target_pairs={{0,7},{1,6},{2,5},{3,4},{4,3},{5,2},{6,1},{7,0},{8,15},{9,14},{10,... | collective-permute-start | bytes 417800 | tf_op jit(solution)/shard_map/ppermute | solution.py:259
  48.8 3.4 %collective-permute-start.17 = (bf16[272,256]{1,0:T(8,128)(2,1)S(1)}, bf16[272,256]{1,0:T(8,128)(2,1)S(1)}, u32[]{:S(2)}, u32[]{:S(2)}) collective-permute-start(bf16[272,256]{1,0:T(8,128)(2,1)S(1)} %gate.82.__2_), channel_id=1, source_target_pairs={{0,16},{1,17},{2,18},{3,19},{4,20},{5,21},{6,22},{7,23},{8,24},{9,... | collective-permute-start | bytes 417800 | tf_op jit(solution)/shard_map/ppermute | solution.py:259
  52.2 4.3 %collective-permute-start.24 = (bf16[272,256]{1,0:T(8,128)(2,1)S(1)}, bf16[272,256]{1,0:T(8,128)(2,1)S(1)}, u32[]{:S(2)}, u32[]{:S(2)}) collective-permute-start(bf16[272,256]{1,0:T(8,128)(2,1)S(1)} %gate.83.__2_), channel_id=1, source_target_pairs={{0,13},{1,12},{2,15},{3,14},{4,9},{5,8},{6,11},{7,10},{8,5},{9,4},... | collective-permute-start | bytes 417800 | tf_op jit(solution)/shard_map/ppermute | solution.py:259
  56.5 3.5 %collective-permute-start.22 = (bf16[272,256]{1,0:T(8,128)(2,1)S(1)}, bf16[272,256]{1,0:T(8,128)(2,1)S(1)}, u32[]{:S(2)}, u32[]{:S(2)}) collective-permute-start(bf16[272,256]{1,0:T(8,128)(2,1)S(1)} %gate.85.__2_), channel_id=1, source_target_pairs={{0,14},{1,15},{2,12},{3,13},{4,10},{5,11},{6,8},{7,9},{8,6},{9,7},... | collective-permute-start | bytes 417800 | tf_op jit(solution)/shard_map/ppermute | solution.py:259
  62.3 2.2 collective-permute-start.28
  64.8 4.1 %collective-permute-start.26 = (bf16[272,256]{1,0:T(8,128)(2,1)S(1)}, bf16[272,256]{1,0:T(8,128)(2,1)S(1)}, u32[]{:S(2)}, u32[]{:S(2)}) collective-permute-start(bf16[272,256]{1,0:T(8,128)(2,1)S(1)} %gate.89.__2_), channel_id=1, source_target_pairs={{0,15},{1,14},{2,13},{3,12},{4,11},{5,10},{6,9},{7,8},{8,7},{9,6},... | collective-permute-start | bytes 417800 | tf_op jit(solution)/shard_map/ppermute | solution.py:259
  69.4 2.6 %collective-permute-done.21.__1_.rest_5_ = bf16[272,256]{1,0:T(8,128)(2,1)S(1)} collective-permute-done((bf16[272,256]{1,0:T(8,128)(2,1)S(1)}, bf16[272,256]{1,0:T(8,128)(2,1)S(1)}, u32[]{:S(2)}, u32[]{:S(2)}) %collective-permute-start.21) | collective-permute-done | bytes 139296 | tf_op jit(solution)/shard_map/ppermute | solution.py:259
  73.0 7.9 %collective-permute-done.28.__1_.rest_0_ = bf16[272,256]{1,0:T(8,128)(2,1)S(1)} collective-permute-done((bf16[272,256]{1,0:T(8,128)(2,1)S(1)}, bf16[272,256]{1,0:T(8,128)(2,1)S(1)}, u32[]{:S(2)}, u32[]{:S(2)}) %collective-permute-start.28) | collective-permute-done | bytes 139296 | tf_op jit(solution)/shard_map/ppermute | solution.py:259
  80.9 3.9 %collective-permute-start.34 = (bf16[272,256]{1,0:T(8,128)(2,1)S(1)}, bf16[272,256]{1,0:T(8,128)(2,1)S(1)}, u32[]{:S(2)}, u32[]{:S(2)}) collective-permute-start(bf16[272,256]{1,0:T(8,128)(2,1)S(1)} %gate.93.__2_), channel_id=1, source_target_pairs={{0,18},{1,19},{2,16},{3,17},{4,22},{5,23},{6,20},{7,21},{8,26},{9,... | collective-permute-start | bytes 417800 | tf_op jit(solution)/shard_map/ppermute | solution.py:259
  86.4 3.1 %combine.4 = (bf16[128,8192]{1,0:T(8,128)(2,1)}, bf16[272,256]{1,0:T(8,128)(2,1)S(1)}, bf16[272,256]{1,0:T(8,128)(2,1)S(1)}, bf16[272,256]{1,0:T(8,128)(2,1)S(1)...) custom-call(s32[2]{0:T(128)S(1)} %pad_add_fusion.1.at_ref.place_in_r, ...), custom_call_target="tpu_custom_call" | custom-call | flops 285212672 | bytes 3276800 | tf_op jit(solution)/shard_map/combine/pallas_call | solution.py:320
  89.5 2.3 %collective-permute-start.38 = (bf16[272,256]{1,0:T(8,128)(2,1)S(1)}, bf16[272,256]{1,0:T(8,128)(2,1)S(1)}, u32[]{:S(2)}, u32[]{:S(2)}) collective-permute-start(bf16[272,256]{1,0:T(8,128)(2,1)S(1)} %gate.96.__2_), channel_id=1, source_target_pairs={{0,19},{1,18},{2,17},{3,16},{4,23},{5,22},{6,21},{7,20},{8,27},{9,... | collective-permute-start | bytes 417800 | tf_op jit(solution)/shard_map/ppermute | solution.py:259
  94.8 4.5 %collective-permute-done.38.__1_.rest_5_ = bf16[272,256]{1,0:T(8,128)(2,1)S(1)} collective-permute-done((bf16[272,256]{1,0:T(8,128)(2,1)S(1)}, bf16[272,256]{1,0:T(8,128)(2,1)S(1)}, u32[]{:S(2)}, u32[]{:S(2)}) %collective-permute-start.38) | collective-permute-done | bytes 139296 | tf_op jit(solution)/shard_map/ppermute | solution.py:259
  99.3 3.3 %collective-permute-start.40 = (bf16[272,256]{1,0:T(8,128)(2,1)S(1)}, bf16[272,256]{1,0:T(8,128)(2,1)S(1)}, u32[]{:S(2)}, u32[]{:S(2)}) collective-permute-start(bf16[272,256]{1,0:T(8,128)(2,1)S(1)} %gate.101.__2_), channel_id=1, source_target_pairs={{0,23},{1,22},{2,21},{3,20},{4,19},{5,18},{6,17},{7,16},{8,31},{9,... | collective-permute-start | bytes 417800 | tf_op jit(solution)/shard_map/ppermute | solution.py:259
  104.0 2.1 collective-permute-start.46
  110.7 6.0 %collective-permute-start.43 = (bf16[272,256]{1,0:T(8,128)(2,1)S(1)}, bf16[272,256]{1,0:T(8,128)(2,1)S(1)}, u32[]{:S(2)}, u32[]{:S(2)}) collective-permute-start(bf16[272,256]{1,0:T(8,128)(2,1)S(1)} %gate.107.__2_), channel_id=1, source_target_pairs={{0,29},{1,28},{2,31},{3,30},{4,25},{5,24},{6,27},{7,26},{8,21},{9,... | collective-permute-start | bytes 417800 | tf_op jit(solution)/shard_map/ppermute | solution.py:259
  118.1 2.3 %collective-permute-start.49 = (bf16[272,256]{1,0:T(8,128)(2,1)S(1)}, bf16[272,256]{1,0:T(8,128)(2,1)S(1)}, u32[]{:S(2)}, u32[]{:S(2)}) collective-permute-start(bf16[272,256]{1,0:T(8,128)(2,1)S(1)} %gate.109.__2_), channel_id=1, source_target_pairs={{0,6},{1,7},{2,4},{3,5},{4,2},{5,3},{6,0},{7,1},{8,14},{9,15},{10,... | collective-permute-start | bytes 417800 | tf_op jit(solution)/shard_map/ppermute | solution.py:259
  120.3 4.5 %collective-permute-done.39.__1_.rest_0_ = bf16[272,256]{1,0:T(8,128)(2,1)S(1)} collective-permute-done((bf16[272,256]{1,0:T(8,128)(2,1)S(1)}, bf16[272,256]{1,0:T(8,128)(2,1)S(1)}, u32[]{:S(2)}, u32[]{:S(2)}) %collective-permute-start.39) | collective-permute-done | bytes 139296 | tf_op jit(solution)/shard_map/ppermute | solution.py:259
  125.2 3.9 %collective-permute-done.43.__1_.rest_2_ = bf16[272,256]{1,0:T(8,128)(2,1)S(1)} collective-permute-done((bf16[272,256]{1,0:T(8,128)(2,1)S(1)}, bf16[272,256]{1,0:T(8,128)(2,1)S(1)}, u32[]{:S(2)}, u32[]{:S(2)}) %collective-permute-start.43) | collective-permute-done | bytes 139296 | tf_op jit(solution)/shard_map/ppermute | solution.py:259
  129.8 2.5 %collective-permute-done.45.__1_.rest_3_ = bf16[272,256]{1,0:T(8,128)(2,1)S(1)} collective-permute-done((bf16[272,256]{1,0:T(8,128)(2,1)S(1)}, bf16[272,256]{1,0:T(8,128)(2,1)S(1)}, u32[]{:S(2)}, u32[]{:S(2)}) %collective-permute-start.45) | collective-permute-done | bytes 139296 | tf_op jit(solution)/shard_map/ppermute | solution.py:259
  132.2 5.1 %collective-permute-start.54 = (bf16[272,256]{1,0:T(8,128)(2,1)S(1)}, bf16[272,256]{1,0:T(8,128)(2,1)S(1)}, u32[]{:S(2)}, u32[]{:S(2)}) collective-permute-start(bf16[272,256]{1,0:T(8,128)(2,1)S(1)} %gate.113.__2_), channel_id=1, source_target_pairs={{0,7},{1,6},{2,5},{3,4},{4,3},{5,2},{6,1},{7,0},{8,15},{9,14},{10,... | collective-permute-start | bytes 417800 | tf_op jit(solution)/shard_map/ppermute | solution.py:259
  137.3 2.3 %collective-permute-done.51.__1_.refs_5_ = bf16[272,256]{1,0:T(8,128)(2,1)S(1)} collective-permute-done((bf16[272,256]{1,0:T(8,128)(2,1)S(1)}, bf16[272,256]{1,0:T(8,128)(2,1)S(1)}, u32[]{:S(2)}, u32[]{:S(2)}) %collective-permute-start.51) | collective-permute-done | bytes 139296 | tf_op jit(solution)/shard_map/ppermute | solution.py:259
  139.6 3.1 %combine.5 = (bf16[128,8192]{1,0:T(8,128)(2,1)}, bf16[272,256]{1,0:T(8,128)(2,1)S(1)}, bf16[272,256]{1,0:T(8,128)(2,1)S(1)}, bf16[272,256]{1,0:T(8,128)(2,1)S(1)...) custom-call(s32[2]{0:T(128)S(1)} %pad_add_fusion.1.at_ref.place_in_r, ...), custom_call_target="tpu_custom_call", output_to_operand_aliasing={{0}: (15, {})} | custom-call | flops 285212672 | bytes 3276800 | tf_op jit(solution)/shard_map/combine/pallas_call | solution.py:320
  142.7 3.2 %combine.6 = (bf16[128,8192]{1,0:T(8,128)(2,1)}, bf16[272,256]{1,0:T(8,128)(2,1)S(1)}, bf16[272,256]{1,0:T(8,128)(2,1)S(1)}, bf16[272,256]{1,0:T(8,128)(2,1)S(1)...) custom-call(s32[2]{0:T(128)S(1)} %pad_add_fusion.1.at_ref.place_in_r, ...), custom_call_target="tpu_custom_call", output_to_operand_aliasing={{0}: (15, {})} | custom-call | flops 285212672 | bytes 3276800 | tf_op jit(solution)/shard_map/combine/pallas_call | solution.py:320
  146.0 3.7 %collective-permute-start.59 = (bf16[272,256]{1,0:T(8,128)(2,1)S(1)}, bf16[272,256]{1,0:T(8,128)(2,1)S(1)}, u32[]{:S(2)}, u32[]{:S(2)}) collective-permute-start(bf16[272,256]{1,0:T(8,128)(2,1)S(1)} %gate.117.__2_), channel_id=1, source_target_pairs={{0,17},{1,16},{2,19},{3,18},{4,21},{5,20},{6,23},{7,22},{8,25},{9,... | collective-permute-start | bytes 417800 | tf_op jit(solution)/shard_map/ppermute | solution.py:259
  152.3 5.3 %collective-permute-start.56 = (bf16[272,256]{1,0:T(8,128)(2,1)S(1)}, bf16[272,256]{1,0:T(8,128)(2,1)S(1)}, u32[]{:S(2)}, u32[]{:S(2)}) collective-permute-start(bf16[272,256]{1,0:T(8,128)(2,1)S(1)} %gate.120.__2_), channel_id=1, source_target_pairs={{0,21},{1,20},{2,23},{3,22},{4,17},{5,16},{6,19},{7,18},{8,29},{9,... | collective-permute-start | bytes 417800 | tf_op jit(solution)/shard_map/ppermute | solution.py:259
  157.6 3.2 %collective-permute-done.53.__1_.refs_8_ = bf16[272,256]{1,0:T(8,128)(2,1)S(1)} collective-permute-done((bf16[272,256]{1,0:T(8,128)(2,1)S(1)}, bf16[272,256]{1,0:T(8,128)(2,1)S(1)}, u32[]{:S(2)}, u32[]{:S(2)}) %collective-permute-start.53) | collective-permute-done | bytes 139296 | tf_op jit(solution)/shard_map/ppermute | solution.py:259
  161.4 4.8 %collective-permute-start.64 = (bf16[272,256]{1,0:T(8,128)(2,1)S(1)}, bf16[272,256]{1,0:T(8,128)(2,1)S(1)}, u32[]{:S(2)}, u32[]{:S(2)}) collective-permute-start(bf16[272,256]{1,0:T(8,128)(2,1)S(1)} %gate.122.__2_), channel_id=1, source_target_pairs={{0,22},{1,23},{2,20},{3,21},{4,18},{5,19},{6,16},{7,17},{8,30},{9,... | collective-permute-start | bytes 417800 | tf_op jit(solution)/shard_map/ppermute | solution.py:259
  166.1 2.5 %collective-permute-start.63 = (bf16[272,256]{1,0:T(8,128)(2,1)S(1)}, bf16[272,256]{1,0:T(8,128)(2,1)S(1)}, u32[]{:S(2)}, u32[]{:S(2)}) collective-permute-start(bf16[272,256]{1,0:T(8,128)(2,1)S(1)} %gate.123.__2_), channel_id=1, source_target_pairs={{0,19},{1,18},{2,17},{3,16},{4,23},{5,22},{6,21},{7,20},{8,27},{9,... | collective-permute-start | bytes 417800 | tf_op jit(solution)/shard_map/ppermute | solution.py:259
  168.7 4.5 %collective-permute-done.56.__1_.refs_10_ = bf16[272,256]{1,0:T(8,128)(2,1)S(1)} collective-permute-done((bf16[272,256]{1,0:T(8,128)(2,1)S(1)}, bf16[272,256]{1,0:T(8,128)(2,1)S(1)}, u32[]{:S(2)}, u32[]{:S(2)}) %collective-permute-start.56) | collective-permute-done | bytes 139296 | tf_op jit(solution)/shard_map/ppermute | solution.py:259
  173.2 3.1 %combine.7 = (bf16[128,8192]{1,0:T(8,128)(2,1)}, bf16[272,256]{1,0:T(8,128)(2,1)S(1)}, bf16[272,256]{1,0:T(8,128)(2,1)S(1)}, bf16[272,256]{1,0:T(8,128)(2,1)S(1)...) custom-call(s32[2]{0:T(128)S(1)} %pad_add_fusion.1.at_ref.place_in_r, ...), custom_call_target="tpu_custom_call", output_to_operand_aliasing={{0}: (15, {})} | custom-call | flops 285212672 | bytes 3276800 | tf_op jit(solution)/shard_map/combine/pallas_call | solution.py:320
  176.2 3.6 %collective-permute-start.60 = (bf16[272,256]{1,0:T(8,128)(2,1)S(1)}, bf16[272,256]{1,0:T(8,128)(2,1)S(1)}, u32[]{:S(2)}, u32[]{:S(2)}) collective-permute-start(bf16[272,256]{1,0:T(8,128)(2,1)S(1)} %gate.126.__2_), channel_id=1, source_target_pairs={{0,23},{1,22},{2,21},{3,20},{4,19},{5,18},{6,17},{7,16},{8,31},{9,... | collective-permute-start | bytes 417800 | tf_op jit(solution)/shard_map/ppermute | solution.py:259
  180.3 2.5 %collective-permute-done.62.__1_.refs_18_ = bf16[272,256]{1,0:T(8,128)(2,1)S(1)} collective-permute-done((bf16[272,256]{1,0:T(8,128)(2,1)S(1)}, bf16[272,256]{1,0:T(8,128)(2,1)S(1)}, u32[]{:S(2)}, u32[]{:S(2)}) %collective-permute-start.62) | collective-permute-done | bytes 139296 | tf_op jit(solution)/shard_map/ppermute | solution.py:259
  182.8 5.7 %collective-permute-done.61.__1_.refs_19_ = bf16[272,256]{1,0:T(8,128)(2,1)S(1)} collective-permute-done((bf16[272,256]{1,0:T(8,128)(2,1)S(1)}, bf16[272,256]{1,0:T(8,128)(2,1)S(1)}, u32[]{:S(2)}, u32[]{:S(2)}) %collective-permute-start.61) | collective-permute-done | bytes 139296 | tf_op jit(solution)/shard_map/ppermute | solution.py:259
  188.5 3.3 %collective-permute-start.65 = (bf16[272,256]{1,0:T(8,128)(2,1)S(1)}, bf16[272,256]{1,0:T(8,128)(2,1)S(1)}, u32[]{:S(2)}, u32[]{:S(2)}) collective-permute-start(bf16[272,256]{1,0:T(8,128)(2,1)S(1)} %gate.131.__2_), channel_id=1, source_target_pairs={{0,25},{1,24},{2,27},{3,26},{4,29},{5,28},{6,31},{7,30},{8,17},{9,... | collective-permute-start | bytes 417800 | tf_op jit(solution)/shard_map/ppermute | solution.py:259
  191.7 4.6 %collective-permute-start.71 = (bf16[272,256]{1,0:T(8,128)(2,1)S(1)}, bf16[272,256]{1,0:T(8,128)(2,1)S(1)}, u32[]{:S(2)}, u32[]{:S(2)}) collective-permute-start(bf16[272,256]{1,0:T(8,128)(2,1)S(1)} %gate.132.__2_), channel_id=1, source_target_pairs={{0,29},{1,28},{2,31},{3,30},{4,25},{5,24},{6,27},{7,26},{8,21},{9,... | collective-permute-start | bytes 417800 | tf_op jit(solution)/shard_map/ppermute | solution.py:259
  200.7 3.1 %collective-permute-start.70 = (bf16[272,256]{1,0:T(8,128)(2,1)S(1)}, bf16[272,256]{1,0:T(8,128)(2,1)S(1)}, u32[]{:S(2)}, u32[]{:S(2)}) collective-permute-start(bf16[272,256]{1,0:T(8,128)(2,1)S(1)} %gate.136.__2_), channel_id=1, source_target_pairs={{0,30},{1,31},{2,28},{3,29},{4,26},{5,27},{6,24},{7,25},{8,22},{9,... | collective-permute-start | bytes 417800 | tf_op jit(solution)/shard_map/ppermute | solution.py:259
  203.8 6.3 %collective-permute-done.71.__1_.refs_26_ = bf16[272,256]{1,0:T(8,128)(2,1)S(1)} collective-permute-done((bf16[272,256]{1,0:T(8,128)(2,1)S(1)}, bf16[272,256]{1,0:T(8,128)(2,1)S(1)}, u32[]{:S(2)}, u32[]{:S(2)}) %collective-permute-start.71) | collective-permute-done | bytes 139296 | tf_op jit(solution)/shard_map/ppermute | solution.py:259
  210.1 4.7 %collective-permute-start.74 = (bf16[272,256]{1,0:T(8,128)(2,1)S(1)}, bf16[272,256]{1,0:T(8,128)(2,1)S(1)}, u32[]{:S(2)}, u32[]{:S(2)}) collective-permute-start(bf16[272,256]{1,0:T(8,128)(2,1)S(1)} %gate.138.__2_), channel_id=1, source_target_pairs={{0,31},{1,30},{2,29},{3,28},{4,27},{5,26},{6,25},{7,24},{8,23},{9,... | collective-permute-start | bytes 417800 | tf_op jit(solution)/shard_map/ppermute | solution.py:259
  214.8 4.6 %gradient.2.refs_4_ = f32[1024,2048]{1,0:T(8,128)S(1)} custom-call(bf16[1024,952]{1,0:T(8,128)(2,1)S(1)} %turn.3.codes_ref, bf16[272,256]{1,0:T(8,128)(2,1)S(1)} %collective-permute-done.37.__1_.refs_0_, bf16[272,256]{1,0:T(8,128)(2,1)S(1)} %collective-permute-done.36.__1_.refs_1_, bf16[272,256]{1,0:T(8,128)(2,1)S(1)} %collective-permute-done.44.__1_.refs_2_, ...), custom_call_target="tpu_custom_call" | custom-call | flops 3992977408 | bytes 8388608 | tf_op jit(solution)/shard_map/gradient/pallas_call | solution.py:355
  219.4 2.2 collective-permute-done.74.refs_2_
  222.5 2.8 %gradient.3 = bf16[1024,2048]{1,0:T(8,128)(2,1)} custom-call(bf16[1024,136]{1,0:T(8,128)(2,1)S(1)} %turn.2.codes_ref, bf16[272,256]{1,0:T(8,128)(2,1)S(1)} %collective-permute-done.70.refs_0_, bf16[272,256]{1,0:T(8,128)(2,1)S(1)} %collective-permute-done.72.refs_1_, bf16[272,256]{1,0:T(8,128)(2,1)S(1)} %collective-permute-done.74.refs_2_, ...), custom_call_target="tpu_custom_call" | custom-call | flops 570425344 | bytes 8388608 | tf_op jit(solution)/shard_map/gradient/pallas_call | solution.py:355
  (204 shorter events, 49.2 us)
Async XLA Ops:
  24.3 12.3 %collective-permute-start.11 = (bf16[272,256]{1,0:T(8,128)(2,1)S(1)}, bf16[272,256]{1,0:T(8,128)(2,1)S(1)}, u32[]{:S(2)}, u32[]{:S(2)}) collective-permute-start(bf16[272,256]{1,0:T(8,128)(2,1)S(1)} %gate.70.__1_), channel_id=1, source_target_pairs={{0,4},{1,5},{2,6},{3,7},{4,0},{5,1},{6,2},{7,3},{8,12},{9,13},{10,... | collective-permute-start | bytes 417800 | tf_op jit(solution)/shard_map/ppermute | solution.py:259
  26.1 13.5 %collective-permute-start.10 = (bf16[272,256]{1,0:T(8,128)(2,1)S(1)}, bf16[272,256]{1,0:T(8,128)(2,1)S(1)}, u32[]{:S(2)}, u32[]{:S(2)}) collective-permute-start(bf16[272,256]{1,0:T(8,128)(2,1)S(1)} %gate.71.__1_), channel_id=1, source_target_pairs={{0,1},{1,0},{2,3},{3,2},{4,5},{5,4},{6,7},{7,6},{8,9},{9,8},{10,11... | collective-permute-start | bytes 417800 | tf_op jit(solution)/shard_map/ppermute | solution.py:259
  27.2 13.5 %collective-permute-start.9 = (bf16[272,256]{1,0:T(8,128)(2,1)S(1)}, bf16[272,256]{1,0:T(8,128)(2,1)S(1)}, u32[]{:S(2)}, u32[]{:S(2)}) collective-permute-start(bf16[272,256]{1,0:T(8,128)(2,1)S(1)} %gate.72.__1_), channel_id=1, source_target_pairs={{0,5},{1,4},{2,7},{3,6},{4,1},{5,0},{6,3},{7,2},{8,13},{9,12},{10,... | collective-permute-start | bytes 417800 | tf_op jit(solution)/shard_map/ppermute | solution.py:259
  28.8 13.3 %collective-permute-start.13 = (bf16[272,256]{1,0:T(8,128)(2,1)S(1)}, bf16[272,256]{1,0:T(8,128)(2,1)S(1)}, u32[]{:S(2)}, u32[]{:S(2)}) collective-permute-start(bf16[272,256]{1,0:T(8,128)(2,1)S(1)} %gate.73.__2_), channel_id=1, source_target_pairs={{0,2},{1,3},{2,0},{3,1},{4,6},{5,7},{6,4},{7,5},{8,10},{9,11},{10,... | collective-permute-start | bytes 417800 | tf_op jit(solution)/shard_map/ppermute | solution.py:259
  29.7 16.8 %collective-permute-start.8 = (bf16[272,256]{1,0:T(8,128)(2,1)S(1)}, bf16[272,256]{1,0:T(8,128)(2,1)S(1)}, u32[]{:S(2)}, u32[]{:S(2)}) collective-permute-start(bf16[272,256]{1,0:T(8,128)(2,1)S(1)} %gate.74.__2_), channel_id=1, source_target_pairs={{0,16},{1,17},{2,18},{3,19},{4,20},{5,21},{6,22},{7,23},{8,24},{9,... | collective-permute-start | bytes 417800 | tf_op jit(solution)/shard_map/ppermute | solution.py:259
  48.8 12.0 %collective-permute-start.17 = (bf16[272,256]{1,0:T(8,128)(2,1)S(1)}, bf16[272,256]{1,0:T(8,128)(2,1)S(1)}, u32[]{:S(2)}, u32[]{:S(2)}) collective-permute-start(bf16[272,256]{1,0:T(8,128)(2,1)S(1)} %gate.82.__2_), channel_id=1, source_target_pairs={{0,16},{1,17},{2,18},{3,19},{4,20},{5,21},{6,22},{7,23},{8,24},{9,... | collective-permute-start | bytes 417800 | tf_op jit(solution)/shard_map/ppermute | solution.py:259
  52.2 12.3 %collective-permute-start.24 = (bf16[272,256]{1,0:T(8,128)(2,1)S(1)}, bf16[272,256]{1,0:T(8,128)(2,1)S(1)}, u32[]{:S(2)}, u32[]{:S(2)}) collective-permute-start(bf16[272,256]{1,0:T(8,128)(2,1)S(1)} %gate.83.__2_), channel_id=1, source_target_pairs={{0,13},{1,12},{2,15},{3,14},{4,9},{5,8},{6,11},{7,10},{8,5},{9,4},... | collective-permute-start | bytes 417800 | tf_op jit(solution)/shard_map/ppermute | solution.py:259
  56.5 12.8 %collective-permute-start.22 = (bf16[272,256]{1,0:T(8,128)(2,1)S(1)}, bf16[272,256]{1,0:T(8,128)(2,1)S(1)}, u32[]{:S(2)}, u32[]{:S(2)}) collective-permute-start(bf16[272,256]{1,0:T(8,128)(2,1)S(1)} %gate.85.__2_), channel_id=1, source_target_pairs={{0,14},{1,15},{2,12},{3,13},{4,10},{5,11},{6,8},{7,9},{8,6},{9,7},... | collective-permute-start | bytes 417800 | tf_op jit(solution)/shard_map/ppermute | solution.py:259
  60.1 11.9 %collective-permute-start.21 = (bf16[272,256]{1,0:T(8,128)(2,1)S(1)}, bf16[272,256]{1,0:T(8,128)(2,1)S(1)}, u32[]{:S(2)}, u32[]{:S(2)}) collective-permute-start(bf16[272,256]{1,0:T(8,128)(2,1)S(1)} %gate.86.__2_), channel_id=1, source_target_pairs={{0,11},{1,10},{2,9},{3,8},{4,15},{5,14},{6,13},{7,12},{8,3},{9,2},... | collective-permute-start | bytes 417800 | tf_op jit(solution)/shard_map/ppermute | solution.py:259
  62.3 18.6 %collective-permute-start.28 = (bf16[272,256]{1,0:T(8,128)(2,1)S(1)}, bf16[272,256]{1,0:T(8,128)(2,1)S(1)}, u32[]{:S(2)}, u32[]{:S(2)}) collective-permute-start(bf16[272,256]{1,0:T(8,128)(2,1)S(1)} %gate.87.__2_), channel_id=1, source_target_pairs={{0,20},{1,21},{2,22},{3,23},{4,16},{5,17},{6,18},{7,19},{8,28},{9,... | collective-permute-start | bytes 417800 | tf_op jit(solution)/shard_map/ppermute | solution.py:259
  64.5 16.4 %collective-permute-start.27 = (bf16[272,256]{1,0:T(8,128)(2,1)S(1)}, bf16[272,256]{1,0:T(8,128)(2,1)S(1)}, u32[]{:S(2)}, u32[]{:S(2)}) collective-permute-start(bf16[272,256]{1,0:T(8,128)(2,1)S(1)} %gate.88.__2_), channel_id=1, source_target_pairs={{0,17},{1,16},{2,19},{3,18},{4,21},{5,20},{6,23},{7,22},{8,25},{9,... | collective-permute-start | bytes 417800 | tf_op jit(solution)/shard_map/ppermute | solution.py:259
  64.8 19.9 %collective-permute-start.26 = (bf16[272,256]{1,0:T(8,128)(2,1)S(1)}, bf16[272,256]{1,0:T(8,128)(2,1)S(1)}, u32[]{:S(2)}, u32[]{:S(2)}) collective-permute-start(bf16[272,256]{1,0:T(8,128)(2,1)S(1)} %gate.89.__2_), channel_id=1, source_target_pairs={{0,15},{1,14},{2,13},{3,12},{4,11},{5,10},{6,9},{7,8},{8,7},{9,6},... | collective-permute-start | bytes 417800 | tf_op jit(solution)/shard_map/ppermute | solution.py:259
  69.3 15.5 %collective-permute-start.31 = (bf16[272,256]{1,0:T(8,128)(2,1)S(1)}, bf16[272,256]{1,0:T(8,128)(2,1)S(1)}, u32[]{:S(2)}, u32[]{:S(2)}) collective-permute-start(bf16[272,256]{1,0:T(8,128)(2,1)S(1)} %gate.90.__2_), channel_id=1, source_target_pairs={{0,8},{1,9},{2,10},{3,11},{4,12},{5,13},{6,14},{7,15},{8,0},{9,1},... | collective-permute-start | bytes 417800 | tf_op jit(solution)/shard_map/ppermute | solution.py:259
  72.0 17.5 %collective-permute-start.25 = (bf16[272,256]{1,0:T(8,128)(2,1)S(1)}, bf16[272,256]{1,0:T(8,128)(2,1)S(1)}, u32[]{:S(2)}, u32[]{:S(2)}) collective-permute-start(bf16[272,256]{1,0:T(8,128)(2,1)S(1)} %gate.91.__2_), channel_id=1, source_target_pairs={{0,8},{1,9},{2,10},{3,11},{4,12},{5,13},{6,14},{7,15},{8,0},{9,1},... | collective-permute-start | bytes 417800 | tf_op jit(solution)/shard_map/ppermute | solution.py:259
  102.6 15.4 %collective-permute-start.44 = (bf16[272,256]{1,0:T(8,128)(2,1)S(1)}, bf16[272,256]{1,0:T(8,128)(2,1)S(1)}, u32[]{:S(2)}, u32[]{:S(2)}) collective-permute-start(bf16[272,256]{1,0:T(8,128)(2,1)S(1)} %gate.103.__2_), channel_id=1, source_target_pairs={{0,5},{1,4},{2,7},{3,6},{4,1},{5,0},{6,3},{7,2},{8,13},{9,12},{10,... | collective-permute-start | bytes 417800 | tf_op jit(solution)/shard_map/ppermute | solution.py:259
  104.0 14.1 %collective-permute-start.46 = (bf16[272,256]{1,0:T(8,128)(2,1)S(1)}, bf16[272,256]{1,0:T(8,128)(2,1)S(1)}, u32[]{:S(2)}, u32[]{:S(2)}) collective-permute-start(bf16[272,256]{1,0:T(8,128)(2,1)S(1)} %gate.104.__2_), channel_id=1, source_target_pairs={{0,2},{1,3},{2,0},{3,1},{4,6},{5,7},{6,4},{7,5},{8,10},{9,11},{10,... | collective-permute-start | bytes 417800 | tf_op jit(solution)/shard_map/ppermute | solution.py:259
  107.5 17.3 %collective-permute-start.39 = (bf16[272,256]{1,0:T(8,128)(2,1)S(1)}, bf16[272,256]{1,0:T(8,128)(2,1)S(1)}, u32[]{:S(2)}, u32[]{:S(2)}) collective-permute-start(bf16[272,256]{1,0:T(8,128)(2,1)S(1)} %gate.105.__2_), channel_id=1, source_target_pairs={{0,28},{1,29},{2,30},{3,31},{4,24},{5,25},{6,26},{7,27},{8,20},{9,... | collective-permute-start | bytes 417800 | tf_op jit(solution)/shard_map/ppermute | solution.py:259
  109.5 15.4 %collective-permute-start.41 = (bf16[272,256]{1,0:T(8,128)(2,1)S(1)}, bf16[272,256]{1,0:T(8,128)(2,1)S(1)}, u32[]{:S(2)}, u32[]{:S(2)}) collective-permute-start(bf16[272,256]{1,0:T(8,128)(2,1)S(1)} %gate.106.__2_), channel_id=1, source_target_pairs={{0,25},{1,24},{2,27},{3,26},{4,29},{5,28},{6,31},{7,30},{8,17},{9,... | collective-permute-start | bytes 417800 | tf_op jit(solution)/shard_map/ppermute | solution.py:259
  110.7 18.4 %collective-permute-start.43 = (bf16[272,256]{1,0:T(8,128)(2,1)S(1)}, bf16[272,256]{1,0:T(8,128)(2,1)S(1)}, u32[]{:S(2)}, u32[]{:S(2)}) collective-permute-start(bf16[272,256]{1,0:T(8,128)(2,1)S(1)} %gate.107.__2_), channel_id=1, source_target_pairs={{0,29},{1,28},{2,31},{3,30},{4,25},{5,24},{6,27},{7,26},{8,21},{9,... | collective-permute-start | bytes 417800 | tf_op jit(solution)/shard_map/ppermute | solution.py:259
  118.0 14.2 %collective-permute-start.45 = (bf16[272,256]{1,0:T(8,128)(2,1)S(1)}, bf16[272,256]{1,0:T(8,128)(2,1)S(1)}, u32[]{:S(2)}, u32[]{:S(2)}) collective-permute-start(bf16[272,256]{1,0:T(8,128)(2,1)S(1)} %gate.108.__2_), channel_id=1, source_target_pairs={{0,26},{1,27},{2,24},{3,25},{4,30},{5,31},{6,28},{7,29},{8,18},{9,... | collective-permute-start | bytes 417800 | tf_op jit(solution)/shard_map/ppermute | solution.py:259
  118.1 19.3 %collective-permute-start.49 = (bf16[272,256]{1,0:T(8,128)(2,1)S(1)}, bf16[272,256]{1,0:T(8,128)(2,1)S(1)}, u32[]{:S(2)}, u32[]{:S(2)}) collective-permute-start(bf16[272,256]{1,0:T(8,128)(2,1)S(1)} %gate.109.__2_), channel_id=1, source_target_pairs={{0,6},{1,7},{2,4},{3,5},{4,2},{5,3},{6,0},{7,1},{8,14},{9,15},{10,... | collective-permute-start | bytes 417800 | tf_op jit(solution)/shard_map/ppermute | solution.py:259
  124.8 14.8 %collective-permute-start.51 = (bf16[272,256]{1,0:T(8,128)(2,1)S(1)}, bf16[272,256]{1,0:T(8,128)(2,1)S(1)}, u32[]{:S(2)}, u32[]{:S(2)}) collective-permute-start(bf16[272,256]{1,0:T(8,128)(2,1)S(1)} %gate.110.__2_), channel_id=1, source_target_pairs={{0,3},{1,2},{2,1},{3,0},{4,7},{5,6},{6,5},{7,4},{8,11},{9,10},{10,... | collective-permute-start | bytes 417800 | tf_op jit(solution)/shard_map/ppermute | solution.py:259
  124.8 21.1 %collective-permute-start.47 = (bf16[272,256]{1,0:T(8,128)(2,1)S(1)}, bf16[272,256]{1,0:T(8,128)(2,1)S(1)}, u32[]{:S(2)}, u32[]{:S(2)}) collective-permute-start(bf16[272,256]{1,0:T(8,128)(2,1)S(1)} %gate.111.__2_), channel_id=1, source_target_pairs={{0,30},{1,31},{2,28},{3,29},{4,26},{5,27},{6,24},{7,25},{8,22},{9,... | collective-permute-start | bytes 417800 | tf_op jit(solution)/shard_map/ppermute | solution.py:259
  129.1 16.9 %collective-permute-start.48 = (bf16[272,256]{1,0:T(8,128)(2,1)S(1)}, bf16[272,256]{1,0:T(8,128)(2,1)S(1)}, u32[]{:S(2)}, u32[]{:S(2)}) collective-permute-start(bf16[272,256]{1,0:T(8,128)(2,1)S(1)} %gate.112.__2_), channel_id=1, source_target_pairs={{0,27},{1,26},{2,25},{3,24},{4,31},{5,30},{6,29},{7,28},{8,19},{9,... | collective-permute-start | bytes 417800 | tf_op jit(solution)/shard_map/ppermute | solution.py:259
  132.2 17.4 %collective-permute-start.54 = (bf16[272,256]{1,0:T(8,128)(2,1)S(1)}, bf16[272,256]{1,0:T(8,128)(2,1)S(1)}, u32[]{:S(2)}, u32[]{:S(2)}) collective-permute-start(bf16[272,256]{1,0:T(8,128)(2,1)S(1)} %gate.113.__2_), channel_id=1, source_target_pairs={{0,7},{1,6},{2,5},{3,4},{4,3},{5,2},{6,1},{7,0},{8,15},{9,14},{10,... | collective-permute-start | bytes 417800 | tf_op jit(solution)/shard_map/ppermute | solution.py:259
  137.3 14.1 %collective-permute-start.50 = (bf16[272,256]{1,0:T(8,128)(2,1)S(1)}, bf16[272,256]{1,0:T(8,128)(2,1)S(1)}, u32[]{:S(2)}, u32[]{:S(2)}) collective-permute-start(bf16[272,256]{1,0:T(8,128)(2,1)S(1)} %gate.114.__2_), channel_id=1, source_target_pairs={{0,31},{1,30},{2,29},{3,28},{4,27},{5,26},{6,25},{7,24},{8,23},{9,... | collective-permute-start | bytes 417800 | tf_op jit(solution)/shard_map/ppermute | solution.py:259
  139.6 12.7 %collective-permute-start.52 = (bf16[272,256]{1,0:T(8,128)(2,1)S(1)}, bf16[272,256]{1,0:T(8,128)(2,1)S(1)}, u32[]{:S(2)}, u32[]{:S(2)}) collective-permute-start(bf16[272,256]{1,0:T(8,128)(2,1)S(1)} %gate.115.__2_), channel_id=1, source_target_pairs={{0,24},{1,25},{2,26},{3,27},{4,28},{5,29},{6,30},{7,31},{8,16},{9,... | collective-permute-start | bytes 417800 | tf_op jit(solution)/shard_map/ppermute | solution.py:259
  146.0 14.9 %collective-permute-start.53 = (bf16[272,256]{1,0:T(8,128)(2,1)S(1)}, bf16[272,256]{1,0:T(8,128)(2,1)S(1)}, u32[]{:S(2)}, u32[]{:S(2)}) collective-permute-start(bf16[272,256]{1,0:T(8,128)(2,1)S(1)} %gate.116.__2_), channel_id=1, source_target_pairs={{0,20},{1,21},{2,22},{3,23},{4,16},{5,17},{6,18},{7,19},{8,28},{9,... | collective-permute-start | bytes 417800 | tf_op jit(solution)/shard_map/ppermute | solution.py:259
  146.0 15.4 %collective-permute-start.59 = (bf16[272,256]{1,0:T(8,128)(2,1)S(1)}, bf16[272,256]{1,0:T(8,128)(2,1)S(1)}, u32[]{:S(2)}, u32[]{:S(2)}) collective-permute-start(bf16[272,256]{1,0:T(8,128)(2,1)S(1)} %gate.117.__2_), channel_id=1, source_target_pairs={{0,17},{1,16},{2,19},{3,18},{4,21},{5,20},{6,23},{7,22},{8,25},{9,... | collective-permute-start | bytes 417800 | tf_op jit(solution)/shard_map/ppermute | solution.py:259
  149.6 16.5 %collective-permute-start.58 = (bf16[272,256]{1,0:T(8,128)(2,1)S(1)}, bf16[272,256]{1,0:T(8,128)(2,1)S(1)}, u32[]{:S(2)}, u32[]{:S(2)}) collective-permute-start(bf16[272,256]{1,0:T(8,128)(2,1)S(1)} %gate.118.__2_), channel_id=1, source_target_pairs={{0,12},{1,13},{2,14},{3,15},{4,8},{5,9},{6,10},{7,11},{8,4},{9,5},... | collective-permute-start | bytes 417800 | tf_op jit(solution)/shard_map/ppermute | solution.py:259
  151.4 17.3 %collective-permute-start.57 = (bf16[272,256]{1,0:T(8,128)(2,1)S(1)}, bf16[272,256]{1,0:T(8,128)(2,1)S(1)}, u32[]{:S(2)}, u32[]{:S(2)}) collective-permute-start(bf16[272,256]{1,0:T(8,128)(2,1)S(1)} %gate.119.__2_), channel_id=1, source_target_pairs={{0,9},{1,8},{2,11},{3,10},{4,13},{5,12},{6,15},{7,14},{8,1},{9,0},... | collective-permute-start | bytes 417800 | tf_op jit(solution)/shard_map/ppermute | solution.py:259
  152.3 20.9 %collective-permute-start.56 = (bf16[272,256]{1,0:T(8,128)(2,1)S(1)}, bf16[272,256]{1,0:T(8,128)(2,1)S(1)}, u32[]{:S(2)}, u32[]{:S(2)}) collective-permute-start(bf16[272,256]{1,0:T(8,128)(2,1)S(1)} %gate.120.__2_), channel_id=1, source_target_pairs={{0,21},{1,20},{2,23},{3,22},{4,17},{5,16},{6,19},{7,18},{8,29},{9,... | collective-permute-start | bytes 417800 | tf_op jit(solution)/shard_map/ppermute | solution.py:259
  160.9 15.4 %collective-permute-start.55 = (bf16[272,256]{1,0:T(8,128)(2,1)S(1)}, bf16[272,256]{1,0:T(8,128)(2,1)S(1)}, u32[]{:S(2)}, u32[]{:S(2)}) collective-permute-start(bf16[272,256]{1,0:T(8,128)(2,1)S(1)} %gate.121.__2_), channel_id=1, source_target_pairs={{0,18},{1,19},{2,16},{3,17},{4,22},{5,23},{6,20},{7,21},{8,26},{9,... | collective-permute-start | bytes 417800 | tf_op jit(solution)/shard_map/ppermute | solution.py:259
  161.4 18.5 %collective-permute-start.64 = (bf16[272,256]{1,0:T(8,128)(2,1)S(1)}, bf16[272,256]{1,0:T(8,128)(2,1)S(1)}, u32[]{:S(2)}, u32[]{:S(2)}) collective-permute-start(bf16[272,256]{1,0:T(8,128)(2,1)S(1)} %gate.122.__2_), channel_id=1, source_target_pairs={{0,22},{1,23},{2,20},{3,21},{4,18},{5,19},{6,16},{7,17},{8,30},{9,... | collective-permute-start | bytes 417800 | tf_op jit(solution)/shard_map/ppermute | solution.py:259
  166.1 14.1 %collective-permute-start.63 = (bf16[272,256]{1,0:T(8,128)(2,1)S(1)}, bf16[272,256]{1,0:T(8,128)(2,1)S(1)}, u32[]{:S(2)}, u32[]{:S(2)}) collective-permute-start(bf16[272,256]{1,0:T(8,128)(2,1)S(1)} %gate.123.__2_), channel_id=1, source_target_pairs={{0,19},{1,18},{2,17},{3,16},{4,23},{5,22},{6,21},{7,20},{8,27},{9,... | collective-permute-start | bytes 417800 | tf_op jit(solution)/shard_map/ppermute | solution.py:259
  168.6 14.1 %collective-permute-start.62 = (bf16[272,256]{1,0:T(8,128)(2,1)S(1)}, bf16[272,256]{1,0:T(8,128)(2,1)S(1)}, u32[]{:S(2)}, u32[]{:S(2)}) collective-permute-start(bf16[272,256]{1,0:T(8,128)(2,1)S(1)} %gate.124.__2_), channel_id=1, source_target_pairs={{0,13},{1,12},{2,15},{3,14},{4,9},{5,8},{6,11},{7,10},{8,5},{9,4},... | collective-permute-start | bytes 417800 | tf_op jit(solution)/shard_map/ppermute | solution.py:259
  173.2 15.3 %collective-permute-start.61 = (bf16[272,256]{1,0:T(8,128)(2,1)S(1)}, bf16[272,256]{1,0:T(8,128)(2,1)S(1)}, u32[]{:S(2)}, u32[]{:S(2)}) collective-permute-start(bf16[272,256]{1,0:T(8,128)(2,1)S(1)} %gate.125.__2_), channel_id=1, source_target_pairs={{0,10},{1,11},{2,8},{3,9},{4,14},{5,15},{6,12},{7,13},{8,2},{9,3},... | collective-permute-start | bytes 417800 | tf_op jit(solution)/shard_map/ppermute | solution.py:259
  176.2 12.2 %collective-permute-start.60 = (bf16[272,256]{1,0:T(8,128)(2,1)S(1)}, bf16[272,256]{1,0:T(8,128)(2,1)S(1)}, u32[]{:S(2)}, u32[]{:S(2)}) collective-permute-start(bf16[272,256]{1,0:T(8,128)(2,1)S(1)} %gate.126.__2_), channel_id=1, source_target_pairs={{0,23},{1,22},{2,21},{3,20},{4,19},{5,18},{6,17},{7,16},{8,31},{9,... | collective-permute-start | bytes 417800 | tf_op jit(solution)/shard_map/ppermute | solution.py:259
  179.8 11.9 %collective-permute-start.69 = (bf16[272,256]{1,0:T(8,128)(2,1)S(1)}, bf16[272,256]{1,0:T(8,128)(2,1)S(1)}, u32[]{:S(2)}, u32[]{:S(2)}) collective-permute-start(bf16[272,256]{1,0:T(8,128)(2,1)S(1)} %gate.127.__2_), channel_id=1, source_target_pairs={{0,16},{1,17},{2,18},{3,19},{4,20},{5,21},{6,22},{7,23},{8,24},{9,... | collective-permute-start | bytes 417800 | tf_op jit(solution)/shard_map/ppermute | solution.py:259
  180.3 16.0 %collective-permute-start.68 = (bf16[272,256]{1,0:T(8,128)(2,1)S(1)}, bf16[272,256]{1,0:T(8,128)(2,1)S(1)}, u32[]{:S(2)}, u32[]{:S(2)}) collective-permute-start(bf16[272,256]{1,0:T(8,128)(2,1)S(1)} %gate.128.__2_), channel_id=1, source_target_pairs={{0,14},{1,15},{2,12},{3,13},{4,10},{5,11},{6,8},{7,9},{8,6},{9,7},... | collective-permute-start | bytes 417800 | tf_op jit(solution)/shard_map/ppermute | solution.py:259
  182.8 14.2 %collective-permute-start.67 = (bf16[272,256]{1,0:T(8,128)(2,1)S(1)}, bf16[272,256]{1,0:T(8,128)(2,1)S(1)}, u32[]{:S(2)}, u32[]{:S(2)}) collective-permute-start(bf16[272,256]{1,0:T(8,128)(2,1)S(1)} %gate.129.__2_), channel_id=1, source_target_pairs={{0,11},{1,10},{2,9},{3,8},{4,15},{5,14},{6,13},{7,12},{8,3},{9,2},... | collective-permute-start | bytes 417800 | tf_op jit(solution)/shard_map/ppermute | solution.py:259
  188.5 12.2 %collective-permute-start.65 = (bf16[272,256]{1,0:T(8,128)(2,1)S(1)}, bf16[272,256]{1,0:T(8,128)(2,1)S(1)}, u32[]{:S(2)}, u32[]{:S(2)}) collective-permute-start(bf16[272,256]{1,0:T(8,128)(2,1)S(1)} %gate.131.__2_), channel_id=1, source_target_pairs={{0,25},{1,24},{2,27},{3,26},{4,29},{5,28},{6,31},{7,30},{8,17},{9,... | collective-permute-start | bytes 417800 | tf_op jit(solution)/shard_map/ppermute | solution.py:259
  191.7 18.4 %collective-permute-start.71 = (bf16[272,256]{1,0:T(8,128)(2,1)S(1)}, bf16[272,256]{1,0:T(8,128)(2,1)S(1)}, u32[]{:S(2)}, u32[]{:S(2)}) collective-permute-start(bf16[272,256]{1,0:T(8,128)(2,1)S(1)} %gate.132.__2_), channel_id=1, source_target_pairs={{0,29},{1,28},{2,31},{3,30},{4,25},{5,24},{6,27},{7,26},{8,21},{9,... | collective-permute-start | bytes 417800 | tf_op jit(solution)/shard_map/ppermute | solution.py:259
  196.3 13.8 %collective-permute-start.73 = (bf16[272,256]{1,0:T(8,128)(2,1)S(1)}, bf16[272,256]{1,0:T(8,128)(2,1)S(1)}, u32[]{:S(2)}, u32[]{:S(2)}) collective-permute-start(bf16[272,256]{1,0:T(8,128)(2,1)S(1)} %gate.133.__2_), channel_id=1, source_target_pairs={{0,26},{1,27},{2,24},{3,25},{4,30},{5,31},{6,28},{7,29},{8,18},{9,... | collective-permute-start | bytes 417800 | tf_op jit(solution)/shard_map/ppermute | solution.py:259
  197.0 17.8 %collective-permute-start.75 = (bf16[272,256]{1,0:T(8,128)(2,1)S(1)}, bf16[272,256]{1,0:T(8,128)(2,1)S(1)}, u32[]{:S(2)}, u32[]{:S(2)}) collective-permute-start(bf16[272,256]{1,0:T(8,128)(2,1)S(1)} %gate.134.__2_), channel_id=1, source_target_pairs={{0,15},{1,14},{2,13},{3,12},{4,11},{5,10},{6,9},{7,8},{8,7},{9,6},... | collective-permute-start | bytes 417800 | tf_op jit(solution)/shard_map/ppermute | solution.py:259
  199.6 15.2 %collective-permute-start.77 = (bf16[272,256]{1,0:T(8,128)(2,1)S(1)}, bf16[272,256]{1,0:T(8,128)(2,1)S(1)}, u32[]{:S(2)}, u32[]{:S(2)}) collective-permute-start(bf16[272,256]{1,0:T(8,128)(2,1)S(1)} %gate.135.__2_), channel_id=1, source_target_pairs={{0,8},{1,9},{2,10},{3,11},{4,12},{5,13},{6,14},{7,15},{8,0},{9,1},... | collective-permute-start | bytes 417800 | tf_op jit(solution)/shard_map/ppermute | solution.py:259
  200.7 21.0 %collective-permute-start.70 = (bf16[272,256]{1,0:T(8,128)(2,1)S(1)}, bf16[272,256]{1,0:T(8,128)(2,1)S(1)}, u32[]{:S(2)}, u32[]{:S(2)}) collective-permute-start(bf16[272,256]{1,0:T(8,128)(2,1)S(1)} %gate.136.__2_), channel_id=1, source_target_pairs={{0,30},{1,31},{2,28},{3,29},{4,26},{5,27},{6,24},{7,25},{8,22},{9,... | collective-permute-start | bytes 417800 | tf_op jit(solution)/shard_map/ppermute | solution.py:259
  210.1 11.6 %collective-permute-start.72 = (bf16[272,256]{1,0:T(8,128)(2,1)S(1)}, bf16[272,256]{1,0:T(8,128)(2,1)S(1)}, u32[]{:S(2)}, u32[]{:S(2)}) collective-permute-start(bf16[272,256]{1,0:T(8,128)(2,1)S(1)} %gate.137.__2_), channel_id=1, source_target_pairs={{0,27},{1,26},{2,25},{3,24},{4,31},{5,30},{6,29},{7,28},{8,19},{9,... | collective-permute-start | bytes 417800 | tf_op jit(solution)/shard_map/ppermute | solution.py:259
  (34 other events, 336.5 us)

commit v6 on v5

--- a/solution.py
+++ b/solution.py
@@ -11,9 +11,9 @@
 SPARE = 2
 STACK = 8
 SENDS = (
-    ["T00", "T01", "C20", "T02", "C21", "T03", "C22", "T10", "C23", "T11", "T12", "T20", "T13", "C30", "T21", "C31"]
+    ["T01", "C20", "T02", "C21", "T03", "C22", "T10", "C23", "T11", "T12", "T20", "T13", "C30", "T21", "C31"]
     + ["T22", "C32", "E00", "C33", "T23", "E01", "T30", "T31", "E02", "T32", "E03", "T33", "E20", "E10", "E21", "E22"]
-    + ["E11", "E23", "E12", "E30", "E31", "E13", "E32", "E33"]
+    + ["E11", "E23", "E30", "E12", "E31", "E13", "E33", "E32"]
 )
 WINDOW = 5
 PIECES = 4
@@ -148,8 +148,21 @@
     stack_spare(messages, main, jnp.concatenate(spares, axis=0))
 
 
-def touch_kernel(*refs):
-    refs[-1][...] = jnp.zeros_like(refs[-1])
+def half_decode_kernel(count, w_ref, *refs):
+    given, messages = refs[:count], refs[-count:]
+    main, part = main_of(given[0]), messages[0].shape[1]
+    spares = count * SPARE
+    lone = unstacked_spare(given, main).astype(F32)
+    lone = jnp.concatenate([lone[q * spares : (q + 1) * spares, :] for q in range(STACK)], axis=1)
+    lone = jnp.concatenate([lone, jnp.zeros((-spares % 16, lone.shape[1]), F32)], axis=0).astype(BF16)
+    codes = jnp.concatenate([unstacked(given, q, main) for q in range(STACK)], axis=1)
+    codes = jnp.concatenate([codes, lone], axis=0)
+    out = []
+    for q in range(STACK):
+        term = mm(codes, w_ref[:, q * part : (q + 1) * part])
+        stack(messages, q, main, term[: count * main, :].astype(BF16))
+        out.append(term[count * main : count * main + spares, :])
+    stack_spare(messages, main, jnp.concatenate(out, axis=0).astype(BF16))
 
 
 def combine_kernel(owners, place_in_ref, pick_ref, pick_spare_ref, place_ref, place_spare_ref, b_ref, act_ref, *rest):
@@ -284,14 +297,38 @@
     )(position, small, latent_codes.reshape(rows, -1))
     picks = packed[owners:]
     arrived = move_all(packed[:owners], 0)
-    touched = pl.pallas_call(
-        touch_kernel,
-        in_specs=[whole(w_dec.shape), ANYWHERE],
-        out_shape=some((8, 128), F32),
-        compiler_params=params(12),
-        cost_estimate=cost(0, 2 * width * local),
-        name="touch",
-    )(w_dec, arrived[0])
+    def gate(messages, after):
+        held = pl.pallas_call(
+            gate_kernel,
+            in_specs=[ANYWHERE] * (len(messages) + len(after)),
+            out_specs=[ANYWHERE] * len(messages),
+            out_shape=[some(m.shape) for m in messages],
+            input_output_aliases={i: i for i in range(len(messages))},
+            compiler_params=params(1),
+            cost_estimate=cost(0, 0),
+            name="gate",
+        )(*messages, *after)
+        return list(held)
+
+    def half_decode(first, after):
+        count = owners // 2
+        return pl.pallas_call(
+            functools.partial(half_decode_kernel, count),
+            in_specs=[whole((width, local))]
+            + [whole((depth, width // STACK))] * count
+            + [ANYWHERE] * len(after),
+            out_specs=[whole((depth, part))] * count,
+            out_shape=[some((depth, part))] * count,
+            compiler_params=params(16),
+            cost_estimate=cost(slots * width * local, 2 * width * local),
+            name="half_decode",
+        )(w_dec, *arrived[first : first + count], *after)
+
+    leaving, held = {("T", 0): list(half_decode(0, []))}, []
+    terms, errors = [[None] * owners for _ in range(groups)], [[None] * owners for _ in range(groups)]
+    for p in (0, 1):
+        held = gate([leaving["T", 0][p]], held)
+        terms[0][p] = move(held[0], 0, order[p])
     piece = (slots, width // PIECES)
     own_codes, *sent_codes = pl.pallas_call(
         functools.partial(unpack_kernel, owners),
@@ -300,8 +337,9 @@
         compiler_params=params(8),
         cost_estimate=cost(0, 4 * slots * width),
         name="unpack",
-    )(*arrived, touched)
+    )(*arrived, held[0])
     codes = [[own_codes], [move(own_codes, 1, 0)], [None] * PIECES, [None] * PIECES]
+    leaving["T", 0] += half_decode(owners // 2, [held[0]])
 
     def decode(j):
         copied = [piece] * PIECES if j == 2 else []
@@ -366,21 +404,7 @@
             name="gradient",
         )(turned, *[m for j, f, n in picked for m in errors[j][f : f + n]], *([base] if last else []), *after)
 
-    def gate(messages, after):
-        held = pl.pallas_call(
-            gate_kernel,
-            in_specs=[ANYWHERE] * (len(messages) + len(after)),
-            out_specs=[ANYWHERE] * len(messages),
-            out_shape=[some(m.shape) for m in messages],
-            input_output_aliases={i: i for i in range(len(messages))},
-            compiler_params=params(1),
-            cost_estimate=cost(0, 0),
-            name="gate",
-        )(*messages, *after)
-        return list(held)
-
-    terms, errors, leaving = [[None] * owners for _ in range(groups)], [[None] * owners for _ in range(groups)], {}
-    rebuilt, arrivals, held = None, list(codes[1]), []
+    rebuilt, arrivals = None, codes[1] + terms[0][:2]
     for kind, j, at in SENDS:
         j, at = int(j), int(at)
         if kind == "C":

time: 229 us -> 228 us (level); the launches traced: 225 us -> 227 us
  starting transfers between devices: 125 us -> 138 us
  waiting for transfers between devices: 66.9 us -> 54.4 us
    ppermute x78, starting transfers between devices: 125 us -> 138 us  [move(): return lax.ppermute(x, ('dp', 'latent'), pairs)]
    ppermute x78, waiting for transfers between devices: 66.9 us -> 54.4 us  [move(): return lax.ppermute(x, ('dp', 'latent'), pairs)]
    pallas_call x4 -> x3, Pallas kernels: 5.82 us -> 4.37 us  [decode(): pl.pallas_call(functools.partial(decode_kernel, owners, len(codes[j])), i...]
  transfers between devices with their start and end apart: 78 -> 78, of which waited for: 21 -> 26; matrix products, arithmetic and copies ran while one was open for 0% -> 0% of each run, Pallas kernels for 11% -> 11%
where the time goes in v6:
time: 228 us; the launch traced here: 227 us
  starting transfers between devices  138 us (61%)
  waiting for transfers between devices  54.4 us (24%)
  Pallas kernels  28.8 us (13%)
  local copies, waits for them, and re-layouts  3.35 us (1%)
    ppermute x78, starting transfers between devices, move(): return lax.ppermute(x, ('dp', 'latent'), pairs)  138 us
    ppermute x78, waiting for transfers between devices, move(): return lax.ppermute(x, ('dp', 'latent'), pairs)  54.4 us
    pallas_call x4, Pallas kernels, combine(): pl.pallas_call(functools.partial(combine_kernel, owners), grid_spec=pltpu...  12.4 us
    pallas_call x2, Pallas kernels, gradient(): pl.pallas_call(functools.partial(gradient_kernel, counts, last), in_specs...  7.41 us
  transfers between devices with their start and end apart: 78, of which 26 were waited for; matrix products, arithmetic and copies ran while one was open for 0% of the time, Pallas kernels for 11%

profile of v6, /device:TPU:0, one launch (start us, length us, event | category | flops | bytes accessed | tf_op | source)
XLA Modules:
  0.0 226.9 jit_solution(9627218855002100040)
XLA Ops:
  4.0 4.0 %collective-permute-start = (bf16[272,128]{1,0:T(8,128)(2,1)S(1)}, bf16[272,128]{1,0:T(8,128)(2,1)S(1)}, u32[]{:S(2)}, u32[]{:S(2)}) collective-permute-start(bf16[272,128]{1,0:T(8,128)(2,1)S(1)} %get-tuple-element.95), channel_id=1, source_target_pairs={{0,4},{1,5},{2,6},{3,7},{4,0},{5,1},{6,2},{7,3},{8,12},{9,13},{10,... | collective-permute-start | bytes 208904 | tf_op jit(solution)/shard_map/ppermute | solution.py:272
  11.4 2.5 %collective-permute-start.4 = (bf16[272,128]{1,0:T(8,128)(2,1)S(1)}, bf16[272,128]{1,0:T(8,128)(2,1)S(1)}, u32[]{:S(2)}, u32[]{:S(2)}) collective-permute-start(bf16[272,128]{1,0:T(8,128)(2,1)S(1)} %get-tuple-element.99), channel_id=1, source_target_pairs={{0,6},{1,7},{2,4},{3,5},{4,2},{5,3},{6,0},{7,1},{8,14},{9,15},{10,... | collective-permute-start | bytes 208904 | tf_op jit(solution)/shard_map/ppermute | solution.py:272
  15.5 2.7 %collective-permute-start.6 = (bf16[272,128]{1,0:T(8,128)(2,1)S(1)}, bf16[272,128]{1,0:T(8,128)(2,1)S(1)}, u32[]{:S(2)}, u32[]{:S(2)}) collective-permute-start(bf16[272,128]{1,0:T(8,128)(2,1)S(1)} %get-tuple-element.101), channel_id=1, source_target_pairs={{0,7},{1,6},{2,5},{3,4},{4,3},{5,2},{6,1},{7,0},{8,15},{9,14},{10,... | collective-permute-start | bytes 208904 | tf_op jit(solution)/shard_map/ppermute | solution.py:272
  18.3 2.2 copy-done
  30.2 5.2 %collective-permute-done.11.__1_.rest_0_ = bf16[272,256]{1,0:T(8,128)(2,1)S(1)} collective-permute-done((bf16[272,256]{1,0:T(8,128)(2,1)S(1)}, bf16[272,256]{1,0:T(8,128)(2,1)S(1)}, u32[]{:S(2)}, u32[]{:S(2)}) %collective-permute-start.11) | collective-permute-done | bytes 139296 | tf_op jit(solution)/shard_map/ppermute | solution.py:272
  35.4 2.8 %collective-permute-start.16 = (bf16[272,256]{1,0:T(8,128)(2,1)S(1)}, bf16[272,256]{1,0:T(8,128)(2,1)S(1)}, u32[]{:S(2)}, u32[]{:S(2)}) collective-permute-start(bf16[272,256]{1,0:T(8,128)(2,1)S(1)} %gate.75.__2_), channel_id=1, source_target_pairs={{0,6},{1,7},{2,4},{3,5},{4,2},{5,3},{6,0},{7,1},{8,14},{9,15},{10,... | collective-permute-start | bytes 417800 | tf_op jit(solution)/shard_map/ppermute | solution.py:272
  40.8 2.7 %collective-permute-start.20 = (bf16[272,256]{1,0:T(8,128)(2,1)S(1)}, bf16[272,256]{1,0:T(8,128)(2,1)S(1)}, u32[]{:S(2)}, u32[]{:S(2)}) collective-permute-start(bf16[272,256]{1,0:T(8,128)(2,1)S(1)} %gate.78.__2_), channel_id=1, source_target_pairs={{0,7},{1,6},{2,5},{3,4},{4,3},{5,2},{6,1},{7,0},{8,15},{9,14},{10,... | collective-permute-start | bytes 417800 | tf_op jit(solution)/shard_map/ppermute | solution.py:272
  47.5 3.1 %collective-permute-start.17 = (bf16[272,256]{1,0:T(8,128)(2,1)S(1)}, bf16[272,256]{1,0:T(8,128)(2,1)S(1)}, u32[]{:S(2)}, u32[]{:S(2)}) collective-permute-start(bf16[272,256]{1,0:T(8,128)(2,1)S(1)} %gate.82.__2_), channel_id=1, source_target_pairs={{0,16},{1,17},{2,18},{3,19},{4,20},{5,21},{6,22},{7,23},{8,24},{9,... | collective-permute-start | bytes 417800 | tf_op jit(solution)/shard_map/ppermute | solution.py:272
  50.5 4.4 %collective-permute-start.24 = (bf16[272,256]{1,0:T(8,128)(2,1)S(1)}, bf16[272,256]{1,0:T(8,128)(2,1)S(1)}, u32[]{:S(2)}, u32[]{:S(2)}) collective-permute-start(bf16[272,256]{1,0:T(8,128)(2,1)S(1)} %gate.83.__2_), channel_id=1, source_target_pairs={{0,13},{1,12},{2,15},{3,14},{4,9},{5,8},{6,11},{7,10},{8,5},{9,4},... | collective-permute-start | bytes 417800 | tf_op jit(solution)/shard_map/ppermute | solution.py:272
  55.2 3.3 %collective-permute-start.22 = (bf16[272,256]{1,0:T(8,128)(2,1)S(1)}, bf16[272,256]{1,0:T(8,128)(2,1)S(1)}, u32[]{:S(2)}, u32[]{:S(2)}) collective-permute-start(bf16[272,256]{1,0:T(8,128)(2,1)S(1)} %gate.85.__2_), channel_id=1, source_target_pairs={{0,14},{1,15},{2,12},{3,13},{4,10},{5,11},{6,8},{7,9},{8,6},{9,7},... | collective-permute-start | bytes 417800 | tf_op jit(solution)/shard_map/ppermute | solution.py:272
  60.7 2.5 %collective-permute-start.28 = (bf16[272,256]{1,0:T(8,128)(2,1)S(1)}, bf16[272,256]{1,0:T(8,128)(2,1)S(1)}, u32[]{:S(2)}, u32[]{:S(2)}) collective-permute-start(bf16[272,256]{1,0:T(8,128)(2,1)S(1)} %gate.87.__2_), channel_id=1, source_target_pairs={{0,20},{1,21},{2,22},{3,23},{4,16},{5,17},{6,18},{7,19},{8,28},{9,... | collective-permute-start | bytes 417800 | tf_op jit(solution)/shard_map/ppermute | solution.py:272
  64.6 3.0 %collective-permute-start.26 = (bf16[272,256]{1,0:T(8,128)(2,1)S(1)}, bf16[272,256]{1,0:T(8,128)(2,1)S(1)}, u32[]{:S(2)}, u32[]{:S(2)}) collective-permute-start(bf16[272,256]{1,0:T(8,128)(2,1)S(1)} %gate.89.__2_), channel_id=1, source_target_pairs={{0,15},{1,14},{2,13},{3,12},{4,11},{5,10},{6,9},{7,8},{8,7},{9,6},... | collective-permute-start | bytes 417800 | tf_op jit(solution)/shard_map/ppermute | solution.py:272
  68.4 3.3 %collective-permute-done.21.__1_.rest_5_ = bf16[272,256]{1,0:T(8,128)(2,1)S(1)} collective-permute-done((bf16[272,256]{1,0:T(8,128)(2,1)S(1)}, bf16[272,256]{1,0:T(8,128)(2,1)S(1)}, u32[]{:S(2)}, u32[]{:S(2)}) %collective-permute-start.21) | collective-permute-done | bytes 139296 | tf_op jit(solution)/shard_map/ppermute | solution.py:272
  71.8 7.4 %collective-permute-done.28.__1_.rest_0_ = bf16[272,256]{1,0:T(8,128)(2,1)S(1)} collective-permute-done((bf16[272,256]{1,0:T(8,128)(2,1)S(1)}, bf16[272,256]{1,0:T(8,128)(2,1)S(1)}, u32[]{:S(2)}, u32[]{:S(2)}) %collective-permute-start.28) | collective-permute-done | bytes 139296 | tf_op jit(solution)/shard_map/ppermute | solution.py:272
  79.3 3.9 %collective-permute-start.34 = (bf16[272,256]{1,0:T(8,128)(2,1)S(1)}, bf16[272,256]{1,0:T(8,128)(2,1)S(1)}, u32[]{:S(2)}, u32[]{:S(2)}) collective-permute-start(bf16[272,256]{1,0:T(8,128)(2,1)S(1)} %gate.93.__2_), channel_id=1, source_target_pairs={{0,18},{1,19},{2,16},{3,17},{4,22},{5,23},{6,20},{7,21},{8,26},{9,... | collective-permute-start | bytes 417800 | tf_op jit(solution)/shard_map/ppermute | solution.py:272
  84.8 3.1 %combine.4 = (bf16[128,8192]{1,0:T(8,128)(2,1)}, bf16[272,256]{1,0:T(8,128)(2,1)S(1)}, bf16[272,256]{1,0:T(8,128)(2,1)S(1)}, bf16[272,256]{1,0:T(8,128)(2,1)S(1)...) custom-call(s32[2]{0:T(128)S(1)} %pad_add_fusion.1.at_ref.place_in_r, ...), custom_call_target="tpu_custom_call" | custom-call | flops 285212672 | bytes 3276800 | tf_op jit(solution)/shard_map/combine/pallas_call | solution.py:358
  87.8 3.0 %collective-permute-start.38 = (bf16[272,256]{1,0:T(8,128)(2,1)S(1)}, bf16[272,256]{1,0:T(8,128)(2,1)S(1)}, u32[]{:S(2)}, u32[]{:S(2)}) collective-permute-start(bf16[272,256]{1,0:T(8,128)(2,1)S(1)} %gate.96.__2_), channel_id=1, source_target_pairs={{0,19},{1,18},{2,17},{3,16},{4,23},{5,22},{6,21},{7,20},{8,27},{9,... | collective-permute-start | bytes 417800 | tf_op jit(solution)/shard_map/ppermute | solution.py:272
  93.2 2.3 %collective-permute-done.38.__1_.rest_5_ = bf16[272,256]{1,0:T(8,128)(2,1)S(1)} collective-permute-done((bf16[272,256]{1,0:T(8,128)(2,1)S(1)}, bf16[272,256]{1,0:T(8,128)(2,1)S(1)}, u32[]{:S(2)}, u32[]{:S(2)}) %collective-permute-start.38) | collective-permute-done | bytes 139296 | tf_op jit(solution)/shard_map/ppermute | solution.py:272
  95.5 3.4 %collective-permute-start.40 = (bf16[272,256]{1,0:T(8,128)(2,1)S(1)}, bf16[272,256]{1,0:T(8,128)(2,1)S(1)}, u32[]{:S(2)}, u32[]{:S(2)}) collective-permute-start(bf16[272,256]{1,0:T(8,128)(2,1)S(1)} %gate.101.__2_), channel_id=1, source_target_pairs={{0,23},{1,22},{2,21},{3,20},{4,19},{5,18},{6,17},{7,16},{8,31},{9,... | collective-permute-start | bytes 417800 | tf_op jit(solution)/shard_map/ppermute | solution.py:272
  99.6 4.0 %collective-permute-done.37.__1_.refs_0_ = bf16[272,256]{1,0:T(8,128)(2,1)S(1)} collective-permute-done((bf16[272,256]{1,0:T(8,128)(2,1)S(1)}, bf16[272,256]{1,0:T(8,128)(2,1)S(1)}, u32[]{:S(2)}, u32[]{:S(2)}) %collective-permute-start.37) | collective-permute-done | bytes 139296 | tf_op jit(solution)/shard_map/ppermute | solution.py:272
  103.5 2.8 %collective-permute-start.44 = (bf16[272,256]{1,0:T(8,128)(2,1)S(1)}, bf16[272,256]{1,0:T(8,128)(2,1)S(1)}, u32[]{:S(2)}, u32[]{:S(2)}) collective-permute-start(bf16[272,256]{1,0:T(8,128)(2,1)S(1)} %gate.103.__2_), channel_id=1, source_target_pairs={{0,5},{1,4},{2,7},{3,6},{4,1},{5,0},{6,3},{7,2},{8,13},{9,12},{10,... | collective-permute-start | bytes 417800 | tf_op jit(solution)/shard_map/ppermute | solution.py:272
  111.4 3.0 %collective-permute-start.43 = (bf16[272,256]{1,0:T(8,128)(2,1)S(1)}, bf16[272,256]{1,0:T(8,128)(2,1)S(1)}, u32[]{:S(2)}, u32[]{:S(2)}) collective-permute-start(bf16[272,256]{1,0:T(8,128)(2,1)S(1)} %gate.107.__2_), channel_id=1, source_target_pairs={{0,29},{1,28},{2,31},{3,30},{4,25},{5,24},{6,27},{7,26},{8,21},{9,... | collective-permute-start | bytes 417800 | tf_op jit(solution)/shard_map/ppermute | solution.py:272
  115.6 2.8 %collective-permute-start.49 = (bf16[272,256]{1,0:T(8,128)(2,1)S(1)}, bf16[272,256]{1,0:T(8,128)(2,1)S(1)}, u32[]{:S(2)}, u32[]{:S(2)}) collective-permute-start(bf16[272,256]{1,0:T(8,128)(2,1)S(1)} %gate.109.__2_), channel_id=1, source_target_pairs={{0,6},{1,7},{2,4},{3,5},{4,2},{5,3},{6,0},{7,1},{8,14},{9,15},{10,... | collective-permute-start | bytes 417800 | tf_op jit(solution)/shard_map/ppermute | solution.py:272
  119.3 3.4 %collective-permute-start.51 = (bf16[272,256]{1,0:T(8,128)(2,1)S(1)}, bf16[272,256]{1,0:T(8,128)(2,1)S(1)}, u32[]{:S(2)}, u32[]{:S(2)}) collective-permute-start(bf16[272,256]{1,0:T(8,128)(2,1)S(1)} %gate.110.__2_), channel_id=1, source_target_pairs={{0,3},{1,2},{2,1},{3,0},{4,7},{5,6},{6,5},{7,4},{8,11},{9,10},{10,... | collective-permute-start | bytes 417800 | tf_op jit(solution)/shard_map/ppermute | solution.py:272
  122.7 3.5 %collective-permute-start.47 = (bf16[272,256]{1,0:T(8,128)(2,1)S(1)}, bf16[272,256]{1,0:T(8,128)(2,1)S(1)}, u32[]{:S(2)}, u32[]{:S(2)}) collective-permute-start(bf16[272,256]{1,0:T(8,128)(2,1)S(1)} %gate.111.__2_), channel_id=1, source_target_pairs={{0,30},{1,31},{2,28},{3,29},{4,26},{5,27},{6,24},{7,25},{8,22},{9,... | collective-permute-start | bytes 417800 | tf_op jit(solution)/shard_map/ppermute | solution.py:272
  126.2 2.8 %collective-permute-done.43.__1_.rest_2_ = bf16[272,256]{1,0:T(8,128)(2,1)S(1)} collective-permute-done((bf16[272,256]{1,0:T(8,128)(2,1)S(1)}, bf16[272,256]{1,0:T(8,128)(2,1)S(1)}, u32[]{:S(2)}, u32[]{:S(2)}) %collective-permute-start.43) | collective-permute-done | bytes 139296 | tf_op jit(solution)/shard_map/ppermute | solution.py:272
  129.3 6.1 %collective-permute-start.53 = (bf16[272,256]{1,0:T(8,128)(2,1)S(1)}, bf16[272,256]{1,0:T(8,128)(2,1)S(1)}, u32[]{:S(2)}, u32[]{:S(2)}) collective-permute-start(bf16[272,256]{1,0:T(8,128)(2,1)S(1)} %gate.113.__2_), channel_id=1, source_target_pairs={{0,7},{1,6},{2,5},{3,4},{4,3},{5,2},{6,1},{7,0},{8,15},{9,14},{10,... | collective-permute-start | bytes 417800 | tf_op jit(solution)/shard_map/ppermute | solution.py:272
  136.3 4.0 %collective-permute-start.52 = (bf16[272,256]{1,0:T(8,128)(2,1)S(1)}, bf16[272,256]{1,0:T(8,128)(2,1)S(1)}, u32[]{:S(2)}, u32[]{:S(2)}) collective-permute-start(bf16[272,256]{1,0:T(8,128)(2,1)S(1)} %gate.115.__2_), channel_id=1, source_target_pairs={{0,24},{1,25},{2,26},{3,27},{4,28},{5,29},{6,30},{7,31},{8,16},{9,... | collective-permute-start | bytes 417800 | tf_op jit(solution)/shard_map/ppermute | solution.py:272
  140.2 3.1 %combine.5 = (bf16[128,8192]{1,0:T(8,128)(2,1)}, bf16[272,256]{1,0:T(8,128)(2,1)S(1)}, bf16[272,256]{1,0:T(8,128)(2,1)S(1)}, bf16[272,256]{1,0:T(8,128)(2,1)S(1)...) custom-call(s32[2]{0:T(128)S(1)} %pad_add_fusion.1.at_ref.place_in_r, ...), custom_call_target="tpu_custom_call", output_to_operand_aliasing={{0}: (15, {})} | custom-call | flops 285212672 | bytes 3276800 | tf_op jit(solution)/shard_map/combine/pallas_call | solution.py:358
  143.3 3.2 %combine.6 = (bf16[128,8192]{1,0:T(8,128)(2,1)}, bf16[272,256]{1,0:T(8,128)(2,1)S(1)}, bf16[272,256]{1,0:T(8,128)(2,1)S(1)}, bf16[272,256]{1,0:T(8,128)(2,1)S(1)...) custom-call(s32[2]{0:T(128)S(1)} %pad_add_fusion.1.at_ref.place_in_r, ...), custom_call_target="tpu_custom_call", output_to_operand_aliasing={{0}: (15, {})} | custom-call | flops 285212672 | bytes 3276800 | tf_op jit(solution)/shard_map/combine/pallas_call | solution.py:358
  152.1 5.5 %collective-permute-start.60 = (bf16[272,256]{1,0:T(8,128)(2,1)S(1)}, bf16[272,256]{1,0:T(8,128)(2,1)S(1)}, u32[]{:S(2)}, u32[]{:S(2)}) collective-permute-start(bf16[272,256]{1,0:T(8,128)(2,1)S(1)} %gate.120.__2_), channel_id=1, source_target_pairs={{0,21},{1,20},{2,23},{3,22},{4,17},{5,16},{6,19},{7,18},{8,29},{9,... | collective-permute-start | bytes 417800 | tf_op jit(solution)/shard_map/ppermute | solution.py:272
  158.7 3.4 %collective-permute-start.58 = (bf16[272,256]{1,0:T(8,128)(2,1)S(1)}, bf16[272,256]{1,0:T(8,128)(2,1)S(1)}, u32[]{:S(2)}, u32[]{:S(2)}) collective-permute-start(bf16[272,256]{1,0:T(8,128)(2,1)S(1)} %gate.122.__2_), channel_id=1, source_target_pairs={{0,22},{1,23},{2,20},{3,21},{4,18},{5,19},{6,16},{7,17},{8,30},{9,... | collective-permute-start | bytes 417800 | tf_op jit(solution)/shard_map/ppermute | solution.py:272
  162.1 2.4 %collective-permute-done.54.__1_.refs_16_ = bf16[272,256]{1,0:T(8,128)(2,1)S(1)} collective-permute-done((bf16[272,256]{1,0:T(8,128)(2,1)S(1)}, bf16[272,256]{1,0:T(8,128)(2,1)S(1)}, u32[]{:S(2)}, u32[]{:S(2)}) %collective-permute-start.54) | collective-permute-done | bytes 139296 | tf_op jit(solution)/shard_map/ppermute | solution.py:272
  165.0 3.1 %collective-permute-start.66 = (bf16[272,256]{1,0:T(8,128)(2,1)S(1)}, bf16[272,256]{1,0:T(8,128)(2,1)S(1)}, u32[]{:S(2)}, u32[]{:S(2)}) collective-permute-start(bf16[272,256]{1,0:T(8,128)(2,1)S(1)} %gate.124.__2_), channel_id=1, source_target_pairs={{0,13},{1,12},{2,15},{3,14},{4,9},{5,8},{6,11},{7,10},{8,5},{9,4},... | collective-permute-start | bytes 417800 | tf_op jit(solution)/shard_map/ppermute | solution.py:272
  168.1 4.0 %collective-permute-done.60.__1_.refs_10_ = bf16[272,256]{1,0:T(8,128)(2,1)S(1)} collective-permute-done((bf16[272,256]{1,0:T(8,128)(2,1)S(1)}, bf16[272,256]{1,0:T(8,128)(2,1)S(1)}, u32[]{:S(2)}, u32[]{:S(2)}) %collective-permute-start.60) | collective-permute-done | bytes 139296 | tf_op jit(solution)/shard_map/ppermute | solution.py:272
  172.1 3.1 %combine.7 = (bf16[128,8192]{1,0:T(8,128)(2,1)}, bf16[272,256]{1,0:T(8,128)(2,1)S(1)}, bf16[272,256]{1,0:T(8,128)(2,1)S(1)}, bf16[272,256]{1,0:T(8,128)(2,1)S(1)...) custom-call(s32[2]{0:T(128)S(1)} %pad_add_fusion.1.at_ref.place_in_r, ...), custom_call_target="tpu_custom_call", output_to_operand_aliasing={{0}: (15, {})} | custom-call | flops 285212672 | bytes 3276800 | tf_op jit(solution)/shard_map/combine/pallas_call | solution.py:358
  175.2 2.5 %collective-permute-start.64 = (bf16[272,256]{1,0:T(8,128)(2,1)S(1)}, bf16[272,256]{1,0:T(8,128)(2,1)S(1)}, u32[]{:S(2)}, u32[]{:S(2)}) collective-permute-start(bf16[272,256]{1,0:T(8,128)(2,1)S(1)} %gate.126.__2_), channel_id=1, source_target_pairs={{0,23},{1,22},{2,21},{3,20},{4,19},{5,18},{6,17},{7,16},{8,31},{9,... | collective-permute-start | bytes 417800 | tf_op jit(solution)/shard_map/ppermute | solution.py:272
  178.4 2.7 %collective-permute-start.62 = (bf16[272,256]{1,0:T(8,128)(2,1)S(1)}, bf16[272,256]{1,0:T(8,128)(2,1)S(1)}, u32[]{:S(2)}, u32[]{:S(2)}) collective-permute-start(bf16[272,256]{1,0:T(8,128)(2,1)S(1)} %gate.128.__2_), channel_id=1, source_target_pairs={{0,28},{1,29},{2,30},{3,31},{4,24},{5,25},{6,26},{7,27},{8,20},{9,... | collective-permute-start | bytes 417800 | tf_op jit(solution)/shard_map/ppermute | solution.py:272
  183.8 2.6 %collective-permute-start.70 = (bf16[272,256]{1,0:T(8,128)(2,1)S(1)}, bf16[272,256]{1,0:T(8,128)(2,1)S(1)}, u32[]{:S(2)}, u32[]{:S(2)}) collective-permute-start(bf16[272,256]{1,0:T(8,128)(2,1)S(1)} %gate.130.__2_), channel_id=1, source_target_pairs={{0,14},{1,15},{2,12},{3,13},{4,10},{5,11},{6,8},{7,9},{8,6},{9,7},... | collective-permute-start | bytes 417800 | tf_op jit(solution)/shard_map/ppermute | solution.py:272
  186.4 3.4 %collective-permute-start.69 = (bf16[272,256]{1,0:T(8,128)(2,1)S(1)}, bf16[272,256]{1,0:T(8,128)(2,1)S(1)}, u32[]{:S(2)}, u32[]{:S(2)}) collective-permute-start(bf16[272,256]{1,0:T(8,128)(2,1)S(1)} %gate.131.__2_), channel_id=1, source_target_pairs={{0,11},{1,10},{2,9},{3,8},{4,15},{5,14},{6,13},{7,12},{8,3},{9,2},... | collective-permute-start | bytes 417800 | tf_op jit(solution)/shard_map/ppermute | solution.py:272
  191.6 3.1 %collective-permute-done.62.__1_.refs_24_ = bf16[272,256]{1,0:T(8,128)(2,1)S(1)} collective-permute-done((bf16[272,256]{1,0:T(8,128)(2,1)S(1)}, bf16[272,256]{1,0:T(8,128)(2,1)S(1)}, u32[]{:S(2)}, u32[]{:S(2)}) %collective-permute-start.62) | collective-permute-done | bytes 139296 | tf_op jit(solution)/shard_map/ppermute | solution.py:272
  194.7 4.6 %collective-permute-start.73 = (bf16[272,256]{1,0:T(8,128)(2,1)S(1)}, bf16[272,256]{1,0:T(8,128)(2,1)S(1)}, u32[]{:S(2)}, u32[]{:S(2)}) collective-permute-start(bf16[272,256]{1,0:T(8,128)(2,1)S(1)} %gate.134.__2_), channel_id=1, source_target_pairs={{0,15},{1,14},{2,13},{3,12},{4,11},{5,10},{6,9},{7,8},{8,7},{9,6},... | collective-permute-start | bytes 417800 | tf_op jit(solution)/shard_map/ppermute | solution.py:272
  200.3 3.3 %collective-permute-start.75 = (bf16[272,256]{1,0:T(8,128)(2,1)S(1)}, bf16[272,256]{1,0:T(8,128)(2,1)S(1)}, u32[]{:S(2)}, u32[]{:S(2)}) collective-permute-start(bf16[272,256]{1,0:T(8,128)(2,1)S(1)} %gate.136.__2_), channel_id=1, source_target_pairs={{0,31},{1,30},{2,29},{3,28},{4,27},{5,26},{6,25},{7,24},{8,23},{9,... | collective-permute-start | bytes 417800 | tf_op jit(solution)/shard_map/ppermute | solution.py:272
  203.6 2.1 collective-permute-done.68.__1_.refs_26_
  205.7 8.4 %collective-permute-start.76 = (bf16[272,256]{1,0:T(8,128)(2,1)S(1)}, bf16[272,256]{1,0:T(8,128)(2,1)S(1)}, u32[]{:S(2)}, u32[]{:S(2)}) collective-permute-start(bf16[272,256]{1,0:T(8,128)(2,1)S(1)} %gate.137.__2_), channel_id=1, source_target_pairs={{0,24},{1,25},{2,26},{3,27},{4,28},{5,29},{6,30},{7,31},{8,16},{9,... | collective-permute-start | bytes 417800 | tf_op jit(solution)/shard_map/ppermute | solution.py:272
  215.1 4.6 %gradient.2.refs_4_ = f32[1024,2048]{1,0:T(8,128)S(1)} custom-call(bf16[1024,952]{1,0:T(8,128)(2,1)S(1)} %turn.3.codes_ref, bf16[272,256]{1,0:T(8,128)(2,1)S(1)} %collective-permute-done.37.__1_.refs_0_, bf16[272,256]{1,0:T(8,128)(2,1)S(1)} %collective-permute-done.36.__1_.refs_1_, bf16[272,256]{1,0:T(8,128)(2,1)S(1)} %collective-permute-done.44.__1_.refs_2_, ...), custom_call_target="tpu_custom_call" | custom-call | flops 3992977408 | bytes 8388608 | tf_op jit(solution)/shard_map/gradient/pallas_call | solution.py:393
  219.7 3.0 %collective-permute-done.72.refs_0_ = bf16[272,256]{1,0:T(8,128)(2,1)S(1)} collective-permute-done((bf16[272,256]{1,0:T(8,128)(2,1)S(1)}, bf16[272,256]{1,0:T(8,128)(2,1)S(1)}, u32[]{:S(2)}, u32[]{:S(2)}) %collective-permute-start.72) | collective-permute-done | bytes 139296 | tf_op jit(solution)/shard_map/ppermute | solution.py:272
  223.9 2.8 %gradient.3 = bf16[1024,2048]{1,0:T(8,128)(2,1)} custom-call(bf16[1024,136]{1,0:T(8,128)(2,1)S(1)} %turn.2.codes_ref, bf16[272,256]{1,0:T(8,128)(2,1)S(1)} %collective-permute-done.72.refs_0_, bf16[272,256]{1,0:T(8,128)(2,1)S(1)} %collective-permute-done.74.refs_1_, bf16[272,256]{1,0:T(8,128)(2,1)S(1)} %collective-permute-done.75.refs_2_, ...), custom_call_target="tpu_custom_call" | custom-call | flops 570425344 | bytes 8388608 | tf_op jit(solution)/shard_map/gradient/pallas_call | solution.py:393
  (204 shorter events, 57.8 us)
Async XLA Ops:
  22.9 12.5 %collective-permute-start.11 = (bf16[272,256]{1,0:T(8,128)(2,1)S(1)}, bf16[272,256]{1,0:T(8,128)(2,1)S(1)}, u32[]{:S(2)}, u32[]{:S(2)}) collective-permute-start(bf16[272,256]{1,0:T(8,128)(2,1)S(1)} %gate.70.__1_), channel_id=1, source_target_pairs={{0,4},{1,5},{2,6},{3,7},{4,0},{5,1},{6,2},{7,3},{8,12},{9,13},{10,... | collective-permute-start | bytes 417800 | tf_op jit(solution)/shard_map/ppermute | solution.py:272
  24.6 13.5 %collective-permute-start.10 = (bf16[272,256]{1,0:T(8,128)(2,1)S(1)}, bf16[272,256]{1,0:T(8,128)(2,1)S(1)}, u32[]{:S(2)}, u32[]{:S(2)}) collective-permute-start(bf16[272,256]{1,0:T(8,128)(2,1)S(1)} %gate.71.refs_8_.__1_.refs_4_), channel_id=1, source_target_pairs={{0,1},{1,0},{2,3},{3,2},{4,5},{5,4},{6,7},{7,6},{8,9},{9,8},{10,11... | collective-permute-start | bytes 417800 | tf_op jit(solution)/shard_map/ppermute | solution.py:272
  25.7 13.6 %collective-permute-start.9 = (bf16[272,256]{1,0:T(8,128)(2,1)S(1)}, bf16[272,256]{1,0:T(8,128)(2,1)S(1)}, u32[]{:S(2)}, u32[]{:S(2)}) collective-permute-start(bf16[272,256]{1,0:T(8,128)(2,1)S(1)} %gate.72.__1_), channel_id=1, source_target_pairs={{0,5},{1,4},{2,7},{3,6},{4,1},{5,0},{6,3},{7,2},{8,13},{9,12},{10,... | collective-permute-start | bytes 417800 | tf_op jit(solution)/shard_map/ppermute | solution.py:272
  27.3 13.5 %collective-permute-start.13 = (bf16[272,256]{1,0:T(8,128)(2,1)S(1)}, bf16[272,256]{1,0:T(8,128)(2,1)S(1)}, u32[]{:S(2)}, u32[]{:S(2)}) collective-permute-start(bf16[272,256]{1,0:T(8,128)(2,1)S(1)} %gate.73.__2_), channel_id=1, source_target_pairs={{0,2},{1,3},{2,0},{3,1},{4,6},{5,7},{6,4},{7,5},{8,10},{9,11},{10,... | collective-permute-start | bytes 417800 | tf_op jit(solution)/shard_map/ppermute | solution.py:272
  28.6 16.4 %collective-permute-start.8 = (bf16[272,256]{1,0:T(8,128)(2,1)S(1)}, bf16[272,256]{1,0:T(8,128)(2,1)S(1)}, u32[]{:S(2)}, u32[]{:S(2)}) collective-permute-start(bf16[272,256]{1,0:T(8,128)(2,1)S(1)} %gate.74.__2_), channel_id=1, source_target_pairs={{0,16},{1,17},{2,18},{3,19},{4,20},{5,21},{6,22},{7,23},{8,24},{9,... | collective-permute-start | bytes 417800 | tf_op jit(solution)/shard_map/ppermute | solution.py:272
  47.5 11.7 %collective-permute-start.17 = (bf16[272,256]{1,0:T(8,128)(2,1)S(1)}, bf16[272,256]{1,0:T(8,128)(2,1)S(1)}, u32[]{:S(2)}, u32[]{:S(2)}) collective-permute-start(bf16[272,256]{1,0:T(8,128)(2,1)S(1)} %gate.82.__2_), channel_id=1, source_target_pairs={{0,16},{1,17},{2,18},{3,19},{4,20},{5,21},{6,22},{7,23},{8,24},{9,... | collective-permute-start | bytes 417800 | tf_op jit(solution)/shard_map/ppermute | solution.py:272
  50.5 12.6 %collective-permute-start.24 = (bf16[272,256]{1,0:T(8,128)(2,1)S(1)}, bf16[272,256]{1,0:T(8,128)(2,1)S(1)}, u32[]{:S(2)}, u32[]{:S(2)}) collective-permute-start(bf16[272,256]{1,0:T(8,128)(2,1)S(1)} %gate.83.__2_), channel_id=1, source_target_pairs={{0,13},{1,12},{2,15},{3,14},{4,9},{5,8},{6,11},{7,10},{8,5},{9,4},... | collective-permute-start | bytes 417800 | tf_op jit(solution)/shard_map/ppermute | solution.py:272
  55.2 12.8 %collective-permute-start.22 = (bf16[272,256]{1,0:T(8,128)(2,1)S(1)}, bf16[272,256]{1,0:T(8,128)(2,1)S(1)}, u32[]{:S(2)}, u32[]{:S(2)}) collective-permute-start(bf16[272,256]{1,0:T(8,128)(2,1)S(1)} %gate.85.__2_), channel_id=1, source_target_pairs={{0,14},{1,15},{2,12},{3,13},{4,10},{5,11},{6,8},{7,9},{8,6},{9,7},... | collective-permute-start | bytes 417800 | tf_op jit(solution)/shard_map/ppermute | solution.py:272
  58.5 13.1 %collective-permute-start.21 = (bf16[272,256]{1,0:T(8,128)(2,1)S(1)}, bf16[272,256]{1,0:T(8,128)(2,1)S(1)}, u32[]{:S(2)}, u32[]{:S(2)}) collective-permute-start(bf16[272,256]{1,0:T(8,128)(2,1)S(1)} %gate.86.__2_), channel_id=1, source_target_pairs={{0,11},{1,10},{2,9},{3,8},{4,15},{5,14},{6,13},{7,12},{8,3},{9,2},... | collective-permute-start | bytes 417800 | tf_op jit(solution)/shard_map/ppermute | solution.py:272
  60.7 18.6 %collective-permute-start.28 = (bf16[272,256]{1,0:T(8,128)(2,1)S(1)}, bf16[272,256]{1,0:T(8,128)(2,1)S(1)}, u32[]{:S(2)}, u32[]{:S(2)}) collective-permute-start(bf16[272,256]{1,0:T(8,128)(2,1)S(1)} %gate.87.__2_), channel_id=1, source_target_pairs={{0,20},{1,21},{2,22},{3,23},{4,16},{5,17},{6,18},{7,19},{8,28},{9,... | collective-permute-start | bytes 417800 | tf_op jit(solution)/shard_map/ppermute | solution.py:272
  63.2 16.1 %collective-permute-start.27 = (bf16[272,256]{1,0:T(8,128)(2,1)S(1)}, bf16[272,256]{1,0:T(8,128)(2,1)S(1)}, u32[]{:S(2)}, u32[]{:S(2)}) collective-permute-start(bf16[272,256]{1,0:T(8,128)(2,1)S(1)} %gate.88.__2_), channel_id=1, source_target_pairs={{0,17},{1,16},{2,19},{3,18},{4,21},{5,20},{6,23},{7,22},{8,25},{9,... | collective-permute-start | bytes 417800 | tf_op jit(solution)/shard_map/ppermute | solution.py:272
  64.6 18.6 %collective-permute-start.26 = (bf16[272,256]{1,0:T(8,128)(2,1)S(1)}, bf16[272,256]{1,0:T(8,128)(2,1)S(1)}, u32[]{:S(2)}, u32[]{:S(2)}) collective-permute-start(bf16[272,256]{1,0:T(8,128)(2,1)S(1)} %gate.89.__2_), channel_id=1, source_target_pairs={{0,15},{1,14},{2,13},{3,12},{4,11},{5,10},{6,9},{7,8},{8,7},{9,6},... | collective-permute-start | bytes 417800 | tf_op jit(solution)/shard_map/ppermute | solution.py:272
  68.0 15.1 %collective-permute-start.31 = (bf16[272,256]{1,0:T(8,128)(2,1)S(1)}, bf16[272,256]{1,0:T(8,128)(2,1)S(1)}, u32[]{:S(2)}, u32[]{:S(2)}) collective-permute-start(bf16[272,256]{1,0:T(8,128)(2,1)S(1)} %gate.90.__2_), channel_id=1, source_target_pairs={{0,8},{1,9},{2,10},{3,11},{4,12},{5,13},{6,14},{7,15},{8,0},{9,1},... | collective-permute-start | bytes 417800 | tf_op jit(solution)/shard_map/ppermute | solution.py:272
  71.7 16.2 %collective-permute-start.25 = (bf16[272,256]{1,0:T(8,128)(2,1)S(1)}, bf16[272,256]{1,0:T(8,128)(2,1)S(1)}, u32[]{:S(2)}, u32[]{:S(2)}) collective-permute-start(bf16[272,256]{1,0:T(8,128)(2,1)S(1)} %gate.91.__2_), channel_id=1, source_target_pairs={{0,8},{1,9},{2,10},{3,11},{4,12},{5,13},{6,14},{7,15},{8,0},{9,1},... | collective-permute-start | bytes 417800 | tf_op jit(solution)/shard_map/ppermute | solution.py:272
  79.3 13.6 %collective-permute-start.34 = (bf16[272,256]{1,0:T(8,128)(2,1)S(1)}, bf16[272,256]{1,0:T(8,128)(2,1)S(1)}, u32[]{:S(2)}, u32[]{:S(2)}) collective-permute-start(bf16[272,256]{1,0:T(8,128)(2,1)S(1)} %gate.93.__2_), channel_id=1, source_target_pairs={{0,18},{1,19},{2,16},{3,17},{4,22},{5,23},{6,20},{7,21},{8,26},{9,... | collective-permute-start | bytes 417800 | tf_op jit(solution)/shard_map/ppermute | solution.py:272
  92.9 13.5 %collective-permute-start.36 = (bf16[272,256]{1,0:T(8,128)(2,1)S(1)}, bf16[272,256]{1,0:T(8,128)(2,1)S(1)}, u32[]{:S(2)}, u32[]{:S(2)}) collective-permute-start(bf16[272,256]{1,0:T(8,128)(2,1)S(1)} %gate.99.__2_), channel_id=1, source_target_pairs={{0,1},{1,0},{2,3},{3,2},{4,5},{5,4},{6,7},{7,6},{8,9},{9,8},{10,11... | collective-permute-start | bytes 417800 | tf_op jit(solution)/shard_map/ppermute | solution.py:272
  93.2 13.2 %collective-permute-start.35 = (bf16[272,256]{1,0:T(8,128)(2,1)S(1)}, bf16[272,256]{1,0:T(8,128)(2,1)S(1)}, u32[]{:S(2)}, u32[]{:S(2)}) collective-permute-start(bf16[272,256]{1,0:T(8,128)(2,1)S(1)} %gate.100.__2_), channel_id=1, source_target_pairs={{0,8},{1,9},{2,10},{3,11},{4,12},{5,13},{6,14},{7,15},{8,0},{9,1},... | collective-permute-start | bytes 417800 | tf_op jit(solution)/shard_map/ppermute | solution.py:272
  95.5 14.1 %collective-permute-start.40 = (bf16[272,256]{1,0:T(8,128)(2,1)S(1)}, bf16[272,256]{1,0:T(8,128)(2,1)S(1)}, u32[]{:S(2)}, u32[]{:S(2)}) collective-permute-start(bf16[272,256]{1,0:T(8,128)(2,1)S(1)} %gate.101.__2_), channel_id=1, source_target_pairs={{0,23},{1,22},{2,21},{3,20},{4,19},{5,18},{6,17},{7,16},{8,31},{9,... | collective-permute-start | bytes 417800 | tf_op jit(solution)/shard_map/ppermute | solution.py:272
  98.8 12.6 %collective-permute-start.42 = (bf16[272,256]{1,0:T(8,128)(2,1)S(1)}, bf16[272,256]{1,0:T(8,128)(2,1)S(1)}, u32[]{:S(2)}, u32[]{:S(2)}) collective-permute-start(bf16[272,256]{1,0:T(8,128)(2,1)S(1)} %gate.102.__2_), channel_id=1, source_target_pairs={{0,16},{1,17},{2,18},{3,19},{4,20},{5,21},{6,22},{7,23},{8,24},{9,... | collective-permute-start | bytes 417800 | tf_op jit(solution)/shard_map/ppermute | solution.py:272
  109.6 13.1 %collective-permute-start.41 = (bf16[272,256]{1,0:T(8,128)(2,1)S(1)}, bf16[272,256]{1,0:T(8,128)(2,1)S(1)}, u32[]{:S(2)}, u32[]{:S(2)}) collective-permute-start(bf16[272,256]{1,0:T(8,128)(2,1)S(1)} %gate.106.__2_), channel_id=1, source_target_pairs={{0,25},{1,24},{2,27},{3,26},{4,29},{5,28},{6,31},{7,30},{8,17},{9,... | collective-permute-start | bytes 417800 | tf_op jit(solution)/shard_map/ppermute | solution.py:272
  111.4 17.5 %collective-permute-start.43 = (bf16[272,256]{1,0:T(8,128)(2,1)S(1)}, bf16[272,256]{1,0:T(8,128)(2,1)S(1)}, u32[]{:S(2)}, u32[]{:S(2)}) collective-permute-start(bf16[272,256]{1,0:T(8,128)(2,1)S(1)} %gate.107.__2_), channel_id=1, source_target_pairs={{0,29},{1,28},{2,31},{3,30},{4,25},{5,24},{6,27},{7,26},{8,21},{9,... | collective-permute-start | bytes 417800 | tf_op jit(solution)/shard_map/ppermute | solution.py:272
  114.7 14.6 %collective-permute-start.45 = (bf16[272,256]{1,0:T(8,128)(2,1)S(1)}, bf16[272,256]{1,0:T(8,128)(2,1)S(1)}, u32[]{:S(2)}, u32[]{:S(2)}) collective-permute-start(bf16[272,256]{1,0:T(8,128)(2,1)S(1)} %gate.108.__2_), channel_id=1, source_target_pairs={{0,26},{1,27},{2,24},{3,25},{4,30},{5,31},{6,28},{7,29},{8,18},{9,... | collective-permute-start | bytes 417800 | tf_op jit(solution)/shard_map/ppermute | solution.py:272
  115.6 19.8 %collective-permute-start.49 = (bf16[272,256]{1,0:T(8,128)(2,1)S(1)}, bf16[272,256]{1,0:T(8,128)(2,1)S(1)}, u32[]{:S(2)}, u32[]{:S(2)}) collective-permute-start(bf16[272,256]{1,0:T(8,128)(2,1)S(1)} %gate.109.__2_), channel_id=1, source_target_pairs={{0,6},{1,7},{2,4},{3,5},{4,2},{5,3},{6,0},{7,1},{8,14},{9,15},{10,... | collective-permute-start | bytes 417800 | tf_op jit(solution)/shard_map/ppermute | solution.py:272
  119.3 16.9 %collective-permute-start.51 = (bf16[272,256]{1,0:T(8,128)(2,1)S(1)}, bf16[272,256]{1,0:T(8,128)(2,1)S(1)}, u32[]{:S(2)}, u32[]{:S(2)}) collective-permute-start(bf16[272,256]{1,0:T(8,128)(2,1)S(1)} %gate.110.__2_), channel_id=1, source_target_pairs={{0,3},{1,2},{2,1},{3,0},{4,7},{5,6},{6,5},{7,4},{8,11},{9,10},{10,... | collective-permute-start | bytes 417800 | tf_op jit(solution)/shard_map/ppermute | solution.py:272
  122.7 23.8 %collective-permute-start.47 = (bf16[272,256]{1,0:T(8,128)(2,1)S(1)}, bf16[272,256]{1,0:T(8,128)(2,1)S(1)}, u32[]{:S(2)}, u32[]{:S(2)}) collective-permute-start(bf16[272,256]{1,0:T(8,128)(2,1)S(1)} %gate.111.__2_), channel_id=1, source_target_pairs={{0,30},{1,31},{2,28},{3,29},{4,26},{5,27},{6,24},{7,25},{8,22},{9,... | collective-permute-start | bytes 417800 | tf_op jit(solution)/shard_map/ppermute | solution.py:272
  129.0 18.6 %collective-permute-start.48 = (bf16[272,256]{1,0:T(8,128)(2,1)S(1)}, bf16[272,256]{1,0:T(8,128)(2,1)S(1)}, u32[]{:S(2)}, u32[]{:S(2)}) collective-permute-start(bf16[272,256]{1,0:T(8,128)(2,1)S(1)} %gate.112.__2_), channel_id=1, source_target_pairs={{0,27},{1,26},{2,25},{3,24},{4,31},{5,30},{6,29},{7,28},{8,19},{9,... | collective-permute-start | bytes 417800 | tf_op jit(solution)/shard_map/ppermute | solution.py:272
  129.3 19.8 %collective-permute-start.53 = (bf16[272,256]{1,0:T(8,128)(2,1)S(1)}, bf16[272,256]{1,0:T(8,128)(2,1)S(1)}, u32[]{:S(2)}, u32[]{:S(2)}) collective-permute-start(bf16[272,256]{1,0:T(8,128)(2,1)S(1)} %gate.113.__2_), channel_id=1, source_target_pairs={{0,7},{1,6},{2,5},{3,4},{4,3},{5,2},{6,1},{7,0},{8,15},{9,14},{10,... | collective-permute-start | bytes 417800 | tf_op jit(solution)/shard_map/ppermute | solution.py:272
  135.4 15.4 %collective-permute-start.50 = (bf16[272,256]{1,0:T(8,128)(2,1)S(1)}, bf16[272,256]{1,0:T(8,128)(2,1)S(1)}, u32[]{:S(2)}, u32[]{:S(2)}) collective-permute-start(bf16[272,256]{1,0:T(8,128)(2,1)S(1)} %gate.114.__2_), channel_id=1, source_target_pairs={{0,31},{1,30},{2,29},{3,28},{4,27},{5,26},{6,25},{7,24},{8,23},{9,... | collective-permute-start | bytes 417800 | tf_op jit(solution)/shard_map/ppermute | solution.py:272
  136.3 15.8 %collective-permute-start.52 = (bf16[272,256]{1,0:T(8,128)(2,1)S(1)}, bf16[272,256]{1,0:T(8,128)(2,1)S(1)}, u32[]{:S(2)}, u32[]{:S(2)}) collective-permute-start(bf16[272,256]{1,0:T(8,128)(2,1)S(1)} %gate.115.__2_), channel_id=1, source_target_pairs={{0,24},{1,25},{2,26},{3,27},{4,28},{5,29},{6,30},{7,31},{8,16},{9,... | collective-permute-start | bytes 417800 | tf_op jit(solution)/shard_map/ppermute | solution.py:272
  146.5 12.1 %collective-permute-start.56 = (bf16[272,256]{1,0:T(8,128)(2,1)S(1)}, bf16[272,256]{1,0:T(8,128)(2,1)S(1)}, u32[]{:S(2)}, u32[]{:S(2)}) collective-permute-start(bf16[272,256]{1,0:T(8,128)(2,1)S(1)} %gate.116.__2_), channel_id=1, source_target_pairs={{0,20},{1,21},{2,22},{3,23},{4,16},{5,17},{6,18},{7,19},{8,28},{9,... | collective-permute-start | bytes 417800 | tf_op jit(solution)/shard_map/ppermute | solution.py:272
  149.1 15.4 %collective-permute-start.54 = (bf16[272,256]{1,0:T(8,128)(2,1)S(1)}, bf16[272,256]{1,0:T(8,128)(2,1)S(1)}, u32[]{:S(2)}, u32[]{:S(2)}) collective-permute-start(bf16[272,256]{1,0:T(8,128)(2,1)S(1)} %gate.118.__2_), channel_id=1, source_target_pairs={{0,12},{1,13},{2,14},{3,15},{4,8},{5,9},{6,10},{7,11},{8,4},{9,5},... | collective-permute-start | bytes 417800 | tf_op jit(solution)/shard_map/ppermute | solution.py:272
  150.8 14.2 %collective-permute-start.61 = (bf16[272,256]{1,0:T(8,128)(2,1)S(1)}, bf16[272,256]{1,0:T(8,128)(2,1)S(1)}, u32[]{:S(2)}, u32[]{:S(2)}) collective-permute-start(bf16[272,256]{1,0:T(8,128)(2,1)S(1)} %gate.119.__2_), channel_id=1, source_target_pairs={{0,9},{1,8},{2,11},{3,10},{4,13},{5,12},{6,15},{7,14},{8,1},{9,0},... | collective-permute-start | bytes 417800 | tf_op jit(solution)/shard_map/ppermute | solution.py:272
  152.1 20.0 %collective-permute-start.60 = (bf16[272,256]{1,0:T(8,128)(2,1)S(1)}, bf16[272,256]{1,0:T(8,128)(2,1)S(1)}, u32[]{:S(2)}, u32[]{:S(2)}) collective-permute-start(bf16[272,256]{1,0:T(8,128)(2,1)S(1)} %gate.120.__2_), channel_id=1, source_target_pairs={{0,21},{1,20},{2,23},{3,22},{4,17},{5,16},{6,19},{7,18},{8,29},{9,... | collective-permute-start | bytes 417800 | tf_op jit(solution)/shard_map/ppermute | solution.py:272
  158.7 16.5 %collective-permute-start.59 = (bf16[272,256]{1,0:T(8,128)(2,1)S(1)}, bf16[272,256]{1,0:T(8,128)(2,1)S(1)}, u32[]{:S(2)}, u32[]{:S(2)}) collective-permute-start(bf16[272,256]{1,0:T(8,128)(2,1)S(1)} %gate.121.__2_), channel_id=1, source_target_pairs={{0,18},{1,19},{2,16},{3,17},{4,22},{5,23},{6,20},{7,21},{8,26},{9,... | collective-permute-start | bytes 417800 | tf_op jit(solution)/shard_map/ppermute | solution.py:272
  158.7 19.0 %collective-permute-start.58 = (bf16[272,256]{1,0:T(8,128)(2,1)S(1)}, bf16[272,256]{1,0:T(8,128)(2,1)S(1)}, u32[]{:S(2)}, u32[]{:S(2)}) collective-permute-start(bf16[272,256]{1,0:T(8,128)(2,1)S(1)} %gate.122.__2_), channel_id=1, source_target_pairs={{0,22},{1,23},{2,20},{3,21},{4,18},{5,19},{6,16},{7,17},{8,30},{9,... | collective-permute-start | bytes 417800 | tf_op jit(solution)/shard_map/ppermute | solution.py:272
  164.5 13.9 %collective-permute-start.57 = (bf16[272,256]{1,0:T(8,128)(2,1)S(1)}, bf16[272,256]{1,0:T(8,128)(2,1)S(1)}, u32[]{:S(2)}, u32[]{:S(2)}) collective-permute-start(bf16[272,256]{1,0:T(8,128)(2,1)S(1)} %gate.123.__2_), channel_id=1, source_target_pairs={{0,19},{1,18},{2,17},{3,16},{4,23},{5,22},{6,21},{7,20},{8,27},{9,... | collective-permute-start | bytes 417800 | tf_op jit(solution)/shard_map/ppermute | solution.py:272
  165.0 17.0 %collective-permute-start.66 = (bf16[272,256]{1,0:T(8,128)(2,1)S(1)}, bf16[272,256]{1,0:T(8,128)(2,1)S(1)}, u32[]{:S(2)}, u32[]{:S(2)}) collective-permute-start(bf16[272,256]{1,0:T(8,128)(2,1)S(1)} %gate.124.__2_), channel_id=1, source_target_pairs={{0,13},{1,12},{2,15},{3,14},{4,9},{5,8},{6,11},{7,10},{8,5},{9,4},... | collective-permute-start | bytes 417800 | tf_op jit(solution)/shard_map/ppermute | solution.py:272
  177.7 12.1 %collective-permute-start.63 = (bf16[272,256]{1,0:T(8,128)(2,1)S(1)}, bf16[272,256]{1,0:T(8,128)(2,1)S(1)}, u32[]{:S(2)}, u32[]{:S(2)}) collective-permute-start(bf16[272,256]{1,0:T(8,128)(2,1)S(1)} %gate.127.__2_), channel_id=1, source_target_pairs={{0,16},{1,17},{2,18},{3,19},{4,20},{5,21},{6,22},{7,23},{8,24},{9,... | collective-permute-start | bytes 417800 | tf_op jit(solution)/shard_map/ppermute | solution.py:272
  178.4 16.3 %collective-permute-start.62 = (bf16[272,256]{1,0:T(8,128)(2,1)S(1)}, bf16[272,256]{1,0:T(8,128)(2,1)S(1)}, u32[]{:S(2)}, u32[]{:S(2)}) collective-permute-start(bf16[272,256]{1,0:T(8,128)(2,1)S(1)} %gate.128.__2_), channel_id=1, source_target_pairs={{0,28},{1,29},{2,30},{3,31},{4,24},{5,25},{6,26},{7,27},{8,20},{9,... | collective-permute-start | bytes 417800 | tf_op jit(solution)/shard_map/ppermute | solution.py:272
  182.0 12.7 %collective-permute-start.71 = (bf16[272,256]{1,0:T(8,128)(2,1)S(1)}, bf16[272,256]{1,0:T(8,128)(2,1)S(1)}, u32[]{:S(2)}, u32[]{:S(2)}) collective-permute-start(bf16[272,256]{1,0:T(8,128)(2,1)S(1)} %gate.129.__2_), channel_id=1, source_target_pairs={{0,25},{1,24},{2,27},{3,26},{4,29},{5,28},{6,31},{7,30},{8,17},{9,... | collective-permute-start | bytes 417800 | tf_op jit(solution)/shard_map/ppermute | solution.py:272
  183.8 15.5 %collective-permute-start.70 = (bf16[272,256]{1,0:T(8,128)(2,1)S(1)}, bf16[272,256]{1,0:T(8,128)(2,1)S(1)}, u32[]{:S(2)}, u32[]{:S(2)}) collective-permute-start(bf16[272,256]{1,0:T(8,128)(2,1)S(1)} %gate.130.__2_), channel_id=1, source_target_pairs={{0,14},{1,15},{2,12},{3,13},{4,10},{5,11},{6,8},{7,9},{8,6},{9,7},... | collective-permute-start | bytes 417800 | tf_op jit(solution)/shard_map/ppermute | solution.py:272
  186.4 13.8 %collective-permute-start.69 = (bf16[272,256]{1,0:T(8,128)(2,1)S(1)}, bf16[272,256]{1,0:T(8,128)(2,1)S(1)}, u32[]{:S(2)}, u32[]{:S(2)}) collective-permute-start(bf16[272,256]{1,0:T(8,128)(2,1)S(1)} %gate.131.__2_), channel_id=1, source_target_pairs={{0,11},{1,10},{2,9},{3,8},{4,15},{5,14},{6,13},{7,12},{8,3},{9,2},... | collective-permute-start | bytes 417800 | tf_op jit(solution)/shard_map/ppermute | solution.py:272
  189.8 15.9 %collective-permute-start.68 = (bf16[272,256]{1,0:T(8,128)(2,1)S(1)}, bf16[272,256]{1,0:T(8,128)(2,1)S(1)}, u32[]{:S(2)}, u32[]{:S(2)}) collective-permute-start(bf16[272,256]{1,0:T(8,128)(2,1)S(1)} %gate.132.__2_), channel_id=1, source_target_pairs={{0,29},{1,28},{2,31},{3,30},{4,25},{5,24},{6,27},{7,26},{8,21},{9,... | collective-permute-start | bytes 417800 | tf_op jit(solution)/shard_map/ppermute | solution.py:272
  194.7 19.4 %collective-permute-start.67 = (bf16[272,256]{1,0:T(8,128)(2,1)S(1)}, bf16[272,256]{1,0:T(8,128)(2,1)S(1)}, u32[]{:S(2)}, u32[]{:S(2)}) collective-permute-start(bf16[272,256]{1,0:T(8,128)(2,1)S(1)} %gate.133.__2_), channel_id=1, source_target_pairs={{0,26},{1,27},{2,24},{3,25},{4,30},{5,31},{6,28},{7,29},{8,18},{9,... | collective-permute-start | bytes 417800 | tf_op jit(solution)/shard_map/ppermute | solution.py:272
  194.7 19.4 %collective-permute-start.73 = (bf16[272,256]{1,0:T(8,128)(2,1)S(1)}, bf16[272,256]{1,0:T(8,128)(2,1)S(1)}, u32[]{:S(2)}, u32[]{:S(2)}) collective-permute-start(bf16[272,256]{1,0:T(8,128)(2,1)S(1)} %gate.134.__2_), channel_id=1, source_target_pairs={{0,15},{1,14},{2,13},{3,12},{4,11},{5,10},{6,9},{7,8},{8,7},{9,6},... | collective-permute-start | bytes 417800 | tf_op jit(solution)/shard_map/ppermute | solution.py:272
  199.3 15.7 %collective-permute-start.77 = (bf16[272,256]{1,0:T(8,128)(2,1)S(1)}, bf16[272,256]{1,0:T(8,128)(2,1)S(1)}, u32[]{:S(2)}, u32[]{:S(2)}) collective-permute-start(bf16[272,256]{1,0:T(8,128)(2,1)S(1)} %gate.135.__2_), channel_id=1, source_target_pairs={{0,8},{1,9},{2,10},{3,11},{4,12},{5,13},{6,14},{7,15},{8,0},{9,1},... | collective-permute-start | bytes 417800 | tf_op jit(solution)/shard_map/ppermute | solution.py:272
  200.3 22.4 %collective-permute-start.75 = (bf16[272,256]{1,0:T(8,128)(2,1)S(1)}, bf16[272,256]{1,0:T(8,128)(2,1)S(1)}, u32[]{:S(2)}, u32[]{:S(2)}) collective-permute-start(bf16[272,256]{1,0:T(8,128)(2,1)S(1)} %gate.136.__2_), channel_id=1, source_target_pairs={{0,31},{1,30},{2,29},{3,28},{4,27},{5,26},{6,25},{7,24},{8,23},{9,... | collective-permute-start | bytes 417800 | tf_op jit(solution)/shard_map/ppermute | solution.py:272
  205.7 16.9 %collective-permute-start.76 = (bf16[272,256]{1,0:T(8,128)(2,1)S(1)}, bf16[272,256]{1,0:T(8,128)(2,1)S(1)}, u32[]{:S(2)}, u32[]{:S(2)}) collective-permute-start(bf16[272,256]{1,0:T(8,128)(2,1)S(1)} %gate.137.__2_), channel_id=1, source_target_pairs={{0,24},{1,25},{2,26},{3,27},{4,28},{5,29},{6,30},{7,31},{8,16},{9,... | collective-permute-start | bytes 417800 | tf_op jit(solution)/shard_map/ppermute | solution.py:272
  (34 other events, 337.0 us)

commit v7 on v6

--- a/solution.py
+++ b/solution.py
@@ -36,11 +36,10 @@
 
 
 def pack_kernel(order, visits, at_ref, small_ref, codes_ref, *outs):
-    messages, (pick_ref, pick_spare_ref, place_ref, place_spare_ref) = outs[:-4], outs[-4:]
-    owners = len(messages)
-    rows, width = codes_ref.shape[0], codes_ref.shape[1] // visits
+    owners = len(order)
+    messages, sheets = outs[:owners], outs[-4:]
+    rows = small_ref.shape[1]
     blocks = small_ref.shape[0] // visits - 1
-    block = width // blocks
     main = rows * visits // owners
     slots = owners * (main + SPARE)
     apart = small_ref[:visits, :] ^ at_ref[0]
@@ -61,12 +60,17 @@
     slot_column = slot_of(column, jnp.sum(jnp.where(same & (across < down), 1, 0), axis=1, keepdims=True))
     place = (lax.broadcasted_iota(jnp.int32, (slots, total), 0) == slot_lane).astype(F32)
     pick = (lax.broadcasted_iota(jnp.int32, (total, slots), 1) == slot_column).astype(F32)
-    place_rows = sum(place[:, g * rows : (g + 1) * rows] for g in range(visits)).astype(BF16)
-    pick_rows = sum(pick[g * rows : (g + 1) * rows, :] for g in range(visits)).astype(BF16)
-    pick_ref[...] = pick_rows[:, : owners * main]
-    pick_spare_ref[...] = pick_rows[:, owners * main :]
-    place_ref[...] = place_rows[: owners * main, :]
-    place_spare_ref[...] = place_rows[owners * main :, :]
+    if codes_ref is None:
+        pick_ref, pick_spare_ref, place_ref, place_spare_ref = sheets
+        place_rows = sum(place[:, g * rows : (g + 1) * rows] for g in range(visits)).astype(BF16)
+        pick_rows = sum(pick[g * rows : (g + 1) * rows, :] for g in range(visits)).astype(BF16)
+        pick_ref[...] = pick_rows[:, : owners * main]
+        pick_spare_ref[...] = pick_rows[:, owners * main :]
+        place_ref[...] = place_rows[: owners * main, :]
+        place_spare_ref[...] = place_rows[owners * main :, :]
+        return
+    width = codes_ref.shape[1] // visits
+    block = width // blocks
     live = small_ref[...].astype(F32).T.astype(BF16)[:, visits:]
     used = jnp.concatenate(
         [
@@ -148,6 +152,10 @@
     stack_spare(messages, main, jnp.concatenate(spares, axis=0))
 
 
+def places_kernel(order, visits, at_ref, small_ref, _, *outs):
+    pack_kernel(order, visits, at_ref, small_ref, None, *outs)
+
+
 def half_decode_kernel(count, w_ref, *refs):
     given, messages = refs[:count], refs[-count:]
     main, part = main_of(given[0]), messages[0].shape[1]
@@ -284,19 +292,28 @@
             num_scalar_prefetch=1,
             grid=(1,),
             in_specs=[whole(small.shape), whole((rows, visits * width))],
-            out_specs=[whole((depth, width // STACK))] * owners
-            + [whole((rows, owners * main)), whole((rows, owners * SPARE))]
-            + [whole((owners * main, rows)), whole((owners * SPARE, rows))],
+            out_specs=[whole((depth, width // STACK))] * owners,
         ),
-        out_shape=[some((depth, width // STACK))] * owners
-        + [some((rows, owners * main)), some((rows, owners * SPARE))]
-        + [some((owners * main, rows)), some((owners * SPARE, rows))],
+        out_shape=[some((depth, width // STACK))] * owners,
         compiler_params=params(12),
         cost_estimate=cost(2 * slots * rows * visits * width, 0),
         name="pack",
     )(position, small, latent_codes.reshape(rows, -1))
-    picks = packed[owners:]
-    arrived = move_all(packed[:owners], 0)
+    arrived = move_all(packed, 0)
+    sheets = [(rows, owners * main), (rows, owners * SPARE), (owners * main, rows), (owners * SPARE, rows)]
+    picks = pl.pallas_call(
+        functools.partial(places_kernel, order, visits),
+        grid_spec=pltpu.PrefetchScalarGridSpec(
+            num_scalar_prefetch=1,
+            grid=(1,),
+            in_specs=[whole(small.shape), ANYWHERE],
+            out_specs=[whole(sheet) for sheet in sheets],
+        ),
+        out_shape=[some(sheet) for sheet in sheets],
+        compiler_params=params(8),
+        cost_estimate=cost(0, 4 * slots * rows),
+        name="places",
+    )(position, small, arrived[0])
     def gate(messages, after):
         held = pl.pallas_call(
             gate_kernel,

time: 228 us -> 227 us (level)
    ppermute x78, starting transfers between devices: 138 us -> 136 us  [move(): return lax.ppermute(x, ('dp', 'latent'), pairs)]
  transfers between devices with their start and end apart: 78 -> 78, of which waited for: 26 -> 22; matrix products, arithmetic and copies ran while one was open for 0% -> 0% of each run, Pallas kernels for 11% -> 11%
where the time goes in v7:
time: 227 us
  starting transfers between devices  136 us (60%)
  waiting for transfers between devices  55.9 us (25%)
  Pallas kernels  29.6 us (13%)
  local copies, waits for them, and re-layouts  3.35 us (1%)
    ppermute x78, starting transfers between devices, move(): return lax.ppermute(x, ('dp', 'latent'), pairs)  136 us
    ppermute x78, waiting for transfers between devices, move(): return lax.ppermute(x, ('dp', 'latent'), pairs)  55.9 us
    pallas_call x4, Pallas kernels, combine(): pl.pallas_call(functools.partial(combine_kernel, owners), grid_spec=pltpu...  12.3 us
    pallas_call x2, Pallas kernels, gradient(): pl.pallas_call(functools.partial(gradient_kernel, counts, last), in_specs...  7.41 us
  transfers between devices with their start and end apart: 78, of which 22 were waited for; matrix products, arithmetic and copies ran while one was open for 0% of the time, Pallas kernels for 11%

profile of v7, /device:TPU:0, one launch (start us, length us, event | category | flops | bytes accessed | tf_op | source)
XLA Modules:
  0.0 226.5 jit_solution(14283016955148703953)
XLA Ops:
  3.9 4.0 %collective-permute-start = (bf16[272,128]{1,0:T(8,128)(2,1)S(1)}, bf16[272,128]{1,0:T(8,128)(2,1)S(1)}, u32[]{:S(2)}, u32[]{:S(2)}) collective-permute-start(bf16[272,128]{1,0:T(8,128)(2,1)S(1)} %get-tuple-element.91), channel_id=1, source_target_pairs={{0,4},{1,5},{2,6},{3,7},{4,0},{5,1},{6,2},{7,3},{8,12},{9,13},{10,... | collective-permute-start | bytes 208904 | tf_op jit(solution)/shard_map/ppermute | solution.py:280
  9.5 1.8 collective-permute-start.3
  11.4 2.5 %collective-permute-start.4 = (bf16[272,128]{1,0:T(8,128)(2,1)S(1)}, bf16[272,128]{1,0:T(8,128)(2,1)S(1)}, u32[]{:S(2)}, u32[]{:S(2)}) collective-permute-start(bf16[272,128]{1,0:T(8,128)(2,1)S(1)} %get-tuple-element.99), channel_id=1, source_target_pairs={{0,6},{1,7},{2,4},{3,5},{4,2},{5,3},{6,0},{7,1},{8,14},{9,15},{10,... | collective-permute-start | bytes 208904 | tf_op jit(solution)/shard_map/ppermute | solution.py:280
  15.5 2.7 %collective-permute-start.6 = (bf16[272,128]{1,0:T(8,128)(2,1)S(1)}, bf16[272,128]{1,0:T(8,128)(2,1)S(1)}, u32[]{:S(2)}, u32[]{:S(2)}) collective-permute-start(bf16[272,128]{1,0:T(8,128)(2,1)S(1)} %get-tuple-element.101), channel_id=1, source_target_pairs={{0,7},{1,6},{2,5},{3,4},{4,3},{5,2},{6,1},{7,0},{8,15},{9,14},{10,... | collective-permute-start | bytes 208904 | tf_op jit(solution)/shard_map/ppermute | solution.py:280
  18.2 2.2 copy-done
  30.1 5.2 %collective-permute-done.11.__1_.rest_0_ = bf16[272,256]{1,0:T(8,128)(2,1)S(1)} collective-permute-done((bf16[272,256]{1,0:T(8,128)(2,1)S(1)}, bf16[272,256]{1,0:T(8,128)(2,1)S(1)}, u32[]{:S(2)}, u32[]{:S(2)}) %collective-permute-start.11) | collective-permute-done | bytes 139296 | tf_op jit(solution)/shard_map/ppermute | solution.py:280
  35.3 2.8 %collective-permute-start.16 = (bf16[272,256]{1,0:T(8,128)(2,1)S(1)}, bf16[272,256]{1,0:T(8,128)(2,1)S(1)}, u32[]{:S(2)}, u32[]{:S(2)}) collective-permute-start(bf16[272,256]{1,0:T(8,128)(2,1)S(1)} %gate.75.__2_), channel_id=1, source_target_pairs={{0,6},{1,7},{2,4},{3,5},{4,2},{5,3},{6,0},{7,1},{8,14},{9,15},{10,... | collective-permute-start | bytes 417800 | tf_op jit(solution)/shard_map/ppermute | solution.py:280
  40.7 2.7 %collective-permute-start.20 = (bf16[272,256]{1,0:T(8,128)(2,1)S(1)}, bf16[272,256]{1,0:T(8,128)(2,1)S(1)}, u32[]{:S(2)}, u32[]{:S(2)}) collective-permute-start(bf16[272,256]{1,0:T(8,128)(2,1)S(1)} %gate.78.__2_), channel_id=1, source_target_pairs={{0,7},{1,6},{2,5},{3,4},{4,3},{5,2},{6,1},{7,0},{8,15},{9,14},{10,... | collective-permute-start | bytes 417800 | tf_op jit(solution)/shard_map/ppermute | solution.py:280
  47.4 3.0 %collective-permute-start.17 = (bf16[272,256]{1,0:T(8,128)(2,1)S(1)}, bf16[272,256]{1,0:T(8,128)(2,1)S(1)}, u32[]{:S(2)}, u32[]{:S(2)}) collective-permute-start(bf16[272,256]{1,0:T(8,128)(2,1)S(1)} %gate.82.__2_), channel_id=1, source_target_pairs={{0,16},{1,17},{2,18},{3,19},{4,20},{5,21},{6,22},{7,23},{8,24},{9,... | collective-permute-start | bytes 417800 | tf_op jit(solution)/shard_map/ppermute | solution.py:280
  50.5 4.4 %collective-permute-start.24 = (bf16[272,256]{1,0:T(8,128)(2,1)S(1)}, bf16[272,256]{1,0:T(8,128)(2,1)S(1)}, u32[]{:S(2)}, u32[]{:S(2)}) collective-permute-start(bf16[272,256]{1,0:T(8,128)(2,1)S(1)} %gate.83.__2_), channel_id=1, source_target_pairs={{0,13},{1,12},{2,15},{3,14},{4,9},{5,8},{6,11},{7,10},{8,5},{9,4},... | collective-permute-start | bytes 417800 | tf_op jit(solution)/shard_map/ppermute | solution.py:280
  55.2 3.3 %collective-permute-start.22 = (bf16[272,256]{1,0:T(8,128)(2,1)S(1)}, bf16[272,256]{1,0:T(8,128)(2,1)S(1)}, u32[]{:S(2)}, u32[]{:S(2)}) collective-permute-start(bf16[272,256]{1,0:T(8,128)(2,1)S(1)} %gate.85.__2_), channel_id=1, source_target_pairs={{0,14},{1,15},{2,12},{3,13},{4,10},{5,11},{6,8},{7,9},{8,6},{9,7},... | collective-permute-start | bytes 417800 | tf_op jit(solution)/shard_map/ppermute | solution.py:280
  60.6 2.5 %collective-permute-start.28 = (bf16[272,256]{1,0:T(8,128)(2,1)S(1)}, bf16[272,256]{1,0:T(8,128)(2,1)S(1)}, u32[]{:S(2)}, u32[]{:S(2)}) collective-permute-start(bf16[272,256]{1,0:T(8,128)(2,1)S(1)} %gate.87.__2_), channel_id=1, source_target_pairs={{0,20},{1,21},{2,22},{3,23},{4,16},{5,17},{6,18},{7,19},{8,28},{9,... | collective-permute-start | bytes 417800 | tf_op jit(solution)/shard_map/ppermute | solution.py:280
  64.5 3.0 %collective-permute-start.26 = (bf16[272,256]{1,0:T(8,128)(2,1)S(1)}, bf16[272,256]{1,0:T(8,128)(2,1)S(1)}, u32[]{:S(2)}, u32[]{:S(2)}) collective-permute-start(bf16[272,256]{1,0:T(8,128)(2,1)S(1)} %gate.89.__2_), channel_id=1, source_target_pairs={{0,15},{1,14},{2,13},{3,12},{4,11},{5,10},{6,9},{7,8},{8,7},{9,6},... | collective-permute-start | bytes 417800 | tf_op jit(solution)/shard_map/ppermute | solution.py:280
  68.3 3.3 %collective-permute-done.21.__1_.rest_5_ = bf16[272,256]{1,0:T(8,128)(2,1)S(1)} collective-permute-done((bf16[272,256]{1,0:T(8,128)(2,1)S(1)}, bf16[272,256]{1,0:T(8,128)(2,1)S(1)}, u32[]{:S(2)}, u32[]{:S(2)}) %collective-permute-start.21) | collective-permute-done | bytes 139296 | tf_op jit(solution)/shard_map/ppermute | solution.py:280
  71.8 7.4 %collective-permute-done.28.__1_.rest_0_ = bf16[272,256]{1,0:T(8,128)(2,1)S(1)} collective-permute-done((bf16[272,256]{1,0:T(8,128)(2,1)S(1)}, bf16[272,256]{1,0:T(8,128)(2,1)S(1)}, u32[]{:S(2)}, u32[]{:S(2)}) %collective-permute-start.28) | collective-permute-done | bytes 139296 | tf_op jit(solution)/shard_map/ppermute | solution.py:280
  79.2 3.9 %collective-permute-start.34 = (bf16[272,256]{1,0:T(8,128)(2,1)S(1)}, bf16[272,256]{1,0:T(8,128)(2,1)S(1)}, u32[]{:S(2)}, u32[]{:S(2)}) collective-permute-start(bf16[272,256]{1,0:T(8,128)(2,1)S(1)} %gate.93.__2_), channel_id=1, source_target_pairs={{0,18},{1,19},{2,16},{3,17},{4,22},{5,23},{6,20},{7,21},{8,26},{9,... | collective-permute-start | bytes 417800 | tf_op jit(solution)/shard_map/ppermute | solution.py:280
  85.7 3.1 %combine.4 = (bf16[128,8192]{1,0:T(8,128)(2,1)}, bf16[272,256]{1,0:T(8,128)(2,1)S(1)}, bf16[272,256]{1,0:T(8,128)(2,1)S(1)}, bf16[272,256]{1,0:T(8,128)(2,1)S(1)...) custom-call(s32[2]{0:T(128)S(1)} %pad_add_fusion.1.at_ref.place_in_r, ...), custom_call_target="tpu_custom_call" | custom-call | flops 285212672 | bytes 3276800 | tf_op jit(solution)/shard_map/combine/pallas_call | solution.py:375
  88.8 3.0 %collective-permute-start.38 = (bf16[272,256]{1,0:T(8,128)(2,1)S(1)}, bf16[272,256]{1,0:T(8,128)(2,1)S(1)}, u32[]{:S(2)}, u32[]{:S(2)}) collective-permute-start(bf16[272,256]{1,0:T(8,128)(2,1)S(1)} %gate.96.__2_), channel_id=1, source_target_pairs={{0,19},{1,18},{2,17},{3,16},{4,23},{5,22},{6,21},{7,20},{8,27},{9,... | collective-permute-start | bytes 417800 | tf_op jit(solution)/shard_map/ppermute | solution.py:280
  94.1 2.3 collective-permute-done.38.__1_.rest_5_
  96.4 3.4 %collective-permute-start.40 = (bf16[272,256]{1,0:T(8,128)(2,1)S(1)}, bf16[272,256]{1,0:T(8,128)(2,1)S(1)}, u32[]{:S(2)}, u32[]{:S(2)}) collective-permute-start(bf16[272,256]{1,0:T(8,128)(2,1)S(1)} %gate.101.__2_), channel_id=1, source_target_pairs={{0,23},{1,22},{2,21},{3,20},{4,19},{5,18},{6,17},{7,16},{8,31},{9,... | collective-permute-start | bytes 417800 | tf_op jit(solution)/shard_map/ppermute | solution.py:280
  100.5 3.7 %collective-permute-done.37.__1_.refs_0_ = bf16[272,256]{1,0:T(8,128)(2,1)S(1)} collective-permute-done((bf16[272,256]{1,0:T(8,128)(2,1)S(1)}, bf16[272,256]{1,0:T(8,128)(2,1)S(1)}, u32[]{:S(2)}, u32[]{:S(2)}) %collective-permute-start.37) | collective-permute-done | bytes 139296 | tf_op jit(solution)/shard_map/ppermute | solution.py:280
  104.2 3.0 %collective-permute-start.44 = (bf16[272,256]{1,0:T(8,128)(2,1)S(1)}, bf16[272,256]{1,0:T(8,128)(2,1)S(1)}, u32[]{:S(2)}, u32[]{:S(2)}) collective-permute-start(bf16[272,256]{1,0:T(8,128)(2,1)S(1)} %gate.103.__2_), channel_id=1, source_target_pairs={{0,5},{1,4},{2,7},{3,6},{4,1},{5,0},{6,3},{7,2},{8,13},{9,12},{10,... | collective-permute-start | bytes 417800 | tf_op jit(solution)/shard_map/ppermute | solution.py:280
  110.8 5.0 %collective-permute-start.43 = (bf16[272,256]{1,0:T(8,128)(2,1)S(1)}, bf16[272,256]{1,0:T(8,128)(2,1)S(1)}, u32[]{:S(2)}, u32[]{:S(2)}) collective-permute-start(bf16[272,256]{1,0:T(8,128)(2,1)S(1)} %gate.107.__2_), channel_id=1, source_target_pairs={{0,29},{1,28},{2,31},{3,30},{4,25},{5,24},{6,27},{7,26},{8,21},{9,... | collective-permute-start | bytes 417800 | tf_op jit(solution)/shard_map/ppermute | solution.py:280
  115.8 2.3 %collective-permute-done.44.__1_.refs_2_ = bf16[272,256]{1,0:T(8,128)(2,1)S(1)} collective-permute-done((bf16[272,256]{1,0:T(8,128)(2,1)S(1)}, bf16[272,256]{1,0:T(8,128)(2,1)S(1)}, u32[]{:S(2)}, u32[]{:S(2)}) %collective-permute-start.44) | collective-permute-done | bytes 139296 | tf_op jit(solution)/shard_map/ppermute | solution.py:280
  119.6 4.1 %collective-permute-start.51 = (bf16[272,256]{1,0:T(8,128)(2,1)S(1)}, bf16[272,256]{1,0:T(8,128)(2,1)S(1)}, u32[]{:S(2)}, u32[]{:S(2)}) collective-permute-start(bf16[272,256]{1,0:T(8,128)(2,1)S(1)} %gate.110.__2_), channel_id=1, source_target_pairs={{0,3},{1,2},{2,1},{3,0},{4,7},{5,6},{6,5},{7,4},{8,11},{9,10},{10,... | collective-permute-start | bytes 417800 | tf_op jit(solution)/shard_map/ppermute | solution.py:280
  123.7 1.8 collective-permute-start.47
  125.5 4.5 %collective-permute-done.43.__1_.rest_2_ = bf16[272,256]{1,0:T(8,128)(2,1)S(1)} collective-permute-done((bf16[272,256]{1,0:T(8,128)(2,1)S(1)}, bf16[272,256]{1,0:T(8,128)(2,1)S(1)}, u32[]{:S(2)}, u32[]{:S(2)}) %collective-permute-start.43) | collective-permute-done | bytes 139296 | tf_op jit(solution)/shard_map/ppermute | solution.py:280
  130.5 7.1 %collective-permute-start.53 = (bf16[272,256]{1,0:T(8,128)(2,1)S(1)}, bf16[272,256]{1,0:T(8,128)(2,1)S(1)}, u32[]{:S(2)}, u32[]{:S(2)}) collective-permute-start(bf16[272,256]{1,0:T(8,128)(2,1)S(1)} %gate.113.__2_), channel_id=1, source_target_pairs={{0,7},{1,6},{2,5},{3,4},{4,3},{5,2},{6,1},{7,0},{8,15},{9,14},{10,... | collective-permute-start | bytes 417800 | tf_op jit(solution)/shard_map/ppermute | solution.py:280
  138.9 3.1 %combine.5 = (bf16[128,8192]{1,0:T(8,128)(2,1)}, bf16[272,256]{1,0:T(8,128)(2,1)S(1)}, bf16[272,256]{1,0:T(8,128)(2,1)S(1)}, bf16[272,256]{1,0:T(8,128)(2,1)S(1)...) custom-call(s32[2]{0:T(128)S(1)} %pad_add_fusion.1.at_ref.place_in_r, ...), custom_call_target="tpu_custom_call", output_to_operand_aliasing={{0}: (15, {})} | custom-call | flops 285212672 | bytes 3276800 | tf_op jit(solution)/shard_map/combine/pallas_call | solution.py:375
  142.0 3.1 %combine.6 = (bf16[128,8192]{1,0:T(8,128)(2,1)}, bf16[272,256]{1,0:T(8,128)(2,1)S(1)}, bf16[272,256]{1,0:T(8,128)(2,1)S(1)}, bf16[272,256]{1,0:T(8,128)(2,1)S(1)...) custom-call(s32[2]{0:T(128)S(1)} %pad_add_fusion.1.at_ref.place_in_r, ...), custom_call_target="tpu_custom_call", output_to_operand_aliasing={{0}: (15, {})} | custom-call | flops 285212672 | bytes 3276800 | tf_op jit(solution)/shard_map/combine/pallas_call | solution.py:375
  151.1 5.0 %collective-permute-start.60 = (bf16[272,256]{1,0:T(8,128)(2,1)S(1)}, bf16[272,256]{1,0:T(8,128)(2,1)S(1)}, u32[]{:S(2)}, u32[]{:S(2)}) collective-permute-start(bf16[272,256]{1,0:T(8,128)(2,1)S(1)} %gate.120.__2_), channel_id=1, source_target_pairs={{0,21},{1,20},{2,23},{3,22},{4,17},{5,16},{6,19},{7,18},{8,29},{9,... | collective-permute-start | bytes 417800 | tf_op jit(solution)/shard_map/ppermute | solution.py:280
  157.0 4.1 %collective-permute-start.59 = (bf16[272,256]{1,0:T(8,128)(2,1)S(1)}, bf16[272,256]{1,0:T(8,128)(2,1)S(1)}, u32[]{:S(2)}, u32[]{:S(2)}) collective-permute-start(bf16[272,256]{1,0:T(8,128)(2,1)S(1)} %gate.121.__2_), channel_id=1, source_target_pairs={{0,18},{1,19},{2,16},{3,17},{4,22},{5,23},{6,20},{7,21},{8,26},{9,... | collective-permute-start | bytes 417800 | tf_op jit(solution)/shard_map/ppermute | solution.py:280
  161.1 4.2 %collective-permute-start.58 = (bf16[272,256]{1,0:T(8,128)(2,1)S(1)}, bf16[272,256]{1,0:T(8,128)(2,1)S(1)}, u32[]{:S(2)}, u32[]{:S(2)}) collective-permute-start(bf16[272,256]{1,0:T(8,128)(2,1)S(1)} %gate.122.__2_), channel_id=1, source_target_pairs={{0,22},{1,23},{2,20},{3,21},{4,18},{5,19},{6,16},{7,17},{8,30},{9,... | collective-permute-start | bytes 417800 | tf_op jit(solution)/shard_map/ppermute | solution.py:280
  166.8 2.4 %collective-permute-start.66 = (bf16[272,256]{1,0:T(8,128)(2,1)S(1)}, bf16[272,256]{1,0:T(8,128)(2,1)S(1)}, u32[]{:S(2)}, u32[]{:S(2)}) collective-permute-start(bf16[272,256]{1,0:T(8,128)(2,1)S(1)} %gate.124.__2_), channel_id=1, source_target_pairs={{0,13},{1,12},{2,15},{3,14},{4,9},{5,8},{6,11},{7,10},{8,5},{9,4},... | collective-permute-start | bytes 417800 | tf_op jit(solution)/shard_map/ppermute | solution.py:280
  169.2 3.3 %collective-permute-done.60.__1_.refs_10_ = bf16[272,256]{1,0:T(8,128)(2,1)S(1)} collective-permute-done((bf16[272,256]{1,0:T(8,128)(2,1)S(1)}, bf16[272,256]{1,0:T(8,128)(2,1)S(1)}, u32[]{:S(2)}, u32[]{:S(2)}) %collective-permute-start.60) | collective-permute-done | bytes 139296 | tf_op jit(solution)/shard_map/ppermute | solution.py:280
  172.4 3.1 %combine.7 = (bf16[128,8192]{1,0:T(8,128)(2,1)}, bf16[272,256]{1,0:T(8,128)(2,1)S(1)}, bf16[272,256]{1,0:T(8,128)(2,1)S(1)}, bf16[272,256]{1,0:T(8,128)(2,1)S(1)...) custom-call(s32[2]{0:T(128)S(1)} %pad_add_fusion.1.at_ref.place_in_r, ...), custom_call_target="tpu_custom_call", output_to_operand_aliasing={{0}: (15, {})} | custom-call | flops 285212672 | bytes 3276800 | tf_op jit(solution)/shard_map/combine/pallas_call | solution.py:375
  175.5 2.4 %collective-permute-start.64 = (bf16[272,256]{1,0:T(8,128)(2,1)S(1)}, bf16[272,256]{1,0:T(8,128)(2,1)S(1)}, u32[]{:S(2)}, u32[]{:S(2)}) collective-permute-start(bf16[272,256]{1,0:T(8,128)(2,1)S(1)} %gate.126.__2_), channel_id=1, source_target_pairs={{0,23},{1,22},{2,21},{3,20},{4,19},{5,18},{6,17},{7,16},{8,31},{9,... | collective-permute-start | bytes 417800 | tf_op jit(solution)/shard_map/ppermute | solution.py:280
  177.9 1.8 collective-permute-start.63
  180.6 6.4 %collective-permute-done.66.__1_.refs_18_ = bf16[272,256]{1,0:T(8,128)(2,1)S(1)} collective-permute-done((bf16[272,256]{1,0:T(8,128)(2,1)S(1)}, bf16[272,256]{1,0:T(8,128)(2,1)S(1)}, u32[]{:S(2)}, u32[]{:S(2)}) %collective-permute-start.66) | collective-permute-done | bytes 139296 | tf_op jit(solution)/shard_map/ppermute | solution.py:280
  187.9 1.9 collective-permute-start.69
  189.8 2.6 %collective-permute-start.68 = (bf16[272,256]{1,0:T(8,128)(2,1)S(1)}, bf16[272,256]{1,0:T(8,128)(2,1)S(1)}, u32[]{:S(2)}, u32[]{:S(2)}) collective-permute-start(bf16[272,256]{1,0:T(8,128)(2,1)S(1)} %gate.132.__2_), channel_id=1, source_target_pairs={{0,29},{1,28},{2,31},{3,30},{4,25},{5,24},{6,27},{7,26},{8,21},{9,... | collective-permute-start | bytes 417800 | tf_op jit(solution)/shard_map/ppermute | solution.py:280
  192.5 2.2 collective-permute-done.62.__1_.refs_24_
  196.2 4.0 %collective-permute-start.73 = (bf16[272,256]{1,0:T(8,128)(2,1)S(1)}, bf16[272,256]{1,0:T(8,128)(2,1)S(1)}, u32[]{:S(2)}, u32[]{:S(2)}) collective-permute-start(bf16[272,256]{1,0:T(8,128)(2,1)S(1)} %gate.134.__2_), channel_id=1, source_target_pairs={{0,15},{1,14},{2,13},{3,12},{4,11},{5,10},{6,9},{7,8},{8,7},{9,6},... | collective-permute-start | bytes 417800 | tf_op jit(solution)/shard_map/ppermute | solution.py:280
  202.3 3.4 %collective-permute-done.68.__1_.refs_26_ = bf16[272,256]{1,0:T(8,128)(2,1)S(1)} collective-permute-done((bf16[272,256]{1,0:T(8,128)(2,1)S(1)}, bf16[272,256]{1,0:T(8,128)(2,1)S(1)}, u32[]{:S(2)}, u32[]{:S(2)}) %collective-permute-start.68) | collective-permute-done | bytes 139296 | tf_op jit(solution)/shard_map/ppermute | solution.py:280
  206.2 7.8 %collective-permute-start.72 = (bf16[272,256]{1,0:T(8,128)(2,1)S(1)}, bf16[272,256]{1,0:T(8,128)(2,1)S(1)}, u32[]{:S(2)}, u32[]{:S(2)}) collective-permute-start(bf16[272,256]{1,0:T(8,128)(2,1)S(1)} %gate.138.__2_), channel_id=1, source_target_pairs={{0,30},{1,31},{2,28},{3,29},{4,26},{5,27},{6,24},{7,25},{8,22},{9,... | collective-permute-start | bytes 417800 | tf_op jit(solution)/shard_map/ppermute | solution.py:280
  214.9 4.6 %gradient.2.refs_4_ = f32[1024,2048]{1,0:T(8,128)S(1)} custom-call(bf16[1024,952]{1,0:T(8,128)(2,1)S(1)} %turn.3.codes_ref, bf16[272,256]{1,0:T(8,128)(2,1)S(1)} %collective-permute-done.37.__1_.refs_0_, bf16[272,256]{1,0:T(8,128)(2,1)S(1)} %collective-permute-done.36.__1_.refs_1_, bf16[272,256]{1,0:T(8,128)(2,1)S(1)} %collective-permute-done.44.__1_.refs_2_, ...), custom_call_target="tpu_custom_call" | custom-call | flops 3992977408 | bytes 8388608 | tf_op jit(solution)/shard_map/gradient/pallas_call | solution.py:410
  219.5 4.0 %collective-permute-done.74.refs_1_ = bf16[272,256]{1,0:T(8,128)(2,1)S(1)} collective-permute-done((bf16[272,256]{1,0:T(8,128)(2,1)S(1)}, bf16[272,256]{1,0:T(8,128)(2,1)S(1)}, u32[]{:S(2)}, u32[]{:S(2)}) %collective-permute-start.74) | collective-permute-done | bytes 139296 | tf_op jit(solution)/shard_map/ppermute | solution.py:280
  223.5 2.8 %gradient.3 = bf16[1024,2048]{1,0:T(8,128)(2,1)} custom-call(bf16[1024,136]{1,0:T(8,128)(2,1)S(1)} %turn.2.codes_ref, bf16[272,256]{1,0:T(8,128)(2,1)S(1)} %collective-permute-done.72.refs_0_, bf16[272,256]{1,0:T(8,128)(2,1)S(1)} %collective-permute-done.74.refs_1_, bf16[272,256]{1,0:T(8,128)(2,1)S(1)} %collective-permute-done.75.refs_2_, ...), custom_call_target="tpu_custom_call" | custom-call | flops 570425344 | bytes 8388608 | tf_op jit(solution)/shard_map/gradient/pallas_call | solution.py:410
  (205 shorter events, 54.9 us)
Async XLA Ops:
  22.8 12.5 %collective-permute-start.11 = (bf16[272,256]{1,0:T(8,128)(2,1)S(1)}, bf16[272,256]{1,0:T(8,128)(2,1)S(1)}, u32[]{:S(2)}, u32[]{:S(2)}) collective-permute-start(bf16[272,256]{1,0:T(8,128)(2,1)S(1)} %gate.70.__1_), channel_id=1, source_target_pairs={{0,4},{1,5},{2,6},{3,7},{4,0},{5,1},{6,2},{7,3},{8,12},{9,13},{10,... | collective-permute-start | bytes 417800 | tf_op jit(solution)/shard_map/ppermute | solution.py:280
  24.6 13.5 %collective-permute-start.10 = (bf16[272,256]{1,0:T(8,128)(2,1)S(1)}, bf16[272,256]{1,0:T(8,128)(2,1)S(1)}, u32[]{:S(2)}, u32[]{:S(2)}) collective-permute-start(bf16[272,256]{1,0:T(8,128)(2,1)S(1)} %gate.71.refs_8_.__1_.refs_4_), channel_id=1, source_target_pairs={{0,1},{1,0},{2,3},{3,2},{4,5},{5,4},{6,7},{7,6},{8,9},{9,8},{10,11... | collective-permute-start | bytes 417800 | tf_op jit(solution)/shard_map/ppermute | solution.py:280
  25.7 13.6 %collective-permute-start.9 = (bf16[272,256]{1,0:T(8,128)(2,1)S(1)}, bf16[272,256]{1,0:T(8,128)(2,1)S(1)}, u32[]{:S(2)}, u32[]{:S(2)}) collective-permute-start(bf16[272,256]{1,0:T(8,128)(2,1)S(1)} %gate.72.__1_), channel_id=1, source_target_pairs={{0,5},{1,4},{2,7},{3,6},{4,1},{5,0},{6,3},{7,2},{8,13},{9,12},{10,... | collective-permute-start | bytes 417800 | tf_op jit(solution)/shard_map/ppermute | solution.py:280
  27.3 13.5 %collective-permute-start.13 = (bf16[272,256]{1,0:T(8,128)(2,1)S(1)}, bf16[272,256]{1,0:T(8,128)(2,1)S(1)}, u32[]{:S(2)}, u32[]{:S(2)}) collective-permute-start(bf16[272,256]{1,0:T(8,128)(2,1)S(1)} %gate.73.__2_), channel_id=1, source_target_pairs={{0,2},{1,3},{2,0},{3,1},{4,6},{5,7},{6,4},{7,5},{8,10},{9,11},{10,... | collective-permute-start | bytes 417800 | tf_op jit(solution)/shard_map/ppermute | solution.py:280
  28.5 16.4 %collective-permute-start.8 = (bf16[272,256]{1,0:T(8,128)(2,1)S(1)}, bf16[272,256]{1,0:T(8,128)(2,1)S(1)}, u32[]{:S(2)}, u32[]{:S(2)}) collective-permute-start(bf16[272,256]{1,0:T(8,128)(2,1)S(1)} %gate.74.__2_), channel_id=1, source_target_pairs={{0,16},{1,17},{2,18},{3,19},{4,20},{5,21},{6,22},{7,23},{8,24},{9,... | collective-permute-start | bytes 417800 | tf_op jit(solution)/shard_map/ppermute | solution.py:280
  50.5 12.6 %collective-permute-start.24 = (bf16[272,256]{1,0:T(8,128)(2,1)S(1)}, bf16[272,256]{1,0:T(8,128)(2,1)S(1)}, u32[]{:S(2)}, u32[]{:S(2)}) collective-permute-start(bf16[272,256]{1,0:T(8,128)(2,1)S(1)} %gate.83.__2_), channel_id=1, source_target_pairs={{0,13},{1,12},{2,15},{3,14},{4,9},{5,8},{6,11},{7,10},{8,5},{9,4},... | collective-permute-start | bytes 417800 | tf_op jit(solution)/shard_map/ppermute | solution.py:280
  55.2 12.8 %collective-permute-start.22 = (bf16[272,256]{1,0:T(8,128)(2,1)S(1)}, bf16[272,256]{1,0:T(8,128)(2,1)S(1)}, u32[]{:S(2)}, u32[]{:S(2)}) collective-permute-start(bf16[272,256]{1,0:T(8,128)(2,1)S(1)} %gate.85.__2_), channel_id=1, source_target_pairs={{0,14},{1,15},{2,12},{3,13},{4,10},{5,11},{6,8},{7,9},{8,6},{9,7},... | collective-permute-start | bytes 417800 | tf_op jit(solution)/shard_map/ppermute | solution.py:280
  58.5 13.1 %collective-permute-start.21 = (bf16[272,256]{1,0:T(8,128)(2,1)S(1)}, bf16[272,256]{1,0:T(8,128)(2,1)S(1)}, u32[]{:S(2)}, u32[]{:S(2)}) collective-permute-start(bf16[272,256]{1,0:T(8,128)(2,1)S(1)} %gate.86.__2_), channel_id=1, source_target_pairs={{0,11},{1,10},{2,9},{3,8},{4,15},{5,14},{6,13},{7,12},{8,3},{9,2},... | collective-permute-start | bytes 417800 | tf_op jit(solution)/shard_map/ppermute | solution.py:280
  60.6 18.6 %collective-permute-start.28 = (bf16[272,256]{1,0:T(8,128)(2,1)S(1)}, bf16[272,256]{1,0:T(8,128)(2,1)S(1)}, u32[]{:S(2)}, u32[]{:S(2)}) collective-permute-start(bf16[272,256]{1,0:T(8,128)(2,1)S(1)} %gate.87.__2_), channel_id=1, source_target_pairs={{0,20},{1,21},{2,22},{3,23},{4,16},{5,17},{6,18},{7,19},{8,28},{9,... | collective-permute-start | bytes 417800 | tf_op jit(solution)/shard_map/ppermute | solution.py:280
  63.1 16.1 %collective-permute-start.27 = (bf16[272,256]{1,0:T(8,128)(2,1)S(1)}, bf16[272,256]{1,0:T(8,128)(2,1)S(1)}, u32[]{:S(2)}, u32[]{:S(2)}) collective-permute-start(bf16[272,256]{1,0:T(8,128)(2,1)S(1)} %gate.88.__2_), channel_id=1, source_target_pairs={{0,17},{1,16},{2,19},{3,18},{4,21},{5,20},{6,23},{7,22},{8,25},{9,... | collective-permute-start | bytes 417800 | tf_op jit(solution)/shard_map/ppermute | solution.py:280
  64.5 18.6 %collective-permute-start.26 = (bf16[272,256]{1,0:T(8,128)(2,1)S(1)}, bf16[272,256]{1,0:T(8,128)(2,1)S(1)}, u32[]{:S(2)}, u32[]{:S(2)}) collective-permute-start(bf16[272,256]{1,0:T(8,128)(2,1)S(1)} %gate.89.__2_), channel_id=1, source_target_pairs={{0,15},{1,14},{2,13},{3,12},{4,11},{5,10},{6,9},{7,8},{8,7},{9,6},... | collective-permute-start | bytes 417800 | tf_op jit(solution)/shard_map/ppermute | solution.py:280
  68.0 15.1 %collective-permute-start.31 = (bf16[272,256]{1,0:T(8,128)(2,1)S(1)}, bf16[272,256]{1,0:T(8,128)(2,1)S(1)}, u32[]{:S(2)}, u32[]{:S(2)}) collective-permute-start(bf16[272,256]{1,0:T(8,128)(2,1)S(1)} %gate.90.__2_), channel_id=1, source_target_pairs={{0,8},{1,9},{2,10},{3,11},{4,12},{5,13},{6,14},{7,15},{8,0},{9,1},... | collective-permute-start | bytes 417800 | tf_op jit(solution)/shard_map/ppermute | solution.py:280
  71.6 17.1 %collective-permute-start.25 = (bf16[272,256]{1,0:T(8,128)(2,1)S(1)}, bf16[272,256]{1,0:T(8,128)(2,1)S(1)}, u32[]{:S(2)}, u32[]{:S(2)}) collective-permute-start(bf16[272,256]{1,0:T(8,128)(2,1)S(1)} %gate.91.__2_), channel_id=1, source_target_pairs={{0,8},{1,9},{2,10},{3,11},{4,12},{5,13},{6,14},{7,15},{8,0},{9,1},... | collective-permute-start | bytes 417800 | tf_op jit(solution)/shard_map/ppermute | solution.py:280
  79.2 12.5 %collective-permute-start.30 = (bf16[272,256]{1,0:T(8,128)(2,1)S(1)}, bf16[272,256]{1,0:T(8,128)(2,1)S(1)}, u32[]{:S(2)}, u32[]{:S(2)}) collective-permute-start(bf16[272,256]{1,0:T(8,128)(2,1)S(1)} %gate.92.__2_), channel_id=1, source_target_pairs={{0,21},{1,20},{2,23},{3,22},{4,17},{5,16},{6,19},{7,18},{8,29},{9,... | collective-permute-start | bytes 417800 | tf_op jit(solution)/shard_map/ppermute | solution.py:280
  79.2 13.3 %collective-permute-start.34 = (bf16[272,256]{1,0:T(8,128)(2,1)S(1)}, bf16[272,256]{1,0:T(8,128)(2,1)S(1)}, u32[]{:S(2)}, u32[]{:S(2)}) collective-permute-start(bf16[272,256]{1,0:T(8,128)(2,1)S(1)} %gate.93.__2_), channel_id=1, source_target_pairs={{0,18},{1,19},{2,16},{3,17},{4,22},{5,23},{6,20},{7,21},{8,26},{9,... | collective-permute-start | bytes 417800 | tf_op jit(solution)/shard_map/ppermute | solution.py:280
  92.8 14.4 %collective-permute-start.36 = (bf16[272,256]{1,0:T(8,128)(2,1)S(1)}, bf16[272,256]{1,0:T(8,128)(2,1)S(1)}, u32[]{:S(2)}, u32[]{:S(2)}) collective-permute-start(bf16[272,256]{1,0:T(8,128)(2,1)S(1)} %gate.99.__2_), channel_id=1, source_target_pairs={{0,1},{1,0},{2,3},{3,2},{4,5},{5,4},{6,7},{7,6},{8,9},{9,8},{10,11... | collective-permute-start | bytes 417800 | tf_op jit(solution)/shard_map/ppermute | solution.py:280
  94.1 13.1 %collective-permute-start.35 = (bf16[272,256]{1,0:T(8,128)(2,1)S(1)}, bf16[272,256]{1,0:T(8,128)(2,1)S(1)}, u32[]{:S(2)}, u32[]{:S(2)}) collective-permute-start(bf16[272,256]{1,0:T(8,128)(2,1)S(1)} %gate.100.__2_), channel_id=1, source_target_pairs={{0,8},{1,9},{2,10},{3,11},{4,12},{5,13},{6,14},{7,15},{8,0},{9,1},... | collective-permute-start | bytes 417800 | tf_op jit(solution)/shard_map/ppermute | solution.py:280
  96.4 13.3 %collective-permute-start.40 = (bf16[272,256]{1,0:T(8,128)(2,1)S(1)}, bf16[272,256]{1,0:T(8,128)(2,1)S(1)}, u32[]{:S(2)}, u32[]{:S(2)}) collective-permute-start(bf16[272,256]{1,0:T(8,128)(2,1)S(1)} %gate.101.__2_), channel_id=1, source_target_pairs={{0,23},{1,22},{2,21},{3,20},{4,19},{5,18},{6,17},{7,16},{8,31},{9,... | collective-permute-start | bytes 417800 | tf_op jit(solution)/shard_map/ppermute | solution.py:280
  104.2 13.9 %collective-permute-start.44 = (bf16[272,256]{1,0:T(8,128)(2,1)S(1)}, bf16[272,256]{1,0:T(8,128)(2,1)S(1)}, u32[]{:S(2)}, u32[]{:S(2)}) collective-permute-start(bf16[272,256]{1,0:T(8,128)(2,1)S(1)} %gate.103.__2_), channel_id=1, source_target_pairs={{0,5},{1,4},{2,7},{3,6},{4,1},{5,0},{6,3},{7,2},{8,13},{9,12},{10,... | collective-permute-start | bytes 417800 | tf_op jit(solution)/shard_map/ppermute | solution.py:280
  109.7 14.1 %collective-permute-start.41 = (bf16[272,256]{1,0:T(8,128)(2,1)S(1)}, bf16[272,256]{1,0:T(8,128)(2,1)S(1)}, u32[]{:S(2)}, u32[]{:S(2)}) collective-permute-start(bf16[272,256]{1,0:T(8,128)(2,1)S(1)} %gate.106.__2_), channel_id=1, source_target_pairs={{0,25},{1,24},{2,27},{3,26},{4,29},{5,28},{6,31},{7,30},{8,17},{9,... | collective-permute-start | bytes 417800 | tf_op jit(solution)/shard_map/ppermute | solution.py:280
  110.8 19.2 %collective-permute-start.43 = (bf16[272,256]{1,0:T(8,128)(2,1)S(1)}, bf16[272,256]{1,0:T(8,128)(2,1)S(1)}, u32[]{:S(2)}, u32[]{:S(2)}) collective-permute-start(bf16[272,256]{1,0:T(8,128)(2,1)S(1)} %gate.107.__2_), channel_id=1, source_target_pairs={{0,29},{1,28},{2,31},{3,30},{4,25},{5,24},{6,27},{7,26},{8,21},{9,... | collective-permute-start | bytes 417800 | tf_op jit(solution)/shard_map/ppermute | solution.py:280
  118.1 12.4 %collective-permute-start.45 = (bf16[272,256]{1,0:T(8,128)(2,1)S(1)}, bf16[272,256]{1,0:T(8,128)(2,1)S(1)}, u32[]{:S(2)}, u32[]{:S(2)}) collective-permute-start(bf16[272,256]{1,0:T(8,128)(2,1)S(1)} %gate.108.__2_), channel_id=1, source_target_pairs={{0,26},{1,27},{2,24},{3,25},{4,30},{5,31},{6,28},{7,29},{8,18},{9,... | collective-permute-start | bytes 417800 | tf_op jit(solution)/shard_map/ppermute | solution.py:280
  118.1 19.5 %collective-permute-start.49 = (bf16[272,256]{1,0:T(8,128)(2,1)S(1)}, bf16[272,256]{1,0:T(8,128)(2,1)S(1)}, u32[]{:S(2)}, u32[]{:S(2)}) collective-permute-start(bf16[272,256]{1,0:T(8,128)(2,1)S(1)} %gate.109.__2_), channel_id=1, source_target_pairs={{0,6},{1,7},{2,4},{3,5},{4,2},{5,3},{6,0},{7,1},{8,14},{9,15},{10,... | collective-permute-start | bytes 417800 | tf_op jit(solution)/shard_map/ppermute | solution.py:280
  119.6 18.1 %collective-permute-start.51 = (bf16[272,256]{1,0:T(8,128)(2,1)S(1)}, bf16[272,256]{1,0:T(8,128)(2,1)S(1)}, u32[]{:S(2)}, u32[]{:S(2)}) collective-permute-start(bf16[272,256]{1,0:T(8,128)(2,1)S(1)} %gate.110.__2_), channel_id=1, source_target_pairs={{0,3},{1,2},{2,1},{3,0},{4,7},{5,6},{6,5},{7,4},{8,11},{9,10},{10,... | collective-permute-start | bytes 417800 | tf_op jit(solution)/shard_map/ppermute | solution.py:280
  123.7 21.3 %collective-permute-start.47 = (bf16[272,256]{1,0:T(8,128)(2,1)S(1)}, bf16[272,256]{1,0:T(8,128)(2,1)S(1)}, u32[]{:S(2)}, u32[]{:S(2)}) collective-permute-start(bf16[272,256]{1,0:T(8,128)(2,1)S(1)} %gate.111.__2_), channel_id=1, source_target_pairs={{0,30},{1,31},{2,28},{3,29},{4,26},{5,27},{6,24},{7,25},{8,22},{9,... | collective-permute-start | bytes 417800 | tf_op jit(solution)/shard_map/ppermute | solution.py:280
  130.0 17.8 %collective-permute-start.48 = (bf16[272,256]{1,0:T(8,128)(2,1)S(1)}, bf16[272,256]{1,0:T(8,128)(2,1)S(1)}, u32[]{:S(2)}, u32[]{:S(2)}) collective-permute-start(bf16[272,256]{1,0:T(8,128)(2,1)S(1)} %gate.112.__2_), channel_id=1, source_target_pairs={{0,27},{1,26},{2,25},{3,24},{4,31},{5,30},{6,29},{7,28},{8,19},{9,... | collective-permute-start | bytes 417800 | tf_op jit(solution)/shard_map/ppermute | solution.py:280
  130.5 18.2 %collective-permute-start.53 = (bf16[272,256]{1,0:T(8,128)(2,1)S(1)}, bf16[272,256]{1,0:T(8,128)(2,1)S(1)}, u32[]{:S(2)}, u32[]{:S(2)}) collective-permute-start(bf16[272,256]{1,0:T(8,128)(2,1)S(1)} %gate.113.__2_), channel_id=1, source_target_pairs={{0,7},{1,6},{2,5},{3,4},{4,3},{5,2},{6,1},{7,0},{8,15},{9,14},{10,... | collective-permute-start | bytes 417800 | tf_op jit(solution)/shard_map/ppermute | solution.py:280
  137.6 12.5 %collective-permute-start.50 = (bf16[272,256]{1,0:T(8,128)(2,1)S(1)}, bf16[272,256]{1,0:T(8,128)(2,1)S(1)}, u32[]{:S(2)}, u32[]{:S(2)}) collective-permute-start(bf16[272,256]{1,0:T(8,128)(2,1)S(1)} %gate.114.__2_), channel_id=1, source_target_pairs={{0,31},{1,30},{2,29},{3,28},{4,27},{5,26},{6,25},{7,24},{8,23},{9,... | collective-permute-start | bytes 417800 | tf_op jit(solution)/shard_map/ppermute | solution.py:280
  137.7 13.5 %collective-permute-start.52 = (bf16[272,256]{1,0:T(8,128)(2,1)S(1)}, bf16[272,256]{1,0:T(8,128)(2,1)S(1)}, u32[]{:S(2)}, u32[]{:S(2)}) collective-permute-start(bf16[272,256]{1,0:T(8,128)(2,1)S(1)} %gate.115.__2_), channel_id=1, source_target_pairs={{0,24},{1,25},{2,26},{3,27},{4,28},{5,29},{6,30},{7,31},{8,16},{9,... | collective-permute-start | bytes 417800 | tf_op jit(solution)/shard_map/ppermute | solution.py:280
  147.8 13.3 %collective-permute-start.55 = (bf16[272,256]{1,0:T(8,128)(2,1)S(1)}, bf16[272,256]{1,0:T(8,128)(2,1)S(1)}, u32[]{:S(2)}, u32[]{:S(2)}) collective-permute-start(bf16[272,256]{1,0:T(8,128)(2,1)S(1)} %gate.117.__2_), channel_id=1, source_target_pairs={{0,17},{1,16},{2,19},{3,18},{4,21},{5,20},{6,23},{7,22},{8,25},{9,... | collective-permute-start | bytes 417800 | tf_op jit(solution)/shard_map/ppermute | solution.py:280
  148.7 16.9 %collective-permute-start.54 = (bf16[272,256]{1,0:T(8,128)(2,1)S(1)}, bf16[272,256]{1,0:T(8,128)(2,1)S(1)}, u32[]{:S(2)}, u32[]{:S(2)}) collective-permute-start(bf16[272,256]{1,0:T(8,128)(2,1)S(1)} %gate.118.__2_), channel_id=1, source_target_pairs={{0,12},{1,13},{2,14},{3,15},{4,8},{5,9},{6,10},{7,11},{8,4},{9,5},... | collective-permute-start | bytes 417800 | tf_op jit(solution)/shard_map/ppermute | solution.py:280
  150.2 16.6 %collective-permute-start.61 = (bf16[272,256]{1,0:T(8,128)(2,1)S(1)}, bf16[272,256]{1,0:T(8,128)(2,1)S(1)}, u32[]{:S(2)}, u32[]{:S(2)}) collective-permute-start(bf16[272,256]{1,0:T(8,128)(2,1)S(1)} %gate.119.__2_), channel_id=1, source_target_pairs={{0,9},{1,8},{2,11},{3,10},{4,13},{5,12},{6,15},{7,14},{8,1},{9,0},... | collective-permute-start | bytes 417800 | tf_op jit(solution)/shard_map/ppermute | solution.py:280
  151.1 21.3 %collective-permute-start.60 = (bf16[272,256]{1,0:T(8,128)(2,1)S(1)}, bf16[272,256]{1,0:T(8,128)(2,1)S(1)}, u32[]{:S(2)}, u32[]{:S(2)}) collective-permute-start(bf16[272,256]{1,0:T(8,128)(2,1)S(1)} %gate.120.__2_), channel_id=1, source_target_pairs={{0,21},{1,20},{2,23},{3,22},{4,17},{5,16},{6,19},{7,18},{8,29},{9,... | collective-permute-start | bytes 417800 | tf_op jit(solution)/shard_map/ppermute | solution.py:280
  157.0 18.5 %collective-permute-start.59 = (bf16[272,256]{1,0:T(8,128)(2,1)S(1)}, bf16[272,256]{1,0:T(8,128)(2,1)S(1)}, u32[]{:S(2)}, u32[]{:S(2)}) collective-permute-start(bf16[272,256]{1,0:T(8,128)(2,1)S(1)} %gate.121.__2_), channel_id=1, source_target_pairs={{0,18},{1,19},{2,16},{3,17},{4,22},{5,23},{6,20},{7,21},{8,26},{9,... | collective-permute-start | bytes 417800 | tf_op jit(solution)/shard_map/ppermute | solution.py:280
  161.1 16.8 %collective-permute-start.58 = (bf16[272,256]{1,0:T(8,128)(2,1)S(1)}, bf16[272,256]{1,0:T(8,128)(2,1)S(1)}, u32[]{:S(2)}, u32[]{:S(2)}) collective-permute-start(bf16[272,256]{1,0:T(8,128)(2,1)S(1)} %gate.122.__2_), channel_id=1, source_target_pairs={{0,22},{1,23},{2,20},{3,21},{4,18},{5,19},{6,16},{7,17},{8,30},{9,... | collective-permute-start | bytes 417800 | tf_op jit(solution)/shard_map/ppermute | solution.py:280
  165.7 14.1 %collective-permute-start.57 = (bf16[272,256]{1,0:T(8,128)(2,1)S(1)}, bf16[272,256]{1,0:T(8,128)(2,1)S(1)}, u32[]{:S(2)}, u32[]{:S(2)}) collective-permute-start(bf16[272,256]{1,0:T(8,128)(2,1)S(1)} %gate.123.__2_), channel_id=1, source_target_pairs={{0,19},{1,18},{2,17},{3,16},{4,23},{5,22},{6,21},{7,20},{8,27},{9,... | collective-permute-start | bytes 417800 | tf_op jit(solution)/shard_map/ppermute | solution.py:280
  166.8 20.3 %collective-permute-start.66 = (bf16[272,256]{1,0:T(8,128)(2,1)S(1)}, bf16[272,256]{1,0:T(8,128)(2,1)S(1)}, u32[]{:S(2)}, u32[]{:S(2)}) collective-permute-start(bf16[272,256]{1,0:T(8,128)(2,1)S(1)} %gate.124.__2_), channel_id=1, source_target_pairs={{0,13},{1,12},{2,15},{3,14},{4,9},{5,8},{6,11},{7,10},{8,5},{9,4},... | collective-permute-start | bytes 417800 | tf_op jit(solution)/shard_map/ppermute | solution.py:280
  172.4 14.6 %collective-permute-start.65 = (bf16[272,256]{1,0:T(8,128)(2,1)S(1)}, bf16[272,256]{1,0:T(8,128)(2,1)S(1)}, u32[]{:S(2)}, u32[]{:S(2)}) collective-permute-start(bf16[272,256]{1,0:T(8,128)(2,1)S(1)} %gate.125.__2_), channel_id=1, source_target_pairs={{0,10},{1,11},{2,8},{3,9},{4,14},{5,15},{6,12},{7,13},{8,2},{9,3},... | collective-permute-start | bytes 417800 | tf_op jit(solution)/shard_map/ppermute | solution.py:280
  175.5 12.4 %collective-permute-start.64 = (bf16[272,256]{1,0:T(8,128)(2,1)S(1)}, bf16[272,256]{1,0:T(8,128)(2,1)S(1)}, u32[]{:S(2)}, u32[]{:S(2)}) collective-permute-start(bf16[272,256]{1,0:T(8,128)(2,1)S(1)} %gate.126.__2_), channel_id=1, source_target_pairs={{0,23},{1,22},{2,21},{3,20},{4,19},{5,18},{6,17},{7,16},{8,31},{9,... | collective-permute-start | bytes 417800 | tf_op jit(solution)/shard_map/ppermute | solution.py:280
  179.7 14.9 %collective-permute-start.62 = (bf16[272,256]{1,0:T(8,128)(2,1)S(1)}, bf16[272,256]{1,0:T(8,128)(2,1)S(1)}, u32[]{:S(2)}, u32[]{:S(2)}) collective-permute-start(bf16[272,256]{1,0:T(8,128)(2,1)S(1)} %gate.128.__2_), channel_id=1, source_target_pairs={{0,28},{1,29},{2,30},{3,31},{4,24},{5,25},{6,26},{7,27},{8,20},{9,... | collective-permute-start | bytes 417800 | tf_op jit(solution)/shard_map/ppermute | solution.py:280
  187.0 13.1 %collective-permute-start.70 = (bf16[272,256]{1,0:T(8,128)(2,1)S(1)}, bf16[272,256]{1,0:T(8,128)(2,1)S(1)}, u32[]{:S(2)}, u32[]{:S(2)}) collective-permute-start(bf16[272,256]{1,0:T(8,128)(2,1)S(1)} %gate.130.__2_), channel_id=1, source_target_pairs={{0,14},{1,15},{2,12},{3,13},{4,10},{5,11},{6,8},{7,9},{8,6},{9,7},... | collective-permute-start | bytes 417800 | tf_op jit(solution)/shard_map/ppermute | solution.py:280
  187.9 13.2 %collective-permute-start.69 = (bf16[272,256]{1,0:T(8,128)(2,1)S(1)}, bf16[272,256]{1,0:T(8,128)(2,1)S(1)}, u32[]{:S(2)}, u32[]{:S(2)}) collective-permute-start(bf16[272,256]{1,0:T(8,128)(2,1)S(1)} %gate.131.__2_), channel_id=1, source_target_pairs={{0,11},{1,10},{2,9},{3,8},{4,15},{5,14},{6,13},{7,12},{8,3},{9,2},... | collective-permute-start | bytes 417800 | tf_op jit(solution)/shard_map/ppermute | solution.py:280
  189.8 15.9 %collective-permute-start.68 = (bf16[272,256]{1,0:T(8,128)(2,1)S(1)}, bf16[272,256]{1,0:T(8,128)(2,1)S(1)}, u32[]{:S(2)}, u32[]{:S(2)}) collective-permute-start(bf16[272,256]{1,0:T(8,128)(2,1)S(1)} %gate.132.__2_), channel_id=1, source_target_pairs={{0,29},{1,28},{2,31},{3,30},{4,25},{5,24},{6,27},{7,26},{8,21},{9,... | collective-permute-start | bytes 417800 | tf_op jit(solution)/shard_map/ppermute | solution.py:280
  196.2 17.9 %collective-permute-start.73 = (bf16[272,256]{1,0:T(8,128)(2,1)S(1)}, bf16[272,256]{1,0:T(8,128)(2,1)S(1)}, u32[]{:S(2)}, u32[]{:S(2)}) collective-permute-start(bf16[272,256]{1,0:T(8,128)(2,1)S(1)} %gate.134.__2_), channel_id=1, source_target_pairs={{0,15},{1,14},{2,13},{3,12},{4,11},{5,10},{6,9},{7,8},{8,7},{9,6},... | collective-permute-start | bytes 417800 | tf_op jit(solution)/shard_map/ppermute | solution.py:280
  200.2 14.7 %collective-permute-start.77 = (bf16[272,256]{1,0:T(8,128)(2,1)S(1)}, bf16[272,256]{1,0:T(8,128)(2,1)S(1)}, u32[]{:S(2)}, u32[]{:S(2)}) collective-permute-start(bf16[272,256]{1,0:T(8,128)(2,1)S(1)} %gate.135.__2_), channel_id=1, source_target_pairs={{0,8},{1,9},{2,10},{3,11},{4,12},{5,13},{6,14},{7,15},{8,0},{9,1},... | collective-permute-start | bytes 417800 | tf_op jit(solution)/shard_map/ppermute | solution.py:280
  201.1 18.4 %collective-permute-start.75 = (bf16[272,256]{1,0:T(8,128)(2,1)S(1)}, bf16[272,256]{1,0:T(8,128)(2,1)S(1)}, u32[]{:S(2)}, u32[]{:S(2)}) collective-permute-start(bf16[272,256]{1,0:T(8,128)(2,1)S(1)} %gate.136.__2_), channel_id=1, source_target_pairs={{0,31},{1,30},{2,29},{3,28},{4,27},{5,26},{6,25},{7,24},{8,23},{9,... | collective-permute-start | bytes 417800 | tf_op jit(solution)/shard_map/ppermute | solution.py:280
  205.7 13.8 %collective-permute-start.76 = (bf16[272,256]{1,0:T(8,128)(2,1)S(1)}, bf16[272,256]{1,0:T(8,128)(2,1)S(1)}, u32[]{:S(2)}, u32[]{:S(2)}) collective-permute-start(bf16[272,256]{1,0:T(8,128)(2,1)S(1)} %gate.137.__2_), channel_id=1, source_target_pairs={{0,24},{1,25},{2,26},{3,27},{4,28},{5,29},{6,30},{7,31},{8,16},{9,... | collective-permute-start | bytes 417800 | tf_op jit(solution)/shard_map/ppermute | solution.py:280
  206.2 13.2 %collective-permute-start.72 = (bf16[272,256]{1,0:T(8,128)(2,1)S(1)}, bf16[272,256]{1,0:T(8,128)(2,1)S(1)}, u32[]{:S(2)}, u32[]{:S(2)}) collective-permute-start(bf16[272,256]{1,0:T(8,128)(2,1)S(1)} %gate.138.__2_), channel_id=1, source_target_pairs={{0,30},{1,31},{2,28},{3,29},{4,26},{5,27},{6,24},{7,25},{8,22},{9,... | collective-permute-start | bytes 417800 | tf_op jit(solution)/shard_map/ppermute | solution.py:280
  (34 other events, 352.7 us)

commit v8 on v7

--- a/solution.py
+++ b/solution.py
@@ -12,8 +12,8 @@
 STACK = 8
 SENDS = (
     ["T01", "C20", "T02", "C21", "T03", "C22", "T10", "C23", "T11", "T12", "T20", "T13", "C30", "T21", "C31"]
-    + ["T22", "C32", "E00", "C33", "T23", "E01", "T30", "T31", "E02", "T32", "E03", "T33", "E20", "E10", "E21", "E22"]
-    + ["E11", "E23", "E30", "E12", "E31", "E13", "E33", "E32"]
+    + ["T22", "C32", "E00", "C33", "T23", "E01", "T30", "E02", "T31", "T32", "E03", "T33", "E20", "E10", "E21", "E11"]
+    + ["E22", "E23", "E30", "E12", "E31", "E13", "E33", "E32"]
 )
 WINDOW = 5
 PIECES = 4

time: 227 us -> 229 us (level)
  starting transfers between devices: 136 us -> 140 us
  waiting for transfers between devices: 55.9 us -> 53.5 us
    ppermute x78, starting transfers between devices: 136 us -> 140 us  [move(): return lax.ppermute(x, ('dp', 'latent'), pairs)]
    ppermute x78, waiting for transfers between devices: 55.9 us -> 53.5 us  [move(): return lax.ppermute(x, ('dp', 'latent'), pairs)]
  transfers between devices with their start and end apart: 78 -> 78, of which waited for: 22 -> 18; matrix products, arithmetic and copies ran while one was open for 0% -> 0% of each run, Pallas kernels for 11% -> 11%
where the time goes in v8:
time: 229 us
  starting transfers between devices  140 us (61%)
  waiting for transfers between devices  53.5 us (23%)
  Pallas kernels  29.6 us (13%)
  local copies, waits for them, and re-layouts  3.35 us (1%)
    ppermute x78, starting transfers between devices, move(): return lax.ppermute(x, ('dp', 'latent'), pairs)  140 us
    ppermute x78, waiting for transfers between devices, move(): return lax.ppermute(x, ('dp', 'latent'), pairs)  53.5 us
    pallas_call x4, Pallas kernels, combine(): pl.pallas_call(functools.partial(combine_kernel, owners), grid_spec=pltpu...  12.3 us
    pallas_call x2, Pallas kernels, gradient(): pl.pallas_call(functools.partial(gradient_kernel, counts, last), in_specs...  7.44 us
  transfers between devices with their start and end apart: 78, of which 18 were waited for; matrix products, arithmetic and copies ran while one was open for 0% of the time, Pallas kernels for 11%

profile of v8, /device:TPU:0, one launch (start us, length us, event | category | flops | bytes accessed | tf_op | source)
XLA Modules:
  0.0 228.6 jit_solution(4068353973467841507)
XLA Ops:
  3.9 4.0 %collective-permute-start = (bf16[272,128]{1,0:T(8,128)(2,1)S(1)}, bf16[272,128]{1,0:T(8,128)(2,1)S(1)}, u32[]{:S(2)}, u32[]{:S(2)}) collective-permute-start(bf16[272,128]{1,0:T(8,128)(2,1)S(1)} %get-tuple-element.91), channel_id=1, source_target_pairs={{0,4},{1,5},{2,6},{3,7},{4,0},{5,1},{6,2},{7,3},{8,12},{9,13},{10,... | collective-permute-start | bytes 208904 | tf_op jit(solution)/shard_map/ppermute | solution.py:280
  11.4 2.5 %collective-permute-start.4 = (bf16[272,128]{1,0:T(8,128)(2,1)S(1)}, bf16[272,128]{1,0:T(8,128)(2,1)S(1)}, u32[]{:S(2)}, u32[]{:S(2)}) collective-permute-start(bf16[272,128]{1,0:T(8,128)(2,1)S(1)} %get-tuple-element.99), channel_id=1, source_target_pairs={{0,6},{1,7},{2,4},{3,5},{4,2},{5,3},{6,0},{7,1},{8,14},{9,15},{10,... | collective-permute-start | bytes 208904 | tf_op jit(solution)/shard_map/ppermute | solution.py:280
  15.5 2.7 %collective-permute-start.6 = (bf16[272,128]{1,0:T(8,128)(2,1)S(1)}, bf16[272,128]{1,0:T(8,128)(2,1)S(1)}, u32[]{:S(2)}, u32[]{:S(2)}) collective-permute-start(bf16[272,128]{1,0:T(8,128)(2,1)S(1)} %get-tuple-element.101), channel_id=1, source_target_pairs={{0,7},{1,6},{2,5},{3,4},{4,3},{5,2},{6,1},{7,0},{8,15},{9,14},{10,... | collective-permute-start | bytes 208904 | tf_op jit(solution)/shard_map/ppermute | solution.py:280
  18.2 2.2 copy-done
  30.1 5.2 %collective-permute-done.11.__1_.rest_0_ = bf16[272,256]{1,0:T(8,128)(2,1)S(1)} collective-permute-done((bf16[272,256]{1,0:T(8,128)(2,1)S(1)}, bf16[272,256]{1,0:T(8,128)(2,1)S(1)}, u32[]{:S(2)}, u32[]{:S(2)}) %collective-permute-start.11) | collective-permute-done | bytes 139296 | tf_op jit(solution)/shard_map/ppermute | solution.py:280
  35.3 2.8 %collective-permute-start.16 = (bf16[272,256]{1,0:T(8,128)(2,1)S(1)}, bf16[272,256]{1,0:T(8,128)(2,1)S(1)}, u32[]{:S(2)}, u32[]{:S(2)}) collective-permute-start(bf16[272,256]{1,0:T(8,128)(2,1)S(1)} %gate.75.__2_), channel_id=1, source_target_pairs={{0,6},{1,7},{2,4},{3,5},{4,2},{5,3},{6,0},{7,1},{8,14},{9,15},{10,... | collective-permute-start | bytes 417800 | tf_op jit(solution)/shard_map/ppermute | solution.py:280
  40.7 2.7 %collective-permute-start.20 = (bf16[272,256]{1,0:T(8,128)(2,1)S(1)}, bf16[272,256]{1,0:T(8,128)(2,1)S(1)}, u32[]{:S(2)}, u32[]{:S(2)}) collective-permute-start(bf16[272,256]{1,0:T(8,128)(2,1)S(1)} %gate.78.__2_), channel_id=1, source_target_pairs={{0,7},{1,6},{2,5},{3,4},{4,3},{5,2},{6,1},{7,0},{8,15},{9,14},{10,... | collective-permute-start | bytes 417800 | tf_op jit(solution)/shard_map/ppermute | solution.py:280
  47.4 3.1 %collective-permute-start.17 = (bf16[272,256]{1,0:T(8,128)(2,1)S(1)}, bf16[272,256]{1,0:T(8,128)(2,1)S(1)}, u32[]{:S(2)}, u32[]{:S(2)}) collective-permute-start(bf16[272,256]{1,0:T(8,128)(2,1)S(1)} %gate.82.__2_), channel_id=1, source_target_pairs={{0,16},{1,17},{2,18},{3,19},{4,20},{5,21},{6,22},{7,23},{8,24},{9,... | collective-permute-start | bytes 417800 | tf_op jit(solution)/shard_map/ppermute | solution.py:280
  50.5 4.4 %collective-permute-start.24 = (bf16[272,256]{1,0:T(8,128)(2,1)S(1)}, bf16[272,256]{1,0:T(8,128)(2,1)S(1)}, u32[]{:S(2)}, u32[]{:S(2)}) collective-permute-start(bf16[272,256]{1,0:T(8,128)(2,1)S(1)} %gate.83.__2_), channel_id=1, source_target_pairs={{0,13},{1,12},{2,15},{3,14},{4,9},{5,8},{6,11},{7,10},{8,5},{9,4},... | collective-permute-start | bytes 417800 | tf_op jit(solution)/shard_map/ppermute | solution.py:280
  55.2 3.3 %collective-permute-start.22 = (bf16[272,256]{1,0:T(8,128)(2,1)S(1)}, bf16[272,256]{1,0:T(8,128)(2,1)S(1)}, u32[]{:S(2)}, u32[]{:S(2)}) collective-permute-start(bf16[272,256]{1,0:T(8,128)(2,1)S(1)} %gate.85.__2_), channel_id=1, source_target_pairs={{0,14},{1,15},{2,12},{3,13},{4,10},{5,11},{6,8},{7,9},{8,6},{9,7},... | collective-permute-start | bytes 417800 | tf_op jit(solution)/shard_map/ppermute | solution.py:280
  60.6 2.5 %collective-permute-start.28 = (bf16[272,256]{1,0:T(8,128)(2,1)S(1)}, bf16[272,256]{1,0:T(8,128)(2,1)S(1)}, u32[]{:S(2)}, u32[]{:S(2)}) collective-permute-start(bf16[272,256]{1,0:T(8,128)(2,1)S(1)} %gate.87.__2_), channel_id=1, source_target_pairs={{0,20},{1,21},{2,22},{3,23},{4,16},{5,17},{6,18},{7,19},{8,28},{9,... | collective-permute-start | bytes 417800 | tf_op jit(solution)/shard_map/ppermute | solution.py:280
  64.5 3.0 %collective-permute-start.26 = (bf16[272,256]{1,0:T(8,128)(2,1)S(1)}, bf16[272,256]{1,0:T(8,128)(2,1)S(1)}, u32[]{:S(2)}, u32[]{:S(2)}) collective-permute-start(bf16[272,256]{1,0:T(8,128)(2,1)S(1)} %gate.89.__2_), channel_id=1, source_target_pairs={{0,15},{1,14},{2,13},{3,12},{4,11},{5,10},{6,9},{7,8},{8,7},{9,6},... | collective-permute-start | bytes 417800 | tf_op jit(solution)/shard_map/ppermute | solution.py:280
  68.3 3.3 %collective-permute-done.21.__1_.rest_5_ = bf16[272,256]{1,0:T(8,128)(2,1)S(1)} collective-permute-done((bf16[272,256]{1,0:T(8,128)(2,1)S(1)}, bf16[272,256]{1,0:T(8,128)(2,1)S(1)}, u32[]{:S(2)}, u32[]{:S(2)}) %collective-permute-start.21) | collective-permute-done | bytes 139296 | tf_op jit(solution)/shard_map/ppermute | solution.py:280
  71.8 7.5 %collective-permute-done.28.__1_.rest_0_ = bf16[272,256]{1,0:T(8,128)(2,1)S(1)} collective-permute-done((bf16[272,256]{1,0:T(8,128)(2,1)S(1)}, bf16[272,256]{1,0:T(8,128)(2,1)S(1)}, u32[]{:S(2)}, u32[]{:S(2)}) %collective-permute-start.28) | collective-permute-done | bytes 139296 | tf_op jit(solution)/shard_map/ppermute | solution.py:280
  79.2 3.9 %collective-permute-start.34 = (bf16[272,256]{1,0:T(8,128)(2,1)S(1)}, bf16[272,256]{1,0:T(8,128)(2,1)S(1)}, u32[]{:S(2)}, u32[]{:S(2)}) collective-permute-start(bf16[272,256]{1,0:T(8,128)(2,1)S(1)} %gate.93.__2_), channel_id=1, source_target_pairs={{0,18},{1,19},{2,16},{3,17},{4,22},{5,23},{6,20},{7,21},{8,26},{9,... | collective-permute-start | bytes 417800 | tf_op jit(solution)/shard_map/ppermute | solution.py:280
  85.7 3.1 %combine.4 = (bf16[128,8192]{1,0:T(8,128)(2,1)}, bf16[272,256]{1,0:T(8,128)(2,1)S(1)}, bf16[272,256]{1,0:T(8,128)(2,1)S(1)}, bf16[272,256]{1,0:T(8,128)(2,1)S(1)...) custom-call(s32[2]{0:T(128)S(1)} %pad_add_fusion.1.at_ref.place_in_r, ...), custom_call_target="tpu_custom_call" | custom-call | flops 285212672 | bytes 3276800 | tf_op jit(solution)/shard_map/combine/pallas_call | solution.py:375
  88.8 3.0 %collective-permute-start.38 = (bf16[272,256]{1,0:T(8,128)(2,1)S(1)}, bf16[272,256]{1,0:T(8,128)(2,1)S(1)}, u32[]{:S(2)}, u32[]{:S(2)}) collective-permute-start(bf16[272,256]{1,0:T(8,128)(2,1)S(1)} %gate.96.__2_), channel_id=1, source_target_pairs={{0,19},{1,18},{2,17},{3,16},{4,23},{5,22},{6,21},{7,20},{8,27},{9,... | collective-permute-start | bytes 417800 | tf_op jit(solution)/shard_map/ppermute | solution.py:280
  94.1 2.3 collective-permute-done.38.__1_.rest_5_
  96.4 3.4 %collective-permute-start.40 = (bf16[272,256]{1,0:T(8,128)(2,1)S(1)}, bf16[272,256]{1,0:T(8,128)(2,1)S(1)}, u32[]{:S(2)}, u32[]{:S(2)}) collective-permute-start(bf16[272,256]{1,0:T(8,128)(2,1)S(1)} %gate.101.__2_), channel_id=1, source_target_pairs={{0,23},{1,22},{2,21},{3,20},{4,19},{5,18},{6,17},{7,16},{8,31},{9,... | collective-permute-start | bytes 417800 | tf_op jit(solution)/shard_map/ppermute | solution.py:280
  100.5 3.7 %collective-permute-done.37.__1_.refs_0_ = bf16[272,256]{1,0:T(8,128)(2,1)S(1)} collective-permute-done((bf16[272,256]{1,0:T(8,128)(2,1)S(1)}, bf16[272,256]{1,0:T(8,128)(2,1)S(1)}, u32[]{:S(2)}, u32[]{:S(2)}) %collective-permute-start.37) | collective-permute-done | bytes 139296 | tf_op jit(solution)/shard_map/ppermute | solution.py:280
  104.2 3.0 %collective-permute-start.43 = (bf16[272,256]{1,0:T(8,128)(2,1)S(1)}, bf16[272,256]{1,0:T(8,128)(2,1)S(1)}, u32[]{:S(2)}, u32[]{:S(2)}) collective-permute-start(bf16[272,256]{1,0:T(8,128)(2,1)S(1)} %gate.103.__2_), channel_id=1, source_target_pairs={{0,5},{1,4},{2,7},{3,6},{4,1},{5,0},{6,3},{7,2},{8,13},{9,12},{10,... | collective-permute-start | bytes 417800 | tf_op jit(solution)/shard_map/ppermute | solution.py:280
  110.8 4.1 %collective-permute-start.48 = (bf16[272,256]{1,0:T(8,128)(2,1)S(1)}, bf16[272,256]{1,0:T(8,128)(2,1)S(1)}, u32[]{:S(2)}, u32[]{:S(2)}) collective-permute-start(bf16[272,256]{1,0:T(8,128)(2,1)S(1)} %gate.107.__2_), channel_id=1, source_target_pairs={{0,6},{1,7},{2,4},{3,5},{4,2},{5,3},{6,0},{7,1},{8,14},{9,15},{10,... | collective-permute-start | bytes 417800 | tf_op jit(solution)/shard_map/ppermute | solution.py:280
  114.9 4.8 %collective-permute-done.43.__1_.refs_2_ = bf16[272,256]{1,0:T(8,128)(2,1)S(1)} collective-permute-done((bf16[272,256]{1,0:T(8,128)(2,1)S(1)}, bf16[272,256]{1,0:T(8,128)(2,1)S(1)}, u32[]{:S(2)}, u32[]{:S(2)}) %collective-permute-start.43) | collective-permute-done | bytes 139296 | tf_op jit(solution)/shard_map/ppermute | solution.py:280
  119.7 2.9 %collective-permute-done.39.__1_.rest_0_ = bf16[272,256]{1,0:T(8,128)(2,1)S(1)} collective-permute-done((bf16[272,256]{1,0:T(8,128)(2,1)S(1)}, bf16[272,256]{1,0:T(8,128)(2,1)S(1)}, u32[]{:S(2)}, u32[]{:S(2)}) %collective-permute-start.39) | collective-permute-done | bytes 139296 | tf_op jit(solution)/shard_map/ppermute | solution.py:280
  125.6 4.6 %collective-permute-start.49 = (bf16[272,256]{1,0:T(8,128)(2,1)S(1)}, bf16[272,256]{1,0:T(8,128)(2,1)S(1)}, u32[]{:S(2)}, u32[]{:S(2)}) collective-permute-start(bf16[272,256]{1,0:T(8,128)(2,1)S(1)} %gate.112.__2_), channel_id=1, source_target_pairs={{0,27},{1,26},{2,25},{3,24},{4,31},{5,30},{6,29},{7,28},{8,19},{9,... | collective-permute-start | bytes 417800 | tf_op jit(solution)/shard_map/ppermute | solution.py:280
  130.2 3.3 %collective-permute-start.53 = (bf16[272,256]{1,0:T(8,128)(2,1)S(1)}, bf16[272,256]{1,0:T(8,128)(2,1)S(1)}, u32[]{:S(2)}, u32[]{:S(2)}) collective-permute-start(bf16[272,256]{1,0:T(8,128)(2,1)S(1)} %gate.113.__2_), channel_id=1, source_target_pairs={{0,7},{1,6},{2,5},{3,4},{4,3},{5,2},{6,1},{7,0},{8,15},{9,14},{10,... | collective-permute-start | bytes 417800 | tf_op jit(solution)/shard_map/ppermute | solution.py:280
  133.5 2.0 collective-permute-start.51
  135.4 5.0 %collective-permute-start.52 = (bf16[272,256]{1,0:T(8,128)(2,1)S(1)}, bf16[272,256]{1,0:T(8,128)(2,1)S(1)}, u32[]{:S(2)}, u32[]{:S(2)}) collective-permute-start(bf16[272,256]{1,0:T(8,128)(2,1)S(1)} %gate.115.__2_), channel_id=1, source_target_pairs={{0,24},{1,25},{2,26},{3,27},{4,28},{5,29},{6,30},{7,31},{8,16},{9,... | collective-permute-start | bytes 417800 | tf_op jit(solution)/shard_map/ppermute | solution.py:280
  140.4 3.1 %combine.5 = (bf16[128,8192]{1,0:T(8,128)(2,1)}, bf16[272,256]{1,0:T(8,128)(2,1)S(1)}, bf16[272,256]{1,0:T(8,128)(2,1)S(1)}, bf16[272,256]{1,0:T(8,128)(2,1)S(1)...) custom-call(s32[2]{0:T(128)S(1)} %pad_add_fusion.1.at_ref.place_in_r, ...), custom_call_target="tpu_custom_call", output_to_operand_aliasing={{0}: (15, {})} | custom-call | flops 285212672 | bytes 3276800 | tf_op jit(solution)/shard_map/combine/pallas_call | solution.py:375
  143.4 3.1 %combine.6 = (bf16[128,8192]{1,0:T(8,128)(2,1)}, bf16[272,256]{1,0:T(8,128)(2,1)S(1)}, bf16[272,256]{1,0:T(8,128)(2,1)S(1)}, bf16[272,256]{1,0:T(8,128)(2,1)S(1)...) custom-call(s32[2]{0:T(128)S(1)} %pad_add_fusion.1.at_ref.place_in_r, ...), custom_call_target="tpu_custom_call", output_to_operand_aliasing={{0}: (15, {})} | custom-call | flops 285212672 | bytes 3276800 | tf_op jit(solution)/shard_map/combine/pallas_call | solution.py:375
  147.1 2.9 %collective-permute-start.54 = (bf16[272,256]{1,0:T(8,128)(2,1)S(1)}, bf16[272,256]{1,0:T(8,128)(2,1)S(1)}, u32[]{:S(2)}, u32[]{:S(2)}) collective-permute-start(bf16[272,256]{1,0:T(8,128)(2,1)S(1)} %gate.118.__2_), channel_id=1, source_target_pairs={{0,12},{1,13},{2,14},{3,15},{4,8},{5,9},{6,10},{7,11},{8,4},{9,5},... | collective-permute-start | bytes 417800 | tf_op jit(solution)/shard_map/ppermute | solution.py:280
  150.0 2.1 collective-permute-start.61
  152.1 8.1 %collective-permute-start.60 = (bf16[272,256]{1,0:T(8,128)(2,1)S(1)}, bf16[272,256]{1,0:T(8,128)(2,1)S(1)}, u32[]{:S(2)}, u32[]{:S(2)}) collective-permute-start(bf16[272,256]{1,0:T(8,128)(2,1)S(1)} %gate.120.__2_), channel_id=1, source_target_pairs={{0,21},{1,20},{2,23},{3,22},{4,17},{5,16},{6,19},{7,18},{8,29},{9,... | collective-permute-start | bytes 417800 | tf_op jit(solution)/shard_map/ppermute | solution.py:280
  160.2 3.0 %collective-permute-start.58 = (bf16[272,256]{1,0:T(8,128)(2,1)S(1)}, bf16[272,256]{1,0:T(8,128)(2,1)S(1)}, u32[]{:S(2)}, u32[]{:S(2)}) collective-permute-start(bf16[272,256]{1,0:T(8,128)(2,1)S(1)} %gate.122.__2_), channel_id=1, source_target_pairs={{0,13},{1,12},{2,15},{3,14},{4,9},{5,8},{6,11},{7,10},{8,5},{9,4},... | collective-permute-start | bytes 417800 | tf_op jit(solution)/shard_map/ppermute | solution.py:280
  163.9 2.6 %collective-permute-start.66 = (bf16[272,256]{1,0:T(8,128)(2,1)S(1)}, bf16[272,256]{1,0:T(8,128)(2,1)S(1)}, u32[]{:S(2)}, u32[]{:S(2)}) collective-permute-start(bf16[272,256]{1,0:T(8,128)(2,1)S(1)} %gate.124.__2_), channel_id=1, source_target_pairs={{0,22},{1,23},{2,20},{3,21},{4,18},{5,19},{6,16},{7,17},{8,30},{9,... | collective-permute-start | bytes 417800 | tf_op jit(solution)/shard_map/ppermute | solution.py:280
  166.6 7.4 %collective-permute-done.60.__1_.refs_10_ = bf16[272,256]{1,0:T(8,128)(2,1)S(1)} collective-permute-done((bf16[272,256]{1,0:T(8,128)(2,1)S(1)}, bf16[272,256]{1,0:T(8,128)(2,1)S(1)}, u32[]{:S(2)}, u32[]{:S(2)}) %collective-permute-start.60) | collective-permute-done | bytes 139296 | tf_op jit(solution)/shard_map/ppermute | solution.py:280
  174.0 3.1 %combine.7 = (bf16[128,8192]{1,0:T(8,128)(2,1)}, bf16[272,256]{1,0:T(8,128)(2,1)S(1)}, bf16[272,256]{1,0:T(8,128)(2,1)S(1)}, bf16[272,256]{1,0:T(8,128)(2,1)S(1)...) custom-call(s32[2]{0:T(128)S(1)} %pad_add_fusion.1.at_ref.place_in_r, ...), custom_call_target="tpu_custom_call", output_to_operand_aliasing={{0}: (15, {})} | custom-call | flops 285212672 | bytes 3276800 | tf_op jit(solution)/shard_map/combine/pallas_call | solution.py:375
  177.1 2.6 %collective-permute-start.63 = (bf16[272,256]{1,0:T(8,128)(2,1)S(1)}, bf16[272,256]{1,0:T(8,128)(2,1)S(1)}, u32[]{:S(2)}, u32[]{:S(2)}) collective-permute-start(bf16[272,256]{1,0:T(8,128)(2,1)S(1)} %gate.127.__2_), channel_id=1, source_target_pairs={{0,16},{1,17},{2,18},{3,19},{4,20},{5,21},{6,22},{7,23},{8,24},{9,... | collective-permute-start | bytes 417800 | tf_op jit(solution)/shard_map/ppermute | solution.py:280
  179.7 2.1 collective-permute-start.62
  182.5 5.2 %collective-permute-done.65.__1_.refs_13_ = bf16[272,256]{1,0:T(8,128)(2,1)S(1)} collective-permute-done((bf16[272,256]{1,0:T(8,128)(2,1)S(1)}, bf16[272,256]{1,0:T(8,128)(2,1)S(1)}, u32[]{:S(2)}, u32[]{:S(2)}) %collective-permute-start.65) | collective-permute-done | bytes 139296 | tf_op jit(solution)/shard_map/ppermute | solution.py:280
  187.8 6.8 %collective-permute-start.69 = (bf16[272,256]{1,0:T(8,128)(2,1)S(1)}, bf16[272,256]{1,0:T(8,128)(2,1)S(1)}, u32[]{:S(2)}, u32[]{:S(2)}) collective-permute-start(bf16[272,256]{1,0:T(8,128)(2,1)S(1)} %gate.131.__2_), channel_id=1, source_target_pairs={{0,11},{1,10},{2,9},{3,8},{4,15},{5,14},{6,13},{7,12},{8,3},{9,2},... | collective-permute-start | bytes 417800 | tf_op jit(solution)/shard_map/ppermute | solution.py:280
  196.4 2.5 %collective-permute-start.67 = (bf16[272,256]{1,0:T(8,128)(2,1)S(1)}, bf16[272,256]{1,0:T(8,128)(2,1)S(1)}, u32[]{:S(2)}, u32[]{:S(2)}) collective-permute-start(bf16[272,256]{1,0:T(8,128)(2,1)S(1)} %gate.133.__2_), channel_id=1, source_target_pairs={{0,26},{1,27},{2,24},{3,25},{4,30},{5,31},{6,28},{7,29},{8,18},{9,... | collective-permute-start | bytes 417800 | tf_op jit(solution)/shard_map/ppermute | solution.py:280
  201.7 3.5 %collective-permute-start.75 = (bf16[272,256]{1,0:T(8,128)(2,1)S(1)}, bf16[272,256]{1,0:T(8,128)(2,1)S(1)}, u32[]{:S(2)}, u32[]{:S(2)}) collective-permute-start(bf16[272,256]{1,0:T(8,128)(2,1)S(1)} %gate.136.__2_), channel_id=1, source_target_pairs={{0,31},{1,30},{2,29},{3,28},{4,27},{5,26},{6,25},{7,24},{8,23},{9,... | collective-permute-start | bytes 417800 | tf_op jit(solution)/shard_map/ppermute | solution.py:280
  205.1 2.1 collective-permute-done.68.__1_.refs_26_
  209.6 3.6 %collective-permute-done.73.__1_.refs_22_ = bf16[272,256]{1,0:T(8,128)(2,1)S(1)} collective-permute-done((bf16[272,256]{1,0:T(8,128)(2,1)S(1)}, bf16[272,256]{1,0:T(8,128)(2,1)S(1)}, u32[]{:S(2)}, u32[]{:S(2)}) %collective-permute-start.73) | collective-permute-done | bytes 139296 | tf_op jit(solution)/shard_map/ppermute | solution.py:280
  213.2 7.8 %collective-permute-start.74 = (bf16[272,256]{1,0:T(8,128)(2,1)S(1)}, bf16[272,256]{1,0:T(8,128)(2,1)S(1)}, u32[]{:S(2)}, u32[]{:S(2)}) collective-permute-start(bf16[272,256]{1,0:T(8,128)(2,1)S(1)} %gate.139.refs_28_), channel_id=1, source_target_pairs={{0,27},{1,26},{2,25},{3,24},{4,31},{5,30},{6,29},{7,28},{8,19},{9,... | collective-permute-start | bytes 417800 | tf_op jit(solution)/shard_map/ppermute | solution.py:280
  220.9 4.6 %gradient.2.refs_4_ = f32[1024,2048]{1,0:T(8,128)S(1)} custom-call(bf16[1024,952]{1,0:T(8,128)(2,1)S(1)} %turn.3.codes_ref, bf16[272,256]{1,0:T(8,128)(2,1)S(1)} %collective-permute-done.37.__1_.refs_0_, bf16[272,256]{1,0:T(8,128)(2,1)S(1)} %collective-permute-done.36.__1_.refs_1_, bf16[272,256]{1,0:T(8,128)(2,1)S(1)} %collective-permute-done.43.__1_.refs_2_, ...), custom_call_target="tpu_custom_call" | custom-call | flops 3992977408 | bytes 8388608 | tf_op jit(solution)/shard_map/gradient/pallas_call | solution.py:410
  225.6 2.9 %gradient.3 = bf16[1024,2048]{1,0:T(8,128)(2,1)} custom-call(bf16[1024,136]{1,0:T(8,128)(2,1)S(1)} %turn.2.codes_ref, bf16[272,256]{1,0:T(8,128)(2,1)S(1)} %collective-permute-done.72.refs_0_, bf16[272,256]{1,0:T(8,128)(2,1)S(1)} %collective-permute-done.74.refs_1_, bf16[272,256]{1,0:T(8,128)(2,1)S(1)} %collective-permute-done.75.refs_2_, ...), custom_call_target="tpu_custom_call" | custom-call | flops 570425344 | bytes 8388608 | tf_op jit(solution)/shard_map/gradient/pallas_call | solution.py:410
  (205 shorter events, 50.5 us)
Async XLA Ops:
  24.6 13.5 %collective-permute-start.10 = (bf16[272,256]{1,0:T(8,128)(2,1)S(1)}, bf16[272,256]{1,0:T(8,128)(2,1)S(1)}, u32[]{:S(2)}, u32[]{:S(2)}) collective-permute-start(bf16[272,256]{1,0:T(8,128)(2,1)S(1)} %gate.71.refs_8_.__1_.refs_4_), channel_id=1, source_target_pairs={{0,1},{1,0},{2,3},{3,2},{4,5},{5,4},{6,7},{7,6},{8,9},{9,8},{10,11... | collective-permute-start | bytes 417800 | tf_op jit(solution)/shard_map/ppermute | solution.py:280
  25.7 13.6 %collective-permute-start.9 = (bf16[272,256]{1,0:T(8,128)(2,1)S(1)}, bf16[272,256]{1,0:T(8,128)(2,1)S(1)}, u32[]{:S(2)}, u32[]{:S(2)}) collective-permute-start(bf16[272,256]{1,0:T(8,128)(2,1)S(1)} %gate.72.__1_), channel_id=1, source_target_pairs={{0,5},{1,4},{2,7},{3,6},{4,1},{5,0},{6,3},{7,2},{8,13},{9,12},{10,... | collective-permute-start | bytes 417800 | tf_op jit(solution)/shard_map/ppermute | solution.py:280
  27.3 13.5 %collective-permute-start.13 = (bf16[272,256]{1,0:T(8,128)(2,1)S(1)}, bf16[272,256]{1,0:T(8,128)(2,1)S(1)}, u32[]{:S(2)}, u32[]{:S(2)}) collective-permute-start(bf16[272,256]{1,0:T(8,128)(2,1)S(1)} %gate.73.__2_), channel_id=1, source_target_pairs={{0,2},{1,3},{2,0},{3,1},{4,6},{5,7},{6,4},{7,5},{8,10},{9,11},{10,... | collective-permute-start | bytes 417800 | tf_op jit(solution)/shard_map/ppermute | solution.py:280
  28.5 16.4 %collective-permute-start.8 = (bf16[272,256]{1,0:T(8,128)(2,1)S(1)}, bf16[272,256]{1,0:T(8,128)(2,1)S(1)}, u32[]{:S(2)}, u32[]{:S(2)}) collective-permute-start(bf16[272,256]{1,0:T(8,128)(2,1)S(1)} %gate.74.__2_), channel_id=1, source_target_pairs={{0,16},{1,17},{2,18},{3,19},{4,20},{5,21},{6,22},{7,23},{8,24},{9,... | collective-permute-start | bytes 417800 | tf_op jit(solution)/shard_map/ppermute | solution.py:280
  50.5 12.6 %collective-permute-start.24 = (bf16[272,256]{1,0:T(8,128)(2,1)S(1)}, bf16[272,256]{1,0:T(8,128)(2,1)S(1)}, u32[]{:S(2)}, u32[]{:S(2)}) collective-permute-start(bf16[272,256]{1,0:T(8,128)(2,1)S(1)} %gate.83.__2_), channel_id=1, source_target_pairs={{0,13},{1,12},{2,15},{3,14},{4,9},{5,8},{6,11},{7,10},{8,5},{9,4},... | collective-permute-start | bytes 417800 | tf_op jit(solution)/shard_map/ppermute | solution.py:280
  55.2 12.8 %collective-permute-start.22 = (bf16[272,256]{1,0:T(8,128)(2,1)S(1)}, bf16[272,256]{1,0:T(8,128)(2,1)S(1)}, u32[]{:S(2)}, u32[]{:S(2)}) collective-permute-start(bf16[272,256]{1,0:T(8,128)(2,1)S(1)} %gate.85.__2_), channel_id=1, source_target_pairs={{0,14},{1,15},{2,12},{3,13},{4,10},{5,11},{6,8},{7,9},{8,6},{9,7},... | collective-permute-start | bytes 417800 | tf_op jit(solution)/shard_map/ppermute | solution.py:280
  58.5 13.1 %collective-permute-start.21 = (bf16[272,256]{1,0:T(8,128)(2,1)S(1)}, bf16[272,256]{1,0:T(8,128)(2,1)S(1)}, u32[]{:S(2)}, u32[]{:S(2)}) collective-permute-start(bf16[272,256]{1,0:T(8,128)(2,1)S(1)} %gate.86.__2_), channel_id=1, source_target_pairs={{0,11},{1,10},{2,9},{3,8},{4,15},{5,14},{6,13},{7,12},{8,3},{9,2},... | collective-permute-start | bytes 417800 | tf_op jit(solution)/shard_map/ppermute | solution.py:280
  60.6 18.6 %collective-permute-start.28 = (bf16[272,256]{1,0:T(8,128)(2,1)S(1)}, bf16[272,256]{1,0:T(8,128)(2,1)S(1)}, u32[]{:S(2)}, u32[]{:S(2)}) collective-permute-start(bf16[272,256]{1,0:T(8,128)(2,1)S(1)} %gate.87.__2_), channel_id=1, source_target_pairs={{0,20},{1,21},{2,22},{3,23},{4,16},{5,17},{6,18},{7,19},{8,28},{9,... | collective-permute-start | bytes 417800 | tf_op jit(solution)/shard_map/ppermute | solution.py:280
  63.1 16.1 %collective-permute-start.27 = (bf16[272,256]{1,0:T(8,128)(2,1)S(1)}, bf16[272,256]{1,0:T(8,128)(2,1)S(1)}, u32[]{:S(2)}, u32[]{:S(2)}) collective-permute-start(bf16[272,256]{1,0:T(8,128)(2,1)S(1)} %gate.88.__2_), channel_id=1, source_target_pairs={{0,17},{1,16},{2,19},{3,18},{4,21},{5,20},{6,23},{7,22},{8,25},{9,... | collective-permute-start | bytes 417800 | tf_op jit(solution)/shard_map/ppermute | solution.py:280
  64.5 18.6 %collective-permute-start.26 = (bf16[272,256]{1,0:T(8,128)(2,1)S(1)}, bf16[272,256]{1,0:T(8,128)(2,1)S(1)}, u32[]{:S(2)}, u32[]{:S(2)}) collective-permute-start(bf16[272,256]{1,0:T(8,128)(2,1)S(1)} %gate.89.__2_), channel_id=1, source_target_pairs={{0,15},{1,14},{2,13},{3,12},{4,11},{5,10},{6,9},{7,8},{8,7},{9,6},... | collective-permute-start | bytes 417800 | tf_op jit(solution)/shard_map/ppermute | solution.py:280
  68.0 15.1 %collective-permute-start.31 = (bf16[272,256]{1,0:T(8,128)(2,1)S(1)}, bf16[272,256]{1,0:T(8,128)(2,1)S(1)}, u32[]{:S(2)}, u32[]{:S(2)}) collective-permute-start(bf16[272,256]{1,0:T(8,128)(2,1)S(1)} %gate.90.__2_), channel_id=1, source_target_pairs={{0,8},{1,9},{2,10},{3,11},{4,12},{5,13},{6,14},{7,15},{8,0},{9,1},... | collective-permute-start | bytes 417800 | tf_op jit(solution)/shard_map/ppermute | solution.py:280
  71.6 17.2 %collective-permute-start.25 = (bf16[272,256]{1,0:T(8,128)(2,1)S(1)}, bf16[272,256]{1,0:T(8,128)(2,1)S(1)}, u32[]{:S(2)}, u32[]{:S(2)}) collective-permute-start(bf16[272,256]{1,0:T(8,128)(2,1)S(1)} %gate.91.__2_), channel_id=1, source_target_pairs={{0,8},{1,9},{2,10},{3,11},{4,12},{5,13},{6,14},{7,15},{8,0},{9,1},... | collective-permute-start | bytes 417800 | tf_op jit(solution)/shard_map/ppermute | solution.py:280
  79.2 13.3 %collective-permute-start.34 = (bf16[272,256]{1,0:T(8,128)(2,1)S(1)}, bf16[272,256]{1,0:T(8,128)(2,1)S(1)}, u32[]{:S(2)}, u32[]{:S(2)}) collective-permute-start(bf16[272,256]{1,0:T(8,128)(2,1)S(1)} %gate.93.__2_), channel_id=1, source_target_pairs={{0,18},{1,19},{2,16},{3,17},{4,22},{5,23},{6,20},{7,21},{8,26},{9,... | collective-permute-start | bytes 417800 | tf_op jit(solution)/shard_map/ppermute | solution.py:280
  92.8 14.4 %collective-permute-start.36 = (bf16[272,256]{1,0:T(8,128)(2,1)S(1)}, bf16[272,256]{1,0:T(8,128)(2,1)S(1)}, u32[]{:S(2)}, u32[]{:S(2)}) collective-permute-start(bf16[272,256]{1,0:T(8,128)(2,1)S(1)} %gate.99.__2_), channel_id=1, source_target_pairs={{0,1},{1,0},{2,3},{3,2},{4,5},{5,4},{6,7},{7,6},{8,9},{9,8},{10,11... | collective-permute-start | bytes 417800 | tf_op jit(solution)/shard_map/ppermute | solution.py:280
  94.1 13.1 %collective-permute-start.35 = (bf16[272,256]{1,0:T(8,128)(2,1)S(1)}, bf16[272,256]{1,0:T(8,128)(2,1)S(1)}, u32[]{:S(2)}, u32[]{:S(2)}) collective-permute-start(bf16[272,256]{1,0:T(8,128)(2,1)S(1)} %gate.100.__2_), channel_id=1, source_target_pairs={{0,8},{1,9},{2,10},{3,11},{4,12},{5,13},{6,14},{7,15},{8,0},{9,1},... | collective-permute-start | bytes 417800 | tf_op jit(solution)/shard_map/ppermute | solution.py:280
  96.4 13.3 %collective-permute-start.40 = (bf16[272,256]{1,0:T(8,128)(2,1)S(1)}, bf16[272,256]{1,0:T(8,128)(2,1)S(1)}, u32[]{:S(2)}, u32[]{:S(2)}) collective-permute-start(bf16[272,256]{1,0:T(8,128)(2,1)S(1)} %gate.101.__2_), channel_id=1, source_target_pairs={{0,23},{1,22},{2,21},{3,20},{4,19},{5,18},{6,17},{7,16},{8,31},{9,... | collective-permute-start | bytes 417800 | tf_op jit(solution)/shard_map/ppermute | solution.py:280
  104.2 15.4 %collective-permute-start.43 = (bf16[272,256]{1,0:T(8,128)(2,1)S(1)}, bf16[272,256]{1,0:T(8,128)(2,1)S(1)}, u32[]{:S(2)}, u32[]{:S(2)}) collective-permute-start(bf16[272,256]{1,0:T(8,128)(2,1)S(1)} %gate.103.__2_), channel_id=1, source_target_pairs={{0,5},{1,4},{2,7},{3,6},{4,1},{5,0},{6,3},{7,2},{8,13},{9,12},{10,... | collective-permute-start | bytes 417800 | tf_op jit(solution)/shard_map/ppermute | solution.py:280
  108.7 14.0 %collective-permute-start.39 = (bf16[272,256]{1,0:T(8,128)(2,1)S(1)}, bf16[272,256]{1,0:T(8,128)(2,1)S(1)}, u32[]{:S(2)}, u32[]{:S(2)}) collective-permute-start(bf16[272,256]{1,0:T(8,128)(2,1)S(1)} %gate.105.__2_), channel_id=1, source_target_pairs={{0,28},{1,29},{2,30},{3,31},{4,24},{5,25},{6,26},{7,27},{8,20},{9,... | collective-permute-start | bytes 417800 | tf_op jit(solution)/shard_map/ppermute | solution.py:280
  109.7 14.4 %collective-permute-start.41 = (bf16[272,256]{1,0:T(8,128)(2,1)S(1)}, bf16[272,256]{1,0:T(8,128)(2,1)S(1)}, u32[]{:S(2)}, u32[]{:S(2)}) collective-permute-start(bf16[272,256]{1,0:T(8,128)(2,1)S(1)} %gate.106.__2_), channel_id=1, source_target_pairs={{0,25},{1,24},{2,27},{3,26},{4,29},{5,28},{6,31},{7,30},{8,17},{9,... | collective-permute-start | bytes 417800 | tf_op jit(solution)/shard_map/ppermute | solution.py:280
  110.8 14.9 %collective-permute-start.48 = (bf16[272,256]{1,0:T(8,128)(2,1)S(1)}, bf16[272,256]{1,0:T(8,128)(2,1)S(1)}, u32[]{:S(2)}, u32[]{:S(2)}) collective-permute-start(bf16[272,256]{1,0:T(8,128)(2,1)S(1)} %gate.107.__2_), channel_id=1, source_target_pairs={{0,6},{1,7},{2,4},{3,5},{4,2},{5,3},{6,0},{7,1},{8,14},{9,15},{10,... | collective-permute-start | bytes 417800 | tf_op jit(solution)/shard_map/ppermute | solution.py:280
  119.6 13.8 %collective-permute-start.45 = (bf16[272,256]{1,0:T(8,128)(2,1)S(1)}, bf16[272,256]{1,0:T(8,128)(2,1)S(1)}, u32[]{:S(2)}, u32[]{:S(2)}) collective-permute-start(bf16[272,256]{1,0:T(8,128)(2,1)S(1)} %gate.109.__2_), channel_id=1, source_target_pairs={{0,29},{1,28},{2,31},{3,30},{4,25},{5,24},{6,27},{7,26},{8,21},{9,... | collective-permute-start | bytes 417800 | tf_op jit(solution)/shard_map/ppermute | solution.py:280
  122.7 12.7 %collective-permute-start.46 = (bf16[272,256]{1,0:T(8,128)(2,1)S(1)}, bf16[272,256]{1,0:T(8,128)(2,1)S(1)}, u32[]{:S(2)}, u32[]{:S(2)}) collective-permute-start(bf16[272,256]{1,0:T(8,128)(2,1)S(1)} %gate.110.__2_), channel_id=1, source_target_pairs={{0,26},{1,27},{2,24},{3,25},{4,30},{5,31},{6,28},{7,29},{8,18},{9,... | collective-permute-start | bytes 417800 | tf_op jit(solution)/shard_map/ppermute | solution.py:280
  124.1 22.4 %collective-permute-start.47 = (bf16[272,256]{1,0:T(8,128)(2,1)S(1)}, bf16[272,256]{1,0:T(8,128)(2,1)S(1)}, u32[]{:S(2)}, u32[]{:S(2)}) collective-permute-start(bf16[272,256]{1,0:T(8,128)(2,1)S(1)} %gate.111.__2_), channel_id=1, source_target_pairs={{0,30},{1,31},{2,28},{3,29},{4,26},{5,27},{6,24},{7,25},{8,22},{9,... | collective-permute-start | bytes 417800 | tf_op jit(solution)/shard_map/ppermute | solution.py:280
  125.6 20.9 %collective-permute-start.49 = (bf16[272,256]{1,0:T(8,128)(2,1)S(1)}, bf16[272,256]{1,0:T(8,128)(2,1)S(1)}, u32[]{:S(2)}, u32[]{:S(2)}) collective-permute-start(bf16[272,256]{1,0:T(8,128)(2,1)S(1)} %gate.112.__2_), channel_id=1, source_target_pairs={{0,27},{1,26},{2,25},{3,24},{4,31},{5,30},{6,29},{7,28},{8,19},{9,... | collective-permute-start | bytes 417800 | tf_op jit(solution)/shard_map/ppermute | solution.py:280
  130.2 16.9 %collective-permute-start.53 = (bf16[272,256]{1,0:T(8,128)(2,1)S(1)}, bf16[272,256]{1,0:T(8,128)(2,1)S(1)}, u32[]{:S(2)}, u32[]{:S(2)}) collective-permute-start(bf16[272,256]{1,0:T(8,128)(2,1)S(1)} %gate.113.__2_), channel_id=1, source_target_pairs={{0,7},{1,6},{2,5},{3,4},{4,3},{5,2},{6,1},{7,0},{8,15},{9,14},{10,... | collective-permute-start | bytes 417800 | tf_op jit(solution)/shard_map/ppermute | solution.py:280
  133.5 16.6 %collective-permute-start.51 = (bf16[272,256]{1,0:T(8,128)(2,1)S(1)}, bf16[272,256]{1,0:T(8,128)(2,1)S(1)}, u32[]{:S(2)}, u32[]{:S(2)}) collective-permute-start(bf16[272,256]{1,0:T(8,128)(2,1)S(1)} %gate.114.__2_), channel_id=1, source_target_pairs={{0,31},{1,30},{2,29},{3,28},{4,27},{5,26},{6,25},{7,24},{8,23},{9,... | collective-permute-start | bytes 417800 | tf_op jit(solution)/shard_map/ppermute | solution.py:280
  135.4 16.7 %collective-permute-start.52 = (bf16[272,256]{1,0:T(8,128)(2,1)S(1)}, bf16[272,256]{1,0:T(8,128)(2,1)S(1)}, u32[]{:S(2)}, u32[]{:S(2)}) collective-permute-start(bf16[272,256]{1,0:T(8,128)(2,1)S(1)} %gate.115.__2_), channel_id=1, source_target_pairs={{0,24},{1,25},{2,26},{3,27},{4,28},{5,29},{6,30},{7,31},{8,16},{9,... | collective-permute-start | bytes 417800 | tf_op jit(solution)/shard_map/ppermute | solution.py:280
  146.5 13.6 %collective-permute-start.56 = (bf16[272,256]{1,0:T(8,128)(2,1)S(1)}, bf16[272,256]{1,0:T(8,128)(2,1)S(1)}, u32[]{:S(2)}, u32[]{:S(2)}) collective-permute-start(bf16[272,256]{1,0:T(8,128)(2,1)S(1)} %gate.116.__2_), channel_id=1, source_target_pairs={{0,20},{1,21},{2,22},{3,23},{4,16},{5,17},{6,18},{7,19},{8,28},{9,... | collective-permute-start | bytes 417800 | tf_op jit(solution)/shard_map/ppermute | solution.py:280
  146.5 13.6 %collective-permute-start.55 = (bf16[272,256]{1,0:T(8,128)(2,1)S(1)}, bf16[272,256]{1,0:T(8,128)(2,1)S(1)}, u32[]{:S(2)}, u32[]{:S(2)}) collective-permute-start(bf16[272,256]{1,0:T(8,128)(2,1)S(1)} %gate.117.__2_), channel_id=1, source_target_pairs={{0,17},{1,16},{2,19},{3,18},{4,21},{5,20},{6,23},{7,22},{8,25},{9,... | collective-permute-start | bytes 417800 | tf_op jit(solution)/shard_map/ppermute | solution.py:280
  147.1 16.0 %collective-permute-start.54 = (bf16[272,256]{1,0:T(8,128)(2,1)S(1)}, bf16[272,256]{1,0:T(8,128)(2,1)S(1)}, u32[]{:S(2)}, u32[]{:S(2)}) collective-permute-start(bf16[272,256]{1,0:T(8,128)(2,1)S(1)} %gate.118.__2_), channel_id=1, source_target_pairs={{0,12},{1,13},{2,14},{3,15},{4,8},{5,9},{6,10},{7,11},{8,4},{9,5},... | collective-permute-start | bytes 417800 | tf_op jit(solution)/shard_map/ppermute | solution.py:280
  150.0 13.9 %collective-permute-start.61 = (bf16[272,256]{1,0:T(8,128)(2,1)S(1)}, bf16[272,256]{1,0:T(8,128)(2,1)S(1)}, u32[]{:S(2)}, u32[]{:S(2)}) collective-permute-start(bf16[272,256]{1,0:T(8,128)(2,1)S(1)} %gate.119.__2_), channel_id=1, source_target_pairs={{0,9},{1,8},{2,11},{3,10},{4,13},{5,12},{6,15},{7,14},{8,1},{9,0},... | collective-permute-start | bytes 417800 | tf_op jit(solution)/shard_map/ppermute | solution.py:280
  152.1 21.9 %collective-permute-start.60 = (bf16[272,256]{1,0:T(8,128)(2,1)S(1)}, bf16[272,256]{1,0:T(8,128)(2,1)S(1)}, u32[]{:S(2)}, u32[]{:S(2)}) collective-permute-start(bf16[272,256]{1,0:T(8,128)(2,1)S(1)} %gate.120.__2_), channel_id=1, source_target_pairs={{0,21},{1,20},{2,23},{3,22},{4,17},{5,16},{6,19},{7,18},{8,29},{9,... | collective-permute-start | bytes 417800 | tf_op jit(solution)/shard_map/ppermute | solution.py:280
  160.2 16.9 %collective-permute-start.59 = (bf16[272,256]{1,0:T(8,128)(2,1)S(1)}, bf16[272,256]{1,0:T(8,128)(2,1)S(1)}, u32[]{:S(2)}, u32[]{:S(2)}) collective-permute-start(bf16[272,256]{1,0:T(8,128)(2,1)S(1)} %gate.121.__2_), channel_id=1, source_target_pairs={{0,18},{1,19},{2,16},{3,17},{4,22},{5,23},{6,20},{7,21},{8,26},{9,... | collective-permute-start | bytes 417800 | tf_op jit(solution)/shard_map/ppermute | solution.py:280
  160.2 16.9 %collective-permute-start.58 = (bf16[272,256]{1,0:T(8,128)(2,1)S(1)}, bf16[272,256]{1,0:T(8,128)(2,1)S(1)}, u32[]{:S(2)}, u32[]{:S(2)}) collective-permute-start(bf16[272,256]{1,0:T(8,128)(2,1)S(1)} %gate.122.__2_), channel_id=1, source_target_pairs={{0,13},{1,12},{2,15},{3,14},{4,9},{5,8},{6,11},{7,10},{8,5},{9,4},... | collective-permute-start | bytes 417800 | tf_op jit(solution)/shard_map/ppermute | solution.py:280
  163.2 16.6 %collective-permute-start.57 = (bf16[272,256]{1,0:T(8,128)(2,1)S(1)}, bf16[272,256]{1,0:T(8,128)(2,1)S(1)}, u32[]{:S(2)}, u32[]{:S(2)}) collective-permute-start(bf16[272,256]{1,0:T(8,128)(2,1)S(1)} %gate.123.__2_), channel_id=1, source_target_pairs={{0,10},{1,11},{2,8},{3,9},{4,14},{5,15},{6,12},{7,13},{8,2},{9,3},... | collective-permute-start | bytes 417800 | tf_op jit(solution)/shard_map/ppermute | solution.py:280
  163.9 17.9 %collective-permute-start.66 = (bf16[272,256]{1,0:T(8,128)(2,1)S(1)}, bf16[272,256]{1,0:T(8,128)(2,1)S(1)}, u32[]{:S(2)}, u32[]{:S(2)}) collective-permute-start(bf16[272,256]{1,0:T(8,128)(2,1)S(1)} %gate.124.__2_), channel_id=1, source_target_pairs={{0,22},{1,23},{2,20},{3,21},{4,18},{5,19},{6,16},{7,17},{8,30},{9,... | collective-permute-start | bytes 417800 | tf_op jit(solution)/shard_map/ppermute | solution.py:280
  174.0 13.8 %collective-permute-start.65 = (bf16[272,256]{1,0:T(8,128)(2,1)S(1)}, bf16[272,256]{1,0:T(8,128)(2,1)S(1)}, u32[]{:S(2)}, u32[]{:S(2)}) collective-permute-start(bf16[272,256]{1,0:T(8,128)(2,1)S(1)} %gate.125.__2_), channel_id=1, source_target_pairs={{0,19},{1,18},{2,17},{3,16},{4,23},{5,22},{6,21},{7,20},{8,27},{9,... | collective-permute-start | bytes 417800 | tf_op jit(solution)/shard_map/ppermute | solution.py:280
  177.1 17.5 %collective-permute-start.63 = (bf16[272,256]{1,0:T(8,128)(2,1)S(1)}, bf16[272,256]{1,0:T(8,128)(2,1)S(1)}, u32[]{:S(2)}, u32[]{:S(2)}) collective-permute-start(bf16[272,256]{1,0:T(8,128)(2,1)S(1)} %gate.127.__2_), channel_id=1, source_target_pairs={{0,16},{1,17},{2,18},{3,19},{4,20},{5,21},{6,22},{7,23},{8,24},{9,... | collective-permute-start | bytes 417800 | tf_op jit(solution)/shard_map/ppermute | solution.py:280
  179.7 16.7 %collective-permute-start.62 = (bf16[272,256]{1,0:T(8,128)(2,1)S(1)}, bf16[272,256]{1,0:T(8,128)(2,1)S(1)}, u32[]{:S(2)}, u32[]{:S(2)}) collective-permute-start(bf16[272,256]{1,0:T(8,128)(2,1)S(1)} %gate.128.__2_), channel_id=1, source_target_pairs={{0,28},{1,29},{2,30},{3,31},{4,24},{5,25},{6,26},{7,27},{8,20},{9,... | collective-permute-start | bytes 417800 | tf_op jit(solution)/shard_map/ppermute | solution.py:280
  181.8 17.1 %collective-permute-start.71 = (bf16[272,256]{1,0:T(8,128)(2,1)S(1)}, bf16[272,256]{1,0:T(8,128)(2,1)S(1)}, u32[]{:S(2)}, u32[]{:S(2)}) collective-permute-start(bf16[272,256]{1,0:T(8,128)(2,1)S(1)} %gate.129.__2_), channel_id=1, source_target_pairs={{0,25},{1,24},{2,27},{3,26},{4,29},{5,28},{6,31},{7,30},{8,17},{9,... | collective-permute-start | bytes 417800 | tf_op jit(solution)/shard_map/ppermute | solution.py:280
  187.8 13.0 %collective-permute-start.70 = (bf16[272,256]{1,0:T(8,128)(2,1)S(1)}, bf16[272,256]{1,0:T(8,128)(2,1)S(1)}, u32[]{:S(2)}, u32[]{:S(2)}) collective-permute-start(bf16[272,256]{1,0:T(8,128)(2,1)S(1)} %gate.130.__2_), channel_id=1, source_target_pairs={{0,14},{1,15},{2,12},{3,13},{4,10},{5,11},{6,8},{7,9},{8,6},{9,7},... | collective-permute-start | bytes 417800 | tf_op jit(solution)/shard_map/ppermute | solution.py:280
  187.8 13.9 %collective-permute-start.69 = (bf16[272,256]{1,0:T(8,128)(2,1)S(1)}, bf16[272,256]{1,0:T(8,128)(2,1)S(1)}, u32[]{:S(2)}, u32[]{:S(2)}) collective-permute-start(bf16[272,256]{1,0:T(8,128)(2,1)S(1)} %gate.131.__2_), channel_id=1, source_target_pairs={{0,11},{1,10},{2,9},{3,8},{4,15},{5,14},{6,13},{7,12},{8,3},{9,2},... | collective-permute-start | bytes 417800 | tf_op jit(solution)/shard_map/ppermute | solution.py:280
  194.6 12.6 %collective-permute-start.68 = (bf16[272,256]{1,0:T(8,128)(2,1)S(1)}, bf16[272,256]{1,0:T(8,128)(2,1)S(1)}, u32[]{:S(2)}, u32[]{:S(2)}) collective-permute-start(bf16[272,256]{1,0:T(8,128)(2,1)S(1)} %gate.132.__2_), channel_id=1, source_target_pairs={{0,29},{1,28},{2,31},{3,30},{4,25},{5,24},{6,27},{7,26},{8,21},{9,... | collective-permute-start | bytes 417800 | tf_op jit(solution)/shard_map/ppermute | solution.py:280
  198.9 14.3 %collective-permute-start.73 = (bf16[272,256]{1,0:T(8,128)(2,1)S(1)}, bf16[272,256]{1,0:T(8,128)(2,1)S(1)}, u32[]{:S(2)}, u32[]{:S(2)}) collective-permute-start(bf16[272,256]{1,0:T(8,128)(2,1)S(1)} %gate.134.__2_), channel_id=1, source_target_pairs={{0,15},{1,14},{2,13},{3,12},{4,11},{5,10},{6,9},{7,8},{8,7},{9,6},... | collective-permute-start | bytes 417800 | tf_op jit(solution)/shard_map/ppermute | solution.py:280
  200.7 20.2 %collective-permute-start.77 = (bf16[272,256]{1,0:T(8,128)(2,1)S(1)}, bf16[272,256]{1,0:T(8,128)(2,1)S(1)}, u32[]{:S(2)}, u32[]{:S(2)}) collective-permute-start(bf16[272,256]{1,0:T(8,128)(2,1)S(1)} %gate.135.__2_), channel_id=1, source_target_pairs={{0,8},{1,9},{2,10},{3,11},{4,12},{5,13},{6,14},{7,15},{8,0},{9,1},... | collective-permute-start | bytes 417800 | tf_op jit(solution)/shard_map/ppermute | solution.py:280
  201.7 23.9 %collective-permute-start.75 = (bf16[272,256]{1,0:T(8,128)(2,1)S(1)}, bf16[272,256]{1,0:T(8,128)(2,1)S(1)}, u32[]{:S(2)}, u32[]{:S(2)}) collective-permute-start(bf16[272,256]{1,0:T(8,128)(2,1)S(1)} %gate.136.__2_), channel_id=1, source_target_pairs={{0,31},{1,30},{2,29},{3,28},{4,27},{5,26},{6,25},{7,24},{8,23},{9,... | collective-permute-start | bytes 417800 | tf_op jit(solution)/shard_map/ppermute | solution.py:280
  207.2 18.3 %collective-permute-start.76 = (bf16[272,256]{1,0:T(8,128)(2,1)S(1)}, bf16[272,256]{1,0:T(8,128)(2,1)S(1)}, u32[]{:S(2)}, u32[]{:S(2)}) collective-permute-start(bf16[272,256]{1,0:T(8,128)(2,1)S(1)} %gate.137.__2_), channel_id=1, source_target_pairs={{0,24},{1,25},{2,26},{3,27},{4,28},{5,29},{6,30},{7,31},{8,16},{9,... | collective-permute-start | bytes 417800 | tf_op jit(solution)/shard_map/ppermute | solution.py:280
  208.3 17.2 %collective-permute-start.72 = (bf16[272,256]{1,0:T(8,128)(2,1)S(1)}, bf16[272,256]{1,0:T(8,128)(2,1)S(1)}, u32[]{:S(2)}, u32[]{:S(2)}) collective-permute-start(bf16[272,256]{1,0:T(8,128)(2,1)S(1)} %gate.138.__2_), channel_id=1, source_target_pairs={{0,30},{1,31},{2,28},{3,29},{4,26},{5,27},{6,24},{7,25},{8,22},{9,... | collective-permute-start | bytes 417800 | tf_op jit(solution)/shard_map/ppermute | solution.py:280
  (34 other events, 359.8 us)
